TPU v7x, 32 devices: a whole 2x2x4 slice. The times are simulated.
32 devices in a mesh: seq: 8 (over z, x), tp: 4 (over y, core).
Axes of the slice: x: 2, y: 2, z: 4, core: 2. Of those that a mesh axis runs over, the one named last changes fastest.
Arguments:
- panels: bfloat16 [256, 8, 5120], P('seq', None, 'tp'), may hold values from -60 to 60
- w_merge: bfloat16 [5120, 8192], P('seq', 'tp'), may hold values from -2 to 2
- ln_gain: bfloat16 [8192], P('tp'), may hold values from 0.099609375 to 1.8984375
- w_kv: bfloat16 [8192, 1024], P('tp'), may hold values from -0.0625 to 0.0625
- page_src: int32 [256, 1], P('seq'), may hold values from 0 to 7; in each aligned block of 32 rows (0 to 31, 32 to 63, ...) at most 8 rows name the same one
- page_tile: int32 [256], P('seq'), may hold values from 0 to 31
- doc_pages: int32 [8, 4], P('seq'), may hold values from 1 to 16, 32 in all within a row
- prefix_id: int32 [32], P('seq'), may hold values from 0 to 7
- prefix_cache: bfloat16 [8, 32, 1024], P('seq', None, 'tp'), may hold values from -4 to 4
- queries: bfloat16 [32, 128, 4096], P('seq', None, 'tp'), may hold values from -9 to 9
- text_kv: bfloat16 [32, 128, 1024], P('seq', None, 'tp'), may hold values from -4 to 4
Outputs:
- attended: bfloat16 [32, 128, 4096], P('seq', None, 'tp')
- vision_kv: bfloat16 [2048, 1024], P('seq', 'tp')
Inputs may be any that keep to these rules, and one draw needn't show every extreme that they name: `page_src`: in the 32 rows of one owner index (aligned blocks), no encoder index is named more than 8 times, and some encoder index is named exactly 8 times in some block.
All inputs are finite; a program needn't handle non-finite values.
Results may differ from a plain program's by a relative error of at most 0.015.
Values may be sent and summed in bfloat16 or wider, within the bound.
No kernel may reach another device: no remote copies, remote signals or barrier semaphores. Data moves between devices by JAX's collectives and lax.ppermute only.
A program may use at most 128 MiB of HBM per device.

v0:
```python
import functools

import jax
import jax.numpy as jnp
from jax import lax
from jax.experimental import pallas as pl
from jax.experimental.pallas import tpu as pltpu
from jax.sharding import PartitionSpec as P

D = 8192
HD = 128
GROUP = 8
MOST_PAGES = 16
VMEM = 16 * 1024 * 1024


def bits_of(count):
    return [1 << bit for bit in range(count.bit_length() - 1)]


def flip(value, axis, bit):
    count = lax.axis_size(axis)
    return lax.ppermute(value, axis, [(i, i ^ bit) for i in range(count)])


def transpose_panels(local, swap):
    seq_count, tp_count = lax.axis_size("seq"), lax.axis_size("tp")
    width = seq_count // tp_count
    half = tp_count // 2
    pairs = []
    for origin in range(tp_count):
        for inner in range(width):
            for block in range(tp_count):
                source = (origin * width + inner) * tp_count + (block ^ swap)
                slot = ((origin ^ block) & 1) * half + origin // 2
                pairs.append((source, (block * width + inner) * tp_count + slot))
    return lax.ppermute(local, ("seq", "tp"), pairs)


def share_panels(moved):
    held = [moved]
    bits = bits_of(lax.axis_size("tp"))
    for bit in bits[-1:] + bits[:-1]:
        held = held + [flip(piece, "tp", bit) for piece in held]
    return held


def panel_base():
    group = lax.axis_index("seq") // (lax.axis_size("seq") // lax.axis_size("tp"))
    place = lax.axis_index("tp")
    half = lax.axis_size("tp") // 2
    return 2 * (place % half) + ((place // half) ^ (group & 1))


ROLE_GROUPS = (3, 2, 1, 0)


def order_kernel(share, scalars_ref, *refs):
    out_ref = refs[-1]
    rows, depth = refs[0].shape
    members = depth // share
    for place in range(4):
        at = pl.ds(pl.multiple_of(scalars_ref[place] * rows, rows), rows)
        for member in range(members):
            if members == 1:
                out_ref[at, :] = refs[place][...]
            else:
                source = lax.rem(scalars_ref[4] + member, members)
                columns = pl.ds(pl.multiple_of(source * share, share), share)
                out_ref[at, member * share : (member + 1) * share] = refs[place][:, columns]


def order_rows(scalars, held, share):
    rows, depth = held[0].shape
    return pl.pallas_call(
        functools.partial(order_kernel, share),
        grid_spec=pltpu.PrefetchScalarGridSpec(
            num_scalar_prefetch=1,
            grid=(1,),
            in_specs=[pl.BlockSpec((rows, depth), lambda i, scalars: (0, 0))] * 4,
            out_specs=pl.BlockSpec((4 * rows, depth), lambda i, scalars: (0, 0)),
        ),
        out_shape=jax.ShapeDtypeStruct((4 * rows, depth), jnp.bfloat16),
        compiler_params=pltpu.CompilerParams(vmem_limit_bytes=VMEM),
        cost_estimate=pl.CostEstimate(flops=0, bytes_accessed=2 * depth, transcendentals=0),
    )(scalars, *held)


def partial_kernel(halves, *refs):
    rows_refs, weights_refs = refs[:halves], refs[halves:-2]
    inner_ref, end_ref = refs[-2:]
    for half, rows_ref in enumerate(rows_refs):
        total = None
        at = 0
        for weights_ref in weights_refs:
            depth = weights_ref.shape[0]
            term = jnp.dot(
                rows_ref[:, at : at + depth],
                weights_ref[...],
                preferred_element_type=jnp.float32,
            )
            total = term if total is None else total + term
            at += depth
        total = total.astype(jnp.bfloat16)
        rows = total.shape[0] // 4
        for role in range(3):
            to = (role * halves + half) * rows
            inner_ref[to : to + rows] = total[role * rows : (role + 1) * rows]
        end_ref[half * rows : (half + 1) * rows] = total[3 * rows :]


def partial_products(held, weights, count):
    halves = len(held)
    rows, depth = held[0].shape
    rows = rows * halves
    tile = min(count, 256)

    def block(used, first):
        return pl.BlockSpec((used, tile), lambda i: (0, i + first // tile))

    outs = (3 * rows // 4, rows // 4)
    return pl.pallas_call(
        functools.partial(partial_kernel, halves),
        grid=(count // tile,),
        in_specs=[pl.BlockSpec((rows // halves, depth), lambda i: (0, 0))] * halves
        + [block(used, first) for _, used, first in weights],
        out_specs=[pl.BlockSpec((out, tile), lambda i: (0, i)) for out in outs],
        out_shape=[jax.ShapeDtypeStruct((out, count), jnp.bfloat16) for out in outs],
        compiler_params=pltpu.CompilerParams(vmem_limit_bytes=VMEM),
        cost_estimate=pl.CostEstimate(flops=0, bytes_accessed=2 * count, transcendentals=0),
    )(*held, *[array for array, _, _ in weights])


def along(pairs):
    width = lax.axis_size("seq") // lax.axis_size("tp")
    return [(a * width + i, b * width + i) for a, b in pairs for i in range(width)]


INWARD = ((0, 1), (3, 2))
OUTWARD = ((1, 0), (2, 3))
ACROSS = ((1, 2), (2, 1))
BEYOND = ((1, 3), (2, 0))


def ride(value, extra):
    return jnp.concatenate([value] + extra, axis=0) if extra else value


def send_sums(parts, small):
    inner, end = parts
    inward = lax.ppermute(ride(inner, small), "seq", along(INWARD))
    outward = lax.ppermute(ride(end, small), "seq", along(OUTWARD))
    return inward, outward


def finish_sums(parts, arrived, is_end, small):
    inner, end = parts
    inward, outward = arrived
    rows = end.shape[0]

    def add(mine, other):
        return (mine.astype(jnp.float32) + other.astype(jnp.float32)).astype(jnp.bfloat16)

    def part(value, first, index=0):
        count = small[0].shape[0]
        return value[first + index * count : first + (index + 1) * count]

    extra = [part(inward, 3 * rows)] + small if small else []
    beyond = lax.ppermute(ride(add(inner[:rows], inward[:rows]), extra), "seq", along(BEYOND))
    across = lax.ppermute(
        ride(add(inner[rows : 2 * rows], inward[rows : 2 * rows]), extra), "seq", along(ACROSS)
    )
    at_end = end.astype(jnp.float32) + outward[:rows] + beyond[:rows]
    at_middle = inner[2 * rows :].astype(jnp.float32) + inward[2 * rows : 3 * rows] + across[:rows]
    shared = None
    if small:
        ends = [part(outward, rows), part(beyond, rows, 1), part(beyond, rows, 0)]
        middles = [part(inward, 3 * rows), part(across, rows, 0), part(across, rows, 1)]
        shared = small + [jnp.where(is_end, e, m) for e, m in zip(ends, middles)]
    return jnp.where(is_end, at_end, at_middle).astype(jnp.bfloat16), shared


PLAN = (((0,), 0, 4), ((1,), 0, 4), ((0, 1), 4, 2), ((0, 1), 6, 2))
RIDE = 2


def merge_tiles(panels, w_merge, ln_gain, w_kv, small):
    seq_count, tp_count = lax.axis_size("seq"), lax.axis_size("tp")
    assert tp_count == 4 and seq_count % 4 == 0
    width = seq_count // tp_count
    tiles, panel_rows, depth = panels.shape
    share = w_merge.shape[0]
    group = lax.axis_index("seq") // width
    member = lax.axis_index("seq") % width
    is_end = (group == 0) | (group == 3)
    local = panels.reshape(tiles * panel_rows, depth)
    half = local.shape[0] // 2
    swapped = flip(local[half:], "tp", 2)
    moved = [transpose_panels(local[:half], 0), transpose_panels(swapped, 2)]
    columns = w_merge.shape[1] // 2
    small = small.reshape(-1, columns)
    extra = small.shape[0]
    received = []
    for side in range(2):
        own = w_merge[:, side * columns : (side + 1) * columns]
        if side == 1:
            own = jnp.concatenate([own, small], axis=0)
            own, _ = lax.optimization_barrier((own, swapped))
        others = []
        for offset in range(1, width):
            pairs = [
                (g * width + (i + offset) % width, g * width + i)
                for g in range(tp_count)
                for i in range(width)
            ]
            others.append(lax.ppermute(own, "seq", pairs))
        received.append(others)
    aligned = width == 2 and share % 128 == 0
    if not aligned:
        share = depth
    shift = jnp.where(group < 2, 0, 3)
    groups = (panel_base() ^ jnp.arange(4, dtype=jnp.int32)) ^ shift
    roles = jnp.array([ROLE_GROUPS.index(g) for g in range(4)], jnp.int32)[groups]
    scalars = jnp.concatenate([roles, jnp.full((4,), member, jnp.int32)])
    early = share_panels(moved[0])
    early, moved[1] = lax.optimization_barrier((early, moved[1]))
    held = [order_rows(scalars, early, share)]
    kv = [0.0, 0.0]
    squares = [0.0, 0.0]
    everyone = None
    eighth = w_merge.shape[1] // 8
    sent = []
    for step in range(len(PLAN) + 1):
        if step < len(PLAN):
            halves, first, count = PLAN[step]
            first, count = first * eighth, count * eighth
            if step == 1:
                late, _ = lax.optimization_barrier((moved[1], sent[0][0][0]))
                held.append(order_rows(scalars, share_panels(late), share))
            if step == RIDE:
                received[1], _ = lax.optimization_barrier((received[1], sent[step - 1][0][0]))
                small = [small] + [other[-extra:] for other in received[1]]
                small_shape = (width,) + small[0].shape
                small = [jnp.stack(small).reshape(-1, count)]
            side = first // columns
            inside = first - side * columns
            if aligned:
                operands = [(w_merge, share, first), (received[side][0], share, inside)]
            else:
                parts = [w_merge[:, side * columns : (side + 1) * columns]]
                parts += [other[: w_merge.shape[0]] for other in received[side]]
                parts = jnp.concatenate(parts, axis=0)
                operands = [(jnp.roll(parts, member * w_merge.shape[0], axis=0), depth, inside)]
            rows = [held[h] for h in halves]
            if step >= 2:
                rows, _ = lax.optimization_barrier((rows, sent[step - 2][1][0]))
            parts = partial_products(rows, operands, count)
            riding = small if step == RIDE else []
            sent.append((parts, send_sums(parts, riding), riding))
        if step >= 1:
            parts, arrived, riding = sent[step - 1]
            if step < len(PLAN):
                arrived, _ = lax.optimization_barrier((arrived, sent[step][0][0]))
            halves, first, count = PLAN[step - 1]
            first, count = first * eighth, count * eighth
            merged, shared = finish_sums(parts, arrived, is_end, riding)
            if shared is not None:
                everyone = jnp.stack(shared).reshape((4,) + small_shape)
            merged = merged.astype(jnp.float32)
            at = slice(first, first + count)
            gained = (merged * ln_gain[at].astype(jnp.float32)[None, :]).astype(jnp.bfloat16)
            squared = jnp.sum(merged * merged, axis=1)
            product = jnp.dot(gained, w_kv[at], preferred_element_type=jnp.float32)
            for i, h in enumerate(halves):
                squares[h] = squares[h] + squared[i * half : (i + 1) * half]
                kv[h] = kv[h] + product[i * half : (i + 1) * half]
    return jnp.concatenate(kv), jnp.concatenate(squares), everyone


def scatter_heads(kv, squares):
    tp_count = lax.axis_size("tp")
    place = lax.axis_index("tp")
    rows = kv.shape[0]
    blocks = jnp.stack(jnp.split(kv, tp_count, axis=1))
    for bit in bits_of(tp_count):
        paired = blocks.reshape(blocks.shape[0] // 2, 2, rows, blocks.shape[2])
        mine = (place // bit) % 2
        keep = lax.dynamic_index_in_dim(paired, mine, 1, keepdims=False)
        give = lax.dynamic_index_in_dim(paired, 1 - mine, 1, keepdims=False)
        blocks = keep + flip(give.astype(jnp.bfloat16), "tp", bit).astype(jnp.float32)
        squares = squares + flip(squares, "tp", bit)
    return blocks[0], squares


SMALL_ROWS = 64


def pack_small(prefix_cache, sources, tiles):
    width = prefix_cache.shape[2]
    asks = jnp.stack([sources, tiles]).astype(jnp.bfloat16)
    rows = SMALL_ROWS - prefix_cache.shape[1]
    asks = jnp.pad(asks, ((0, rows - 2), (0, width - asks.shape[1])))
    return jnp.concatenate([prefix_cache[0], asks], axis=0)


def attend_kernel(
    place_ref, query_ref, prefix_ref, text_ref, pages_ref, pick_ref, seen_ref, all_ref, out_ref, vision_ref
):
    pages = pages_ref[...]
    count = pages.shape[0]

    def pick(index):
        one_hot = lax.broadcasted_iota(jnp.int32, (index.shape[0], count), 1) == index
        one_hot = jnp.where(one_hot, 1.0, 0.0).astype(jnp.bfloat16)
        return jnp.dot(one_hot, pages, preferred_element_type=jnp.float32).astype(jnp.bfloat16)

    @pl.when(pl.program_id(0) == 0)
    def _():
        vision_ref[...] = pick(all_ref[...])

    window = pick(pick_ref[0])
    keys_values = jnp.concatenate([prefix_ref[0], window, text_ref[0]], axis=0)
    text_rows = text_ref.shape[1]
    heads = keys_values.shape[1] // (2 * HD)
    query = query_ref[0]
    for head in range(heads):
        keys = keys_values[:, 2 * head * HD : (2 * head + 1) * HD]
        values = keys_values[:, (2 * head + 1) * HD : (2 * head + 2) * HD]
        stacked = jnp.concatenate(
            [
                query[:, (head * GROUP + a) * HD : (head * GROUP + a + 1) * HD]
                for a in range(GROUP)
            ],
            axis=0,
        )
        scores = lax.dot_general(
            stacked, keys, (((1,), (1,)), ((), ())), preferred_element_type=jnp.float32
        ) * (HD**-0.5)
        row = lax.broadcasted_iota(jnp.int32, scores.shape, 0) % text_rows
        column = lax.broadcasted_iota(jnp.int32, scores.shape, 1)
        text_column = column - (scores.shape[1] - text_rows)
        allowed = (text_column <= row) & (seen_ref[0] > 0)
        scores = jnp.where(allowed, scores, -1e30)
        best = jnp.max(scores, axis=1, keepdims=True)
        weights = jnp.exp(scores - best)
        total = jnp.sum(weights, axis=1, keepdims=True)
        result = jnp.dot(weights.astype(jnp.bfloat16), values, preferred_element_type=jnp.float32)
        result = (result / total).astype(jnp.bfloat16)
        for a in range(GROUP):
            out_ref[0, :, (head * GROUP + a) * HD : (head * GROUP + a + 1) * HD] = result[
                a * text_rows : (a + 1) * text_rows
            ]


def attend(place, queries, prefixes, text_kv, pages, picks, seen, all_rows):
    docs, rows, width = queries.shape
    kv_width = text_kv.shape[2]
    vision_rows = all_rows.shape[0]
    keys = seen.shape[2]
    return pl.pallas_call(
        attend_kernel,
        grid_spec=pltpu.PrefetchScalarGridSpec(
            num_scalar_prefetch=1,
            grid=(docs,),
            in_specs=[
                pl.BlockSpec((1, rows, width), lambda d, place: (d, 0, 0)),
                pl.BlockSpec((1,) + prefixes.shape[1:], lambda d, place: (place[d], 0, 0)),
                pl.BlockSpec((1, rows, kv_width), lambda d, place: (d, 0, 0)),
                pl.BlockSpec(pages.shape, lambda d, place: (0, 0)),
                pl.BlockSpec((1,) + picks.shape[1:], lambda d, place: (d, 0, 0)),
                pl.BlockSpec((1, 1, keys), lambda d, place: (d, 0, 0)),
                pl.BlockSpec(all_rows.shape, lambda d, place: (0, 0)),
            ],
            out_specs=[
                pl.BlockSpec((1, rows, width), lambda d, place: (d, 0, 0)),
                pl.BlockSpec((vision_rows, kv_width), lambda d, place: (0, 0)),
            ],
        ),
        out_shape=[
            jax.ShapeDtypeStruct(queries.shape, jnp.bfloat16),
            jax.ShapeDtypeStruct((vision_rows, kv_width), jnp.bfloat16),
        ],
        compiler_params=pltpu.CompilerParams(vmem_limit_bytes=VMEM),
        cost_estimate=pl.CostEstimate(
            flops=4 * docs * rows * width * keys,
            bytes_accessed=8 * docs * rows * width,
            transcendentals=docs * rows * keys * width // HD,
        ),
    )(place, queries, prefixes, text_kv, pages, picks, seen, all_rows)


def shards(
    panels,
    w_merge,
    ln_gain,
    w_kv,
    page_src,
    page_tile,
    doc_pages,
    prefix_id,
    prefix_cache,
    queries,
    text_kv,
):
    seq_count = lax.axis_size("seq")
    holder = lax.axis_index("seq")
    tile_count, panel_rows, _ = panels.shape
    page_count = page_src.shape[0]
    capacity = max(2, 2 * page_count // seq_count)
    sources = page_src[:, 0]

    kv, squares, small = merge_tiles(
        panels, w_merge, ln_gain, w_kv, pack_small(prefix_cache, sources, page_tile)
    )
    width = seq_count // lax.axis_size("tp")
    small = small.reshape(seq_count, SMALL_ROWS, -1)

    def place_of(index):
        group = (index // width) ^ (holder // width)
        return group * width + (index - holder) % width

    prefix_rows = prefix_cache.shape[1]
    prefixes = small[:, :prefix_rows]
    place = place_of(jnp.arange(seq_count, dtype=jnp.int32))
    asked_sources = small[:, prefix_rows, :page_count].astype(jnp.int32)[place]
    asked_tiles = small[:, prefix_rows + 1, :page_count].astype(jnp.int32)[place]
    asked = (asked_sources == holder).astype(jnp.int32)
    order = jnp.cumsum(asked, axis=1) - 1
    slots = jnp.arange(capacity, dtype=jnp.int32)
    picked = asked[:, None, :] * (order[:, None, :] == slots[None, :, None]).astype(jnp.int32)
    wanted = jnp.sum(picked * asked_tiles[:, None, :], axis=2)
    within = jnp.arange(panel_rows, dtype=jnp.int32)
    wanted_rows = (wanted.reshape(-1, 1) * panel_rows + within[None, :]).reshape(-1)
    chooser = wanted_rows[:, None] == jnp.arange(tile_count * panel_rows, dtype=jnp.int32)[None, :]
    chooser = chooser.astype(jnp.bfloat16)

    position = jnp.arange(page_count, dtype=jnp.int32)
    earlier = (sources[:, None] == sources[None, :]) & (position[None, :] < position[:, None])
    rank = jnp.sum(earlier.astype(jnp.int32), axis=1)
    arrival = sources * capacity + rank
    all_rows = (arrival[:, None] * panel_rows + within[None, :]).reshape(-1, 1)
    lengths = doc_pages[0]
    starts = jnp.cumsum(lengths) - lengths
    step = jnp.arange(MOST_PAGES, dtype=jnp.int32)
    inside = step[None, :] < lengths[:, None]
    page = jnp.minimum(starts[:, None] + step[None, :], page_count - 1)
    doc_rows = arrival[page][:, :, None] * panel_rows + within[None, None, :]
    doc_rows = jnp.where(inside[:, :, None], doc_rows, -1)
    doc_count, query_rows, _ = queries.shape
    picks = doc_rows.reshape(doc_count, -1, 1)
    seen = jnp.concatenate(
        [
            jnp.ones((doc_count, prefixes.shape[1]), jnp.int32),
            (doc_rows >= 0).reshape(doc_count, -1).astype(jnp.int32),
            jnp.ones((doc_count, query_rows), jnp.int32),
        ],
        axis=1,
    )[:, None, :]

    kv, squares = scatter_heads(kv, squares)
    row_scale = lax.rsqrt(squares / D + 1e-06)
    tile_kv = (kv * row_scale[:, None]).astype(jnp.bfloat16)
    outgoing = jnp.dot(chooser, tile_kv, preferred_element_type=jnp.float32).astype(jnp.bfloat16)
    pages = lax.all_to_all(outgoing, "seq", split_axis=0, concat_axis=0, tiled=True)
    attended, vision_kv = attend(
        place_of(prefix_id), queries, prefixes, text_kv, pages, picks, seen, all_rows
    )
    return (attended, vision_kv)


def solution(mesh):
    return jax.shard_map(
        shards,
        mesh=mesh,
        in_specs=(
            P("seq", None, "tp"),
            P("seq", "tp"),
            P("tp"),
            P("tp", None),
            P("seq", None),
            P("seq"),
            P("seq", None),
            P("seq"),
            P("seq", None, "tp"),
            P("seq", None, "tp"),
            P("seq", None, "tp"),
        ),
        out_specs=(P("seq", None, "tp"), P("seq", "tp")),
        check_vma=False,
    )
```

profile of v0, /device:TPU:0, one launch (start us, length us, event | category | flops | bytes accessed | tf_op | source)
XLA Modules:
  0.0 196.4 jit_solution(15797856221835788898)
XLA Ops:
  0.6 1.8 slice_bitcast_fusion
  3.2 6.8 %collective-permute-start = (bf16[128,1280]{1,0:T(8,128)(2,1)}, bf16[128,1280]{1,0:T(8,128)(2,1)}, u32[]{:S(2)}, u32[]{:S(2)}) collective-permute-start(bf16[128,1280]{1,0:T(8,128)(2,1)} %get-tuple-element.81), channel_id=1, source_target_pairs={{0,2},{1,3},{2,0},{3,1},{4,6},{5,7},{6,4},{7,5},{8,10},{9,11},{10,... | collective-permute-start | bytes 983048 | tf_op jit(solution)/shard_map/ppermute | solution.py:23
  10.0 3.0 %fusion.70 = (bf16[640,1024]{1,0:T(8,128)(2,1)}, bf16[640,1024]{1,0:T(8,128)(2,1)S(1)}) fusion(bf16[640,2048]{1,0:T(8,128)(2,1)} %refs_2_.3), kind=kLoop, calls=%fused_computation.161 | loop fusion | bytes 5242880 | tf_op jit(solution)/shard_map/slice | solution.py:205
  13.0 1.5 collective-permute-start.7
  15.9 3.0 %collective-permute-start.3 = (bf16[128,1280]{1,0:T(8,128)(2,1)S(1)}, bf16[128,1280]{1,0:T(8,128)(2,1)S(1)}, u32[]{:S(2)}, u32[]{:S(2)}) collective-permute-start(bf16[128,1280]{1,0:T(8,128)(2,1)S(1)} %collective-permute-done.2.refs_0_), channel_id=1, source_target_pairs={{0,2},{1,3},{2,0},{3,1},{4,6},{5,7},{6,4},{7,5},{8,10},{9,11},{10,... | collective-permute-start | bytes 983048 | tf_op jit(solution)/shard_map/ppermute | solution.py:23
  19.0 1.2 pad_maximum_fusion
  20.2 3.2 %collective-permute-done = bf16[128,1280]{1,0:T(8,128)(2,1)} collective-permute-done((bf16[128,1280]{1,0:T(8,128)(2,1)}, bf16[128,1280]{1,0:T(8,128)(2,1)}, u32[]{:S(2)}, u32[]{:S(2)}) %collective-permute-start) | collective-permute-done | bytes 327712 | tf_op jit(solution)/shard_map/ppermute | solution.py:23
  23.4 1.5 collective-permute-start.1
  24.9 1.1 collective-permute-start.4
  26.0 5.8 %collective-permute-start.6 = (bf16[128,1280]{1,0:T(8,128)(2,1)}, bf16[128,1280]{1,0:T(8,128)(2,1)}, u32[]{:S(2)}, u32[]{:S(2)}) collective-permute-start(bf16[128,1280]{1,0:T(8,128)(2,1)} %collective-permute-done), channel_id=1, source_target_pairs={{2,0},{3,10},{0,16},{1,26},{6,4},{7,14},{4,20},{5,30},{10,2},{11,8... | collective-permute-start | bytes 983048 | tf_op jit(solution)/shard_map/ppermute | solution.py:37
  31.9 2.4 %collective-permute-start.5 = (bf16[128,1280]{1,0:T(8,128)(2,1)S(1)}, bf16[128,1280]{1,0:T(8,128)(2,1)}, u32[]{:S(2)}, u32[]{:S(2)}) collective-permute-start(bf16[128,1280]{1,0:T(8,128)(2,1)S(1)} %collective-permute-done.3.refs_1_), channel_id=1, source_target_pairs={{0,1},{1,0},{2,3},{3,2},{4,5},{5,4},{6,7},{7,6},{8,9},{9,8},{10,11... | collective-permute-start | bytes 983048 | tf_op jit(solution)/shard_map/ppermute | solution.py:23
  35.5 3.1 %collective-permute-done.6.refs_0_ = bf16[128,1280]{1,0:T(8,128)(2,1)} collective-permute-done((bf16[128,1280]{1,0:T(8,128)(2,1)}, bf16[128,1280]{1,0:T(8,128)(2,1)}, u32[]{:S(2)}, u32[]{:S(2)}) %collective-permute-start.6) | collective-permute-done | bytes 327712 | tf_op jit(solution)/shard_map/ppermute | solution.py:37
  38.7 1.7 shard_map.131.refs_0_
  40.4 4.5 %collective-permute-done.7.refs_2_ = bf16[640,1024]{1,0:T(8,128)(2,1)} collective-permute-done((bf16[640,1024]{1,0:T(8,128)(2,1)}, bf16[640,1024]{1,0:T(8,128)(2,1)}, u32[]{:S(2)}, u32[]{:S(2)}) %collective-permute-start.7) | collective-permute-done | bytes 1310752 | tf_op jit(solution)/shard_map/ppermute | solution.py:216
  45.0 4.5 %shard_map.132 = (bf16[384,1024]{1,0:T(8,128)(2,1)S(1)}, bf16[128,1024]{1,0:T(8,128)(2,1)}) custom-call(bf16[512,1280]{1,0:T(8,128)(2,1)S(1)} %shard_map.131.refs_0_, bf16[640,2048]{1,0:T(8,128)(2,1)S(1)} %copy-done, bf16[640,1024]{1,0:T(8,128)(2,1)} %collective-permute-done.7.refs_2_), custom_call_target="tpu_custom_call" | custom-call | bytes 2048 | tf_op jit(solution)/shard_map/pallas_call | solution.py:122
  50.3 3.9 %collective-permute-start.9 = (bf16[128,1280]{1,0:T(8,128)(2,1)}, bf16[128,1280]{1,0:T(8,128)(2,1)}, u32[]{:S(2)}, u32[]{:S(2)}) collective-permute-start(bf16[128,1280]{1,0:T(8,128)(2,1)} %collective-permute-done.6.refs_0_), channel_id=1, source_target_pairs={{0,1},{1,0},{2,3},{3,2},{4,5},{5,4},{6,7},{7,6},{8,9},{9,8},{10,11... | collective-permute-start | bytes 983048 | tf_op jit(solution)/shard_map/ppermute | solution.py:23
  54.2 3.7 %collective-permute-start.11 = (bf16[384,1024]{1,0:T(8,128)(2,1)S(1)}, bf16[384,1024]{1,0:T(8,128)(2,1)}, u32[]{:S(2)}, u32[]{:S(2)}) collective-permute-start(bf16[384,1024]{1,0:T(8,128)(2,1)S(1)} %get-tuple-element.34), channel_id=1, source_target_pairs={{0,8},{4,12},{24,16},{28,20},{1,9},{5,13},{25,17},{29,21},{2,10},{... | collective-permute-start | bytes 2359304 | tf_op jit(solution)/shard_map/ppermute | solution.py:151
  58.0 2.5 %collective-permute-start.10 = (bf16[128,1280]{1,0:T(8,128)(2,1)}, bf16[128,1280]{1,0:T(8,128)(2,1)}, u32[]{:S(2)}, u32[]{:S(2)}) collective-permute-start(bf16[128,1280]{1,0:T(8,128)(2,1)} %collective-permute-done.8.refs_1_), channel_id=1, source_target_pairs={{0,1},{1,0},{2,3},{3,2},{4,5},{5,4},{6,7},{7,6},{8,9},{9,8},{10,11... | collective-permute-start | bytes 983048 | tf_op jit(solution)/shard_map/ppermute | solution.py:23
  62.1 1.9 shard_map.133.refs_0_.refs_1_
  64.0 4.8 %shard_map.134 = (bf16[384,1024]{1,0:T(8,128)(2,1)}, bf16[128,1024]{1,0:T(8,128)(2,1)S(1)}) custom-call(bf16[512,1280]{1,0:T(8,128)(2,1)S(1)} %shard_map.133.refs_0_.refs_1_, bf16[640,2048]{1,0:T(8,128)(2,1)S(1)} %copy-done, bf16[640,1024]{1,0:T(8,128)(2,1)} %collective-permute-done.7.refs_2_), custom_call_target="tpu_custom_call" | custom-call | bytes 2048 | tf_op jit(solution)/shard_map/pallas_call | solution.py:122
  69.6 6.6 %collective-permute-start.14 = (bf16[384,1024]{1,0:T(8,128)(2,1)}, bf16[384,1024]{1,0:T(8,128)(2,1)}, u32[]{:S(2)}, u32[]{:S(2)}) collective-permute-start(bf16[384,1024]{1,0:T(8,128)(2,1)} %get-tuple-element.36), channel_id=1, source_target_pairs={{0,8},{4,12},{24,16},{28,20},{1,9},{5,13},{25,17},{29,21},{2,10},{... | collective-permute-start | bytes 2359304 | tf_op jit(solution)/shard_map/ppermute | solution.py:151
  77.6 1.3 copy-done.2
  78.9 1.3 copy-done.5
  80.2 3.1 %shard_map.135 = (bf16[768,512]{1,0:T(8,128)(2,1)S(1)}, bf16[256,512]{1,0:T(8,128)(2,1)S(1)}) custom-call(bf16[512,1280]{1,0:T(8,128)(2,1)S(1)} %copy-done.2, bf16[512,1280]{1,0:T(8,128)(2,1)S(1)} %copy-done.5, bf16[640,2048]{1,0:T(8,128)(2,1)S(1)} %copy-done, bf16[656,1024]{1,0:T(8,128)(2,1)} %collective-permute-done.1.refs_3_), custom_call_target="tpu_custom_call" | custom-call | bytes 1024 | tf_op jit(solution)/shard_map/pallas_call | solution.py:122
  84.0 1.0 pad_maximum_fusion.2
  85.0 2.2 %collective-permute-start.12 = (bf16[832,512]{1,0:T(8,128)(2,1)}, bf16[832,512]{1,0:T(8,128)(2,1)}, u32[]{:S(2)}, u32[]{:S(2)}) collective-permute-start(bf16[832,512]{1,0:T(8,128)(2,1)} %pad_maximum_fusion.2), channel_id=1, source_target_pairs={{0,8},{4,12},{24,16},{28,20},{1,9},{5,13},{25,17},{29,21},{2,10},{... | collective-permute-start | bytes 2555912 | tf_op jit(solution)/shard_map/ppermute | solution.py:151
  87.8 1.3 collective-permute-start.17
  90.4 0.8 add.413
  91.2 0.8 add.414.all_ref
  92.7 1.5 stack_reshape.7
  94.2 1.5 collective-permute-start.24
  95.7 1.0 pad_maximum_fusion.7
  96.7 1.3 collective-permute-done.17
  98.1 1.3 collective-permute-start.13
  99.4 1.4 add_convert_fusion.5
  100.7 1.3 collective-permute-start.18
  102.7 3.7 %collective-permute-done.24 = bf16[128,1024]{1,0:T(8,128)(2,1)S(1)} collective-permute-done((bf16[128,1024]{1,0:T(8,128)(2,1)}, bf16[128,1024]{1,0:T(8,128)(2,1)S(1)}, u32[]{:S(2)}, u32[]{:S(2)}) %collective-permute-start.24) | collective-permute-done | bytes 262176 | tf_op jit(solution)/shard_map/ppermute | solution.py:152
  106.5 1.4 add_convert_fusion.1
  107.9 1.4 collective-permute-start.25
  109.3 3.8 %shard_map.136 = (bf16[768,512]{1,0:T(8,128)(2,1)}, bf16[256,512]{1,0:T(8,128)(2,1)}) custom-call(bf16[512,1280]{1,0:T(8,128)(2,1)S(1)} %copy-done.3, bf16[512,1280]{1,0:T(8,128)(2,1)S(1)} %copy-done.6, bf16[640,2048]{1,0:T(8,128)(2,1)S(1)} %copy-done, bf16[656,1024]{1,0:T(8,128)(2,1)} %collective-permute-done.1.refs_3_), custom_call_target="tpu_custom_call" | custom-call | bytes 1024 | tf_op jit(solution)/shard_map/pallas_call | solution.py:122
  113.1 9.6 %collective-permute-done.13 = bf16[320,512]{1,0:T(8,128)(2,1)S(1)} collective-permute-done((bf16[320,512]{1,0:T(8,128)(2,1)S(1)}, bf16[320,512]{1,0:T(8,128)(2,1)S(1)}, u32[]{:S(2)}, u32[]{:S(2)}) %collective-permute-start.13) | collective-permute-done | bytes 327712 | tf_op jit(solution)/shard_map/ppermute | solution.py:152
  123.4 1.2 add_convert_fusion.7
  124.6 0.9 select_bitcast_fusion
  125.5 1.4 collective-permute-start.15
  127.7 2.6 %fusion.21 = (f32[128]{0:T(128)}, bf16[128,1024]{1,0:T(8,128)(2,1)}) fusion(bf16[128,1024]{1,0:T(8,128)(2,1)S(1)} %collective-permute-done.19, bf16[384,1024]{1,0:T(8,128)(2,1)} %collective-permute-done.11, bf16[384,1024]{1,0:T(8,128)(2,1)} %copy-done.9, bf16[128,1024]{1,0:T(8,128)(2,1)S(1)} %collective-permute-done.18, ...), kind=kLoop, calls=%fused_computation.35 | loop fusion | flops 1965952 | bytes 1835521 | tf_op jit(solution)/shard_map/reduce_sum | solution.py:272
  130.3 8.0 %collective-permute-start.21 = (bf16[768,512]{1,0:T(8,128)(2,1)}, bf16[768,512]{1,0:T(8,128)(2,1)S(1)}, u32[]{:S(2)}, u32[]{:S(2)}) collective-permute-start(bf16[768,512]{1,0:T(8,128)(2,1)} %get-tuple-element.44), channel_id=1, source_target_pairs={{0,8},{4,12},{24,16},{28,20},{1,9},{5,13},{25,17},{29,21},{2,10},{... | collective-permute-start | bytes 2359304 | tf_op jit(solution)/shard_map/ppermute | solution.py:151
  138.3 1.3 collective-permute-start.20
  139.7 2.4 %fusion.27 = (f32[128]{0:T(128)}, bf16[128,1024]{1,0:T(8,128)(2,1)}) fusion(bf16[128,1024]{1,0:T(8,128)(2,1)S(1)} %collective-permute-done.26, bf16[384,1024]{1,0:T(8,128)(2,1)} %collective-permute-done.14, bf16[384,1024]{1,0:T(8,128)(2,1)} %get-tuple-element.36, bf16[128,1024]{1,0:T(8,128)(2,1)S(1)} %collective-permute-done.25, ...), kind=kLoop, calls=%fused_computation.41 | loop fusion | flops 1965952 | bytes 1835521 | tf_op jit(solution)/shard_map/reduce_sum | solution.py:272
  145.3 1.5 fusion.23
  146.8 4.2 %collective-permute-done.21 = bf16[768,512]{1,0:T(8,128)(2,1)S(1)} collective-permute-done((bf16[768,512]{1,0:T(8,128)(2,1)}, bf16[768,512]{1,0:T(8,128)(2,1)S(1)}, u32[]{:S(2)}, u32[]{:S(2)}) %collective-permute-start.21) | collective-permute-done | bytes 786464 | tf_op jit(solution)/shard_map/ppermute | solution.py:151
  151.0 1.2 add_convert_fusion.3
  152.1 1.3 collective-permute-start.22
  154.2 1.8 fusion.18
  156.0 6.7 %collective-permute-done.22 = bf16[256,512]{1,0:T(8,128)(2,1)S(1)} collective-permute-done((bf16[256,512]{1,0:T(8,128)(2,1)S(1)}, bf16[256,512]{1,0:T(8,128)(2,1)S(1)}, u32[]{:S(2)}, u32[]{:S(2)}) %collective-permute-start.22) | collective-permute-done | bytes 262176 | tf_op jit(solution)/shard_map/ppermute | solution.py:169
  162.8 1.4 fusion.25
  168.2 0.8 add.351
  169.7 1.0 collective-permute-start.30
  170.9 1.1 collective-permute-start.28
  171.9 1.4 collective-permute-done.30
  173.3 3.0 %collective-permute-done.28 = bf16[1,256,256]{2,1,0:T(8,128)(2,1)S(1)} collective-permute-done((bf16[1,256,256]{2,1,0:T(8,128)(2,1)S(1)}, bf16[1,256,256]{2,1,0:T(8,128)(2,1)S(1)}, u32[]{:S(2)}, u32[]{:S(2)}) %collective-permute-start.28) | collective-permute-done | bytes 131104 | tf_op jit(solution)/shard_map/ppermute | solution.py:23
  176.4 1.0 convolution_convert_fusion
  177.4 5.1 %all-to-all-start = ((bf16[8,64,256]{2,1,0:T(8,128)(2,1)}), bf16[8,64,256]{2,1,0:T(8,128)(2,1)S(1)}, u32[]{:S(2)}, u32[]{:S(2)}) async-start(bf16[8,64,256]{2,1,0:T(8,128)(2,1)} %bitcast.21), calls=%async_computation | async-start | bytes 524288 | tf_op jit(solution)/shard_map/all_to_all | solution.py:464
  183.9 7.0 %all-to-all-done = bf16[8,64,256]{2,1,0:T(8,128)(2,1)S(1)} async-done(((bf16[8,64,256]{2,1,0:T(8,128)(2,1)}), bf16[8,64,256]{2,1,0:T(8,128)(2,1)S(1)}, u32[]{:S(2)}, u32[]{:S(2)}) %all-to-all-start) | async-done | bytes 262176 | tf_op jit(solution)/shard_map/all_to_all | solution.py:464
  190.9 5.5 %shard_map.137 = (bf16[4,128,1024]{2,1,0:T(8,128)(2,1)}, bf16[256,256]{1,0:T(8,128)(2,1)}) custom-call(s32[4]{0:T(128)S(1)} %fusion.59.place_ref, bf16[4,128,1024]{2,1,0:T(8,128)(2,1)S(1)} %copy-done.12, bf16[8,32,256]{2,1,0:T(8,128)(2,1)S(1)} %slice.243.prefix_ref, bf16[4,128,256]{2,1,0:T(8,128)(2,1)S(1)} %copy-done.13, bf16[512,256]{1,0:T(8,128)(2,1)S(1)} %bitcast.60, ...), custom_call_target="tpu_custom_call" | custom-call | flops 603979776 | bytes 4194304 | tf_op jit(solution)/shard_map/pallas_call | solution.py:360
  (191 shorter events, 23.1 us)
Async XLA Ops:
  2.5 13.5 %collective-permute-start.2 = (bf16[128,1280]{1,0:T(8,128)(2,1)S(1)}, bf16[128,1280]{1,0:T(8,128)(2,1)S(1)}, u32[]{:S(2)}, u32[]{:S(2)}) collective-permute-start(bf16[128,1280]{1,0:T(8,128)(2,1)S(1)} %get-tuple-element.80), channel_id=1, source_target_pairs={{0,0},{1,10},{2,16},{3,26},{4,4},{5,14},{6,20},{7,30},{8,2},{9,8},... | collective-permute-start | bytes 983048 | tf_op jit(solution)/shard_map/ppermute | solution.py:37
  3.1 11.3 %copy-start.43 = (s32[32,1]{0,1:T(1,128)S(1)}, s32[32,1]{0,1:T(1,128)}, u32[]{:S(2)}) copy-start(s32[32,1]{0,1:T(1,128)} %param.16) | copy-start | bytes 388
  3.2 11.5 %copy-start.44 = (s32[32]{0:T(128)S(1)}, s32[32]{0:T(128)}, u32[]{:S(2)}) copy-start(s32[32]{0:T(128)} %param.17) | copy-start | bytes 388
  3.2 11.5 %copy-start.45 = (s32[1,4]{1,0:T(1,128)S(1)}, s32[1,4]{1,0:T(1,128)}, u32[]{:S(2)}) copy-start(s32[1,4]{1,0:T(1,128)} %param.18) | copy-start | bytes 52
  3.2 11.9 %copy-start.33 = (bf16[1,32,256]{2,1,0:T(8,128)(2,1)S(1)}, bf16[1,32,256]{2,1,0:T(8,128)(2,1)}, u32[]{:S(2)}) copy-start(bf16[1,32,256]{2,1,0:T(8,128)(2,1)} %param.20) | copy-start | bytes 49156
  3.2 20.2 %collective-permute-start = (bf16[128,1280]{1,0:T(8,128)(2,1)}, bf16[128,1280]{1,0:T(8,128)(2,1)}, u32[]{:S(2)}, u32[]{:S(2)}) collective-permute-start(bf16[128,1280]{1,0:T(8,128)(2,1)} %get-tuple-element.81), channel_id=1, source_target_pairs={{0,2},{1,3},{2,0},{3,1},{4,6},{5,7},{6,4},{7,5},{8,10},{9,11},{10,... | collective-permute-start | bytes 983048 | tf_op jit(solution)/shard_map/ppermute | solution.py:23
  13.0 32.0 %collective-permute-start.7 = (bf16[640,1024]{1,0:T(8,128)(2,1)}, bf16[640,1024]{1,0:T(8,128)(2,1)}, u32[]{:S(2)}, u32[]{:S(2)}) collective-permute-start(bf16[640,1024]{1,0:T(8,128)(2,1)} %get-tuple-element.62), channel_id=1, source_target_pairs={{4,0},{0,4},{12,8},{8,12},{20,16},{16,20},{28,24},{24,28},{5,1},{1... | collective-permute-start | bytes 3932168 | tf_op jit(solution)/shard_map/ppermute | solution.py:216
  15.1 19.7 %copy-start.14 = (s32[4]{0:T(128)S(1)}, s32[4]{0:T(128)}, u32[]{:S(2)}) copy-start(s32[4]{0:T(128)} %constant.163.clone) | copy-start | bytes 52
  15.9 16.0 %collective-permute-start.3 = (bf16[128,1280]{1,0:T(8,128)(2,1)S(1)}, bf16[128,1280]{1,0:T(8,128)(2,1)S(1)}, u32[]{:S(2)}, u32[]{:S(2)}) collective-permute-start(bf16[128,1280]{1,0:T(8,128)(2,1)S(1)} %collective-permute-done.2.refs_0_), channel_id=1, source_target_pairs={{0,2},{1,3},{2,0},{3,1},{4,6},{5,7},{6,4},{7,5},{8,10},{9,11},{10,... | collective-permute-start | bytes 983048 | tf_op jit(solution)/shard_map/ppermute | solution.py:23
  20.2 24.8 %copy-start = (bf16[640,2048]{1,0:T(8,128)(2,1)S(1)}, bf16[640,2048]{1,0:T(8,128)(2,1)}, u32[]{:S(2)}) copy-start(bf16[640,2048]{1,0:T(8,128)(2,1)} %refs_2_.3) | copy-start | bytes 7864324
  23.4 52.7 %collective-permute-start.1 = (bf16[656,1024]{1,0:T(8,128)(2,1)}, bf16[656,1024]{1,0:T(8,128)(2,1)}, u32[]{:S(2)}, u32[]{:S(2)}) collective-permute-start(bf16[656,1024]{1,0:T(8,128)(2,1)} %pad_maximum_fusion), channel_id=1, source_target_pairs={{4,0},{0,4},{12,8},{8,12},{20,16},{16,20},{28,24},{24,28},{5,1},{1... | collective-permute-start | bytes 4030472 | tf_op jit(solution)/shard_map/ppermute | solution.py:216
  24.9 10.6 %collective-permute-start.4 = (bf16[128,1280]{1,0:T(8,128)(2,1)S(1)}, bf16[128,1280]{1,0:T(8,128)(2,1)}, u32[]{:S(2)}, u32[]{:S(2)}) collective-permute-start(bf16[128,1280]{1,0:T(8,128)(2,1)S(1)} %collective-permute-done.2.refs_0_), channel_id=1, source_target_pairs={{0,1},{1,0},{2,3},{3,2},{4,5},{5,4},{6,7},{7,6},{8,9},{9,8},{10,11... | collective-permute-start | bytes 983048 | tf_op jit(solution)/shard_map/ppermute | solution.py:23
  26.0 12.6 %collective-permute-start.6 = (bf16[128,1280]{1,0:T(8,128)(2,1)}, bf16[128,1280]{1,0:T(8,128)(2,1)}, u32[]{:S(2)}, u32[]{:S(2)}) collective-permute-start(bf16[128,1280]{1,0:T(8,128)(2,1)} %collective-permute-done), channel_id=1, source_target_pairs={{2,0},{3,10},{0,16},{1,26},{6,4},{7,14},{4,20},{5,30},{10,2},{11,8... | collective-permute-start | bytes 983048 | tf_op jit(solution)/shard_map/ppermute | solution.py:37
  31.9 6.8 %collective-permute-start.5 = (bf16[128,1280]{1,0:T(8,128)(2,1)S(1)}, bf16[128,1280]{1,0:T(8,128)(2,1)}, u32[]{:S(2)}, u32[]{:S(2)}) collective-permute-start(bf16[128,1280]{1,0:T(8,128)(2,1)S(1)} %collective-permute-done.3.refs_1_), channel_id=1, source_target_pairs={{0,1},{1,0},{2,3},{3,2},{4,5},{5,4},{6,7},{7,6},{8,9},{9,8},{10,11... | collective-permute-start | bytes 983048 | tf_op jit(solution)/shard_map/ppermute | solution.py:23
  34.6 14.9 %copy-start.37 = (s32[128]{0:T(128)}, s32[128]{0:T(128)S(1)}, u32[]{:S(2)}) copy-start(s32[128]{0:T(128)S(1)} %add.401) | copy-start | bytes 1540
  40.4 9.1 %copy-start.1 = (bf16[512,1280]{1,0:T(8,128)(2,1)}, bf16[512,1280]{1,0:T(8,128)(2,1)S(1)}, u32[]{:S(2)}) copy-start(bf16[512,1280]{1,0:T(8,128)(2,1)S(1)} %shard_map.131.refs_0_) | copy-start | bytes 3932164
  40.4 20.1 %copy-start.38 = (bf16[2048]{0:T(1024)(128)(2,1)S(1)}, bf16[2048]{0:T(1024)(128)(2,1)}, u32[]{:S(2)}) copy-start(bf16[2048]{0:T(1024)(128)(2,1)} %param.14) | copy-start | bytes 12292
  49.5 19.4 %copy-start.9 = (bf16[384,1024]{1,0:T(8,128)(2,1)}, bf16[384,1024]{1,0:T(8,128)(2,1)S(1)}, u32[]{:S(2)}) copy-start(bf16[384,1024]{1,0:T(8,128)(2,1)S(1)} %get-tuple-element.34) | copy-start | bytes 2359300
  49.5 8.5 %collective-permute-start.8 = (bf16[128,1280]{1,0:T(8,128)(2,1)}, bf16[128,1280]{1,0:T(8,128)(2,1)}, u32[]{:S(2)}, u32[]{:S(2)}) collective-permute-start(bf16[128,1280]{1,0:T(8,128)(2,1)} %collective-permute-done.6.refs_0_), channel_id=1, source_target_pairs={{0,2},{1,3},{2,0},{3,1},{4,6},{5,7},{6,4},{7,5},{8,10},{9,11},{10,... | collective-permute-start | bytes 983048 | tf_op jit(solution)/shard_map/ppermute | solution.py:23
  50.3 11.5 %collective-permute-start.9 = (bf16[128,1280]{1,0:T(8,128)(2,1)}, bf16[128,1280]{1,0:T(8,128)(2,1)}, u32[]{:S(2)}, u32[]{:S(2)}) collective-permute-start(bf16[128,1280]{1,0:T(8,128)(2,1)} %collective-permute-done.6.refs_0_), channel_id=1, source_target_pairs={{0,1},{1,0},{2,3},{3,2},{4,5},{5,4},{6,7},{7,6},{8,9},{9,8},{10,11... | collective-permute-start | bytes 983048 | tf_op jit(solution)/shard_map/ppermute | solution.py:23
  54.2 23.4 %collective-permute-start.11 = (bf16[384,1024]{1,0:T(8,128)(2,1)S(1)}, bf16[384,1024]{1,0:T(8,128)(2,1)}, u32[]{:S(2)}, u32[]{:S(2)}) collective-permute-start(bf16[384,1024]{1,0:T(8,128)(2,1)S(1)} %get-tuple-element.34), channel_id=1, source_target_pairs={{0,8},{4,12},{24,16},{28,20},{1,9},{5,13},{25,17},{29,21},{2,10},{... | collective-permute-start | bytes 2359304 | tf_op jit(solution)/shard_map/ppermute | solution.py:151
  58.0 4.1 %collective-permute-start.10 = (bf16[128,1280]{1,0:T(8,128)(2,1)}, bf16[128,1280]{1,0:T(8,128)(2,1)}, u32[]{:S(2)}, u32[]{:S(2)}) collective-permute-start(bf16[128,1280]{1,0:T(8,128)(2,1)} %collective-permute-done.8.refs_1_), channel_id=1, source_target_pairs={{0,1},{1,0},{2,3},{3,2},{4,5},{5,4},{6,7},{7,6},{8,9},{9,8},{10,11... | collective-permute-start | bytes 983048 | tf_op jit(solution)/shard_map/ppermute | solution.py:23
  69.6 32.5 %collective-permute-start.14 = (bf16[384,1024]{1,0:T(8,128)(2,1)}, bf16[384,1024]{1,0:T(8,128)(2,1)}, u32[]{:S(2)}, u32[]{:S(2)}) collective-permute-start(bf16[384,1024]{1,0:T(8,128)(2,1)} %get-tuple-element.36), channel_id=1, source_target_pairs={{0,8},{4,12},{24,16},{28,20},{1,9},{5,13},{25,17},{29,21},{2,10},{... | collective-permute-start | bytes 2359304 | tf_op jit(solution)/shard_map/ppermute | solution.py:151
  80.2 10.2 %copy-start.28 = (s32[4,16,8]{2,1,0:T(8,128)S(1)}, s32[4,16,8]{2,1,0:T(8,128)}, u32[]{:S(2)}) copy-start(s32[4,16,8]{2,1,0:T(8,128)} %copy-done.27) | copy-start | bytes 6148
  84.0 7.2 %copy-start.32 = (s32[4,288]{1,0:T(4,128)S(1)}, s32[4,288]{1,0:T(4,128)}, u32[]{:S(2)}) copy-start(s32[4,288]{1,0:T(4,128)} %add_add_fusion) | copy-start | bytes 13828
  85.0 38.4 %collective-permute-start.12 = (bf16[832,512]{1,0:T(8,128)(2,1)}, bf16[832,512]{1,0:T(8,128)(2,1)}, u32[]{:S(2)}, u32[]{:S(2)}) collective-permute-start(bf16[832,512]{1,0:T(8,128)(2,1)} %pad_maximum_fusion.2), channel_id=1, source_target_pairs={{0,8},{4,12},{24,16},{28,20},{1,9},{5,13},{25,17},{29,21},{2,10},{... | collective-permute-start | bytes 2555912 | tf_op jit(solution)/shard_map/ppermute | solution.py:151
  87.8 10.3 %collective-permute-start.17 = (bf16[128,1024]{1,0:T(8,128)(2,1)}, bf16[128,1024]{1,0:T(8,128)(2,1)}, u32[]{:S(2)}, u32[]{:S(2)}) collective-permute-start(bf16[128,1024]{1,0:T(8,128)(2,1)} %get-tuple-element.47), channel_id=1, source_target_pairs={{8,0},{12,4},{16,24},{20,28},{9,1},{13,5},{17,25},{21,29},{10,2},{... | collective-permute-start | bytes 786440 | tf_op jit(solution)/shard_map/ppermute | solution.py:152
  94.2 15.1 %copy-start.3 = (bf16[512,1280]{1,0:T(8,128)(2,1)S(1)}, bf16[512,1280]{1,0:T(8,128)(2,1)}, u32[]{:S(2)}) copy-start(bf16[512,1280]{1,0:T(8,128)(2,1)} %copy-done.1) | copy-start | bytes 3932164
  94.2 15.1 %copy-start.6 = (bf16[512,1280]{1,0:T(8,128)(2,1)S(1)}, bf16[512,1280]{1,0:T(8,128)(2,1)}, u32[]{:S(2)}) copy-start(bf16[512,1280]{1,0:T(8,128)(2,1)} %copy-done.4) | copy-start | bytes 3932164
  94.2 12.3 %collective-permute-start.24 = (bf16[128,1024]{1,0:T(8,128)(2,1)}, bf16[128,1024]{1,0:T(8,128)(2,1)S(1)}, u32[]{:S(2)}, u32[]{:S(2)}) collective-permute-start(bf16[128,1024]{1,0:T(8,128)(2,1)} %copy-done.10), channel_id=1, source_target_pairs={{8,0},{12,4},{16,24},{20,28},{9,1},{13,5},{17,25},{21,29},{10,2},{... | collective-permute-start | bytes 786440 | tf_op jit(solution)/shard_map/ppermute | solution.py:152
  98.1 24.6 %collective-permute-start.13 = (bf16[320,512]{1,0:T(8,128)(2,1)S(1)}, bf16[320,512]{1,0:T(8,128)(2,1)S(1)}, u32[]{:S(2)}, u32[]{:S(2)}) collective-permute-start(bf16[320,512]{1,0:T(8,128)(2,1)S(1)} %pad_maximum_fusion.7), channel_id=1, source_target_pairs={{8,0},{12,4},{16,24},{20,28},{9,1},{13,5},{17,25},{21,29},{10,2},{... | collective-permute-start | bytes 983048 | tf_op jit(solution)/shard_map/ppermute | solution.py:152
  100.7 26.2 %collective-permute-start.18 = (bf16[128,1024]{1,0:T(8,128)(2,1)S(1)}, bf16[128,1024]{1,0:T(8,128)(2,1)S(1)}, u32[]{:S(2)}, u32[]{:S(2)}) collective-permute-start(bf16[128,1024]{1,0:T(8,128)(2,1)S(1)} %get-tuple-element.66), channel_id=1, source_target_pairs={{8,24},{12,28},{16,0},{20,4},{9,25},{13,29},{17,1},{21,5},{10,26},... | collective-permute-start | bytes 786440 | tf_op jit(solution)/shard_map/ppermute | solution.py:169
  102.1 25.6 %collective-permute-start.19 = (bf16[128,1024]{1,0:T(8,128)(2,1)S(1)}, bf16[128,1024]{1,0:T(8,128)(2,1)S(1)}, u32[]{:S(2)}, u32[]{:S(2)}) collective-permute-start(bf16[128,1024]{1,0:T(8,128)(2,1)S(1)} %get-tuple-element.67), channel_id=1, source_target_pairs={{8,16},{12,20},{16,8},{20,12},{9,17},{13,21},{17,9},{21,13},{10,18... | collective-permute-start | bytes 786440 | tf_op jit(solution)/shard_map/ppermute | solution.py:170
  107.8 17.6 %copy-start.20 = (bf16[64,512]{1,0:T(8,128)(2,1)S(1)}, bf16[64,512]{1,0:T(8,128)(2,1)}, u32[]{:S(2)}) copy-start(bf16[64,512]{1,0:T(8,128)(2,1)} %reshape.360) | copy-start | bytes 196612
  107.9 30.5 %collective-permute-start.25 = (bf16[128,1024]{1,0:T(8,128)(2,1)S(1)}, bf16[128,1024]{1,0:T(8,128)(2,1)S(1)}, u32[]{:S(2)}, u32[]{:S(2)}) collective-permute-start(bf16[128,1024]{1,0:T(8,128)(2,1)S(1)} %get-tuple-element.68), channel_id=1, source_target_pairs={{8,24},{12,28},{16,0},{20,4},{9,25},{13,29},{17,1},{21,5},{10,26},... | collective-permute-start | bytes 786440 | tf_op jit(solution)/shard_map/ppermute | solution.py:169
  122.7 7.6 %copy-start.26 = (bf16[320,512]{1,0:T(8,128)(2,1)}, bf16[320,512]{1,0:T(8,128)(2,1)S(1)}, u32[]{:S(2)}) copy-start(bf16[320,512]{1,0:T(8,128)(2,1)S(1)} %collective-permute-done.13) | copy-start | bytes 983044
  122.7 16.9 %collective-permute-start.26 = (bf16[128,1024]{1,0:T(8,128)(2,1)S(1)}, bf16[128,1024]{1,0:T(8,128)(2,1)S(1)}, u32[]{:S(2)}, u32[]{:S(2)}) collective-permute-start(bf16[128,1024]{1,0:T(8,128)(2,1)S(1)} %get-tuple-element.69), channel_id=1, source_target_pairs={{8,16},{12,20},{16,8},{20,12},{9,17},{13,21},{17,9},{21,13},{10,18... | collective-permute-start | bytes 786440 | tf_op jit(solution)/shard_map/ppermute | solution.py:170
  124.6 15.1 %copy-start.11 = (bf16[128,1024]{1,0:T(8,128)(2,1)S(1)}, bf16[128,1024]{1,0:T(8,128)(2,1)}, u32[]{:S(2)}) copy-start(bf16[128,1024]{1,0:T(8,128)(2,1)} %copy-done.10) | copy-start | bytes 786436
  125.5 17.5 %copy-start.30 = (bf16[1,64,512]{2,1,0:T(8,128)(2,1)S(1)}, bf16[1,64,512]{2,1,0:T(8,128)(2,1)}, u32[]{:S(2)}) copy-start(bf16[1,64,512]{2,1,0:T(8,128)(2,1)} %stack_reshape.7) | copy-start | bytes 196612
  125.5 16.6 %collective-permute-start.15 = (bf16[384,512]{1,0:T(8,128)(2,1)S(1)}, bf16[384,512]{1,0:T(8,128)(2,1)S(1)}, u32[]{:S(2)}, u32[]{:S(2)}) collective-permute-start(bf16[384,512]{1,0:T(8,128)(2,1)S(1)} %get-tuple-element.84), channel_id=1, source_target_pairs={{8,24},{12,28},{16,0},{20,4},{9,25},{13,29},{17,1},{21,5},{10,26},... | collective-permute-start | bytes 1179656 | tf_op jit(solution)/shard_map/ppermute | solution.py:169
  127.0 15.1 %collective-permute-start.16 = (bf16[384,512]{1,0:T(8,128)(2,1)S(1)}, bf16[384,512]{1,0:T(8,128)(2,1)S(1)}, u32[]{:S(2)}, u32[]{:S(2)}) collective-permute-start(bf16[384,512]{1,0:T(8,128)(2,1)S(1)} %get-tuple-element.85), channel_id=1, source_target_pairs={{8,16},{12,20},{16,8},{20,12},{9,17},{13,21},{17,9},{21,13},{10,18... | collective-permute-start | bytes 1179656 | tf_op jit(solution)/shard_map/ppermute | solution.py:170
  130.3 15.0 %copy-start.8 = (bf16[256,512]{1,0:T(8,128)(2,1)S(1)}, bf16[256,512]{1,0:T(8,128)(2,1)}, u32[]{:S(2)}) copy-start(bf16[256,512]{1,0:T(8,128)(2,1)} %copy-done.7) | copy-start | bytes 786436
  130.3 20.6 %collective-permute-start.21 = (bf16[768,512]{1,0:T(8,128)(2,1)}, bf16[768,512]{1,0:T(8,128)(2,1)S(1)}, u32[]{:S(2)}, u32[]{:S(2)}) collective-permute-start(bf16[768,512]{1,0:T(8,128)(2,1)} %get-tuple-element.44), channel_id=1, source_target_pairs={{0,8},{4,12},{24,16},{28,20},{1,9},{5,13},{25,17},{29,21},{2,10},{... | collective-permute-start | bytes 2359304 | tf_op jit(solution)/shard_map/ppermute | solution.py:151
  138.3 17.7 %collective-permute-start.20 = (bf16[256,512]{1,0:T(8,128)(2,1)}, bf16[256,512]{1,0:T(8,128)(2,1)}, u32[]{:S(2)}, u32[]{:S(2)}) collective-permute-start(bf16[256,512]{1,0:T(8,128)(2,1)} %get-tuple-element.50), channel_id=1, source_target_pairs={{8,0},{12,4},{16,24},{20,28},{9,1},{13,5},{17,25},{21,29},{10,2},{... | collective-permute-start | bytes 786440 | tf_op jit(solution)/shard_map/ppermute | solution.py:152
  143.0 11.1 %copy-start.35 = (f32[512]{0:T(512)S(1)}, f32[512]{0:T(512)}, u32[]{:S(2)}) copy-start(f32[512]{0:T(512)} %get-tuple-element.86) | copy-start | bytes 6148
  143.1 12.9 %copy-start.21 = (bf16[8,64,256]{2,1,0:T(8,128)(2,1)}, bf16[8,64,256]{2,1,0:T(8,128)(2,1)S(1)}, u32[]{:S(2)}) copy-start(bf16[8,64,256]{2,1,0:T(8,128)(2,1)S(1)} %reshape_reshape.3) | copy-start | bytes 786436
  152.1 10.6 %collective-permute-start.22 = (bf16[256,512]{1,0:T(8,128)(2,1)S(1)}, bf16[256,512]{1,0:T(8,128)(2,1)S(1)}, u32[]{:S(2)}, u32[]{:S(2)}) collective-permute-start(bf16[256,512]{1,0:T(8,128)(2,1)S(1)} %get-tuple-element.70), channel_id=1, source_target_pairs={{8,24},{12,28},{16,0},{20,4},{9,25},{13,29},{17,1},{21,5},{10,26},... | collective-permute-start | bytes 786440 | tf_op jit(solution)/shard_map/ppermute | solution.py:169
  153.4 9.3 %collective-permute-start.23 = (bf16[256,512]{1,0:T(8,128)(2,1)S(1)}, bf16[256,512]{1,0:T(8,128)(2,1)S(1)}, u32[]{:S(2)}, u32[]{:S(2)}) collective-permute-start(bf16[256,512]{1,0:T(8,128)(2,1)S(1)} %get-tuple-element.71), channel_id=1, source_target_pairs={{8,16},{12,20},{16,8},{20,12},{9,17},{13,21},{17,9},{21,13},{10,18... | collective-permute-start | bytes 786440 | tf_op jit(solution)/shard_map/ppermute | solution.py:170
  154.1 10.0 %copy-start.41 = (f32[128]{0:T(128)S(1)}, f32[128]{0:T(128)}, u32[]{:S(2)}) copy-start(f32[128]{0:T(128)} %get-tuple-element.54) | copy-start | bytes 1540
  154.1 10.0 %copy-start.42 = (f32[128]{0:T(128)S(1)}, f32[128]{0:T(128)}, u32[]{:S(2)}) copy-start(f32[128]{0:T(128)} %get-tuple-element.58) | copy-start | bytes 1540
  154.2 10.6 %copy-start.15 = (bf16[2048,1024]{1,0:T(8,128)(2,1)S(1)}, bf16[2048,1024]{1,0:T(8,128)(2,1)}, u32[]{:S(2)}) copy-start(bf16[2048,1024]{1,0:T(8,128)(2,1)} %param.15) | copy-start | bytes 12582916
  154.2 10.6 %copy-start.34 = (f32[512]{0:T(512)S(1)}, f32[512]{0:T(512)}, u32[]{:S(2)}) copy-start(f32[512]{0:T(512)} %get-tuple-element.87) | copy-start | bytes 6148
  156.0 9.2 %copy-start.17 = (bf16[128,1024]{1,0:T(8,128)(2,1)S(1)}, bf16[128,1024]{1,0:T(8,128)(2,1)}, u32[]{:S(2)}) copy-start(bf16[128,1024]{1,0:T(8,128)(2,1)} %get-tuple-element.59) | copy-start | bytes 786436
  156.0 9.2 %copy-start.31 = (f32[1024]{0:T(1024)S(1)}, f32[1024]{0:T(1024)}, u32[]{:S(2)}) copy-start(f32[1024]{0:T(1024)} %slice_convert_fusion.2) | copy-start | bytes 12292
  164.8 4.3 %collective-permute-start.29 = (f32[256]{0:T(256)}, f32[256]{0:T(256)}, u32[]{:S(2)}, u32[]{:S(2)}) collective-permute-start(f32[256]{0:T(256)} %pad_maximum_fusion.12), channel_id=1, source_target_pairs={{0,1},{1,0},{2,3},{3,2},{4,5},{5,4},{6,7},{7,6},{8,9},{9,8},{10,11... | collective-permute-start | bytes 3080 | tf_op jit(solution)/shard_map/ppermute | solution.py:23
  166.8 16.3 %copy-start.18 = (s32[4,128,1]{2,1,0:T(8,128)S(1)}, s32[4,128,1]{2,1,0:T(8,128)}, u32[]{:S(2)}) copy-start(s32[4,128,1]{2,1,0:T(8,128)} %add.413) | copy-start | bytes 6148
  166.9 17.0 %copy-start.22 = (bf16[8,64,256]{2,1,0:T(8,128)(2,1)S(1)}, bf16[8,64,256]{2,1,0:T(8,128)(2,1)}, u32[]{:S(2)}) copy-start(bf16[8,64,256]{2,1,0:T(8,128)(2,1)} %copy-done.21) | copy-start | bytes 786436
  166.9 24.0 %copy-start.12 = (bf16[4,128,1024]{2,1,0:T(8,128)(2,1)S(1)}, bf16[4,128,1024]{2,1,0:T(8,128)(2,1)}, u32[]{:S(2)}) copy-start(bf16[4,128,1024]{2,1,0:T(8,128)(2,1)} %query_ref.1) | copy-start | bytes 3145732
  166.9 24.0 %copy-start.13 = (bf16[4,128,256]{2,1,0:T(8,128)(2,1)S(1)}, bf16[4,128,256]{2,1,0:T(8,128)(2,1)}, u32[]{:S(2)}) copy-start(bf16[4,128,256]{2,1,0:T(8,128)(2,1)} %text_ref.1) | copy-start | bytes 786436
  166.9 3.8 %collective-permute-start.27 = (bf16[2,256,256]{2,1,0:T(8,128)(2,1)S(1)}, bf16[2,256,256]{2,1,0:T(8,128)(2,1)S(1)}, u32[]{:S(2)}, u32[]{:S(2)}) collective-permute-start(bf16[2,256,256]{2,1,0:T(8,128)(2,1)S(1)} %fusion.28), channel_id=1, source_target_pairs={{0,1},{1,0},{2,3},{3,2},{4,5},{5,4},{6,7},{7,6},{8,9},{9,8},{10,11... | collective-permute-start | bytes 786440 | tf_op jit(solution)/shard_map/ppermute | solution.py:23
  169.7 3.6 %collective-permute-start.30 = (f32[256]{0:T(256)S(1)}, f32[256]{0:T(256)S(1)}, u32[]{:S(2)}, u32[]{:S(2)}) collective-permute-start(f32[256]{0:T(256)S(1)} %fusion.69), channel_id=1, source_target_pairs={{0,2},{1,3},{2,0},{3,1},{4,6},{5,7},{6,4},{7,5},{8,10},{9,11},{10,... | collective-permute-start | bytes 3080 | tf_op jit(solution)/shard_map/ppermute | solution.py:23
  170.8 12.4 %copy-start.29 = (pred[4,128,1]{2,1,0:T(8,128)(4,1)S(1)}, pred[4,128,1]{2,1,0:T(8,128)(4,1)}, u32[]{:S(2)}) copy-start(pred[4,128,1]{2,1,0:T(8,128)(4,1)} %broadcast_in_dim.28) | copy-start | bytes 1540
  170.9 5.5 %collective-permute-start.28 = (bf16[1,256,256]{2,1,0:T(8,128)(2,1)S(1)}, bf16[1,256,256]{2,1,0:T(8,128)(2,1)S(1)}, u32[]{:S(2)}, u32[]{:S(2)}) collective-permute-start(bf16[1,256,256]{2,1,0:T(8,128)(2,1)S(1)} %dynamic-slice_convert_fusion.1), channel_id=1, source_target_pairs={{0,2},{1,3},{2,0},{3,1},{4,6},{5,7},{6,4},{7,5},{8,10},{9,11},{10,... | collective-permute-start | bytes 393224 | tf_op jit(solution)/shard_map/ppermute | solution.py:23
  177.4 13.5 %all-to-all-start = ((bf16[8,64,256]{2,1,0:T(8,128)(2,1)}), bf16[8,64,256]{2,1,0:T(8,128)(2,1)S(1)}, u32[]{:S(2)}, u32[]{:S(2)}) async-start(bf16[8,64,256]{2,1,0:T(8,128)(2,1)} %bitcast.21), calls=%async_computation | async-start | bytes 524288 | tf_op jit(solution)/shard_map/all_to_all | solution.py:464
  (14 other events, 31.0 us)
where the time goes:
time: 198 us; the launch traced here: 196 us
  starting transfers between devices  71.1 us (36%)
  waiting for transfers between devices  48.1 us (24%)
  other arithmetic  25.5 us (13%)
  Pallas kernels  25.4 us (13%)
  local copies, waits for them, and re-layouts  20.5 us (10%)
  matrix products  4.17 us (2%)
    ppermute x11, starting transfers between devices, flip(): return lax.ppermute(value, axis, [(i, i ^ bit) for i in range(count)])  22.4 us
    ppermute x4, starting transfers between devices, send_sums(): inward = lax.ppermute(ride(inner, small), 'seq', along(INWARD))  20.5 us
    pallas_call x4, Pallas kernels, partial_products(): pl.pallas_call(functools.partial(partial_kernel, halves), grid=(count //...  16.2 us
    ppermute x4, waiting for transfers between devices, send_sums(): outward = lax.ppermute(ride(end, small), 'seq', along(OUTWARD))  14.6 us
    reduce_sum x4, other arithmetic, merge_tiles(): squared = jnp.sum(merged * merged, axis=1)  7.99 us
    ppermute x11, waiting for transfers between devices, flip(): return lax.ppermute(value, axis, [(i, i ^ bit) for i in range(count)])  7.91 us
    all_to_all x1, waiting for transfers between devices, shards(): lax.all_to_all(outgoing, 'seq', split_axis=0, concat_axis=0, tiled=True)  6.98 us
    ppermute x4, waiting for transfers between devices, finish_sums(): lax.ppermute(ride(add(inner[:rows], inward[:rows]), extra), 'seq', along(...  6.72 us
  transfers between devices with their start and end apart: 32, of which 12 were waited for; matrix products, arithmetic and copies ran while one was open for 20% of the time, Pallas kernels for 10%

commit v1 on v0

--- a/solution.py
+++ b/solution.py
@@ -50,9 +50,6 @@
     place = lax.axis_index("tp")
     half = lax.axis_size("tp") // 2
     return 2 * (place % half) + ((place // half) ^ (group & 1))
-
-
-ROLE_GROUPS = (3, 2, 1, 0)
 
 
 def order_kernel(share, scalars_ref, *refs):
@@ -87,45 +84,32 @@
 
 
 def partial_kernel(halves, *refs):
-    rows_refs, weights_refs = refs[:halves], refs[halves:-2]
-    inner_ref, end_ref = refs[-2:]
+    rows_refs, weights_refs, out_refs = refs[:halves], refs[halves:-4], refs[-4:]
+    weights = jnp.concatenate([ref[...] for ref in weights_refs], axis=0)
     for half, rows_ref in enumerate(rows_refs):
-        total = None
-        at = 0
-        for weights_ref in weights_refs:
-            depth = weights_ref.shape[0]
-            term = jnp.dot(
-                rows_ref[:, at : at + depth],
-                weights_ref[...],
-                preferred_element_type=jnp.float32,
-            )
-            total = term if total is None else total + term
-            at += depth
+        total = jnp.dot(rows_ref[...], weights, preferred_element_type=jnp.float32)
         total = total.astype(jnp.bfloat16)
         rows = total.shape[0] // 4
-        for role in range(3):
-            to = (role * halves + half) * rows
-            inner_ref[to : to + rows] = total[role * rows : (role + 1) * rows]
-        end_ref[half * rows : (half + 1) * rows] = total[3 * rows :]
+        for k, out_ref in enumerate(out_refs):
+            out_ref[half * rows : (half + 1) * rows] = total[k * rows : (k + 1) * rows]
 
 
 def partial_products(held, weights, count):
     halves = len(held)
     rows, depth = held[0].shape
-    rows = rows * halves
-    tile = min(count, 256)
+    tile = min(count, 512)
 
     def block(used, first):
         return pl.BlockSpec((used, tile), lambda i: (0, i + first // tile))
 
-    outs = (3 * rows // 4, rows // 4)
+    out = halves * rows // 4
     return pl.pallas_call(
         functools.partial(partial_kernel, halves),
         grid=(count // tile,),
-        in_specs=[pl.BlockSpec((rows // halves, depth), lambda i: (0, 0))] * halves
+        in_specs=[pl.BlockSpec((rows, depth), lambda i: (0, 0))] * halves
         + [block(used, first) for _, used, first in weights],
-        out_specs=[pl.BlockSpec((out, tile), lambda i: (0, i)) for out in outs],
-        out_shape=[jax.ShapeDtypeStruct((out, count), jnp.bfloat16) for out in outs],
+        out_specs=[pl.BlockSpec((out, tile), lambda i: (0, i))] * 4,
+        out_shape=[jax.ShapeDtypeStruct((out, count), jnp.bfloat16)] * 4,
         compiler_params=pltpu.CompilerParams(vmem_limit_bytes=VMEM),
         cost_estimate=pl.CostEstimate(flops=0, bytes_accessed=2 * count, transcendentals=0),
     )(*held, *[array for array, _, _ in weights])
@@ -136,51 +120,26 @@
     return [(a * width + i, b * width + i) for a, b in pairs for i in range(width)]
 
 
-INWARD = ((0, 1), (3, 2))
-OUTWARD = ((1, 0), (2, 3))
-ACROSS = ((1, 2), (2, 1))
-BEYOND = ((1, 3), (2, 0))
-
-
 def ride(value, extra):
     return jnp.concatenate([value] + extra, axis=0) if extra else value
 
 
-def send_sums(parts, small):
-    inner, end = parts
-    inward = lax.ppermute(ride(inner, small), "seq", along(INWARD))
-    outward = lax.ppermute(ride(end, small), "seq", along(OUTWARD))
-    return inward, outward
-
-
-def finish_sums(parts, arrived, is_end, small):
-    inner, end = parts
-    inward, outward = arrived
-    rows = end.shape[0]
-
-    def add(mine, other):
-        return (mine.astype(jnp.float32) + other.astype(jnp.float32)).astype(jnp.bfloat16)
-
-    def part(value, first, index=0):
-        count = small[0].shape[0]
-        return value[first + index * count : first + (index + 1) * count]
-
-    extra = [part(inward, 3 * rows)] + small if small else []
-    beyond = lax.ppermute(ride(add(inner[:rows], inward[:rows]), extra), "seq", along(BEYOND))
-    across = lax.ppermute(
-        ride(add(inner[rows : 2 * rows], inward[rows : 2 * rows]), extra), "seq", along(ACROSS)
-    )
-    at_end = end.astype(jnp.float32) + outward[:rows] + beyond[:rows]
-    at_middle = inner[2 * rows :].astype(jnp.float32) + inward[2 * rows : 3 * rows] + across[:rows]
-    shared = None
-    if small:
-        ends = [part(outward, rows), part(beyond, rows, 1), part(beyond, rows, 0)]
-        middles = [part(inward, 3 * rows), part(across, rows, 0), part(across, rows, 1)]
-        shared = small + [jnp.where(is_end, e, m) for e, m in zip(ends, middles)]
-    return jnp.where(is_end, at_end, at_middle).astype(jnp.bfloat16), shared
-
-
-PLAN = (((0,), 0, 4), ((1,), 0, 4), ((0, 1), 4, 2), ((0, 1), 6, 2))
+def send_direct(parts, small):
+    return [
+        lax.ppermute(ride(part, small), "seq", along([(a, a ^ k) for a in range(4)]))
+        for k, part in enumerate(parts[1:], 1)
+    ]
+
+
+def sum_direct(parts, arrived):
+    rows = parts[0].shape[0]
+    total = parts[0].astype(jnp.float32)
+    for other in arrived:
+        total = total + other[:rows]
+    return total.astype(jnp.bfloat16)
+
+
+PLAN = (((0,), 0, 4), ((1,), 0, 4), ((0, 1), 4, 4))
 RIDE = 2
 
 
@@ -192,7 +151,6 @@
     share = w_merge.shape[0]
     group = lax.axis_index("seq") // width
     member = lax.axis_index("seq") % width
-    is_end = (group == 0) | (group == 3)
     local = panels.reshape(tiles * panel_rows, depth)
     half = local.shape[0] // 2
     swapped = flip(local[half:], "tp", 2)
@@ -218,62 +176,57 @@
     aligned = width == 2 and share % 128 == 0
     if not aligned:
         share = depth
-    shift = jnp.where(group < 2, 0, 3)
-    groups = (panel_base() ^ jnp.arange(4, dtype=jnp.int32)) ^ shift
-    roles = jnp.array([ROLE_GROUPS.index(g) for g in range(4)], jnp.int32)[groups]
-    scalars = jnp.concatenate([roles, jnp.full((4,), member, jnp.int32)])
-    early = share_panels(moved[0])
-    early, moved[1] = lax.optimization_barrier((early, moved[1]))
-    held = [order_rows(scalars, early, share)]
+    places = panel_base() ^ jnp.arange(4, dtype=jnp.int32) ^ group
+    scalars = jnp.concatenate([places, jnp.full((4,), member, jnp.int32)])
+    early, _ = lax.optimization_barrier((moved[0], swapped))
+    held = [order_rows(scalars, share_panels(early), share)]
     kv = [0.0, 0.0]
     squares = [0.0, 0.0]
     everyone = None
     eighth = w_merge.shape[1] // 8
     sent = []
-    for step in range(len(PLAN) + 1):
-        if step < len(PLAN):
-            halves, first, count = PLAN[step]
-            first, count = first * eighth, count * eighth
-            if step == 1:
-                late, _ = lax.optimization_barrier((moved[1], sent[0][0][0]))
-                held.append(order_rows(scalars, share_panels(late), share))
-            if step == RIDE:
-                received[1], _ = lax.optimization_barrier((received[1], sent[step - 1][0][0]))
-                small = [small] + [other[-extra:] for other in received[1]]
-                small_shape = (width,) + small[0].shape
-                small = [jnp.stack(small).reshape(-1, count)]
-            side = first // columns
-            inside = first - side * columns
-            if aligned:
-                operands = [(w_merge, share, first), (received[side][0], share, inside)]
-            else:
-                parts = [w_merge[:, side * columns : (side + 1) * columns]]
-                parts += [other[: w_merge.shape[0]] for other in received[side]]
-                parts = jnp.concatenate(parts, axis=0)
-                operands = [(jnp.roll(parts, member * w_merge.shape[0], axis=0), depth, inside)]
-            rows = [held[h] for h in halves]
-            if step >= 2:
-                rows, _ = lax.optimization_barrier((rows, sent[step - 2][1][0]))
-            parts = partial_products(rows, operands, count)
-            riding = small if step == RIDE else []
-            sent.append((parts, send_sums(parts, riding), riding))
-        if step >= 1:
-            parts, arrived, riding = sent[step - 1]
-            if step < len(PLAN):
-                arrived, _ = lax.optimization_barrier((arrived, sent[step][0][0]))
-            halves, first, count = PLAN[step - 1]
-            first, count = first * eighth, count * eighth
-            merged, shared = finish_sums(parts, arrived, is_end, riding)
-            if shared is not None:
-                everyone = jnp.stack(shared).reshape((4,) + small_shape)
-            merged = merged.astype(jnp.float32)
-            at = slice(first, first + count)
-            gained = (merged * ln_gain[at].astype(jnp.float32)[None, :]).astype(jnp.bfloat16)
-            squared = jnp.sum(merged * merged, axis=1)
-            product = jnp.dot(gained, w_kv[at], preferred_element_type=jnp.float32)
-            for i, h in enumerate(halves):
-                squares[h] = squares[h] + squared[i * half : (i + 1) * half]
-                kv[h] = kv[h] + product[i * half : (i + 1) * half]
+
+    def finish(step):
+        halves, first, count = PLAN[step]
+        merged = sum_direct(*sent[step]).astype(jnp.float32)
+        at = slice(first * eighth, (first + count) * eighth)
+        gained = (merged * ln_gain[at].astype(jnp.float32)[None, :]).astype(jnp.bfloat16)
+        squared = jnp.sum(merged * merged, axis=1)
+        product = jnp.dot(gained, w_kv[at], preferred_element_type=jnp.float32)
+        for i, h in enumerate(halves):
+            squares[h] = squares[h] + squared[i * half : (i + 1) * half]
+            kv[h] = kv[h] + product[i * half : (i + 1) * half]
+
+    for step, (halves, first, count) in enumerate(PLAN):
+        first, count = first * eighth, count * eighth
+        if step == 1:
+            late, _ = lax.optimization_barrier((moved[1], sent[0][0][0]))
+            held.append(order_rows(scalars, share_panels(late), share))
+        riding = []
+        if step == RIDE:
+            received[1], _ = lax.optimization_barrier((received[1], sent[step - 1][0][0]))
+            small = [small] + [other[-extra:] for other in received[1]]
+            small_shape = (width,) + small[0].shape
+            riding = [jnp.stack(small).reshape(-1, count)]
+        side = first // columns
+        inside = first - side * columns
+        if aligned:
+            operands = [(w_merge, share, first), (received[side][0], share, inside)]
+        else:
+            parts = [w_merge[:, side * columns : (side + 1) * columns]]
+            parts += [other[: w_merge.shape[0]] for other in received[side]]
+            parts = jnp.concatenate(parts, axis=0)
+            operands = [(jnp.roll(parts, member * w_merge.shape[0], axis=0), depth, inside)]
+        parts = partial_products([held[h] for h in halves], operands, count)
+        if step:
+            before = [sent[step - 1][1][1]] + ([sent[step - 2][1][2]] if step >= 2 else [])
+            parts, _ = lax.optimization_barrier((parts, before))
+        sent.append((parts, send_direct(parts, riding)))
+    for step in range(len(PLAN)):
+        finish(step)
+    rows = sent[RIDE][0][0].shape[0]
+    everyone = riding + [other[rows:] for other in sent[RIDE][1]]
+    everyone = jnp.stack(everyone).reshape((4,) + small_shape)
     return jnp.concatenate(kv), jnp.concatenate(squares), everyone
 
 

time: 198 us -> 183 us (0.924)
  waiting for transfers between devices: 48.1 us -> 75.1 us
  starting transfers between devices: 71.1 us -> 55.6 us
  other arithmetic: 25.5 us -> 11.4 us
  local copies, waits for them, and re-layouts: 20.5 us -> 13.9 us
  Pallas kernels: 25.4 us -> 20.4 us
    ppermute x16 -> x9, waiting for transfers between devices: 25.5 us -> 43.8 us  [send_direct(): lax.ppermute(ride(part, small), 'seq', along([(a, a ^ k) for a in range(4...]
    ppermute x16 -> x9, starting transfers between devices: 34.1 us -> 20 us  [send_direct(): lax.ppermute(ride(part, small), 'seq', along([(a, a ^ k) for a in range(4...]
    ppermute x11, waiting for transfers between devices: 7.91 us -> 17.7 us  [flip(): return lax.ppermute(value, axis, [(i, i ^ bit) for i in range(count)])]
    all_to_all x1, starting transfers between devices: 5.06 us -> 13.9 us  [shards(): lax.all_to_all(outgoing, 'seq', split_axis=0, concat_axis=0, tiled=True)]
    ppermute x11, starting transfers between devices: 22.4 us -> 14.5 us  [flip(): return lax.ppermute(value, axis, [(i, i ^ bit) for i in range(count)])]
    convert_element_type x6 -> x1, other arithmetic: 6.26 us -> 0.6 us  [finish(): ln_gain[at].astype(jnp.float32)[None, :]]
    pallas_call x4 -> x3, Pallas kernels: 16.2 us -> 11.6 us  [partial_products(): pl.pallas_call(functools.partial(partial_kernel, halves), grid=(count //...]
    reduce_sum x4 -> x3, other arithmetic: 7.99 us -> 4.28 us  [finish(): squared = jnp.sum(merged * merged, axis=1)]
  transfers between devices with their start and end apart: 32 -> 25, of which waited for: 12 -> 11; matrix products, arithmetic and copies ran while one was open for 20% -> 13% of each run, Pallas kernels for 10% -> 8%
where the time goes in v1:
time: 183 us; the launch traced here: 182 us
  waiting for transfers between devices  75.1 us (41%)
  starting transfers between devices  55.6 us (30%)
  Pallas kernels  20.4 us (11%)
  local copies, waits for them, and re-layouts  13.9 us (8%)
  other arithmetic  11.4 us (6%)
  matrix products  4.52 us (2%)
    ppermute x9, waiting for transfers between devices, send_direct(): lax.ppermute(ride(part, small), 'seq', along([(a, a ^ k) for a in range(4...  43.8 us
    ppermute x9, starting transfers between devices, send_direct(): lax.ppermute(ride(part, small), 'seq', along([(a, a ^ k) for a in range(4...  20 us
    ppermute x11, waiting for transfers between devices, flip(): return lax.ppermute(value, axis, [(i, i ^ bit) for i in range(count)])  17.7 us
    ppermute x11, starting transfers between devices, flip(): return lax.ppermute(value, axis, [(i, i ^ bit) for i in range(count)])  14.5 us
    all_to_all x1, starting transfers between devices, shards(): lax.all_to_all(outgoing, 'seq', split_axis=0, concat_axis=0, tiled=True)  13.9 us
    pallas_call x3, Pallas kernels, partial_products(): pl.pallas_call(functools.partial(partial_kernel, halves), grid=(count //...  11.6 us
    all_to_all x1, waiting for transfers between devices, shards(): lax.all_to_all(outgoing, 'seq', split_axis=0, concat_axis=0, tiled=True)  8.19 us
    pallas_call x1, Pallas kernels, attend(): pl.pallas_call(attend_kernel, grid_spec=pltpu.PrefetchScalarGridSpec(num_...  5.51 us
  transfers between devices with their start and end apart: 25, of which 11 were waited for; matrix products, arithmetic and copies ran while one was open for 13% of the time, Pallas kernels for 8%

profile of v1, /device:TPU:0, one launch (start us, length us, event | category | flops | bytes accessed | tf_op | source)
XLA Modules:
  0.0 182.4 jit_solution(13086445078208180959)
XLA Ops:
  0.6 1.1 slice_bitcast_fusion
  1.7 0.7 collective-permute-start.3
  2.5 6.8 %collective-permute-start = (bf16[128,1280]{1,0:T(8,128)(2,1)S(1)}, bf16[128,1280]{1,0:T(8,128)(2,1)S(1)}, u32[]{:S(2)}, u32[]{:S(2)}) collective-permute-start(bf16[128,1280]{1,0:T(8,128)(2,1)S(1)} %get-tuple-element.63), channel_id=1, source_target_pairs={{0,2},{1,3},{2,0},{3,1},{4,6},{5,7},{6,4},{7,5},{8,10},{9,11},{10,... | collective-permute-start | bytes 983048 | tf_op jit(solution)/shard_map/ppermute | solution.py:23
  9.3 3.0 %fusion.55 = (bf16[640,1024]{1,0:T(8,128)(2,1)}, bf16[640,1024]{1,0:T(8,128)(2,1)S(1)}) fusion(bf16[640,2048]{1,0:T(8,128)(2,1)} %refs_2_.1), kind=kLoop, calls=%fused_computation.134 | loop fusion | bytes 5242880 | tf_op jit(solution)/shard_map/slice | solution.py:163
  12.3 1.5 collective-permute-start.7
  13.8 0.2 convert_reduce_fusion
  14.0 0.6 fusion.53
  14.9 0.8 gather_fusion.2
  15.9 6.7 %collective-permute-done = bf16[128,1280]{1,0:T(8,128)(2,1)S(1)} collective-permute-done((bf16[128,1280]{1,0:T(8,128)(2,1)S(1)}, bf16[128,1280]{1,0:T(8,128)(2,1)S(1)}, u32[]{:S(2)}, u32[]{:S(2)}) %collective-permute-start) | collective-permute-done | bytes 327712 | tf_op jit(solution)/shard_map/ppermute | solution.py:23
  22.6 2.5 %collective-permute-start.4 = (bf16[128,1280]{1,0:T(8,128)(2,1)S(1)}, bf16[128,1280]{1,0:T(8,128)(2,1)}, u32[]{:S(2)}, u32[]{:S(2)}) collective-permute-start(bf16[128,1280]{1,0:T(8,128)(2,1)S(1)} %collective-permute-done.3.refs_0_), channel_id=1, source_target_pairs={{0,2},{1,3},{2,0},{3,1},{4,6},{5,7},{6,4},{7,5},{8,10},{9,11},{10,... | collective-permute-start | bytes 983048 | tf_op jit(solution)/shard_map/ppermute | solution.py:23
  25.1 1.2 pad_maximum_fusion
  26.3 1.5 collective-permute-start.1
  27.9 0.6 broadcast_in_dim.24
  28.6 0.6 add.314
  29.3 0.5 copy-done.10
  29.8 3.4 %collective-permute-start.2 = (bf16[128,1280]{1,0:T(8,128)(2,1)}, bf16[128,1280]{1,0:T(8,128)(2,1)S(1)}, u32[]{:S(2)}, u32[]{:S(2)}) collective-permute-start(bf16[128,1280]{1,0:T(8,128)(2,1)} %copy-done.31), channel_id=1, source_target_pairs={{2,0},{3,10},{0,16},{1,26},{6,4},{7,14},{4,20},{5,30},{10,2},{11,8... | collective-permute-start | bytes 983048 | tf_op jit(solution)/shard_map/ppermute | solution.py:37
  33.3 2.3 %collective-permute-start.6 = (bf16[128,1280]{1,0:T(8,128)(2,1)}, bf16[128,1280]{1,0:T(8,128)(2,1)S(1)}, u32[]{:S(2)}, u32[]{:S(2)}) collective-permute-start(bf16[128,1280]{1,0:T(8,128)(2,1)} %collective-permute-done.4.refs_1_), channel_id=1, source_target_pairs={{0,1},{1,0},{2,3},{3,2},{4,5},{5,4},{6,7},{7,6},{8,9},{9,8},{10,11... | collective-permute-start | bytes 983048 | tf_op jit(solution)/shard_map/ppermute | solution.py:23
  35.7 0.6 slice_convert_fusion.3
  36.3 0.8 collective-permute-done.6.refs_3_
  37.1 1.6 shard_map.122.refs_0_
  38.8 5.5 %collective-permute-done.7.refs_2_ = bf16[640,1024]{1,0:T(8,128)(2,1)} collective-permute-done((bf16[640,1024]{1,0:T(8,128)(2,1)}, bf16[640,1024]{1,0:T(8,128)(2,1)}, u32[]{:S(2)}, u32[]{:S(2)}) %collective-permute-start.7) | collective-permute-done | bytes 1310752 | tf_op jit(solution)/shard_map/ppermute | solution.py:174
  44.2 3.5 %shard_map.123 = (bf16[128,1024]{1,0:T(8,128)(2,1)S(1)}, bf16[128,1024]{1,0:T(8,128)(2,1)S(1)}, bf16[128,1024]{1,0:T(8,128)(2,1)}, bf16[128,1024]{1,0:T(8,128)(2,1)S(1)}) custom-call(bf16[512,1280]{1,0:T(8,128)(2,1)S(1)} %shard_map.122.refs_0_, bf16[640,2048]{1,0:T(8,128)(2,1)S(1)} %copy-done, bf16[640,1024]{1,0:T(8,128)(2,1)} %collective-permute-done.7.refs_2_), custom_call_target="tpu_custom_call" | custom-call | bytes 2048 | tf_op jit(solution)/shard_map/pallas_call | solution.py:106
  47.8 0.7 copy-done.7
  48.6 0.7 add_add_fusion
  49.3 0.2 collective-permute-start.9
  49.6 3.2 %collective-permute-start.11 = (bf16[128,1024]{1,0:T(8,128)(2,1)}, bf16[128,1024]{1,0:T(8,128)(2,1)}, u32[]{:S(2)}, u32[]{:S(2)}) collective-permute-start(bf16[128,1024]{1,0:T(8,128)(2,1)} %get-tuple-element.34), channel_id=1, source_target_pairs={{0,16},{4,20},{8,24},{12,28},{16,0},{20,4},{24,8},{28,12},{1,17},{... | collective-permute-start | bytes 786440 | tf_op jit(solution)/shard_map/ppermute | solution.py:129
  52.7 5.6 %collective-permute-done.8.refs_1_ = bf16[128,1280]{1,0:T(8,128)(2,1)S(1)} collective-permute-done((bf16[128,1280]{1,0:T(8,128)(2,1)S(1)}, bf16[128,1280]{1,0:T(8,128)(2,1)S(1)}, u32[]{:S(2)}, u32[]{:S(2)}) %collective-permute-start.8) | collective-permute-done | bytes 327712 | tf_op jit(solution)/shard_map/ppermute | solution.py:23
  58.4 1.4 stack_reshape.6
  59.8 1.3 iota_add_fusion.1
  61.1 0.4 collective-permute-start.13
  61.6 1.7 shard_map.124.refs_0_.refs_1_
  63.3 3.7 %shard_map.125 = (bf16[128,1024]{1,0:T(8,128)(2,1)S(1)}, bf16[128,1024]{1,0:T(8,128)(2,1)}, bf16[128,1024]{1,0:T(8,128)(2,1)S(1)}, bf16[128,1024]{1,0:T(8,128)(2,1)}) custom-call(bf16[512,1280]{1,0:T(8,128)(2,1)S(1)} %shard_map.124.refs_0_.refs_1_, bf16[640,2048]{1,0:T(8,128)(2,1)S(1)} %copy-done, bf16[640,1024]{1,0:T(8,128)(2,1)} %collective-permute-done.7.refs_2_), custom_call_target="tpu_custom_call" | custom-call | bytes 2048 | tf_op jit(solution)/shard_map/pallas_call | solution.py:106
  67.0 0.7 copy-done.3
  67.7 4.0 %collective-permute-start.12 = (bf16[128,1024]{1,0:T(8,128)(2,1)S(1)}, bf16[128,1024]{1,0:T(8,128)(2,1)S(1)}, u32[]{:S(2)}, u32[]{:S(2)}) collective-permute-start(bf16[128,1024]{1,0:T(8,128)(2,1)S(1)} %get-tuple-element.41), channel_id=1, source_target_pairs={{0,16},{4,20},{8,24},{12,28},{16,0},{20,4},{24,8},{28,12},{1,17},{... | collective-permute-start | bytes 786440 | tf_op jit(solution)/shard_map/ppermute | solution.py:129
  71.6 3.1 %collective-permute-start.18 = (bf16[128,1024]{1,0:T(8,128)(2,1)}, bf16[128,1024]{1,0:T(8,128)(2,1)}, u32[]{:S(2)}, u32[]{:S(2)}) collective-permute-start(bf16[128,1024]{1,0:T(8,128)(2,1)} %get-tuple-element.48), channel_id=1, source_target_pairs={{0,8},{4,12},{8,0},{12,4},{16,24},{20,28},{24,16},{28,20},{1,9},{5... | collective-permute-start | bytes 786440 | tf_op jit(solution)/shard_map/ppermute | solution.py:129
  74.7 4.4 %shard_map.126 = (bf16[256,1024]{1,0:T(8,128)(2,1)S(1)}, bf16[256,1024]{1,0:T(8,128)(2,1)S(1)}, bf16[256,1024]{1,0:T(8,128)(2,1)S(1)}, bf16[256,1024]{1,0:T(8,128)(2,1)S(1)}) custom-call(bf16[512,1280]{1,0:T(8,128)(2,1)S(1)} %copy-done.2, bf16[512,1280]{1,0:T(8,128)(2,1)S(1)} %shard_map.124.refs_0_.refs_1_, bf16[640,2048]{1,0:T(8,128)(2,1)S(1)} %copy-done, ...), custom_call_target="tpu_custom_call" | custom-call | bytes 2048 | tf_op jit(solution)/shard_map/pallas_call | solution.py:106
  79.1 0.8 slice_bitcast_fusion.5
  79.9 7.9 %collective-permute-done.12 = bf16[128,1024]{1,0:T(8,128)(2,1)S(1)} collective-permute-done((bf16[128,1024]{1,0:T(8,128)(2,1)S(1)}, bf16[128,1024]{1,0:T(8,128)(2,1)S(1)}, u32[]{:S(2)}, u32[]{:S(2)}) %collective-permute-start.12) | collective-permute-done | bytes 262176 | tf_op jit(solution)/shard_map/ppermute | solution.py:129
  87.8 1.3 pad_maximum_fusion.4
  89.1 5.9 %collective-permute-start.14 = (bf16[288,1024]{1,0:T(8,128)(2,1)}, bf16[288,1024]{1,0:T(8,128)(2,1)S(1)}, u32[]{:S(2)}, u32[]{:S(2)}) collective-permute-start(bf16[288,1024]{1,0:T(8,128)(2,1)} %get-tuple-element.66), channel_id=1, source_target_pairs={{0,8},{4,12},{8,0},{12,4},{16,24},{20,28},{24,16},{28,20},{1,9},{5... | collective-permute-start | bytes 1769480 | tf_op jit(solution)/shard_map/ppermute | solution.py:129
  95.2 0.9 add.326
  96.2 3.4 %collective-permute-start.15 = (bf16[288,1024]{1,0:T(8,128)(2,1)}, bf16[288,1024]{1,0:T(8,128)(2,1)S(1)}, u32[]{:S(2)}, u32[]{:S(2)}) collective-permute-start(bf16[288,1024]{1,0:T(8,128)(2,1)} %get-tuple-element.67), channel_id=1, source_target_pairs={{0,16},{4,20},{8,24},{12,28},{16,0},{20,4},{24,8},{28,12},{1,17},{... | collective-permute-start | bytes 1769480 | tf_op jit(solution)/shard_map/ppermute | solution.py:129
  99.7 2.0 %fusion.15 = (f32[128]{0:T(128)S(1)}, bf16[128,1024]{1,0:T(8,128)(2,1)}) fusion(bf16[128,1024]{1,0:T(8,128)(2,1)} %copy-done.13, bf16[128,1024]{1,0:T(8,128)(2,1)} %collective-permute-done.11, bf16[128,1024]{1,0:T(8,128)(2,1)} %collective-permute-done.17, bf16[128,1024]{1,0:T(8,128)(2,1)S(1)} %get-tuple-element.28), kind=kLoop, calls=%fused_computation.33 | loop fusion | flops 1441664 | bytes 1311232 | tf_op jit(solution)/shard_map/reduce_sum | solution.py:194
  101.7 1.9 %fusion.17 = (f32[128]{0:T(128)S(1)}, bf16[128,1024]{1,0:T(8,128)(2,1)}) fusion(bf16[128,1024]{1,0:T(8,128)(2,1)} %collective-permute-done.19, bf16[128,1024]{1,0:T(8,128)(2,1)S(1)} %copy-done.15, bf16[128,1024]{1,0:T(8,128)(2,1)} %collective-permute-done.18, bf16[128,1024]{1,0:T(8,128)(2,1)S(1)} %copy-done.4), kind=kLoop, calls=%fused_computation.35 | loop fusion | flops 1441664 | bytes 1311232 | tf_op jit(solution)/shard_map/reduce_sum | solution.py:194
  103.6 15.4 %collective-permute-done.14 = bf16[288,1024]{1,0:T(8,128)(2,1)S(1)} collective-permute-done((bf16[288,1024]{1,0:T(8,128)(2,1)}, bf16[288,1024]{1,0:T(8,128)(2,1)S(1)}, u32[]{:S(2)}, u32[]{:S(2)}) %collective-permute-start.14) | collective-permute-done | bytes 589856 | tf_op jit(solution)/shard_map/ppermute | solution.py:129
  119.0 20.4 %collective-permute-done.15 = bf16[288,1024]{1,0:T(8,128)(2,1)S(1)} collective-permute-done((bf16[288,1024]{1,0:T(8,128)(2,1)}, bf16[288,1024]{1,0:T(8,128)(2,1)S(1)}, u32[]{:S(2)}, u32[]{:S(2)}) %collective-permute-start.15) | collective-permute-done | bytes 589856 | tf_op jit(solution)/shard_map/ppermute | solution.py:129
  139.7 0.6 gather_fusion
  140.2 0.6 gather_fusion.1
  140.8 0.2 reduce_window_sum.18
  141.0 0.2 multiply_reduce_fusion
  141.3 0.4 fusion.13
  141.9 2.6 %fusion = f32[256,1024]{1,0:T(8,128)S(1)} fusion(bf16[2048,1024]{1,0:T(8,128)(2,1)} %param.14, bf16[256,1024]{1,0:T(8,128)(2,1)S(1)} %get-tuple-element.53, f32[1024]{0:T(1024)S(1)} %copy-done.26), kind=kOutput, calls=%fused_computation.3 | convolution fusion | flops 537657344 | bytes 3674112 | tf_op jit(solution)/shard_map/dot_general | solution.py:195
  144.5 0.5 fusion.9
  145.0 0.5 copy-done.16
  145.4 0.5 fusion.6
  146.1 0.3 collective-permute-start.20
  146.7 1.3 collective-permute-start.23
  148.0 1.1 collective-permute-start.21
  149.1 1.2 collective-permute-done.23
  150.3 3.2 %collective-permute-done.21 = bf16[1,256,256]{2,1,0:T(8,128)(2,1)S(1)} collective-permute-done((bf16[1,256,256]{2,1,0:T(8,128)(2,1)S(1)}, bf16[1,256,256]{2,1,0:T(8,128)(2,1)S(1)}, u32[]{:S(2)}, u32[]{:S(2)}) %collective-permute-start.21) | collective-permute-done | bytes 131104 | tf_op jit(solution)/shard_map/ppermute | solution.py:23
  153.6 1.0 convolution_convert_fusion
  154.6 13.9 %all-to-all-start = ((bf16[8,64,256]{2,1,0:T(8,128)(2,1)}), bf16[8,64,256]{2,1,0:T(8,128)(2,1)S(1)}, u32[]{:S(2)}, u32[]{:S(2)}) async-start(bf16[8,64,256]{2,1,0:T(8,128)(2,1)} %bitcast.22), calls=%async_computation | async-start | bytes 524288 | tf_op jit(solution)/shard_map/all_to_all | solution.py:417
  168.7 8.2 %all-to-all-done = bf16[8,64,256]{2,1,0:T(8,128)(2,1)S(1)} async-done(((bf16[8,64,256]{2,1,0:T(8,128)(2,1)}), bf16[8,64,256]{2,1,0:T(8,128)(2,1)S(1)}, u32[]{:S(2)}, u32[]{:S(2)}) %all-to-all-start) | async-done | bytes 262176 | tf_op jit(solution)/shard_map/all_to_all | solution.py:417
  176.9 5.5 %shard_map.127 = (bf16[4,128,1024]{2,1,0:T(8,128)(2,1)}, bf16[256,256]{1,0:T(8,128)(2,1)}) custom-call(s32[4]{0:T(128)S(1)} %fusion.45.place_ref, bf16[4,128,1024]{2,1,0:T(8,128)(2,1)S(1)} %copy-done.5, bf16[8,32,256]{2,1,0:T(8,128)(2,1)S(1)} %slice.107.prefix_ref, bf16[4,128,256]{2,1,0:T(8,128)(2,1)S(1)} %copy-done.6, bf16[512,256]{1,0:T(8,128)(2,1)S(1)} %bitcast.60, ...), custom_call_target="tpu_custom_call" | custom-call | flops 603979776 | bytes 4194304 | tf_op jit(solution)/shard_map/pallas_call | solution.py:313
  (140 shorter events, 2.4 us)
Async XLA Ops:
  1.7 14.2 %collective-permute-start.3 = (bf16[128,1280]{1,0:T(8,128)(2,1)S(1)}, bf16[128,1280]{1,0:T(8,128)(2,1)S(1)}, u32[]{:S(2)}, u32[]{:S(2)}) collective-permute-start(bf16[128,1280]{1,0:T(8,128)(2,1)S(1)} %get-tuple-element.62), channel_id=1, source_target_pairs={{0,0},{1,10},{2,16},{3,26},{4,4},{5,14},{6,20},{7,30},{8,2},{9,8},... | collective-permute-start | bytes 983048 | tf_op jit(solution)/shard_map/ppermute | solution.py:37
  2.4 11.3 %copy-start.28 = (s32[32,1]{0,1:T(1,128)S(1)}, s32[32,1]{0,1:T(1,128)}, u32[]{:S(2)}) copy-start(s32[32,1]{0,1:T(1,128)} %param.15) | copy-start | bytes 388
  2.4 12.1 %copy-start.33 = (s32[1,4]{1,0:T(1,128)S(1)}, s32[1,4]{1,0:T(1,128)}, u32[]{:S(2)}) copy-start(s32[1,4]{1,0:T(1,128)} %param.17) | copy-start | bytes 52
  2.5 20.2 %collective-permute-start = (bf16[128,1280]{1,0:T(8,128)(2,1)S(1)}, bf16[128,1280]{1,0:T(8,128)(2,1)S(1)}, u32[]{:S(2)}, u32[]{:S(2)}) collective-permute-start(bf16[128,1280]{1,0:T(8,128)(2,1)S(1)} %get-tuple-element.63), channel_id=1, source_target_pairs={{0,2},{1,3},{2,0},{3,1},{4,6},{5,7},{6,4},{7,5},{8,10},{9,11},{10,... | collective-permute-start | bytes 983048 | tf_op jit(solution)/shard_map/ppermute | solution.py:23
  12.3 3.4 %copy-start.32 = (s32[32]{0:T(128)S(1)}, s32[32]{0:T(128)}, u32[]{:S(2)}) copy-start(s32[32]{0:T(128)} %param.16) | copy-start | bytes 388
  12.3 3.6 %copy-start.21 = (bf16[1,32,256]{2,1,0:T(8,128)(2,1)S(1)}, bf16[1,32,256]{2,1,0:T(8,128)(2,1)}, u32[]{:S(2)}) copy-start(bf16[1,32,256]{2,1,0:T(8,128)(2,1)} %param.19) | copy-start | bytes 49156
  12.3 32.0 %collective-permute-start.7 = (bf16[640,1024]{1,0:T(8,128)(2,1)}, bf16[640,1024]{1,0:T(8,128)(2,1)}, u32[]{:S(2)}, u32[]{:S(2)}) collective-permute-start(bf16[640,1024]{1,0:T(8,128)(2,1)} %get-tuple-element.56), channel_id=1, source_target_pairs={{4,0},{0,4},{12,8},{8,12},{20,16},{16,20},{28,24},{24,28},{5,1},{1... | collective-permute-start | bytes 3932168 | tf_op jit(solution)/shard_map/ppermute | solution.py:174
  15.9 13.3 %copy-start.12 = (bf16[64,256]{1,0:T(8,128)(2,1)}, bf16[64,256]{1,0:T(8,128)(2,1)S(1)}, u32[]{:S(2)}) copy-start(bf16[64,256]{1,0:T(8,128)(2,1)S(1)} %pad_maximum_fusion.8) | copy-start | bytes 98308
  22.6 3.7 %copy-start.31 = (bf16[128,1280]{1,0:T(8,128)(2,1)}, bf16[128,1280]{1,0:T(8,128)(2,1)S(1)}, u32[]{:S(2)}) copy-start(bf16[128,1280]{1,0:T(8,128)(2,1)S(1)} %collective-permute-done) | copy-start | bytes 983044
  22.6 10.7 %collective-permute-start.4 = (bf16[128,1280]{1,0:T(8,128)(2,1)S(1)}, bf16[128,1280]{1,0:T(8,128)(2,1)}, u32[]{:S(2)}, u32[]{:S(2)}) collective-permute-start(bf16[128,1280]{1,0:T(8,128)(2,1)S(1)} %collective-permute-done.3.refs_0_), channel_id=1, source_target_pairs={{0,2},{1,3},{2,0},{3,1},{4,6},{5,7},{6,4},{7,5},{8,10},{9,11},{10,... | collective-permute-start | bytes 983048 | tf_op jit(solution)/shard_map/ppermute | solution.py:23
  25.1 10.6 %copy-start.24 = (bf16[2048]{0:T(1024)(128)(2,1)S(1)}, bf16[2048]{0:T(1024)(128)(2,1)}, u32[]{:S(2)}) copy-start(bf16[2048]{0:T(1024)(128)(2,1)} %param.13) | copy-start | bytes 12292
  26.3 48.4 %collective-permute-start.1 = (bf16[656,1024]{1,0:T(8,128)(2,1)}, bf16[656,1024]{1,0:T(8,128)(2,1)}, u32[]{:S(2)}, u32[]{:S(2)}) collective-permute-start(bf16[656,1024]{1,0:T(8,128)(2,1)} %pad_maximum_fusion), channel_id=1, source_target_pairs={{4,0},{0,4},{12,8},{8,12},{20,16},{16,20},{28,24},{24,28},{5,1},{1... | collective-permute-start | bytes 4030472 | tf_op jit(solution)/shard_map/ppermute | solution.py:174
  29.2 0.6 copy-start.10
  29.2 15.0 %copy-start = (bf16[640,2048]{1,0:T(8,128)(2,1)S(1)}, bf16[640,2048]{1,0:T(8,128)(2,1)}, u32[]{:S(2)}) copy-start(bf16[640,2048]{1,0:T(8,128)(2,1)} %refs_2_.1) | copy-start | bytes 7864324
  29.8 6.5 %collective-permute-start.5 = (bf16[128,1280]{1,0:T(8,128)(2,1)S(1)}, bf16[128,1280]{1,0:T(8,128)(2,1)S(1)}, u32[]{:S(2)}, u32[]{:S(2)}) collective-permute-start(bf16[128,1280]{1,0:T(8,128)(2,1)S(1)} %collective-permute-done.3.refs_0_), channel_id=1, source_target_pairs={{0,1},{1,0},{2,3},{3,2},{4,5},{5,4},{6,7},{7,6},{8,9},{9,8},{10,11... | collective-permute-start | bytes 983048 | tf_op jit(solution)/shard_map/ppermute | solution.py:23
  29.8 18.0 %collective-permute-start.2 = (bf16[128,1280]{1,0:T(8,128)(2,1)}, bf16[128,1280]{1,0:T(8,128)(2,1)S(1)}, u32[]{:S(2)}, u32[]{:S(2)}) collective-permute-start(bf16[128,1280]{1,0:T(8,128)(2,1)} %copy-done.31), channel_id=1, source_target_pairs={{2,0},{3,10},{0,16},{1,26},{6,4},{7,14},{4,20},{5,30},{10,2},{11,8... | collective-permute-start | bytes 983048 | tf_op jit(solution)/shard_map/ppermute | solution.py:37
  33.3 3.8 %collective-permute-start.6 = (bf16[128,1280]{1,0:T(8,128)(2,1)}, bf16[128,1280]{1,0:T(8,128)(2,1)S(1)}, u32[]{:S(2)}, u32[]{:S(2)}) collective-permute-start(bf16[128,1280]{1,0:T(8,128)(2,1)} %collective-permute-done.4.refs_1_), channel_id=1, source_target_pairs={{0,1},{1,0},{2,3},{3,2},{4,5},{5,4},{6,7},{7,6},{8,9},{9,8},{10,11... | collective-permute-start | bytes 983048 | tf_op jit(solution)/shard_map/ppermute | solution.py:23
  38.7 9.0 %copy-start.1 = (bf16[512,1280]{1,0:T(8,128)(2,1)}, bf16[512,1280]{1,0:T(8,128)(2,1)S(1)}, u32[]{:S(2)}) copy-start(bf16[512,1280]{1,0:T(8,128)(2,1)S(1)} %shard_map.122.refs_0_) | copy-start | bytes 3932164
  38.8 9.8 %copy-start.22 = (s32[128]{0:T(128)S(1)}, s32[128]{0:T(128)}, u32[]{:S(2)}) copy-start(s32[128]{0:T(128)} %add.314) | copy-start | bytes 1540
  38.8 9.8 %copy-start.27 = (pred[4,128]{1,0:T(4,128)(4,1)S(1)}, pred[4,128]{1,0:T(4,128)(4,1)}, u32[]{:S(2)}) copy-start(pred[4,128]{1,0:T(4,128)(4,1)} %broadcast_in_dim.24) | copy-start | bytes 1540
  47.8 0.7 copy-start.7
  47.8 10.6 %copy-start.8 = (bf16[128,1024]{1,0:T(8,128)(2,1)}, bf16[128,1024]{1,0:T(8,128)(2,1)S(1)}, u32[]{:S(2)}) copy-start(bf16[128,1024]{1,0:T(8,128)(2,1)S(1)} %get-tuple-element.42) | copy-start | bytes 786436
  48.5 9.8 %collective-permute-start.8 = (bf16[128,1280]{1,0:T(8,128)(2,1)S(1)}, bf16[128,1280]{1,0:T(8,128)(2,1)S(1)}, u32[]{:S(2)}, u32[]{:S(2)}) collective-permute-start(bf16[128,1280]{1,0:T(8,128)(2,1)S(1)} %collective-permute-done.2.refs_0_), channel_id=1, source_target_pairs={{0,2},{1,3},{2,0},{3,1},{4,6},{5,7},{6,4},{7,5},{8,10},{9,11},{10,... | collective-permute-start | bytes 983048 | tf_op jit(solution)/shard_map/ppermute | solution.py:23
  49.3 12.2 %collective-permute-start.9 = (bf16[128,1280]{1,0:T(8,128)(2,1)S(1)}, bf16[128,1280]{1,0:T(8,128)(2,1)}, u32[]{:S(2)}, u32[]{:S(2)}) collective-permute-start(bf16[128,1280]{1,0:T(8,128)(2,1)S(1)} %collective-permute-done.2.refs_0_), channel_id=1, source_target_pairs={{0,1},{1,0},{2,3},{3,2},{4,5},{5,4},{6,7},{7,6},{8,9},{9,8},{10,11... | collective-permute-start | bytes 983048 | tf_op jit(solution)/shard_map/ppermute | solution.py:23
  49.6 18.1 %collective-permute-start.11 = (bf16[128,1024]{1,0:T(8,128)(2,1)}, bf16[128,1024]{1,0:T(8,128)(2,1)}, u32[]{:S(2)}, u32[]{:S(2)}) collective-permute-start(bf16[128,1024]{1,0:T(8,128)(2,1)} %get-tuple-element.34), channel_id=1, source_target_pairs={{0,16},{4,20},{8,24},{12,28},{16,0},{20,4},{24,8},{28,12},{1,17},{... | collective-permute-start | bytes 786440 | tf_op jit(solution)/shard_map/ppermute | solution.py:129
  58.4 3.2 %collective-permute-start.10 = (bf16[128,1280]{1,0:T(8,128)(2,1)S(1)}, bf16[128,1280]{1,0:T(8,128)(2,1)}, u32[]{:S(2)}, u32[]{:S(2)}) collective-permute-start(bf16[128,1280]{1,0:T(8,128)(2,1)S(1)} %collective-permute-done.8.refs_1_), channel_id=1, source_target_pairs={{0,1},{1,0},{2,3},{3,2},{4,5},{5,4},{6,7},{7,6},{8,9},{9,8},{10,11... | collective-permute-start | bytes 983048 | tf_op jit(solution)/shard_map/ppermute | solution.py:23
  61.1 18.7 %collective-permute-start.13 = (bf16[128,1024]{1,0:T(8,128)(2,1)}, bf16[128,1024]{1,0:T(8,128)(2,1)S(1)}, u32[]{:S(2)}, u32[]{:S(2)}) collective-permute-start(bf16[128,1024]{1,0:T(8,128)(2,1)} %copy-done.8), channel_id=1, source_target_pairs={{0,24},{4,28},{8,16},{12,20},{16,8},{20,12},{24,0},{28,4},{1,25},{... | collective-permute-start | bytes 786440 | tf_op jit(solution)/shard_map/ppermute | solution.py:129
  61.5 38.1 %collective-permute-start.17 = (bf16[128,1024]{1,0:T(8,128)(2,1)}, bf16[128,1024]{1,0:T(8,128)(2,1)}, u32[]{:S(2)}, u32[]{:S(2)}) collective-permute-start(bf16[128,1024]{1,0:T(8,128)(2,1)} %copy-done.7), channel_id=1, source_target_pairs={{0,8},{4,12},{8,0},{12,4},{16,24},{20,28},{24,16},{28,20},{1,9},{5... | collective-permute-start | bytes 786440 | tf_op jit(solution)/shard_map/ppermute | solution.py:129
  63.3 11.4 %copy-start.2 = (bf16[512,1280]{1,0:T(8,128)(2,1)S(1)}, bf16[512,1280]{1,0:T(8,128)(2,1)}, u32[]{:S(2)}) copy-start(bf16[512,1280]{1,0:T(8,128)(2,1)} %copy-done.1) | copy-start | bytes 3932164
  67.0 0.7 copy-start.3
  67.7 12.2 %copy-start.18 = (bf16[1,16,1024]{2,1,0:T(8,128)(2,1)S(1)}, bf16[1,16,1024]{2,1,0:T(8,128)(2,1)}, u32[]{:S(2)}) copy-start(bf16[1,16,1024]{2,1,0:T(8,128)(2,1)} %stack_reshape.6) | copy-start | bytes 98308
  67.7 20.1 %collective-permute-start.12 = (bf16[128,1024]{1,0:T(8,128)(2,1)S(1)}, bf16[128,1024]{1,0:T(8,128)(2,1)S(1)}, u32[]{:S(2)}, u32[]{:S(2)}) collective-permute-start(bf16[128,1024]{1,0:T(8,128)(2,1)S(1)} %get-tuple-element.41), channel_id=1, source_target_pairs={{0,16},{4,20},{8,24},{12,28},{16,0},{20,4},{24,8},{28,12},{1,17},{... | collective-permute-start | bytes 786440 | tf_op jit(solution)/shard_map/ppermute | solution.py:129
  71.6 30.0 %collective-permute-start.18 = (bf16[128,1024]{1,0:T(8,128)(2,1)}, bf16[128,1024]{1,0:T(8,128)(2,1)}, u32[]{:S(2)}, u32[]{:S(2)}) collective-permute-start(bf16[128,1024]{1,0:T(8,128)(2,1)} %get-tuple-element.48), channel_id=1, source_target_pairs={{0,8},{4,12},{8,0},{12,4},{16,24},{20,28},{24,16},{28,20},{1,9},{5... | collective-permute-start | bytes 786440 | tf_op jit(solution)/shard_map/ppermute | solution.py:129
  74.7 27.0 %collective-permute-start.19 = (bf16[128,1024]{1,0:T(8,128)(2,1)}, bf16[128,1024]{1,0:T(8,128)(2,1)}, u32[]{:S(2)}, u32[]{:S(2)}) collective-permute-start(bf16[128,1024]{1,0:T(8,128)(2,1)} %get-tuple-element.49), channel_id=1, source_target_pairs={{0,24},{4,28},{8,16},{12,20},{16,8},{20,12},{24,0},{28,4},{1,25},{... | collective-permute-start | bytes 786440 | tf_op jit(solution)/shard_map/ppermute | solution.py:129
  79.9 9.3 %copy-start.13 = (bf16[128,1024]{1,0:T(8,128)(2,1)}, bf16[128,1024]{1,0:T(8,128)(2,1)S(1)}, u32[]{:S(2)}) copy-start(bf16[128,1024]{1,0:T(8,128)(2,1)S(1)} %collective-permute-done.13) | copy-start | bytes 786436
  87.8 1.3 copy-start.14
  87.8 7.4 %copy-start.11 = (s32[4,16,8]{2,1,0:T(8,128)S(1)}, s32[4,16,8]{2,1,0:T(8,128)}, u32[]{:S(2)}) copy-start(s32[4,16,8]{2,1,0:T(8,128)} %copy-done.10) | copy-start | bytes 6148
  87.8 8.3 %copy-start.20 = (s32[4,288]{1,0:T(4,128)S(1)}, s32[4,288]{1,0:T(4,128)}, u32[]{:S(2)}) copy-start(s32[4,288]{1,0:T(4,128)} %add_add_fusion) | copy-start | bytes 13828
  87.8 8.3 %copy-start.19 = (s32[32,8]{1,0:T(8,128)S(1)}, s32[32,8]{1,0:T(8,128)}, u32[]{:S(2)}) copy-start(s32[32,8]{1,0:T(8,128)} %iota_add_fusion.1) | copy-start | bytes 3076
  89.1 12.6 %copy-start.4 = (bf16[128,1024]{1,0:T(8,128)(2,1)S(1)}, bf16[128,1024]{1,0:T(8,128)(2,1)}, u32[]{:S(2)}) copy-start(bf16[128,1024]{1,0:T(8,128)(2,1)} %copy-done.3) | copy-start | bytes 786436
  89.1 12.6 %copy-start.15 = (bf16[128,1024]{1,0:T(8,128)(2,1)S(1)}, bf16[128,1024]{1,0:T(8,128)(2,1)}, u32[]{:S(2)}) copy-start(bf16[128,1024]{1,0:T(8,128)(2,1)} %copy-done.14) | copy-start | bytes 786436
  89.1 29.9 %collective-permute-start.14 = (bf16[288,1024]{1,0:T(8,128)(2,1)}, bf16[288,1024]{1,0:T(8,128)(2,1)S(1)}, u32[]{:S(2)}, u32[]{:S(2)}) collective-permute-start(bf16[288,1024]{1,0:T(8,128)(2,1)} %get-tuple-element.66), channel_id=1, source_target_pairs={{0,8},{4,12},{8,0},{12,4},{16,24},{20,28},{24,16},{28,20},{1,9},{5... | collective-permute-start | bytes 1769480 | tf_op jit(solution)/shard_map/ppermute | solution.py:129
  96.2 43.2 %collective-permute-start.15 = (bf16[288,1024]{1,0:T(8,128)(2,1)}, bf16[288,1024]{1,0:T(8,128)(2,1)S(1)}, u32[]{:S(2)}, u32[]{:S(2)}) collective-permute-start(bf16[288,1024]{1,0:T(8,128)(2,1)} %get-tuple-element.67), channel_id=1, source_target_pairs={{0,16},{4,20},{8,24},{12,28},{16,0},{20,4},{24,8},{28,12},{1,17},{... | collective-permute-start | bytes 1769480 | tf_op jit(solution)/shard_map/ppermute | solution.py:129
  101.7 37.8 %collective-permute-start.16 = (bf16[288,1024]{1,0:T(8,128)(2,1)}, bf16[288,1024]{1,0:T(8,128)(2,1)S(1)}, u32[]{:S(2)}, u32[]{:S(2)}) collective-permute-start(bf16[288,1024]{1,0:T(8,128)(2,1)} %get-tuple-element.68), channel_id=1, source_target_pairs={{0,24},{4,28},{8,16},{12,20},{16,8},{20,12},{24,0},{28,4},{1,25},{... | collective-permute-start | bytes 1769480 | tf_op jit(solution)/shard_map/ppermute | solution.py:129
  140.8 1.0 copy-start.26
  141.3 3.1 %copy-start.30 = (bf16[2048,1024]{1,0:T(8,128)(2,1)S(1)}, bf16[2048,1024]{1,0:T(8,128)(2,1)}, u32[]{:S(2)}) copy-start(bf16[2048,1024]{1,0:T(8,128)(2,1)} %param.14) | copy-start | bytes 12582916
  141.7 4.9 %collective-permute-start.22 = (f32[256]{0:T(256)S(1)}, f32[256]{0:T(256)S(1)}, u32[]{:S(2)}, u32[]{:S(2)}) collective-permute-start(f32[256]{0:T(256)S(1)} %pad_maximum_fusion.9), channel_id=1, source_target_pairs={{0,1},{1,0},{2,3},{3,2},{4,5},{5,4},{6,7},{7,6},{8,9},{9,8},{10,11... | collective-permute-start | bytes 3080 | tf_op jit(solution)/shard_map/ppermute | solution.py:23
  141.8 2.6 %copy-start.17 = (bf16[128,1024]{1,0:T(8,128)(2,1)S(1)}, bf16[128,1024]{1,0:T(8,128)(2,1)}, u32[]{:S(2)}) copy-start(bf16[128,1024]{1,0:T(8,128)(2,1)} %get-tuple-element.55) | copy-start | bytes 786436
  141.8 2.6 %copy-start.25 = (f32[1024]{0:T(1024)S(1)}, f32[1024]{0:T(1024)}, u32[]{:S(2)}) copy-start(f32[1024]{0:T(1024)} %get-tuple-element.69) | copy-start | bytes 12292
  144.5 1.0 copy-start.16
  146.1 1.8 collective-permute-start.20
  146.6 21.9 %copy-start.29 = (s32[4]{0:T(128)S(1)}, s32[4]{0:T(128)}, u32[]{:S(2)}) copy-start(s32[4]{0:T(128)} %param.18) | copy-start | bytes 52
  146.7 21.9 %copy-start.9 = (s32[4,128,1]{2,1,0:T(8,128)S(1)}, s32[4,128,1]{2,1,0:T(8,128)}, u32[]{:S(2)}) copy-start(s32[4,128,1]{2,1,0:T(8,128)} %add.326) | copy-start | bytes 6148
  146.7 21.9 %copy-start.23 = (s32[128]{0:T(128)S(1)}, s32[128]{0:T(128)}, u32[]{:S(2)}) copy-start(s32[128]{0:T(128)} %add.314) | copy-start | bytes 1540
  146.7 3.6 %collective-permute-start.23 = (f32[256]{0:T(256)S(1)}, f32[256]{0:T(256)S(1)}, u32[]{:S(2)}, u32[]{:S(2)}) collective-permute-start(f32[256]{0:T(256)S(1)} %fusion.54), channel_id=1, source_target_pairs={{0,2},{1,3},{2,0},{3,1},{4,6},{5,7},{6,4},{7,5},{8,10},{9,11},{10,... | collective-permute-start | bytes 3080 | tf_op jit(solution)/shard_map/ppermute | solution.py:23
  148.0 28.9 %copy-start.5 = (bf16[4,128,1024]{2,1,0:T(8,128)(2,1)S(1)}, bf16[4,128,1024]{2,1,0:T(8,128)(2,1)}, u32[]{:S(2)}) copy-start(bf16[4,128,1024]{2,1,0:T(8,128)(2,1)} %query_ref.1) | copy-start | bytes 3145732
  148.0 28.9 %copy-start.6 = (bf16[4,128,256]{2,1,0:T(8,128)(2,1)S(1)}, bf16[4,128,256]{2,1,0:T(8,128)(2,1)}, u32[]{:S(2)}) copy-start(bf16[4,128,256]{2,1,0:T(8,128)(2,1)} %text_ref.1) | copy-start | bytes 786436
  148.0 5.5 %collective-permute-start.21 = (bf16[1,256,256]{2,1,0:T(8,128)(2,1)S(1)}, bf16[1,256,256]{2,1,0:T(8,128)(2,1)S(1)}, u32[]{:S(2)}, u32[]{:S(2)}) collective-permute-start(bf16[1,256,256]{2,1,0:T(8,128)(2,1)S(1)} %dynamic-slice_convert_fusion.1), channel_id=1, source_target_pairs={{0,2},{1,3},{2,0},{3,1},{4,6},{5,7},{6,4},{7,5},{8,10},{9,11},{10,... | collective-permute-start | bytes 393224 | tf_op jit(solution)/shard_map/ppermute | solution.py:23
  154.6 22.3 %all-to-all-start = ((bf16[8,64,256]{2,1,0:T(8,128)(2,1)}), bf16[8,64,256]{2,1,0:T(8,128)(2,1)S(1)}, u32[]{:S(2)}, u32[]{:S(2)}) async-start(bf16[8,64,256]{2,1,0:T(8,128)(2,1)} %bitcast.22), calls=%async_computation | async-start | bytes 524288 | tf_op jit(solution)/shard_map/all_to_all | solution.py:417

commit v2 on v1

--- a/solution.py
+++ b/solution.py
@@ -84,35 +84,51 @@
 
 
 def partial_kernel(halves, *refs):
-    rows_refs, weights_refs, out_refs = refs[:halves], refs[halves:-4], refs[-4:]
-    weights = jnp.concatenate([ref[...] for ref in weights_refs], axis=0)
-    for half, rows_ref in enumerate(rows_refs):
-        total = jnp.dot(rows_ref[...], weights, preferred_element_type=jnp.float32)
-        total = total.astype(jnp.bfloat16)
-        rows = total.shape[0] // 4
-        for k, out_ref in enumerate(out_refs):
-            out_ref[half * rows : (half + 1) * rows] = total[k * rows : (k + 1) * rows]
-
-
-def partial_products(held, weights, count):
+    rows_refs, own_ref, others, out_refs = refs[:halves], refs[halves], refs[halves + 1 : -4], refs[-4:]
+
+    def multiply(weights):
+        for half, rows_ref in enumerate(rows_refs):
+            total = jnp.dot(rows_ref[...], weights, preferred_element_type=jnp.float32)
+            total = total.astype(jnp.bfloat16)
+            rows = total.shape[0] // 4
+            for k, out_ref in enumerate(out_refs):
+                out_ref[half * rows : (half + 1) * rows] = total[k * rows : (k + 1) * rows]
+
+    def joined(other):
+        return multiply(jnp.concatenate([own_ref[...], other[...]], axis=0))
+
+    if not others:
+        multiply(own_ref[...])
+    elif len(others) == 1:
+        joined(others[0])
+    else:
+        for index, other in enumerate(others):
+            pl.when(pl.program_id(0) == index)(functools.partial(joined, other))
+
+
+def partial_products(held, operands, count):
+    array, first, others = operands
     halves = len(held)
     rows, depth = held[0].shape
     tile = min(count, 512)
-
-    def block(used, first):
-        return pl.BlockSpec((used, tile), lambda i: (0, i + first // tile))
-
+    used = depth // 2 if others else depth
+    if len(others) > 1:
+        assert all(other.shape[1] == tile for other in others)
     out = halves * rows // 4
     return pl.pallas_call(
         functools.partial(partial_kernel, halves),
         grid=(count // tile,),
         in_specs=[pl.BlockSpec((rows, depth), lambda i: (0, 0))] * halves
-        + [block(used, first) for _, used, first in weights],
+        + [pl.BlockSpec((used, tile), lambda i: (0, i + first // tile))]
+        + [
+            pl.BlockSpec((used, tile), (lambda i: (0, 0)) if len(others) > 1 else (lambda i: (0, i)))
+            for _ in others
+        ],
         out_specs=[pl.BlockSpec((out, tile), lambda i: (0, i))] * 4,
         out_shape=[jax.ShapeDtypeStruct((out, count), jnp.bfloat16)] * 4,
         compiler_params=pltpu.CompilerParams(vmem_limit_bytes=VMEM),
         cost_estimate=pl.CostEstimate(flops=0, bytes_accessed=2 * count, transcendentals=0),
-    )(*held, *[array for array, _, _ in weights])
+    )(*held, array, *others)
 
 
 def along(pairs):
@@ -139,8 +155,9 @@
     return total.astype(jnp.bfloat16)
 
 
-PLAN = (((0,), 0, 4), ((1,), 0, 4), ((0, 1), 4, 4))
-RIDE = 2
+PLAN = (((0,), 0, 2), ((0,), 2, 2), ((1,), 0, 4), ((0, 1), 4, 4))
+RIDE = 3
+WEIGHT_PARTS = (2, 2, 4)
 
 
 def merge_tiles(panels, w_merge, ln_gain, w_kv, small):
@@ -155,14 +172,16 @@
     half = local.shape[0] // 2
     swapped = flip(local[half:], "tp", 2)
     moved = [transpose_panels(local[:half], 0), transpose_panels(swapped, 2)]
-    columns = w_merge.shape[1] // 2
-    small = small.reshape(-1, columns)
+    eighth = w_merge.shape[1] // 8
+    small = small.reshape(-1, WEIGHT_PARTS[-1] * eighth)
     extra = small.shape[0]
     received = []
-    for side in range(2):
-        own = w_merge[:, side * columns : (side + 1) * columns]
-        if side == 1:
+    for index, part in enumerate(WEIGHT_PARTS):
+        first = sum(WEIGHT_PARTS[:index]) * eighth
+        own = w_merge[:, first : first + part * eighth]
+        if index == len(WEIGHT_PARTS) - 1:
             own = jnp.concatenate([own, small], axis=0)
+        if index:
             own, _ = lax.optimization_barrier((own, swapped))
         others = []
         for offset in range(1, width):
@@ -180,67 +199,76 @@
     scalars = jnp.concatenate([places, jnp.full((4,), member, jnp.int32)])
     early, _ = lax.optimization_barrier((moved[0], swapped))
     held = [order_rows(scalars, share_panels(early), share)]
-    kv = [0.0, 0.0]
-    squares = [0.0, 0.0]
-    everyone = None
-    eighth = w_merge.shape[1] // 8
     sent = []
 
     def finish(step):
-        halves, first, count = PLAN[step]
+        _, first, count = PLAN[step]
         merged = sum_direct(*sent[step]).astype(jnp.float32)
         at = slice(first * eighth, (first + count) * eighth)
         gained = (merged * ln_gain[at].astype(jnp.float32)[None, :]).astype(jnp.bfloat16)
         squared = jnp.sum(merged * merged, axis=1)
-        product = jnp.dot(gained, w_kv[at], preferred_element_type=jnp.float32)
-        for i, h in enumerate(halves):
-            squares[h] = squares[h] + squared[i * half : (i + 1) * half]
-            kv[h] = kv[h] + product[i * half : (i + 1) * half]
+        return squared, jnp.dot(gained, w_kv[at], preferred_element_type=jnp.float32)
 
     for step, (halves, first, count) in enumerate(PLAN):
-        first, count = first * eighth, count * eighth
-        if step == 1:
+        if step == 2:
             late, _ = lax.optimization_barrier((moved[1], sent[0][0][0]))
             held.append(order_rows(scalars, share_panels(late), share))
         riding = []
         if step == RIDE:
-            received[1], _ = lax.optimization_barrier((received[1], sent[step - 1][0][0]))
-            small = [small] + [other[-extra:] for other in received[1]]
+            received[-1], _ = lax.optimization_barrier((received[-1], sent[step - 1][0][0]))
+            small = [small] + [other[-extra:] for other in received[-1]]
             small_shape = (width,) + small[0].shape
-            riding = [jnp.stack(small).reshape(-1, count)]
-        side = first // columns
-        inside = first - side * columns
+            riding = [jnp.stack(small).reshape(-1, count * eighth)]
+        others = []
+        for index, part in enumerate(WEIGHT_PARTS):
+            begin = sum(WEIGHT_PARTS[:index])
+            if begin < first + count and begin + part > first:
+                others.append(received[index])
+        own = w_merge[:, first * eighth : (first + count) * eighth]
         if aligned:
-            operands = [(w_merge, share, first), (received[side][0], share, inside)]
+            operands = (w_merge, first * eighth, [other[0] for other in others])
         else:
-            parts = [w_merge[:, side * columns : (side + 1) * columns]]
-            parts += [other[: w_merge.shape[0]] for other in received[side]]
-            parts = jnp.concatenate(parts, axis=0)
-            operands = [(jnp.roll(parts, member * w_merge.shape[0], axis=0), depth, inside)]
-        parts = partial_products([held[h] for h in halves], operands, count)
+            rows = [own] + [
+                jnp.concatenate([other[i][: own.shape[0]] for other in others], axis=1)
+                for i in range(width - 1)
+            ]
+            rows = jnp.concatenate(rows, axis=0)
+            operands = (jnp.roll(rows, member * own.shape[0], axis=0), 0, [])
+        parts = partial_products([held[h] for h in halves], operands, count * eighth)
         if step:
             before = [sent[step - 1][1][1]] + ([sent[step - 2][1][2]] if step >= 2 else [])
             parts, _ = lax.optimization_barrier((parts, before))
         sent.append((parts, send_direct(parts, riding)))
-    for step in range(len(PLAN)):
-        finish(step)
+    done = [finish(step) for step in range(len(PLAN))]
+    squares, kv = [
+        jnp.concatenate([done[0][i] + done[1][i], done[2][i]], axis=0) + done[3][i] for i in range(2)
+    ]
     rows = sent[RIDE][0][0].shape[0]
     everyone = riding + [other[rows:] for other in sent[RIDE][1]]
     everyone = jnp.stack(everyone).reshape((4,) + small_shape)
-    return jnp.concatenate(kv), jnp.concatenate(squares), everyone
+    return kv, squares, everyone
 
 
 def scatter_heads(kv, squares):
     tp_count = lax.axis_size("tp")
     place = lax.axis_index("tp")
-    rows = kv.shape[0]
-    blocks = jnp.stack(jnp.split(kv, tp_count, axis=1))
+    width = kv.shape[1] // tp_count
+    blocks = None
     for bit in bits_of(tp_count):
-        paired = blocks.reshape(blocks.shape[0] // 2, 2, rows, blocks.shape[2])
         mine = (place // bit) % 2
-        keep = lax.dynamic_index_in_dim(paired, mine, 1, keepdims=False)
-        give = lax.dynamic_index_in_dim(paired, 1 - mine, 1, keepdims=False)
-        blocks = keep + flip(give.astype(jnp.bfloat16), "tp", bit).astype(jnp.float32)
+
+        def half(which):
+            if blocks is not None:
+                paired = blocks.reshape((-1, 2) + blocks.shape[1:])
+                return lax.dynamic_index_in_dim(paired, which, 1, keepdims=False)
+            columns = [
+                lax.dynamic_slice_in_dim(kv, (2 * i + which) * width, width, axis=1)
+                for i in range(tp_count // 2)
+            ]
+            return jnp.stack(columns)
+
+        arrived = flip(half(1 - mine).astype(jnp.bfloat16), "tp", bit)
+        blocks = half(mine) + arrived.astype(jnp.float32)
         squares = squares + flip(squares, "tp", bit)
     return blocks[0], squares
 
@@ -257,7 +285,7 @@
 
 
 def attend_kernel(
-    place_ref, query_ref, prefix_ref, text_ref, pages_ref, pick_ref, seen_ref, all_ref, out_ref, vision_ref
+    place_ref, query_ref, prefix_ref, text_ref, pages_ref, pick_ref, all_ref, out_ref, vision_ref
 ):
     pages = pages_ref[...]
     count = pages.shape[0]
@@ -271,11 +299,16 @@
     def _():
         vision_ref[...] = pick(all_ref[...])
 
-    window = pick(pick_ref[0])
-    keys_values = jnp.concatenate([prefix_ref[0], window, text_ref[0]], axis=0)
-    text_rows = text_ref.shape[1]
+    picked = pick_ref[0]
+    window = pick(picked)
+    text = text_ref[0]
+    text_rows = text.shape[0]
+    keys_values = jnp.concatenate([prefix_ref[0], window, text], axis=0)
     heads = keys_values.shape[1] // (2 * HD)
     query = query_ref[0]
+    scale = HD**-0.5
+    first = prefix_ref.shape[1]
+    second = first + window.shape[0]
     for head in range(heads):
         keys = keys_values[:, 2 * head * HD : (2 * head + 1) * HD]
         values = keys_values[:, (2 * head + 1) * HD : (2 * head + 2) * HD]
@@ -286,30 +319,40 @@
             ],
             axis=0,
         )
-        scores = lax.dot_general(
-            stacked, keys, (((1,), (1,)), ((), ())), preferred_element_type=jnp.float32
-        ) * (HD**-0.5)
-        row = lax.broadcasted_iota(jnp.int32, scores.shape, 0) % text_rows
-        column = lax.broadcasted_iota(jnp.int32, scores.shape, 1)
-        text_column = column - (scores.shape[1] - text_rows)
-        allowed = (text_column <= row) & (seen_ref[0] > 0)
-        scores = jnp.where(allowed, scores, -1e30)
-        best = jnp.max(scores, axis=1, keepdims=True)
-        weights = jnp.exp(scores - best)
-        total = jnp.sum(weights, axis=1, keepdims=True)
-        result = jnp.dot(weights.astype(jnp.bfloat16), values, preferred_element_type=jnp.float32)
-        result = (result / total).astype(jnp.bfloat16)
+        scores = scale * lax.dot_general(
+            keys, stacked, (((1,), (1,)), ((), ())), preferred_element_type=jnp.float32
+        )
+        shape = (text_rows, scores.shape[1])
+        key_row = lax.broadcasted_iota(jnp.int32, shape, 0)
+        query_row = lax.broadcasted_iota(jnp.int32, shape, 1) % text_rows
+        scores = jnp.concatenate(
+            [
+                scores[:first],
+                jnp.where(picked >= 0, scores[first:second], -1e30),
+                jnp.where(key_row <= query_row, scores[second:], -1e30),
+            ],
+            axis=0,
+        )
+        weights = jnp.exp(scores - jnp.max(scores, axis=0, keepdims=True))
+        total = jnp.sum(weights, axis=0, keepdims=True)
+        result = lax.dot_general(
+            values,
+            weights.astype(jnp.bfloat16),
+            (((0,), (0,)), ((), ())),
+            preferred_element_type=jnp.float32,
+        )
+        result = result / total
         for a in range(GROUP):
-            out_ref[0, :, (head * GROUP + a) * HD : (head * GROUP + a + 1) * HD] = result[
-                a * text_rows : (a + 1) * text_rows
-            ]
-
-
-def attend(place, queries, prefixes, text_kv, pages, picks, seen, all_rows):
+            out_ref[0, :, (head * GROUP + a) * HD : (head * GROUP + a + 1) * HD] = (
+                result[:, a * text_rows : (a + 1) * text_rows].T.astype(jnp.bfloat16)
+            )
+
+
+def attend(place, queries, prefixes, text_kv, pages, picks, all_rows):
     docs, rows, width = queries.shape
     kv_width = text_kv.shape[2]
     vision_rows = all_rows.shape[0]
-    keys = seen.shape[2]
+    keys = prefixes.shape[1] + picks.shape[1] + rows
     return pl.pallas_call(
         attend_kernel,
         grid_spec=pltpu.PrefetchScalarGridSpec(
@@ -321,7 +364,6 @@
                 pl.BlockSpec((1, rows, kv_width), lambda d, place: (d, 0, 0)),
                 pl.BlockSpec(pages.shape, lambda d, place: (0, 0)),
                 pl.BlockSpec((1,) + picks.shape[1:], lambda d, place: (d, 0, 0)),
-                pl.BlockSpec((1, 1, keys), lambda d, place: (d, 0, 0)),
                 pl.BlockSpec(all_rows.shape, lambda d, place: (0, 0)),
             ],
             out_specs=[
@@ -339,7 +381,7 @@
             bytes_accessed=8 * docs * rows * width,
             transcendentals=docs * rows * keys * width // HD,
         ),
-    )(place, queries, prefixes, text_kv, pages, picks, seen, all_rows)
+    )(place, queries, prefixes, text_kv, pages, picks, all_rows)
 
 
 def shards(
@@ -401,22 +443,13 @@
     doc_rows = jnp.where(inside[:, :, None], doc_rows, -1)
     doc_count, query_rows, _ = queries.shape
     picks = doc_rows.reshape(doc_count, -1, 1)
-    seen = jnp.concatenate(
-        [
-            jnp.ones((doc_count, prefixes.shape[1]), jnp.int32),
-            (doc_rows >= 0).reshape(doc_count, -1).astype(jnp.int32),
-            jnp.ones((doc_count, query_rows), jnp.int32),
-        ],
-        axis=1,
-    )[:, None, :]
-
     kv, squares = scatter_heads(kv, squares)
     row_scale = lax.rsqrt(squares / D + 1e-06)
     tile_kv = (kv * row_scale[:, None]).astype(jnp.bfloat16)
     outgoing = jnp.dot(chooser, tile_kv, preferred_element_type=jnp.float32).astype(jnp.bfloat16)
     pages = lax.all_to_all(outgoing, "seq", split_axis=0, concat_axis=0, tiled=True)
     attended, vision_kv = attend(
-        place_of(prefix_id), queries, prefixes, text_kv, pages, picks, seen, all_rows
+        place_of(prefix_id), queries, prefixes, text_kv, pages, picks, all_rows
     )
     return (attended, vision_kv)
 

time: 183 us -> 200 us (1.093)
  starting transfers between devices: 55.6 us -> 69 us
  local copies, waits for them, and re-layouts: 13.9 us -> 18.5 us
  waiting for transfers between devices: 75.1 us -> 79 us
    ppermute x9 -> x12, waiting for transfers between devices: 43.8 us -> 59.8 us  [send_direct(): lax.ppermute(ride(part, small), 'seq', along([(a, a ^ k) for a in range(4...]
    ppermute x11, waiting for transfers between devices: 17.7 us -> 10.8 us  [flip(): return lax.ppermute(value, axis, [(i, i ^ bit) for i in range(count)])]
    ppermute x9 -> x12, starting transfers between devices: 20 us -> 25.7 us  [send_direct(): lax.ppermute(ride(part, small), 'seq', along([(a, a ^ k) for a in range(4...]
    ppermute x2 -> x3, waiting for transfers between devices: 5.47 us -> 0.01 us  [merge_tiles(): others.append(lax.ppermute(own, 'seq', pairs))]
    ppermute x2, starting transfers between devices: 4.12 us -> 7.3 us  [transpose_panels(): return lax.ppermute(local, ('seq', 'tp'), pairs)]
    ppermute x11, starting transfers between devices: 14.5 us -> 17 us  [flip(): return lax.ppermute(value, axis, [(i, i ^ bit) for i in range(count)])]
    reduce_sum x3 -> x4, other arithmetic: 4.28 us -> 2.01 us  [finish(): squared = jnp.sum(merged * merged, axis=1)]
    unnamed x68 -> x48, local copies, waits for them, and re-layouts: 2.49 us -> 4.61 us
  transfers between devices with their start and end apart: 25 -> 29, of which waited for: 11 -> 9; matrix products, arithmetic and copies ran while one was open for 13% -> 12% of each run, Pallas kernels for 8% -> 7%
where the time goes in v2:
time: 200 us; the launch traced here: 199 us
  waiting for transfers between devices  79 us (40%)
  starting transfers between devices  69 us (34%)
  Pallas kernels  18.9 us (9%)
  local copies, waits for them, and re-layouts  18.5 us (9%)
  other arithmetic  9.83 us (5%)
  matrix products  2.8 us (1%)
    ppermute x12, waiting for transfers between devices, send_direct(): lax.ppermute(ride(part, small), 'seq', along([(a, a ^ k) for a in range(4...  59.8 us
    ppermute x12, starting transfers between devices, send_direct(): lax.ppermute(ride(part, small), 'seq', along([(a, a ^ k) for a in range(4...  25.7 us
    ppermute x11, starting transfers between devices, flip(): return lax.ppermute(value, axis, [(i, i ^ bit) for i in range(count)])  17 us
    all_to_all x1, starting transfers between devices, shards(): lax.all_to_all(outgoing, 'seq', split_axis=0, concat_axis=0, tiled=True)  15.5 us
    pallas_call x4, Pallas kernels, partial_products(): pl.pallas_call(functools.partial(partial_kernel, halves), grid=(count //...  11 us
    ppermute x11, waiting for transfers between devices, flip(): return lax.ppermute(value, axis, [(i, i ^ bit) for i in range(count)])  10.8 us
    all_to_all x1, waiting for transfers between devices, shards(): lax.all_to_all(outgoing, 'seq', split_axis=0, concat_axis=0, tiled=True)  8.35 us
    ppermute x2, starting transfers between devices, transpose_panels(): return lax.ppermute(local, ('seq', 'tp'), pairs)  7.3 us
  transfers between devices with their start and end apart: 29, of which 9 were waited for; matrix products, arithmetic and copies ran while one was open for 12% of the time, Pallas kernels for 7%

profile of v2, /device:TPU:0, one launch (start us, length us, event | category | flops | bytes accessed | tf_op | source)
XLA Modules:
  0.0 199.3 jit_solution(4570390968623965881)
XLA Ops:
  0.6 1.1 slice_bitcast_fusion
  1.7 3.0 %collective-permute-start = (bf16[128,1280]{1,0:T(8,128)(2,1)S(1)}, bf16[128,1280]{1,0:T(8,128)(2,1)}, u32[]{:S(2)}, u32[]{:S(2)}) collective-permute-start(bf16[128,1280]{1,0:T(8,128)(2,1)S(1)} %get-tuple-element.83), channel_id=1, source_target_pairs={{0,2},{1,3},{2,0},{3,1},{4,6},{5,7},{6,4},{7,5},{8,10},{9,11},{10,... | collective-permute-start | bytes 983048 | tf_op jit(solution)/shard_map/ppermute | solution.py:23
  4.8 0.8 collective-permute-start.3
  5.6 2.4 %fusion.49 = (bf16[640,512]{1,0:T(8,128)(2,1)}, bf16[640,512]{1,0:T(8,128)(2,1)}) fusion(bf16[640,2048]{1,0:T(8,128)(2,1)} %refs_2_.1), kind=kLoop, calls=%fused_computation.127 | loop fusion | bytes 2621440 | tf_op jit(solution)/shard_map/slice | solution.py:181
  8.1 1.5 collective-permute-start.7
  9.8 0.6 slice_convert_fusion.4
  10.7 0.8 gather_fusion.2
  12.1 0.6 slice_convert_fusion.2
  12.7 6.1 %collective-permute-done = bf16[128,1280]{1,0:T(8,128)(2,1)} collective-permute-done((bf16[128,1280]{1,0:T(8,128)(2,1)S(1)}, bf16[128,1280]{1,0:T(8,128)(2,1)}, u32[]{:S(2)}, u32[]{:S(2)}) %collective-permute-start) | collective-permute-done | bytes 327712 | tf_op jit(solution)/shard_map/ppermute | solution.py:23
  18.8 2.6 %collective-permute-start.4 = (bf16[128,1280]{1,0:T(8,128)(2,1)S(1)}, bf16[128,1280]{1,0:T(8,128)(2,1)S(1)}, u32[]{:S(2)}, u32[]{:S(2)}) collective-permute-start(bf16[128,1280]{1,0:T(8,128)(2,1)S(1)} %collective-permute-done.3.refs_0_), channel_id=1, source_target_pairs={{0,2},{1,3},{2,0},{3,1},{4,6},{5,7},{6,4},{7,5},{8,10},{9,11},{10,... | collective-permute-start | bytes 983048 | tf_op jit(solution)/shard_map/ppermute | solution.py:23
  21.4 2.4 %collective-permute-start.5 = (bf16[128,1280]{1,0:T(8,128)(2,1)S(1)}, bf16[128,1280]{1,0:T(8,128)(2,1)S(1)}, u32[]{:S(2)}, u32[]{:S(2)}) collective-permute-start(bf16[128,1280]{1,0:T(8,128)(2,1)S(1)} %collective-permute-done.3.refs_0_), channel_id=1, source_target_pairs={{0,1},{1,0},{2,3},{3,2},{4,5},{5,4},{6,7},{7,6},{8,9},{9,8},{10,11... | collective-permute-start | bytes 983048 | tf_op jit(solution)/shard_map/ppermute | solution.py:23
  23.8 1.2 pad_maximum_fusion
  25.0 1.5 collective-permute-start.11
  27.0 0.6 iota_compare_fusion.6
  27.7 6.5 %collective-permute-start.2 = (bf16[128,1280]{1,0:T(8,128)(2,1)}, bf16[128,1280]{1,0:T(8,128)(2,1)}, u32[]{:S(2)}, u32[]{:S(2)}) collective-permute-start(bf16[128,1280]{1,0:T(8,128)(2,1)} %collective-permute-done), channel_id=1, source_target_pairs={{2,0},{3,10},{0,16},{1,26},{6,4},{7,14},{4,20},{5,30},{10,2},{11,8... | collective-permute-start | bytes 983048 | tf_op jit(solution)/shard_map/ppermute | solution.py:37
  34.2 2.4 %collective-permute-start.6 = (bf16[128,1280]{1,0:T(8,128)(2,1)S(1)}, bf16[128,1280]{1,0:T(8,128)(2,1)S(1)}, u32[]{:S(2)}, u32[]{:S(2)}) collective-permute-start(bf16[128,1280]{1,0:T(8,128)(2,1)S(1)} %collective-permute-done.4.refs_1_), channel_id=1, source_target_pairs={{0,1},{1,0},{2,3},{3,2},{4,5},{5,4},{6,7},{7,6},{8,9},{9,8},{10,11... | collective-permute-start | bytes 983048 | tf_op jit(solution)/shard_map/ppermute | solution.py:23
  36.6 0.7 iota_add_fusion.1
  37.3 0.6 collective-permute-done.6.refs_3_
  37.8 0.6 shard_map.122.refs_0_
  38.5 2.2 %copy-done = bf16[640,2048]{1,0:T(8,128)(2,1)S(1)} copy-done((bf16[640,2048]{1,0:T(8,128)(2,1)S(1)}, bf16[640,2048]{1,0:T(8,128)(2,1)}, u32[]{:S(2)}) %copy-start) | copy-done | bytes 2621464
  40.7 1.5 shard_map.123
  42.2 3.5 %collective-permute-start.14 = (bf16[128,512]{1,0:T(8,128)(2,1)}, bf16[128,512]{1,0:T(8,128)(2,1)}, u32[]{:S(2)}, u32[]{:S(2)}) collective-permute-start(bf16[128,512]{1,0:T(8,128)(2,1)} %get-tuple-element.50), channel_id=1, source_target_pairs={{0,24},{4,28},{8,16},{12,20},{16,8},{20,12},{24,0},{28,4},{1,25},{... | collective-permute-start | bytes 393224 | tf_op jit(solution)/shard_map/ppermute | solution.py:145
  45.7 9.6 %collective-permute-start.20 = (bf16[128,512]{1,0:T(8,128)(2,1)}, bf16[128,512]{1,0:T(8,128)(2,1)}, u32[]{:S(2)}, u32[]{:S(2)}) collective-permute-start(bf16[128,512]{1,0:T(8,128)(2,1)} %get-tuple-element.62), channel_id=1, source_target_pairs={{0,8},{4,12},{8,0},{12,4},{16,24},{20,28},{24,16},{28,20},{1,9},{5... | collective-permute-start | bytes 393224 | tf_op jit(solution)/shard_map/ppermute | solution.py:145
  55.4 0.6 fusion.46
  56.0 0.6 stack_reshape.6
  56.6 0.8 add.340.all_ref
  57.5 0.7 add.327
  58.2 1.6 add.339
  59.8 0.7 broadcast_in_dim.10
  60.5 0.8 broadcast_in_dim.13
  61.3 0.7 add.330
  61.9 0.7 pad_clamp_fusion.1
  62.6 1.3 copy-done.3
  63.9 2.1 %shard_map.126 = (bf16[128,512]{1,0:T(8,128)(2,1)S(1)}, bf16[128,512]{1,0:T(8,128)(2,1)S(1)}, bf16[128,512]{1,0:T(8,128)(2,1)S(1)}, bf16[128,512]{1,0:T(8,128)(2,1)S(1)}) custom-call(bf16[512,1280]{1,0:T(8,128)(2,1)S(1)} %copy-done.3, bf16[640,2048]{1,0:T(8,128)(2,1)S(1)} %copy-done.1, bf16[640,512]{1,0:T(8,128)(2,1)} %collective-permute-done.11.refs_3_.refs_2_), custom_call_target="tpu_custom_call" | custom-call | bytes 1024 | tf_op jit(solution)/shard_map/pallas_call | solution.py:118
  66.1 3.8 %collective-permute-start.9 = (bf16[128,1280]{1,0:T(8,128)(2,1)}, bf16[128,1280]{1,0:T(8,128)(2,1)S(1)}, u32[]{:S(2)}, u32[]{:S(2)}) collective-permute-start(bf16[128,1280]{1,0:T(8,128)(2,1)} %collective-permute-done.2.refs_0_), channel_id=1, source_target_pairs={{0,1},{1,0},{2,3},{3,2},{4,5},{5,4},{6,7},{7,6},{8,9},{9,8},{10,11... | collective-permute-start | bytes 983048 | tf_op jit(solution)/shard_map/ppermute | solution.py:23
  69.8 1.2 collective-permute-start.13
  71.1 1.4 collective-permute-start.16
  72.5 1.2 fusion.17
  73.7 8.0 %collective-permute-done.13 = bf16[128,512]{1,0:T(8,128)(2,1)S(1)} collective-permute-done((bf16[128,512]{1,0:T(8,128)(2,1)S(1)}, bf16[128,512]{1,0:T(8,128)(2,1)S(1)}, u32[]{:S(2)}, u32[]{:S(2)}) %collective-permute-start.13) | collective-permute-done | bytes 131104 | tf_op jit(solution)/shard_map/ppermute | solution.py:145
  82.0 5.0 %collective-permute-done.21 = bf16[128,512]{1,0:T(8,128)(2,1)S(1)} collective-permute-done((bf16[128,512]{1,0:T(8,128)(2,1)S(1)}, bf16[128,512]{1,0:T(8,128)(2,1)S(1)}, u32[]{:S(2)}, u32[]{:S(2)}) %collective-permute-start.21) | collective-permute-done | bytes 131104 | tf_op jit(solution)/shard_map/ppermute | solution.py:145
  87.2 1.6 shard_map.124.refs_0_.refs_1_
  88.8 3.1 %shard_map.125 = (bf16[128,1024]{1,0:T(8,128)(2,1)S(1)}, bf16[128,1024]{1,0:T(8,128)(2,1)S(1)}, bf16[128,1024]{1,0:T(8,128)(2,1)S(1)}, bf16[128,1024]{1,0:T(8,128)(2,1)S(1)}) custom-call(bf16[512,1280]{1,0:T(8,128)(2,1)S(1)} %shard_map.124.refs_0_.refs_1_, bf16[640,2048]{1,0:T(8,128)(2,1)S(1)} %copy-done.1, ...), custom_call_target="tpu_custom_call" | custom-call | bytes 2048 | tf_op jit(solution)/shard_map/pallas_call | solution.py:118
  92.3 2.0 %collective-permute-start.22 = (bf16[128,1024]{1,0:T(8,128)(2,1)S(1)}, bf16[128,1024]{1,0:T(8,128)(2,1)S(1)}, u32[]{:S(2)}, u32[]{:S(2)}) collective-permute-start(bf16[128,1024]{1,0:T(8,128)(2,1)S(1)} %get-tuple-element.65), channel_id=1, source_target_pairs={{0,8},{4,12},{8,0},{12,4},{16,24},{20,28},{24,16},{28,20},{1,9},{5... | collective-permute-start | bytes 786440 | tf_op jit(solution)/shard_map/ppermute | solution.py:145
  94.4 2.0 collective-permute-start.23
  96.3 4.3 %shard_map.127 = (bf16[256,1024]{1,0:T(8,128)(2,1)S(1)}, bf16[256,1024]{1,0:T(8,128)(2,1)S(1)}, bf16[256,1024]{1,0:T(8,128)(2,1)S(1)}, bf16[256,1024]{1,0:T(8,128)(2,1)S(1)}) custom-call(bf16[512,1280]{1,0:T(8,128)(2,1)S(1)} %copy-done.4, bf16[512,1280]{1,0:T(8,128)(2,1)S(1)} %shard_map.124.refs_0_.refs_1_, bf16[640,2048]{1,0:T(8,128)(2,1)S(1)} %copy-done.1, ...), custom_call_target="tpu_custom_call" | custom-call | bytes 2048 | tf_op jit(solution)/shard_map/pallas_call | solution.py:118
  100.7 0.8 slice_bitcast_fusion.5
  101.4 6.0 %collective-permute-done.15 = bf16[128,1024]{1,0:T(8,128)(2,1)S(1)} collective-permute-done((bf16[128,1024]{1,0:T(8,128)(2,1)S(1)}, bf16[128,1024]{1,0:T(8,128)(2,1)S(1)}, u32[]{:S(2)}, u32[]{:S(2)}) %collective-permute-start.15) | collective-permute-done | bytes 262176 | tf_op jit(solution)/shard_map/ppermute | solution.py:145
  107.7 5.4 %collective-permute-start.18 = (bf16[288,1024]{1,0:T(8,128)(2,1)S(1)}, bf16[288,1024]{1,0:T(8,128)(2,1)S(1)}, u32[]{:S(2)}, u32[]{:S(2)}) collective-permute-start(bf16[288,1024]{1,0:T(8,128)(2,1)S(1)} %get-tuple-element.87), channel_id=1, source_target_pairs={{0,16},{4,20},{8,24},{12,28},{16,0},{20,4},{24,8},{28,12},{1,17},{... | collective-permute-start | bytes 1769480 | tf_op jit(solution)/shard_map/ppermute | solution.py:145
  114.2 17.2 %collective-permute-done.17 = bf16[288,1024]{1,0:T(8,128)(2,1)S(1)} collective-permute-done((bf16[288,1024]{1,0:T(8,128)(2,1)S(1)}, bf16[288,1024]{1,0:T(8,128)(2,1)S(1)}, u32[]{:S(2)}, u32[]{:S(2)}) %collective-permute-start.17) | collective-permute-done | bytes 589856 | tf_op jit(solution)/shard_map/ppermute | solution.py:145
  131.4 23.7 %collective-permute-done.18 = bf16[288,1024]{1,0:T(8,128)(2,1)S(1)} collective-permute-done((bf16[288,1024]{1,0:T(8,128)(2,1)S(1)}, bf16[288,1024]{1,0:T(8,128)(2,1)S(1)}, u32[]{:S(2)}, u32[]{:S(2)}) %collective-permute-start.18) | collective-permute-done | bytes 589856 | tf_op jit(solution)/shard_map/ppermute | solution.py:145
  155.6 0.7 fusion.4
  156.4 0.6 collective-permute-start.24
  157.6 0.6 gather_fusion
  158.3 0.6 gather_fusion.1
  159.3 1.2 dynamic-slice_bitcast_fusion.1
  160.6 0.6 collective-permute-start.27
  161.2 0.7 copy-done.10
  161.9 1.0 maximum_add_fusion
  162.9 1.5 collective-permute-start.25
  164.5 4.1 %collective-permute-done.25 = bf16[1,256,256]{2,1,0:T(8,128)(2,1)S(1)} collective-permute-done((bf16[1,256,256]{2,1,0:T(8,128)(2,1)S(1)}, bf16[1,256,256]{2,1,0:T(8,128)(2,1)S(1)}, u32[]{:S(2)}, u32[]{:S(2)}) %collective-permute-start.25) | collective-permute-done | bytes 131104 | tf_op jit(solution)/shard_map/ppermute | solution.py:23
  168.6 1.0 convolution_convert_fusion
  169.6 15.5 %all-to-all-start = ((bf16[8,64,256]{2,1,0:T(8,128)(2,1)}), bf16[8,64,256]{2,1,0:T(8,128)(2,1)S(1)}, u32[]{:S(2)}, u32[]{:S(2)}) async-start(bf16[8,64,256]{2,1,0:T(8,128)(2,1)} %bitcast.19), calls=%async_computation | async-start | bytes 524288 | tf_op jit(solution)/shard_map/all_to_all | solution.py:450
  185.3 8.3 %all-to-all-done = bf16[8,64,256]{2,1,0:T(8,128)(2,1)S(1)} async-done(((bf16[8,64,256]{2,1,0:T(8,128)(2,1)}), bf16[8,64,256]{2,1,0:T(8,128)(2,1)S(1)}, u32[]{:S(2)}, u32[]{:S(2)}) %all-to-all-start) | async-done | bytes 262176 | tf_op jit(solution)/shard_map/all_to_all | solution.py:450
  193.7 5.6 %shard_map.128 = (bf16[4,128,1024]{2,1,0:T(8,128)(2,1)}, bf16[256,256]{1,0:T(8,128)(2,1)}) custom-call(s32[4]{0:T(128)S(1)} %fusion.40.place_ref, bf16[4,128,1024]{2,1,0:T(8,128)(2,1)S(1)} %copy-done.5, bf16[8,32,256]{2,1,0:T(8,128)(2,1)S(1)} %slice.109.prefix_ref, bf16[4,128,256]{2,1,0:T(8,128)(2,1)S(1)} %copy-done.6, bf16[512,256]{1,0:T(8,128)(2,1)S(1)} %bitcast.55, ...), custom_call_target="tpu_custom_call" | custom-call | flops 603979776 | bytes 4194304 | tf_op jit(solution)/shard_map/pallas_call | solution.py:356
  (125 shorter events, 6.0 us)
Async XLA Ops:
  1.7 17.0 %collective-permute-start = (bf16[128,1280]{1,0:T(8,128)(2,1)S(1)}, bf16[128,1280]{1,0:T(8,128)(2,1)}, u32[]{:S(2)}, u32[]{:S(2)}) collective-permute-start(bf16[128,1280]{1,0:T(8,128)(2,1)S(1)} %get-tuple-element.83), channel_id=1, source_target_pairs={{0,2},{1,3},{2,0},{3,1},{4,6},{5,7},{6,4},{7,5},{8,10},{9,11},{10,... | collective-permute-start | bytes 983048 | tf_op jit(solution)/shard_map/ppermute | solution.py:23
  4.8 4.8 %copy-start.20 = (s32[32,1]{0,1:T(1,128)S(1)}, s32[32,1]{0,1:T(1,128)}, u32[]{:S(2)}) copy-start(s32[32,1]{0,1:T(1,128)} %param.15) | copy-start | bytes 388
  4.8 5.0 %copy-start.22 = (s32[32]{0:T(128)S(1)}, s32[32]{0:T(128)}, u32[]{:S(2)}) copy-start(s32[32]{0:T(128)} %param.16) | copy-start | bytes 388
  4.8 5.0 %copy-start.14 = (bf16[2048]{0:T(1024)(128)(2,1)S(1)}, bf16[2048]{0:T(1024)(128)(2,1)}, u32[]{:S(2)}) copy-start(bf16[2048]{0:T(1024)(128)(2,1)} %param.13) | copy-start | bytes 12292
  4.8 5.6 %copy-start.23 = (s32[1,4]{1,0:T(1,128)S(1)}, s32[1,4]{1,0:T(1,128)}, u32[]{:S(2)}) copy-start(s32[1,4]{1,0:T(1,128)} %param.17) | copy-start | bytes 52
  4.8 14.0 %collective-permute-start.3 = (bf16[128,1280]{1,0:T(8,128)(2,1)S(1)}, bf16[128,1280]{1,0:T(8,128)(2,1)S(1)}, u32[]{:S(2)}, u32[]{:S(2)}) collective-permute-start(bf16[128,1280]{1,0:T(8,128)(2,1)S(1)} %get-tuple-element.82), channel_id=1, source_target_pairs={{0,0},{1,10},{2,16},{3,26},{4,4},{5,14},{6,20},{7,30},{8,2},{9,8},... | collective-permute-start | bytes 983048 | tf_op jit(solution)/shard_map/ppermute | solution.py:37
  8.1 4.0 %copy-start.13 = (bf16[1,32,256]{2,1,0:T(8,128)(2,1)S(1)}, bf16[1,32,256]{2,1,0:T(8,128)(2,1)}, u32[]{:S(2)}) copy-start(bf16[1,32,256]{2,1,0:T(8,128)(2,1)} %param.19) | copy-start | bytes 49156
  8.1 15.7 %slice-start = ((bf16[640,2048]{1,0:T(8,128)(2,1)}), bf16[640,1024]{1,0:T(8,128)(2,1)S(1)}, s32[]{:S(2)}) async-start(bf16[640,2048]{1,0:T(8,128)(2,1)} %refs_2_.1), calls=%async_computation.1 | async-start | bytes 2621440 | tf_op jit(solution)/shard_map/slice | solution.py:181
  8.1 30.4 %collective-permute-start.7 = (bf16[640,512]{1,0:T(8,128)(2,1)}, bf16[640,512]{1,0:T(8,128)(2,1)S(1)}, u32[]{:S(2)}, u32[]{:S(2)}) collective-permute-start(bf16[640,512]{1,0:T(8,128)(2,1)} %get-tuple-element.77), channel_id=1, source_target_pairs={{4,0},{0,4},{12,8},{8,12},{20,16},{16,20},{28,24},{24,28},{5,1},{1... | collective-permute-start | bytes 1966088 | tf_op jit(solution)/shard_map/ppermute | solution.py:193
  18.8 8.9 %collective-permute-start.4 = (bf16[128,1280]{1,0:T(8,128)(2,1)S(1)}, bf16[128,1280]{1,0:T(8,128)(2,1)S(1)}, u32[]{:S(2)}, u32[]{:S(2)}) collective-permute-start(bf16[128,1280]{1,0:T(8,128)(2,1)S(1)} %collective-permute-done.3.refs_0_), channel_id=1, source_target_pairs={{0,2},{1,3},{2,0},{3,1},{4,6},{5,7},{6,4},{7,5},{8,10},{9,11},{10,... | collective-permute-start | bytes 983048 | tf_op jit(solution)/shard_map/ppermute | solution.py:23
  21.4 12.8 %collective-permute-start.5 = (bf16[128,1280]{1,0:T(8,128)(2,1)S(1)}, bf16[128,1280]{1,0:T(8,128)(2,1)S(1)}, u32[]{:S(2)}, u32[]{:S(2)}) collective-permute-start(bf16[128,1280]{1,0:T(8,128)(2,1)S(1)} %collective-permute-done.3.refs_0_), channel_id=1, source_target_pairs={{0,1},{1,0},{2,3},{3,2},{4,5},{5,4},{6,7},{7,6},{8,9},{9,8},{10,11... | collective-permute-start | bytes 983048 | tf_op jit(solution)/shard_map/ppermute | solution.py:23
  25.0 36.9 %collective-permute-start.11 = (bf16[640,512]{1,0:T(8,128)(2,1)}, bf16[640,512]{1,0:T(8,128)(2,1)}, u32[]{:S(2)}, u32[]{:S(2)}) collective-permute-start(bf16[640,512]{1,0:T(8,128)(2,1)} %get-tuple-element.39), channel_id=1, source_target_pairs={{4,0},{0,4},{12,8},{8,12},{20,16},{16,20},{28,24},{24,28},{5,1},{1... | collective-permute-start | bytes 1966088 | tf_op jit(solution)/shard_map/ppermute | solution.py:193
  26.5 69.8 %collective-permute-start.1 = (bf16[656,1024]{1,0:T(8,128)(2,1)}, bf16[656,1024]{1,0:T(8,128)(2,1)}, u32[]{:S(2)}, u32[]{:S(2)}) collective-permute-start(bf16[656,1024]{1,0:T(8,128)(2,1)} %pad_maximum_fusion), channel_id=1, source_target_pairs={{4,0},{0,4},{12,8},{8,12},{20,16},{16,20},{28,24},{24,28},{5,1},{1... | collective-permute-start | bytes 4030472 | tf_op jit(solution)/shard_map/ppermute | solution.py:193
  27.7 18.1 %collective-permute-start.2 = (bf16[128,1280]{1,0:T(8,128)(2,1)}, bf16[128,1280]{1,0:T(8,128)(2,1)}, u32[]{:S(2)}, u32[]{:S(2)}) collective-permute-start(bf16[128,1280]{1,0:T(8,128)(2,1)} %collective-permute-done), channel_id=1, source_target_pairs={{2,0},{3,10},{0,16},{1,26},{6,4},{7,14},{4,20},{5,30},{10,2},{11,8... | collective-permute-start | bytes 983048 | tf_op jit(solution)/shard_map/ppermute | solution.py:37
  34.2 3.7 %collective-permute-start.6 = (bf16[128,1280]{1,0:T(8,128)(2,1)S(1)}, bf16[128,1280]{1,0:T(8,128)(2,1)S(1)}, u32[]{:S(2)}, u32[]{:S(2)}) collective-permute-start(bf16[128,1280]{1,0:T(8,128)(2,1)S(1)} %collective-permute-done.4.refs_1_), channel_id=1, source_target_pairs={{0,1},{1,0},{2,3},{3,2},{4,5},{5,4},{6,7},{7,6},{8,9},{9,8},{10,11... | collective-permute-start | bytes 983048 | tf_op jit(solution)/shard_map/ppermute | solution.py:23
  38.5 3.8 %copy-start.2 = (bf16[512,1280]{1,0:T(8,128)(2,1)}, bf16[512,1280]{1,0:T(8,128)(2,1)S(1)}, u32[]{:S(2)}) copy-start(bf16[512,1280]{1,0:T(8,128)(2,1)S(1)} %shard_map.122.refs_0_) | copy-start | bytes 3932164
  38.5 2.2 %copy-start = (bf16[640,2048]{1,0:T(8,128)(2,1)S(1)}, bf16[640,2048]{1,0:T(8,128)(2,1)}, u32[]{:S(2)}) copy-start(bf16[640,2048]{1,0:T(8,128)(2,1)} %refs_2_.1) | copy-start | bytes 7864324
  40.7 16.7 %copy-start.19 = (s32[64]{0:T(128)S(1)}, s32[64]{0:T(128)}, u32[]{:S(2)}) copy-start(s32[64]{0:T(128)} %broadcast_multiply_fusion.1) | copy-start | bytes 772
  40.7 21.9 %copy-start.1 = (bf16[640,2048]{1,0:T(8,128)(2,1)S(1)}, bf16[640,2048]{1,0:T(8,128)(2,1)}, u32[]{:S(2)}) copy-start(bf16[640,2048]{1,0:T(8,128)(2,1)} %refs_2_.1) | copy-start | bytes 7864324
  42.2 23.8 %collective-permute-start.12 = (bf16[128,512]{1,0:T(8,128)(2,1)}, bf16[128,512]{1,0:T(8,128)(2,1)}, u32[]{:S(2)}, u32[]{:S(2)}) collective-permute-start(bf16[128,512]{1,0:T(8,128)(2,1)} %get-tuple-element.48), channel_id=1, source_target_pairs={{0,16},{4,20},{8,24},{12,28},{16,0},{20,4},{24,8},{28,12},{1,17},{... | collective-permute-start | bytes 393224 | tf_op jit(solution)/shard_map/ppermute | solution.py:145
  42.2 27.6 %collective-permute-start.14 = (bf16[128,512]{1,0:T(8,128)(2,1)}, bf16[128,512]{1,0:T(8,128)(2,1)}, u32[]{:S(2)}, u32[]{:S(2)}) collective-permute-start(bf16[128,512]{1,0:T(8,128)(2,1)} %get-tuple-element.50), channel_id=1, source_target_pairs={{0,24},{4,28},{8,16},{12,20},{16,8},{20,12},{24,0},{28,4},{1,25},{... | collective-permute-start | bytes 393224 | tf_op jit(solution)/shard_map/ppermute | solution.py:145
  45.7 25.3 %collective-permute-start.20 = (bf16[128,512]{1,0:T(8,128)(2,1)}, bf16[128,512]{1,0:T(8,128)(2,1)}, u32[]{:S(2)}, u32[]{:S(2)}) collective-permute-start(bf16[128,512]{1,0:T(8,128)(2,1)} %get-tuple-element.62), channel_id=1, source_target_pairs={{0,8},{4,12},{8,0},{12,4},{16,24},{20,28},{24,16},{28,20},{1,9},{5... | collective-permute-start | bytes 393224 | tf_op jit(solution)/shard_map/ppermute | solution.py:145
  61.9 19.7 %collective-permute-start.8 = (bf16[128,1280]{1,0:T(8,128)(2,1)}, bf16[128,1280]{1,0:T(8,128)(2,1)S(1)}, u32[]{:S(2)}, u32[]{:S(2)}) collective-permute-start(bf16[128,1280]{1,0:T(8,128)(2,1)} %collective-permute-done.2.refs_0_), channel_id=1, source_target_pairs={{0,2},{1,3},{2,0},{3,1},{4,6},{5,7},{6,4},{7,5},{8,10},{9,11},{10,... | collective-permute-start | bytes 983048 | tf_op jit(solution)/shard_map/ppermute | solution.py:23
  62.6 1.3 copy-start.3
  63.9 17.7 %copy-start.7 = (bf16[2048,1024]{1,0:T(8,128)(2,1)S(1)}, bf16[2048,1024]{1,0:T(8,128)(2,1)}, u32[]{:S(2)}) copy-start(bf16[2048,1024]{1,0:T(8,128)(2,1)} %param.14) | copy-start | bytes 12582916
  63.9 17.7 %copy-start.15 = (f32[512]{0:T(512)S(1)}, f32[512]{0:T(512)}, u32[]{:S(2)}) copy-start(f32[512]{0:T(512)} %get-tuple-element.92) | copy-start | bytes 6148
  66.1 21.1 %collective-permute-start.9 = (bf16[128,1280]{1,0:T(8,128)(2,1)}, bf16[128,1280]{1,0:T(8,128)(2,1)S(1)}, u32[]{:S(2)}, u32[]{:S(2)}) collective-permute-start(bf16[128,1280]{1,0:T(8,128)(2,1)} %collective-permute-done.2.refs_0_), channel_id=1, source_target_pairs={{0,1},{1,0},{2,3},{3,2},{4,5},{5,4},{6,7},{7,6},{8,9},{9,8},{10,11... | collective-permute-start | bytes 983048 | tf_op jit(solution)/shard_map/ppermute | solution.py:23
  69.8 11.8 %collective-permute-start.13 = (bf16[128,512]{1,0:T(8,128)(2,1)S(1)}, bf16[128,512]{1,0:T(8,128)(2,1)S(1)}, u32[]{:S(2)}, u32[]{:S(2)}) collective-permute-start(bf16[128,512]{1,0:T(8,128)(2,1)S(1)} %get-tuple-element.49), channel_id=1, source_target_pairs={{0,16},{4,20},{8,24},{12,28},{16,0},{20,4},{24,8},{28,12},{1,17},{... | collective-permute-start | bytes 393224 | tf_op jit(solution)/shard_map/ppermute | solution.py:145
  71.1 10.9 %collective-permute-start.16 = (bf16[128,512]{1,0:T(8,128)(2,1)S(1)}, bf16[128,512]{1,0:T(8,128)(2,1)S(1)}, u32[]{:S(2)}, u32[]{:S(2)}) collective-permute-start(bf16[128,512]{1,0:T(8,128)(2,1)S(1)} %get-tuple-element.58), channel_id=1, source_target_pairs={{0,24},{4,28},{8,16},{12,20},{16,8},{20,12},{24,0},{28,4},{1,25},{... | collective-permute-start | bytes 393224 | tf_op jit(solution)/shard_map/ppermute | solution.py:145
  81.6 5.3 %collective-permute-start.21 = (bf16[128,512]{1,0:T(8,128)(2,1)S(1)}, bf16[128,512]{1,0:T(8,128)(2,1)S(1)}, u32[]{:S(2)}, u32[]{:S(2)}) collective-permute-start(bf16[128,512]{1,0:T(8,128)(2,1)S(1)} %get-tuple-element.64), channel_id=1, source_target_pairs={{0,8},{4,12},{8,0},{12,4},{16,24},{20,28},{24,16},{28,20},{1,9},{5... | collective-permute-start | bytes 393224 | tf_op jit(solution)/shard_map/ppermute | solution.py:145
  81.6 5.5 %collective-permute-start.10 = (bf16[128,1280]{1,0:T(8,128)(2,1)S(1)}, bf16[128,1280]{1,0:T(8,128)(2,1)S(1)}, u32[]{:S(2)}, u32[]{:S(2)}) collective-permute-start(bf16[128,1280]{1,0:T(8,128)(2,1)S(1)} %collective-permute-done.8.refs_1_), channel_id=1, source_target_pairs={{0,1},{1,0},{2,3},{3,2},{4,5},{5,4},{6,7},{7,6},{8,9},{9,8},{10,11... | collective-permute-start | bytes 983048 | tf_op jit(solution)/shard_map/ppermute | solution.py:23
  88.8 7.5 %copy-start.4 = (bf16[512,1280]{1,0:T(8,128)(2,1)S(1)}, bf16[512,1280]{1,0:T(8,128)(2,1)}, u32[]{:S(2)}) copy-start(bf16[512,1280]{1,0:T(8,128)(2,1)} %copy-done.2) | copy-start | bytes 3932164
  91.8 9.6 %copy-start.12 = (bf16[1,16,1024]{2,1,0:T(8,128)(2,1)S(1)}, bf16[1,16,1024]{2,1,0:T(8,128)(2,1)}, u32[]{:S(2)}) copy-start(bf16[1,16,1024]{2,1,0:T(8,128)(2,1)} %stack_reshape.6) | copy-start | bytes 98308
  91.9 15.6 %collective-permute-start.15 = (bf16[128,1024]{1,0:T(8,128)(2,1)S(1)}, bf16[128,1024]{1,0:T(8,128)(2,1)S(1)}, u32[]{:S(2)}, u32[]{:S(2)}) collective-permute-start(bf16[128,1024]{1,0:T(8,128)(2,1)S(1)} %get-tuple-element.57), channel_id=1, source_target_pairs={{0,16},{4,20},{8,24},{12,28},{16,0},{20,4},{24,8},{28,12},{1,17},{... | collective-permute-start | bytes 786440 | tf_op jit(solution)/shard_map/ppermute | solution.py:145
  92.3 21.2 %collective-permute-start.22 = (bf16[128,1024]{1,0:T(8,128)(2,1)S(1)}, bf16[128,1024]{1,0:T(8,128)(2,1)S(1)}, u32[]{:S(2)}, u32[]{:S(2)}) collective-permute-start(bf16[128,1024]{1,0:T(8,128)(2,1)S(1)} %get-tuple-element.65), channel_id=1, source_target_pairs={{0,8},{4,12},{8,0},{12,4},{16,24},{20,28},{24,16},{28,20},{1,9},{5... | collective-permute-start | bytes 786440 | tf_op jit(solution)/shard_map/ppermute | solution.py:145
  94.4 19.1 %collective-permute-start.23 = (bf16[128,1024]{1,0:T(8,128)(2,1)S(1)}, bf16[128,1024]{1,0:T(8,128)(2,1)S(1)}, u32[]{:S(2)}, u32[]{:S(2)}) collective-permute-start(bf16[128,1024]{1,0:T(8,128)(2,1)S(1)} %get-tuple-element.66), channel_id=1, source_target_pairs={{0,24},{4,28},{8,16},{12,20},{16,8},{20,12},{24,0},{28,4},{1,25},{... | collective-permute-start | bytes 786440 | tf_op jit(solution)/shard_map/ppermute | solution.py:145
  107.6 6.1 %copy-start.17 = (f32[1024]{0:T(1024)S(1)}, f32[1024]{0:T(1024)}, u32[]{:S(2)}) copy-start(f32[1024]{0:T(1024)} %get-tuple-element.90) | copy-start | bytes 12292
  107.7 23.7 %collective-permute-start.17 = (bf16[288,1024]{1,0:T(8,128)(2,1)S(1)}, bf16[288,1024]{1,0:T(8,128)(2,1)S(1)}, u32[]{:S(2)}, u32[]{:S(2)}) collective-permute-start(bf16[288,1024]{1,0:T(8,128)(2,1)S(1)} %get-tuple-element.86), channel_id=1, source_target_pairs={{0,8},{4,12},{8,0},{12,4},{16,24},{20,28},{24,16},{28,20},{1,9},{5... | collective-permute-start | bytes 1769480 | tf_op jit(solution)/shard_map/ppermute | solution.py:145
  107.7 47.3 %collective-permute-start.18 = (bf16[288,1024]{1,0:T(8,128)(2,1)S(1)}, bf16[288,1024]{1,0:T(8,128)(2,1)S(1)}, u32[]{:S(2)}, u32[]{:S(2)}) collective-permute-start(bf16[288,1024]{1,0:T(8,128)(2,1)S(1)} %get-tuple-element.87), channel_id=1, source_target_pairs={{0,16},{4,20},{8,24},{12,28},{16,0},{20,4},{24,8},{28,12},{1,17},{... | collective-permute-start | bytes 1769480 | tf_op jit(solution)/shard_map/ppermute | solution.py:145
  113.2 41.9 %collective-permute-start.19 = (bf16[288,1024]{1,0:T(8,128)(2,1)S(1)}, bf16[288,1024]{1,0:T(8,128)(2,1)S(1)}, u32[]{:S(2)}, u32[]{:S(2)}) collective-permute-start(bf16[288,1024]{1,0:T(8,128)(2,1)S(1)} %get-tuple-element.88), channel_id=1, source_target_pairs={{0,24},{4,28},{8,16},{12,20},{16,8},{20,12},{24,0},{28,4},{1,25},{... | collective-permute-start | bytes 1769480 | tf_op jit(solution)/shard_map/ppermute | solution.py:145
  114.2 41.4 %copy-start.16 = (f32[1024]{0:T(1024)S(1)}, f32[1024]{0:T(1024)}, u32[]{:S(2)}) copy-start(f32[1024]{0:T(1024)} %get-tuple-element.89) | copy-start | bytes 12292
  155.5 5.1 %collective-permute-start.26 = (f32[256]{0:T(256)S(1)}, f32[256]{0:T(256)S(1)}, u32[]{:S(2)}, u32[]{:S(2)}) collective-permute-start(f32[256]{0:T(256)S(1)} %maximum_add_fusion.1), channel_id=1, source_target_pairs={{0,1},{1,0},{2,3},{3,2},{4,5},{5,4},{6,7},{7,6},{8,9},{9,8},{10,11... | collective-permute-start | bytes 3080 | tf_op jit(solution)/shard_map/ppermute | solution.py:23
  156.3 1.0 copy-start.9
  156.4 4.8 %collective-permute-start.24 = (bf16[2,256,256]{2,1,0:T(8,128)(2,1)S(1)}, bf16[2,256,256]{2,1,0:T(8,128)(2,1)S(1)}, u32[]{:S(2)}, u32[]{:S(2)}) collective-permute-start(bf16[2,256,256]{2,1,0:T(8,128)(2,1)S(1)} %pad_maximum_fusion.5), channel_id=1, source_target_pairs={{0,1},{1,0},{2,3},{3,2},{4,5},{5,4},{6,7},{7,6},{8,9},{9,8},{10,11... | collective-permute-start | bytes 786440 | tf_op jit(solution)/shard_map/ppermute | solution.py:23
  157.5 27.7 %copy-start.21 = (s32[4]{0:T(128)S(1)}, s32[4]{0:T(128)}, u32[]{:S(2)}) copy-start(s32[4]{0:T(128)} %param.18) | copy-start | bytes 52
  157.5 27.7 %copy-start.8 = (s32[4,128,1]{2,1,0:T(8,128)S(1)}, s32[4,128,1]{2,1,0:T(8,128)}, u32[]{:S(2)}) copy-start(s32[4,128,1]{2,1,0:T(8,128)} %add.339) | copy-start | bytes 6148
  157.5 27.7 %copy-start.11 = (pred[4,128,1]{2,1,0:T(8,128)(4,1)S(1)}, pred[4,128,1]{2,1,0:T(8,128)(4,1)}, u32[]{:S(2)}) copy-start(pred[4,128,1]{2,1,0:T(8,128)(4,1)} %broadcast_in_dim.13) | copy-start | bytes 1540
  157.5 27.7 %copy-start.18 = (s32[128]{0:T(128)S(1)}, s32[128]{0:T(128)}, u32[]{:S(2)}) copy-start(s32[128]{0:T(128)} %add.330) | copy-start | bytes 1540
  159.3 34.4 %copy-start.5 = (bf16[4,128,1024]{2,1,0:T(8,128)(2,1)S(1)}, bf16[4,128,1024]{2,1,0:T(8,128)(2,1)}, u32[]{:S(2)}) copy-start(bf16[4,128,1024]{2,1,0:T(8,128)(2,1)} %query_ref.1) | copy-start | bytes 3145732
  159.3 34.4 %copy-start.6 = (bf16[4,128,256]{2,1,0:T(8,128)(2,1)S(1)}, bf16[4,128,256]{2,1,0:T(8,128)(2,1)}, u32[]{:S(2)}) copy-start(bf16[4,128,256]{2,1,0:T(8,128)(2,1)} %text_ref.1) | copy-start | bytes 786436
  160.6 3.9 %collective-permute-start.27 = (f32[256]{0:T(256)S(1)}, f32[256]{0:T(256)S(1)}, u32[]{:S(2)}, u32[]{:S(2)}) collective-permute-start(f32[256]{0:T(256)S(1)} %add.318), channel_id=1, source_target_pairs={{0,2},{1,3},{2,0},{3,1},{4,6},{5,7},{6,4},{7,5},{8,10},{9,11},{10,... | collective-permute-start | bytes 3080 | tf_op jit(solution)/shard_map/ppermute | solution.py:23
  161.2 0.7 copy-start.10
  162.9 5.7 %collective-permute-start.25 = (bf16[1,256,256]{2,1,0:T(8,128)(2,1)S(1)}, bf16[1,256,256]{2,1,0:T(8,128)(2,1)S(1)}, u32[]{:S(2)}, u32[]{:S(2)}) collective-permute-start(bf16[1,256,256]{2,1,0:T(8,128)(2,1)S(1)} %dynamic-slice_convert_fusion), channel_id=1, source_target_pairs={{0,2},{1,3},{2,0},{3,1},{4,6},{5,7},{6,4},{7,5},{8,10},{9,11},{10,... | collective-permute-start | bytes 393224 | tf_op jit(solution)/shard_map/ppermute | solution.py:23
  169.6 24.0 %all-to-all-start = ((bf16[8,64,256]{2,1,0:T(8,128)(2,1)}), bf16[8,64,256]{2,1,0:T(8,128)(2,1)S(1)}, u32[]{:S(2)}, u32[]{:S(2)}) async-start(bf16[8,64,256]{2,1,0:T(8,128)(2,1)} %bitcast.19), calls=%async_computation | async-start | bytes 524288 | tf_op jit(solution)/shard_map/all_to_all | solution.py:450

commit v3 on v1

--- a/solution.py
+++ b/solution.py
@@ -83,18 +83,21 @@
     )(scalars, *held)
 
 
-def partial_kernel(halves, *refs):
-    rows_refs, weights_refs, out_refs = refs[:halves], refs[halves:-4], refs[-4:]
+def partial_kernel(halves, groups, *refs):
+    inputs = len(refs) - len(groups)
+    rows_refs, weights_refs, out_refs = refs[:halves], refs[halves:inputs], refs[inputs:]
     weights = jnp.concatenate([ref[...] for ref in weights_refs], axis=0)
     for half, rows_ref in enumerate(rows_refs):
         total = jnp.dot(rows_ref[...], weights, preferred_element_type=jnp.float32)
         total = total.astype(jnp.bfloat16)
         rows = total.shape[0] // 4
-        for k, out_ref in enumerate(out_refs):
-            out_ref[half * rows : (half + 1) * rows] = total[k * rows : (k + 1) * rows]
-
-
-def partial_products(held, weights, count):
+        for out_ref, members in zip(out_refs, groups):
+            for i, k in enumerate(members):
+                to = (i * halves + half) * rows
+                out_ref[to : to + rows] = total[k * rows : (k + 1) * rows]
+
+
+def partial_products(held, weights, count, groups):
     halves = len(held)
     rows, depth = held[0].shape
     tile = min(count, 512)
@@ -102,14 +105,14 @@
     def block(used, first):
         return pl.BlockSpec((used, tile), lambda i: (0, i + first // tile))
 
-    out = halves * rows // 4
+    outs = [len(members) * halves * rows // 4 for members in groups]
     return pl.pallas_call(
-        functools.partial(partial_kernel, halves),
+        functools.partial(partial_kernel, halves, groups),
         grid=(count // tile,),
         in_specs=[pl.BlockSpec((rows, depth), lambda i: (0, 0))] * halves
         + [block(used, first) for _, used, first in weights],
-        out_specs=[pl.BlockSpec((out, tile), lambda i: (0, i))] * 4,
-        out_shape=[jax.ShapeDtypeStruct((out, count), jnp.bfloat16)] * 4,
+        out_specs=[pl.BlockSpec((out, tile), lambda i: (0, i)) for out in outs],
+        out_shape=[jax.ShapeDtypeStruct((out, count), jnp.bfloat16) for out in outs],
         compiler_params=pltpu.CompilerParams(vmem_limit_bytes=VMEM),
         cost_estimate=pl.CostEstimate(flops=0, bytes_accessed=2 * count, transcendentals=0),
     )(*held, *[array for array, _, _ in weights])
@@ -120,26 +123,66 @@
     return [(a * width + i, b * width + i) for a, b in pairs for i in range(width)]
 
 
+INWARD = ((0, 1), (3, 2))
+OUTWARD = ((1, 0), (2, 3))
+ACROSS = ((1, 2), (2, 1))
+BEYOND = ((1, 3), (2, 0))
+
+
+def send_direct(parts):
+    return [
+        lax.ppermute(part, "seq", along([(a, a ^ k) for a in range(4)]))
+        for k, part in enumerate(parts[1:], 1)
+    ]
+
+
+def sum_direct(parts, arrived):
+    total = parts[0].astype(jnp.float32)
+    for other in arrived:
+        total = total + other
+    return total.astype(jnp.bfloat16)
+
+
 def ride(value, extra):
     return jnp.concatenate([value] + extra, axis=0) if extra else value
 
 
-def send_direct(parts, small):
-    return [
-        lax.ppermute(ride(part, small), "seq", along([(a, a ^ k) for a in range(4)]))
-        for k, part in enumerate(parts[1:], 1)
-    ]
-
-
-def sum_direct(parts, arrived):
-    rows = parts[0].shape[0]
-    total = parts[0].astype(jnp.float32)
-    for other in arrived:
-        total = total + other[:rows]
-    return total.astype(jnp.bfloat16)
-
-
-PLAN = (((0,), 0, 4), ((1,), 0, 4), ((0, 1), 4, 4))
+def send_sums(parts, small):
+    _, others, first = parts
+    inward = lax.ppermute(ride(others, small), "seq", along(INWARD))
+    outward = lax.ppermute(ride(first, small), "seq", along(OUTWARD))
+    return inward, outward
+
+
+def finish_sums(parts, arrived, is_end, small):
+    own, others, _ = parts
+    inward, outward = arrived
+    rows = own.shape[0]
+
+    def add(mine, other):
+        return (mine.astype(jnp.float32) + other.astype(jnp.float32)).astype(jnp.bfloat16)
+
+    def part(value, first, index=0):
+        count = small[0].shape[0]
+        return value[first + index * count : first + (index + 1) * count]
+
+    extra = [part(inward, 3 * rows)] + small if small else []
+    beyond = add(others[rows : 2 * rows], inward[2 * rows : 3 * rows])
+    beyond = lax.ppermute(ride(beyond, extra), "seq", along(BEYOND))
+    across = add(others[2 * rows :], inward[rows : 2 * rows])
+    across = lax.ppermute(ride(across, extra), "seq", along(ACROSS))
+    mine = own.astype(jnp.float32)
+    at_end = mine + outward[:rows] + beyond[:rows]
+    at_middle = mine + inward[:rows] + across[:rows]
+    shared = None
+    if small:
+        ends = [part(outward, rows), part(beyond, rows, 1), part(beyond, rows, 0)]
+        middles = [part(inward, 3 * rows), part(across, rows, 0), part(across, rows, 1)]
+        shared = small + [jnp.where(is_end, e, m) for e, m in zip(ends, middles)]
+    return jnp.where(is_end, at_end, at_middle).astype(jnp.bfloat16), shared
+
+
+PLAN = (((0,), 0, 4, True), ((1,), 0, 4, True), ((0, 1), 4, 2, False), ((0, 1), 6, 2, False))
 RIDE = 2
 
 
@@ -151,6 +194,7 @@
     share = w_merge.shape[0]
     group = lax.axis_index("seq") // width
     member = lax.axis_index("seq") % width
+    is_end = (group == 0) | (group == 3)
     local = panels.reshape(tiles * panel_rows, depth)
     half = local.shape[0] // 2
     swapped = flip(local[half:], "tp", 2)
@@ -180,31 +224,25 @@
     scalars = jnp.concatenate([places, jnp.full((4,), member, jnp.int32)])
     early, _ = lax.optimization_barrier((moved[0], swapped))
     held = [order_rows(scalars, share_panels(early), share)]
-    kv = [0.0, 0.0]
-    squares = [0.0, 0.0]
-    everyone = None
     eighth = w_merge.shape[1] // 8
     sent = []
 
-    def finish(step):
-        halves, first, count = PLAN[step]
-        merged = sum_direct(*sent[step]).astype(jnp.float32)
+    def finish(step, merged):
+        _, first, count, _ = PLAN[step]
+        merged = merged.astype(jnp.float32)
         at = slice(first * eighth, (first + count) * eighth)
         gained = (merged * ln_gain[at].astype(jnp.float32)[None, :]).astype(jnp.bfloat16)
         squared = jnp.sum(merged * merged, axis=1)
-        product = jnp.dot(gained, w_kv[at], preferred_element_type=jnp.float32)
-        for i, h in enumerate(halves):
-            squares[h] = squares[h] + squared[i * half : (i + 1) * half]
-            kv[h] = kv[h] + product[i * half : (i + 1) * half]
-
-    for step, (halves, first, count) in enumerate(PLAN):
+        return squared, jnp.dot(gained, w_kv[at], preferred_element_type=jnp.float32)
+
+    riding = []
+    for step, (halves, first, count, direct) in enumerate(PLAN):
         first, count = first * eighth, count * eighth
         if step == 1:
             late, _ = lax.optimization_barrier((moved[1], sent[0][0][0]))
             held.append(order_rows(scalars, share_panels(late), share))
-        riding = []
         if step == RIDE:
-            received[1], _ = lax.optimization_barrier((received[1], sent[step - 1][0][0]))
+            received[1], _ = lax.optimization_barrier((received[1], sent[step - 1][1][0]))
             small = [small] + [other[-extra:] for other in received[1]]
             small_shape = (width,) + small[0].shape
             riding = [jnp.stack(small).reshape(-1, count)]
@@ -217,35 +255,58 @@
             parts += [other[: w_merge.shape[0]] for other in received[side]]
             parts = jnp.concatenate(parts, axis=0)
             operands = [(jnp.roll(parts, member * w_merge.shape[0], axis=0), depth, inside)]
-        parts = partial_products([held[h] for h in halves], operands, count)
-        if step:
-            before = [sent[step - 1][1][1]] + ([sent[step - 2][1][2]] if step >= 2 else [])
-            parts, _ = lax.optimization_barrier((parts, before))
-        sent.append((parts, send_direct(parts, riding)))
-    for step in range(len(PLAN)):
-        finish(step)
-    rows = sent[RIDE][0][0].shape[0]
-    everyone = riding + [other[rows:] for other in sent[RIDE][1]]
-    everyone = jnp.stack(everyone).reshape((4,) + small_shape)
-    return jnp.concatenate(kv), jnp.concatenate(squares), everyone
+        groups = ((0,), (1,), (2,), (3,)) if direct else ((0,), (1, 2, 3), (1,))
+        parts = partial_products([held[h] for h in halves], operands, count, groups)
+        if step == 1:
+            parts, _ = lax.optimization_barrier((parts, sent[0][1][1]))
+        elif step:
+            parts, _ = lax.optimization_barrier((parts, sent[step - 2][1][-1 if step == 2 else 1]))
+        if direct:
+            sent.append((parts, send_direct(parts)))
+        else:
+            sent.append((parts, send_sums(parts, riding if step == RIDE else [])))
+    done = []
+    everyone = None
+    for step, (_, _, _, direct) in enumerate(PLAN):
+        parts, arrived = sent[step]
+        if direct:
+            merged = sum_direct(parts, arrived)
+        else:
+            merged, shared = finish_sums(parts, arrived, is_end, riding if step == RIDE else [])
+            if shared is not None:
+                everyone = jnp.stack(shared).reshape((4,) + small_shape)
+        done.append(finish(step, merged))
+    squares, kv = [
+        jnp.concatenate([done[0][i], done[1][i]], axis=0) + done[2][i] + done[3][i] for i in range(2)
+    ]
+    return kv, squares, everyone
 
 
 def scatter_heads(kv, squares):
     tp_count = lax.axis_size("tp")
     place = lax.axis_index("tp")
-    rows = kv.shape[0]
-    blocks = jnp.stack(jnp.split(kv, tp_count, axis=1))
+    width = kv.shape[1] // tp_count
+    blocks = None
     for bit in bits_of(tp_count):
-        paired = blocks.reshape(blocks.shape[0] // 2, 2, rows, blocks.shape[2])
         mine = (place // bit) % 2
-        keep = lax.dynamic_index_in_dim(paired, mine, 1, keepdims=False)
-        give = lax.dynamic_index_in_dim(paired, 1 - mine, 1, keepdims=False)
-        blocks = keep + flip(give.astype(jnp.bfloat16), "tp", bit).astype(jnp.float32)
+
+        def half(which):
+            if blocks is not None:
+                paired = blocks.reshape((-1, 2) + blocks.shape[1:])
+                return lax.dynamic_index_in_dim(paired, which, 1, keepdims=False)
+            columns = [
+                lax.dynamic_slice_in_dim(kv, (2 * i + which) * width, width, axis=1)
+                for i in range(tp_count // 2)
+            ]
+            return jnp.stack(columns)
+
+        arrived = flip(half(1 - mine).astype(jnp.bfloat16), "tp", bit)
+        blocks = half(mine) + arrived.astype(jnp.float32)
         squares = squares + flip(squares, "tp", bit)
     return blocks[0], squares
 
 
-SMALL_ROWS = 64
+SMALL_ROWS = 48
 
 
 def pack_small(prefix_cache, sources, tiles):

time: 183 us -> 188 us (1.027)
  starting transfers between devices: 55.6 us -> 46.8 us
  other arithmetic: 11.4 us -> 18.1 us
  matrix products: 4.52 us -> 8.73 us
  local copies, waits for them, and re-layouts: 13.9 us -> 17.3 us
    all_to_all x1, starting transfers between devices: 13.9 us -> 7.32 us  [shards(): lax.all_to_all(outgoing, 'seq', split_axis=0, concat_axis=0, tiled=True)]
    dot_general x3 -> x4, matrix products: 3.51 us -> 7.71 us  [finish(): jnp.dot(gained, w_kv[at], preferred_element_type=jnp.float32)]
    ppermute x11, waiting for transfers between devices: 17.7 us -> 21.6 us  [flip(): return lax.ppermute(value, axis, [(i, i ^ bit) for i in range(count)])]
    ppermute x9 -> x14, waiting for transfers between devices: 43.8 us -> 40.3 us  [the longest x2 19.8 us: send_sums(): inward = lax.ppermute(ride(others, small), 'seq', along(INWARD))]
    unnamed x68 -> x80, local copies, waits for them, and re-layouts: 2.49 us -> 5.68 us
    reduce_sum x3 -> x4, other arithmetic: 4.28 us -> 7.45 us  [finish(): squared = jnp.sum(merged * merged, axis=1)]
    pallas_call x2, Pallas kernels: 3.33 us -> 1.3 us  [order_rows(): pl.pallas_call(functools.partial(order_kernel, share), grid_spec=pltpu.Pr...]
    ppermute x9 -> x14, starting transfers between devices: 20 us -> 18.7 us  [the longest x6 7.88 us: send_direct(): lax.ppermute(part, 'seq', along([(a, a ^ k) for a in range(4)]))]
  transfers between devices with their start and end apart: 25 -> 30, of which waited for: 11 -> 13; matrix products, arithmetic and copies ran while one was open for 13% -> 17% of each run, Pallas kernels for 8% -> 7%
where the time goes in v3:
time: 188 us; the launch traced here: 187 us
  waiting for transfers between devices  75.5 us (40%)
  starting transfers between devices  46.8 us (25%)
  Pallas kernels  19.3 us (10%)
  other arithmetic  18.1 us (10%)
  local copies, waits for them, and re-layouts  17.3 us (9%)
  matrix products  8.73 us (5%)
    ppermute x11, waiting for transfers between devices, flip(): return lax.ppermute(value, axis, [(i, i ^ bit) for i in range(count)])  21.6 us
    ppermute x2, waiting for transfers between devices, send_sums(): inward = lax.ppermute(ride(others, small), 'seq', along(INWARD))  19.8 us
    ppermute x11, starting transfers between devices, flip(): return lax.ppermute(value, axis, [(i, i ^ bit) for i in range(count)])  13.9 us
    pallas_call x4, Pallas kernels, partial_products(): pl.pallas_call(functools.partial(partial_kernel, halves, groups), grid=(c...  12.4 us
    ppermute x6, waiting for transfers between devices, send_direct(): lax.ppermute(part, 'seq', along([(a, a ^ k) for a in range(4)]))  12 us
    ppermute x2, waiting for transfers between devices, finish_sums(): beyond = lax.ppermute(ride(beyond, extra), 'seq', along(BEYOND))  8.39 us
    ppermute x6, starting transfers between devices, send_direct(): lax.ppermute(part, 'seq', along([(a, a ^ k) for a in range(4)]))  7.88 us
    dot_general x4, matrix products, finish(): jnp.dot(gained, w_kv[at], preferred_element_type=jnp.float32)  7.71 us
  transfers between devices with their start and end apart: 30, of which 13 were waited for; matrix products, arithmetic and copies ran while one was open for 17% of the time, Pallas kernels for 7%

profile of v3, /device:TPU:0, one launch (start us, length us, event | category | flops | bytes accessed | tf_op | source)
XLA Modules:
  0.0 187.2 jit_solution(3373538676628903093)
XLA Ops:
  0.6 1.1 slice_bitcast_fusion
  2.5 6.8 %collective-permute-start = (bf16[128,1280]{1,0:T(8,128)(2,1)S(1)}, bf16[128,1280]{1,0:T(8,128)(2,1)}, u32[]{:S(2)}, u32[]{:S(2)}) collective-permute-start(bf16[128,1280]{1,0:T(8,128)(2,1)S(1)} %get-tuple-element.81), channel_id=1, source_target_pairs={{0,2},{1,3},{2,0},{3,1},{4,6},{5,7},{6,4},{7,5},{8,10},{9,11},{10,... | collective-permute-start | bytes 983048 | tf_op jit(solution)/shard_map/ppermute | solution.py:23
  9.3 3.4 %fusion.60 = (bf16[640,1024]{1,0:T(8,128)(2,1)}, bf16[640,1024]{1,0:T(8,128)(2,1)}) fusion(bf16[640,2048]{1,0:T(8,128)(2,1)} %refs_2_.3), kind=kLoop, calls=%fused_computation.149 | loop fusion | bytes 5242880 | tf_op jit(solution)/shard_map/slice | solution.py:207
  12.7 1.5 collective-permute-start.7
  14.8 0.8 gather_fusion.2
  16.4 6.2 %collective-permute-done = bf16[128,1280]{1,0:T(8,128)(2,1)} collective-permute-done((bf16[128,1280]{1,0:T(8,128)(2,1)S(1)}, bf16[128,1280]{1,0:T(8,128)(2,1)}, u32[]{:S(2)}, u32[]{:S(2)}) %collective-permute-start) | collective-permute-done | bytes 327712 | tf_op jit(solution)/shard_map/ppermute | solution.py:23
  22.6 2.6 %collective-permute-start.4 = (bf16[128,1280]{1,0:T(8,128)(2,1)S(1)}, bf16[128,1280]{1,0:T(8,128)(2,1)S(1)}, u32[]{:S(2)}, u32[]{:S(2)}) collective-permute-start(bf16[128,1280]{1,0:T(8,128)(2,1)S(1)} %collective-permute-done.3.refs_0_), channel_id=1, source_target_pairs={{0,2},{1,3},{2,0},{3,1},{4,6},{5,7},{6,4},{7,5},{8,10},{9,11},{10,... | collective-permute-start | bytes 983048 | tf_op jit(solution)/shard_map/ppermute | solution.py:23
  25.3 3.2 %collective-permute-start.2 = (bf16[128,1280]{1,0:T(8,128)(2,1)}, bf16[128,1280]{1,0:T(8,128)(2,1)S(1)}, u32[]{:S(2)}, u32[]{:S(2)}) collective-permute-start(bf16[128,1280]{1,0:T(8,128)(2,1)} %collective-permute-done), channel_id=1, source_target_pairs={{2,0},{3,10},{0,16},{1,26},{6,4},{7,14},{4,20},{5,30},{10,2},{11,8... | collective-permute-start | bytes 983048 | tf_op jit(solution)/shard_map/ppermute | solution.py:37
  28.5 4.7 %collective-permute-done.4.refs_1_ = bf16[128,1280]{1,0:T(8,128)(2,1)S(1)} collective-permute-done((bf16[128,1280]{1,0:T(8,128)(2,1)S(1)}, bf16[128,1280]{1,0:T(8,128)(2,1)S(1)}, u32[]{:S(2)}, u32[]{:S(2)}) %collective-permute-start.4) | collective-permute-done | bytes 327712 | tf_op jit(solution)/shard_map/ppermute | solution.py:23
  33.2 2.7 %pad_maximum_fusion = bf16[652,1024]{1,0:T(8,128)(2,1)} fusion(bf16[12,1024]{1,0:T(8,128)(2,1)S(1)} %reshape.337, bf16[640,1024]{1,0:T(8,128)(2,1)} %get-tuple-element.67), kind=kLoop, calls=%fused_computation.9 | loop fusion | flops 2670592 | bytes 2670592 | tf_op jit(solution)/shard_map/concatenate | solution.py:209
  35.9 1.5 collective-permute-start.1
  38.1 6.5 %collective-permute-done.7.refs_2_ = bf16[640,1024]{1,0:T(8,128)(2,1)} collective-permute-done((bf16[640,1024]{1,0:T(8,128)(2,1)}, bf16[640,1024]{1,0:T(8,128)(2,1)}, u32[]{:S(2)}, u32[]{:S(2)}) %collective-permute-start.7) | collective-permute-done | bytes 1310752 | tf_op jit(solution)/shard_map/ppermute | solution.py:218
  44.7 2.9 %shard_map.123 = (bf16[128,1024]{1,0:T(8,128)(2,1)S(1)}, bf16[128,1024]{1,0:T(8,128)(2,1)S(1)}, bf16[128,1024]{1,0:T(8,128)(2,1)S(1)}, bf16[128,1024]{1,0:T(8,128)(2,1)S(1)}) custom-call(bf16[512,1280]{1,0:T(8,128)(2,1)S(1)} %shard_map.122.refs_0_, bf16[640,2048]{1,0:T(8,128)(2,1)S(1)} %copy-done, bf16[640,1024]{1,0:T(8,128)(2,1)} %collective-permute-done.7.refs_2_), custom_call_target="tpu_custom_call" | custom-call | bytes 2048 | tf_op jit(solution)/shard_map/pallas_call | solution.py:109
  49.6 2.7 %collective-permute-start.13 = (bf16[128,1024]{1,0:T(8,128)(2,1)S(1)}, bf16[128,1024]{1,0:T(8,128)(2,1)}, u32[]{:S(2)}, u32[]{:S(2)}) collective-permute-start(bf16[128,1024]{1,0:T(8,128)(2,1)S(1)} %get-tuple-element.44), channel_id=1, source_target_pairs={{0,24},{4,28},{8,16},{12,20},{16,8},{20,12},{24,0},{28,4},{1,25},{... | collective-permute-start | bytes 786440 | tf_op jit(solution)/shard_map/ppermute | solution.py:134
  52.8 5.0 %collective-permute-done.8.refs_1_ = bf16[128,1280]{1,0:T(8,128)(2,1)S(1)} collective-permute-done((bf16[128,1280]{1,0:T(8,128)(2,1)S(1)}, bf16[128,1280]{1,0:T(8,128)(2,1)S(1)}, u32[]{:S(2)}, u32[]{:S(2)}) %collective-permute-start.8) | collective-permute-done | bytes 327712 | tf_op jit(solution)/shard_map/ppermute | solution.py:23
  57.8 1.6 collective-permute-done.10.refs_3_
  60.1 4.0 %shard_map.125 = (bf16[128,1024]{1,0:T(8,128)(2,1)S(1)}, bf16[128,1024]{1,0:T(8,128)(2,1)}, bf16[128,1024]{1,0:T(8,128)(2,1)S(1)}, bf16[128,1024]{1,0:T(8,128)(2,1)}) custom-call(bf16[512,1280]{1,0:T(8,128)(2,1)S(1)} %shard_map.124.refs_0_.refs_1_, bf16[640,2048]{1,0:T(8,128)(2,1)S(1)} %copy-done, bf16[640,1024]{1,0:T(8,128)(2,1)} %collective-permute-done.7.refs_2_), custom_call_target="tpu_custom_call" | custom-call | bytes 2048 | tf_op jit(solution)/shard_map/pallas_call | solution.py:109
  64.1 0.7 copy-done.7
  64.8 5.3 %collective-permute-done.11 = bf16[128,1024]{1,0:T(8,128)(2,1)S(1)} collective-permute-done((bf16[128,1024]{1,0:T(8,128)(2,1)S(1)}, bf16[128,1024]{1,0:T(8,128)(2,1)S(1)}, u32[]{:S(2)}, u32[]{:S(2)}) %collective-permute-start.11) | collective-permute-done | bytes 262176 | tf_op jit(solution)/shard_map/ppermute | solution.py:134
  70.1 0.7 copy-done.26
  72.0 0.8 broadcast_in_dim.28
  72.8 0.8 add.377
  73.6 0.8 add.378.all_ref
  74.5 2.6 %fusion.7 = (f32[128]{0:T(128)}, bf16[128,1024]{1,0:T(8,128)(2,1)}) fusion(bf16[128,1024]{1,0:T(8,128)(2,1)} %collective-permute-done.13, bf16[128,1024]{1,0:T(8,128)(2,1)} %copy-done.26, bf16[128,1024]{1,0:T(8,128)(2,1)} %collective-permute-done.18, bf16[128,1024]{1,0:T(8,128)(2,1)S(1)} %get-tuple-element.32), kind=kLoop, calls=%fused_computation.27 | loop fusion | flops 1441664 | bytes 1311232 | tf_op jit(solution)/shard_map/reduce_sum | solution.py:235
  77.1 1.6 collective-permute-start.19
  78.7 2.8 %collective-permute-start.20 = (bf16[128,1024]{1,0:T(8,128)(2,1)}, bf16[128,1024]{1,0:T(8,128)(2,1)}, u32[]{:S(2)}, u32[]{:S(2)}) collective-permute-start(bf16[128,1024]{1,0:T(8,128)(2,1)} %get-tuple-element.50), channel_id=1, source_target_pairs={{0,24},{4,28},{8,16},{12,20},{16,8},{20,12},{24,0},{28,4},{1,25},{... | collective-permute-start | bytes 786440 | tf_op jit(solution)/shard_map/ppermute | solution.py:134
  81.5 1.3 copy-done.4
  82.8 2.6 %shard_map.127 = (bf16[256,512]{1,0:T(8,128)(2,1)S(1)}, bf16[768,512]{1,0:T(8,128)(2,1)S(1)}, bf16[256,512]{1,0:T(8,128)(2,1)S(1)}) custom-call(bf16[512,1280]{1,0:T(8,128)(2,1)S(1)} %copy-done.2, bf16[512,1280]{1,0:T(8,128)(2,1)S(1)} %copy-done.4, bf16[640,2048]{1,0:T(8,128)(2,1)S(1)} %copy-done, bf16[652,1024]{1,0:T(8,128)(2,1)} %collective-permute-done.1.refs_3_), custom_call_target="tpu_custom_call" | custom-call | bytes 1024 | tf_op jit(solution)/shard_map/pallas_call | solution.py:109
  85.5 0.7 copy-done.11
  86.2 0.7 copy-done.18
  86.9 2.9 %shard_map.126 = (bf16[256,512]{1,0:T(8,128)(2,1)S(1)}, bf16[768,512]{1,0:T(8,128)(2,1)S(1)}, bf16[256,512]{1,0:T(8,128)(2,1)S(1)}) custom-call(bf16[512,1280]{1,0:T(8,128)(2,1)S(1)} %copy-done.2, bf16[512,1280]{1,0:T(8,128)(2,1)S(1)} %copy-done.4, bf16[640,2048]{1,0:T(8,128)(2,1)S(1)} %copy-done, bf16[652,1024]{1,0:T(8,128)(2,1)} %collective-permute-done.1.refs_3_), custom_call_target="tpu_custom_call" | custom-call | bytes 1024 | tf_op jit(solution)/shard_map/pallas_call | solution.py:109
  89.8 0.7 copy-done.9
  91.2 0.8 slice_bitcast_fusion.2
  92.1 6.7 %collective-permute-done.19 = bf16[128,1024]{1,0:T(8,128)(2,1)} collective-permute-done((bf16[128,1024]{1,0:T(8,128)(2,1)}, bf16[128,1024]{1,0:T(8,128)(2,1)}, u32[]{:S(2)}, u32[]{:S(2)}) %collective-permute-start.19) | collective-permute-done | bytes 262176 | tf_op jit(solution)/shard_map/ppermute | solution.py:134
  98.8 1.5 collective-permute-start.22
  100.3 1.5 collective-permute-start.15
  101.8 3.0 %fusion.2 = f32[128,1024]{1,0:T(8,128)} fusion(bf16[2048,1024]{1,0:T(8,128)(2,1)} %param.14, bf16[128,1024]{1,0:T(8,128)(2,1)} %get-tuple-element.59, f32[1024]{0:T(1024)} %slice_convert_fusion.2), kind=kOutput, calls=%fused_computation.5 | convolution fusion | flops 268828672 | bytes 2887680 | tf_op jit(solution)/shard_map/dot_general | solution.py:236
  104.8 1.3 collective-permute-start.21
  106.2 1.3 collective-permute-start.14
  107.5 1.9 %fusion.9 = (f32[128]{0:T(128)}, bf16[128,1024]{1,0:T(8,128)(2,1)S(1)}) fusion(bf16[128,1024]{1,0:T(8,128)(2,1)} %collective-permute-done.20, bf16[128,1024]{1,0:T(8,128)(2,1)} %collective-permute-done.19, bf16[128,1024]{1,0:T(8,128)(2,1)} %collective-permute-done.12, bf16[128,1024]{1,0:T(8,128)(2,1)S(1)} %copy-done.8), kind=kLoop, calls=%fused_computation.29 | loop fusion | flops 1441664 | bytes 1311232 | tf_op jit(solution)/shard_map/reduce_sum | solution.py:235
  109.4 9.1 %collective-permute-done.22 = bf16[768,512]{1,0:T(8,128)(2,1)S(1)} collective-permute-done((bf16[768,512]{1,0:T(8,128)(2,1)}, bf16[768,512]{1,0:T(8,128)(2,1)S(1)}, u32[]{:S(2)}, u32[]{:S(2)}) %collective-permute-start.22) | collective-permute-done | bytes 786464 | tf_op jit(solution)/shard_map/ppermute | solution.py:152
  118.5 1.1 add_convert_fusion.1
  119.6 1.3 collective-permute-start.23
  120.9 1.4 collective-permute-start.24
  122.2 10.8 %collective-permute-done.15 = bf16[816,512]{1,0:T(8,128)(2,1)S(1)} collective-permute-done((bf16[816,512]{1,0:T(8,128)(2,1)S(1)}, bf16[816,512]{1,0:T(8,128)(2,1)S(1)}, u32[]{:S(2)}, u32[]{:S(2)}) %collective-permute-start.15) | collective-permute-done | bytes 835616 | tf_op jit(solution)/shard_map/ppermute | solution.py:152
  133.2 0.9 pad_maximum_fusion.3
  134.1 1.3 collective-permute-start.16
  135.4 1.4 collective-permute-start.17
  136.8 1.2 fusion
  138.1 1.5 fusion.21
  139.7 8.4 %collective-permute-done.16 = bf16[352,512]{1,0:T(8,128)(2,1)S(1)} collective-permute-done((bf16[352,512]{1,0:T(8,128)(2,1)}, bf16[352,512]{1,0:T(8,128)(2,1)S(1)}, u32[]{:S(2)}, u32[]{:S(2)}) %collective-permute-start.16) | collective-permute-done | bytes 360480 | tf_op jit(solution)/shard_map/ppermute | solution.py:171
  148.1 0.8 fusion.37
  150.9 1.3 fusion.15
  152.4 1.8 convolution_add_fusion.1
  154.2 1.7 convolution_add_fusion
  156.0 0.7 pad_maximum_fusion.7
  157.4 2.4 %collective-permute-start.28 = (f32[256]{0:T(256)S(1)}, f32[256]{0:T(256)S(1)}, u32[]{:S(2)}, u32[]{:S(2)}) collective-permute-start(f32[256]{0:T(256)S(1)} %add.353), channel_id=1, source_target_pairs={{0,2},{1,3},{2,0},{3,1},{4,6},{5,7},{6,4},{7,5},{8,10},{9,11},{10,... | collective-permute-start | bytes 3080 | tf_op jit(solution)/shard_map/ppermute | solution.py:23
  159.9 1.1 collective-permute-start.26
  161.3 3.8 %collective-permute-done.26 = bf16[1,256,256]{2,1,0:T(8,128)(2,1)S(1)} collective-permute-done((bf16[1,256,256]{2,1,0:T(8,128)(2,1)S(1)}, bf16[1,256,256]{2,1,0:T(8,128)(2,1)S(1)}, u32[]{:S(2)}, u32[]{:S(2)}) %collective-permute-start.26) | collective-permute-done | bytes 131104 | tf_op jit(solution)/shard_map/ppermute | solution.py:23
  165.1 1.0 convolution_convert_fusion
  166.1 7.3 %all-to-all-start = ((bf16[8,64,256]{2,1,0:T(8,128)(2,1)}), bf16[8,64,256]{2,1,0:T(8,128)(2,1)S(1)}, u32[]{:S(2)}, u32[]{:S(2)}) async-start(bf16[8,64,256]{2,1,0:T(8,128)(2,1)} %bitcast.17), calls=%async_computation | async-start | bytes 524288 | tf_op jit(solution)/shard_map/all_to_all | solution.py:478
  173.5 1.0 add_select_fusion.pick_ref
  174.6 7.1 %all-to-all-done = bf16[8,64,256]{2,1,0:T(8,128)(2,1)S(1)} async-done(((bf16[8,64,256]{2,1,0:T(8,128)(2,1)}), bf16[8,64,256]{2,1,0:T(8,128)(2,1)S(1)}, u32[]{:S(2)}, u32[]{:S(2)}) %all-to-all-start) | async-done | bytes 262176 | tf_op jit(solution)/shard_map/all_to_all | solution.py:478
  181.7 5.5 %shard_map.128 = (bf16[4,128,1024]{2,1,0:T(8,128)(2,1)}, bf16[256,256]{1,0:T(8,128)(2,1)}) custom-call(s32[4]{0:T(128)S(1)} %fusion.49.place_ref, bf16[4,128,1024]{2,1,0:T(8,128)(2,1)S(1)} %copy-done.15, bf16[8,32,256]{2,1,0:T(8,128)(2,1)S(1)} %slice.157.prefix_ref, bf16[4,128,256]{2,1,0:T(8,128)(2,1)S(1)} %copy-done.16, bf16[512,256]{1,0:T(8,128)(2,1)S(1)} %bitcast.53, ...), custom_call_target="tpu_custom_call" | custom-call | flops 603979776 | bytes 4194304 | tf_op jit(solution)/shard_map/pallas_call | solution.py:374
  (170 shorter events, 11.5 us)
Async XLA Ops:
  1.7 14.6 %collective-permute-start.3 = (bf16[128,1280]{1,0:T(8,128)(2,1)S(1)}, bf16[128,1280]{1,0:T(8,128)(2,1)S(1)}, u32[]{:S(2)}, u32[]{:S(2)}) collective-permute-start(bf16[128,1280]{1,0:T(8,128)(2,1)S(1)} %get-tuple-element.80), channel_id=1, source_target_pairs={{0,0},{1,10},{2,16},{3,26},{4,4},{5,14},{6,20},{7,30},{8,2},{9,8},... | collective-permute-start | bytes 983048 | tf_op jit(solution)/shard_map/ppermute | solution.py:37
  2.4 11.8 %copy-start.36 = (s32[32,1]{0,1:T(1,128)S(1)}, s32[32,1]{0,1:T(1,128)}, u32[]{:S(2)}) copy-start(s32[32,1]{0,1:T(1,128)} %param.15) | copy-start | bytes 388
  2.4 11.9 %copy-start.38 = (s32[32]{0:T(128)S(1)}, s32[32]{0:T(128)}, u32[]{:S(2)}) copy-start(s32[32]{0:T(128)} %param.16) | copy-start | bytes 388
  2.5 12.0 %copy-start.39 = (s32[1,4]{1,0:T(1,128)S(1)}, s32[1,4]{1,0:T(1,128)}, u32[]{:S(2)}) copy-start(s32[1,4]{1,0:T(1,128)} %param.17) | copy-start | bytes 52
  2.5 20.1 %collective-permute-start = (bf16[128,1280]{1,0:T(8,128)(2,1)S(1)}, bf16[128,1280]{1,0:T(8,128)(2,1)}, u32[]{:S(2)}, u32[]{:S(2)}) collective-permute-start(bf16[128,1280]{1,0:T(8,128)(2,1)S(1)} %get-tuple-element.81), channel_id=1, source_target_pairs={{0,2},{1,3},{2,0},{3,1},{4,6},{5,7},{6,4},{7,5},{8,10},{9,11},{10,... | collective-permute-start | bytes 983048 | tf_op jit(solution)/shard_map/ppermute | solution.py:23
  12.7 3.6 %copy-start.29 = (bf16[1,32,256]{2,1,0:T(8,128)(2,1)S(1)}, bf16[1,32,256]{2,1,0:T(8,128)(2,1)}, u32[]{:S(2)}) copy-start(bf16[1,32,256]{2,1,0:T(8,128)(2,1)} %param.19) | copy-start | bytes 49156
  12.7 32.0 %collective-permute-start.7 = (bf16[640,1024]{1,0:T(8,128)(2,1)}, bf16[640,1024]{1,0:T(8,128)(2,1)}, u32[]{:S(2)}, u32[]{:S(2)}) collective-permute-start(bf16[640,1024]{1,0:T(8,128)(2,1)} %get-tuple-element.66), channel_id=1, source_target_pairs={{4,0},{0,4},{12,8},{8,12},{20,16},{16,20},{28,24},{24,28},{5,1},{1... | collective-permute-start | bytes 3932168 | tf_op jit(solution)/shard_map/ppermute | solution.py:218
  16.1 22.0 %copy-start.30 = (s32[128]{0:T(128)}, s32[128]{0:T(128)S(1)}, u32[]{:S(2)}) copy-start(s32[128]{0:T(128)S(1)} %add.365) | copy-start | bytes 1540
  22.6 10.6 %collective-permute-start.4 = (bf16[128,1280]{1,0:T(8,128)(2,1)S(1)}, bf16[128,1280]{1,0:T(8,128)(2,1)S(1)}, u32[]{:S(2)}, u32[]{:S(2)}) collective-permute-start(bf16[128,1280]{1,0:T(8,128)(2,1)S(1)} %collective-permute-done.3.refs_0_), channel_id=1, source_target_pairs={{0,2},{1,3},{2,0},{3,1},{4,6},{5,7},{6,4},{7,5},{8,10},{9,11},{10,... | collective-permute-start | bytes 983048 | tf_op jit(solution)/shard_map/ppermute | solution.py:23
  25.2 12.2 %collective-permute-start.5 = (bf16[128,1280]{1,0:T(8,128)(2,1)S(1)}, bf16[128,1280]{1,0:T(8,128)(2,1)S(1)}, u32[]{:S(2)}, u32[]{:S(2)}) collective-permute-start(bf16[128,1280]{1,0:T(8,128)(2,1)S(1)} %collective-permute-done.3.refs_0_), channel_id=1, source_target_pairs={{0,1},{1,0},{2,3},{3,2},{4,5},{5,4},{6,7},{7,6},{8,9},{9,8},{10,11... | collective-permute-start | bytes 983048 | tf_op jit(solution)/shard_map/ppermute | solution.py:23
  25.3 22.3 %collective-permute-start.2 = (bf16[128,1280]{1,0:T(8,128)(2,1)}, bf16[128,1280]{1,0:T(8,128)(2,1)S(1)}, u32[]{:S(2)}, u32[]{:S(2)}) collective-permute-start(bf16[128,1280]{1,0:T(8,128)(2,1)} %collective-permute-done), channel_id=1, source_target_pairs={{2,0},{3,10},{0,16},{1,26},{6,4},{7,14},{4,20},{5,30},{10,2},{11,8... | collective-permute-start | bytes 983048 | tf_op jit(solution)/shard_map/ppermute | solution.py:37
  33.2 4.2 %collective-permute-start.6 = (bf16[128,1280]{1,0:T(8,128)(2,1)S(1)}, bf16[128,1280]{1,0:T(8,128)(2,1)S(1)}, u32[]{:S(2)}, u32[]{:S(2)}) collective-permute-start(bf16[128,1280]{1,0:T(8,128)(2,1)S(1)} %collective-permute-done.4.refs_1_), channel_id=1, source_target_pairs={{0,1},{1,0},{2,3},{3,2},{4,5},{5,4},{6,7},{7,6},{8,9},{9,8},{10,11... | collective-permute-start | bytes 983048 | tf_op jit(solution)/shard_map/ppermute | solution.py:23
  33.2 11.5 %copy-start = (bf16[640,2048]{1,0:T(8,128)(2,1)S(1)}, bf16[640,2048]{1,0:T(8,128)(2,1)}, u32[]{:S(2)}) copy-start(bf16[640,2048]{1,0:T(8,128)(2,1)} %refs_2_.3) | copy-start | bytes 7864324
  35.9 45.7 %collective-permute-start.1 = (bf16[652,1024]{1,0:T(8,128)(2,1)}, bf16[652,1024]{1,0:T(8,128)(2,1)}, u32[]{:S(2)}, u32[]{:S(2)}) collective-permute-start(bf16[652,1024]{1,0:T(8,128)(2,1)} %pad_maximum_fusion), channel_id=1, source_target_pairs={{4,0},{0,4},{12,8},{8,12},{20,16},{16,20},{28,24},{24,28},{5,1},{1... | collective-permute-start | bytes 4005896 | tf_op jit(solution)/shard_map/ppermute | solution.py:218
  38.1 9.5 %copy-start.1 = (bf16[512,1280]{1,0:T(8,128)(2,1)}, bf16[512,1280]{1,0:T(8,128)(2,1)S(1)}, u32[]{:S(2)}) copy-start(bf16[512,1280]{1,0:T(8,128)(2,1)S(1)} %shard_map.122.refs_0_) | copy-start | bytes 3932164
  38.1 9.9 %copy-start.32 = (bf16[2048]{0:T(1024)(128)(2,1)S(1)}, bf16[2048]{0:T(1024)(128)(2,1)}, u32[]{:S(2)}) copy-start(bf16[2048]{0:T(1024)(128)(2,1)} %param.13) | copy-start | bytes 12292
  47.6 4.7 %collective-permute-start.9 = (bf16[128,1280]{1,0:T(8,128)(2,1)S(1)}, bf16[128,1280]{1,0:T(8,128)(2,1)S(1)}, u32[]{:S(2)}, u32[]{:S(2)}) collective-permute-start(bf16[128,1280]{1,0:T(8,128)(2,1)S(1)} %collective-permute-done.2.refs_0_), channel_id=1, source_target_pairs={{0,1},{1,0},{2,3},{3,2},{4,5},{5,4},{6,7},{7,6},{8,9},{9,8},{10,11... | collective-permute-start | bytes 983048 | tf_op jit(solution)/shard_map/ppermute | solution.py:23
  47.7 10.1 %collective-permute-start.8 = (bf16[128,1280]{1,0:T(8,128)(2,1)S(1)}, bf16[128,1280]{1,0:T(8,128)(2,1)S(1)}, u32[]{:S(2)}, u32[]{:S(2)}) collective-permute-start(bf16[128,1280]{1,0:T(8,128)(2,1)S(1)} %collective-permute-done.2.refs_0_), channel_id=1, source_target_pairs={{0,2},{1,3},{2,0},{3,1},{4,6},{5,7},{6,4},{7,5},{8,10},{9,11},{10,... | collective-permute-start | bytes 983048 | tf_op jit(solution)/shard_map/ppermute | solution.py:23
  49.3 20.8 %collective-permute-start.11 = (bf16[128,1024]{1,0:T(8,128)(2,1)S(1)}, bf16[128,1024]{1,0:T(8,128)(2,1)S(1)}, u32[]{:S(2)}, u32[]{:S(2)}) collective-permute-start(bf16[128,1024]{1,0:T(8,128)(2,1)S(1)} %get-tuple-element.38), channel_id=1, source_target_pairs={{0,16},{4,20},{8,24},{12,28},{16,0},{20,4},{24,8},{28,12},{1,17},{... | collective-permute-start | bytes 786440 | tf_op jit(solution)/shard_map/ppermute | solution.py:134
  49.6 24.9 %collective-permute-start.13 = (bf16[128,1024]{1,0:T(8,128)(2,1)S(1)}, bf16[128,1024]{1,0:T(8,128)(2,1)}, u32[]{:S(2)}, u32[]{:S(2)}) collective-permute-start(bf16[128,1024]{1,0:T(8,128)(2,1)S(1)} %get-tuple-element.44), channel_id=1, source_target_pairs={{0,24},{4,28},{8,16},{12,20},{16,8},{20,12},{24,0},{28,4},{1,25},{... | collective-permute-start | bytes 786440 | tf_op jit(solution)/shard_map/ppermute | solution.py:134
  52.4 22.1 %collective-permute-start.18 = (bf16[128,1024]{1,0:T(8,128)(2,1)S(1)}, bf16[128,1024]{1,0:T(8,128)(2,1)}, u32[]{:S(2)}, u32[]{:S(2)}) collective-permute-start(bf16[128,1024]{1,0:T(8,128)(2,1)S(1)} %get-tuple-element.47), channel_id=1, source_target_pairs={{0,8},{4,12},{8,0},{12,4},{16,24},{20,28},{24,16},{28,20},{1,9},{5... | collective-permute-start | bytes 786440 | tf_op jit(solution)/shard_map/ppermute | solution.py:134
  57.8 1.6 collective-permute-start.10
  60.1 4.0 %copy-start.3 = (bf16[512,1280]{1,0:T(8,128)(2,1)}, bf16[512,1280]{1,0:T(8,128)(2,1)S(1)}, u32[]{:S(2)}) copy-start(bf16[512,1280]{1,0:T(8,128)(2,1)S(1)} %shard_map.124.refs_0_.refs_1_) | copy-start | bytes 3932164
  64.8 5.3 %copy-start.17 = (bf16[128,1024]{1,0:T(8,128)(2,1)}, bf16[128,1024]{1,0:T(8,128)(2,1)S(1)}, u32[]{:S(2)}) copy-start(bf16[128,1024]{1,0:T(8,128)(2,1)S(1)} %get-tuple-element.49) | copy-start | bytes 786436
  70.8 10.7 %collective-permute-start.12 = (bf16[128,1024]{1,0:T(8,128)(2,1)}, bf16[128,1024]{1,0:T(8,128)(2,1)}, u32[]{:S(2)}, u32[]{:S(2)}) collective-permute-start(bf16[128,1024]{1,0:T(8,128)(2,1)} %get-tuple-element.39), channel_id=1, source_target_pairs={{0,8},{4,12},{8,0},{12,4},{16,24},{20,28},{24,16},{28,20},{1,9},{5... | collective-permute-start | bytes 786440 | tf_op jit(solution)/shard_map/ppermute | solution.py:134
  74.5 7.1 %copy-start.2 = (bf16[512,1280]{1,0:T(8,128)(2,1)S(1)}, bf16[512,1280]{1,0:T(8,128)(2,1)}, u32[]{:S(2)}) copy-start(bf16[512,1280]{1,0:T(8,128)(2,1)} %copy-done.1) | copy-start | bytes 3932164
  77.1 21.7 %collective-permute-start.19 = (bf16[128,1024]{1,0:T(8,128)(2,1)}, bf16[128,1024]{1,0:T(8,128)(2,1)}, u32[]{:S(2)}, u32[]{:S(2)}) collective-permute-start(bf16[128,1024]{1,0:T(8,128)(2,1)} %copy-done.17), channel_id=1, source_target_pairs={{0,16},{4,20},{8,24},{12,28},{16,0},{20,4},{24,8},{28,12},{1,17},{... | collective-permute-start | bytes 786440 | tf_op jit(solution)/shard_map/ppermute | solution.py:134
  78.7 28.7 %collective-permute-start.20 = (bf16[128,1024]{1,0:T(8,128)(2,1)}, bf16[128,1024]{1,0:T(8,128)(2,1)}, u32[]{:S(2)}, u32[]{:S(2)}) collective-permute-start(bf16[128,1024]{1,0:T(8,128)(2,1)} %get-tuple-element.50), channel_id=1, source_target_pairs={{0,24},{4,28},{8,16},{12,20},{16,8},{20,12},{24,0},{28,4},{1,25},{... | collective-permute-start | bytes 786440 | tf_op jit(solution)/shard_map/ppermute | solution.py:134
  81.5 1.3 copy-start.4
  86.9 2.9 %copy-start.5 = (bf16[768,512]{1,0:T(8,128)(2,1)}, bf16[768,512]{1,0:T(8,128)(2,1)S(1)}, u32[]{:S(2)}) copy-start(bf16[768,512]{1,0:T(8,128)(2,1)S(1)} %get-tuple-element.57) | copy-start | bytes 2359300
  86.9 5.1 %copy-start.28 = (bf16[1,12,1024]{2,1,0:T(8,128)(2,1)S(1)}, bf16[1,12,1024]{2,1,0:T(8,128)(2,1)}, u32[]{:S(2)}) copy-start(bf16[1,12,1024]{2,1,0:T(8,128)(2,1)} %stack_reshape.6) | copy-start | bytes 73732
  98.8 6.0 %copy-start.19 = (bf16[256,512]{1,0:T(8,128)(2,1)S(1)}, bf16[256,512]{1,0:T(8,128)(2,1)}, u32[]{:S(2)}) copy-start(bf16[256,512]{1,0:T(8,128)(2,1)} %copy-done.18) | copy-start | bytes 786436
  98.8 7.3 %copy-start.14 = (bf16[256,512]{1,0:T(8,128)(2,1)S(1)}, bf16[256,512]{1,0:T(8,128)(2,1)}, u32[]{:S(2)}) copy-start(bf16[256,512]{1,0:T(8,128)(2,1)} %copy-done.13) | copy-start | bytes 786436
  98.8 19.7 %collective-permute-start.22 = (bf16[768,512]{1,0:T(8,128)(2,1)}, bf16[768,512]{1,0:T(8,128)(2,1)S(1)}, u32[]{:S(2)}, u32[]{:S(2)}) collective-permute-start(bf16[768,512]{1,0:T(8,128)(2,1)} %copy-done.5), channel_id=1, source_target_pairs={{0,8},{4,12},{24,16},{28,20},{1,9},{5,13},{25,17},{29,21},{2,10},{... | collective-permute-start | bytes 2359304 | tf_op jit(solution)/shard_map/ppermute | solution.py:152
  100.3 7.2 %copy-start.8 = (bf16[128,1024]{1,0:T(8,128)(2,1)S(1)}, bf16[128,1024]{1,0:T(8,128)(2,1)}, u32[]{:S(2)}) copy-start(bf16[128,1024]{1,0:T(8,128)(2,1)} %copy-done.7) | copy-start | bytes 786436
  100.3 32.7 %collective-permute-start.15 = (bf16[816,512]{1,0:T(8,128)(2,1)S(1)}, bf16[816,512]{1,0:T(8,128)(2,1)S(1)}, u32[]{:S(2)}, u32[]{:S(2)}) collective-permute-start(bf16[816,512]{1,0:T(8,128)(2,1)S(1)} %pad_maximum_fusion.1), channel_id=1, source_target_pairs={{0,8},{4,12},{24,16},{28,20},{1,9},{5,13},{25,17},{29,21},{2,10},{... | collective-permute-start | bytes 2506760 | tf_op jit(solution)/shard_map/ppermute | solution.py:152
  101.8 16.7 %copy-start.6 = (bf16[768,512]{1,0:T(8,128)(2,1)S(1)}, bf16[768,512]{1,0:T(8,128)(2,1)}, u32[]{:S(2)}) copy-start(bf16[768,512]{1,0:T(8,128)(2,1)} %copy-done.5) | copy-start | bytes 2359300
  104.8 33.2 %collective-permute-start.21 = (bf16[256,512]{1,0:T(8,128)(2,1)S(1)}, bf16[256,512]{1,0:T(8,128)(2,1)}, u32[]{:S(2)}, u32[]{:S(2)}) collective-permute-start(bf16[256,512]{1,0:T(8,128)(2,1)S(1)} %copy-done.19), channel_id=1, source_target_pairs={{8,0},{12,4},{16,24},{20,28},{9,1},{13,5},{17,25},{21,29},{10,2},{... | collective-permute-start | bytes 786440 | tf_op jit(solution)/shard_map/ppermute | solution.py:153
  106.2 27.0 %collective-permute-start.14 = (bf16[304,512]{1,0:T(8,128)(2,1)S(1)}, bf16[304,512]{1,0:T(8,128)(2,1)S(1)}, u32[]{:S(2)}, u32[]{:S(2)}) collective-permute-start(bf16[304,512]{1,0:T(8,128)(2,1)S(1)} %pad_maximum_fusion.6), channel_id=1, source_target_pairs={{8,0},{12,4},{16,24},{20,28},{9,1},{13,5},{17,25},{21,29},{10,2},{... | collective-permute-start | bytes 933896 | tf_op jit(solution)/shard_map/ppermute | solution.py:153
  109.4 27.4 %copy-start.20 = (bf16[2048,1024]{1,0:T(8,128)(2,1)S(1)}, bf16[2048,1024]{1,0:T(8,128)(2,1)}, u32[]{:S(2)}) copy-start(bf16[2048,1024]{1,0:T(8,128)(2,1)} %param.14) | copy-start | bytes 12582916
  109.4 27.4 %copy-start.33 = (f32[1024]{0:T(1024)S(1)}, f32[1024]{0:T(1024)}, u32[]{:S(2)}) copy-start(f32[1024]{0:T(1024)} %slice_convert_fusion.2) | copy-start | bytes 12292
  118.5 15.6 %copy-start.21 = (bf16[768,512]{1,0:T(8,128)(2,1)}, bf16[768,512]{1,0:T(8,128)(2,1)S(1)}, u32[]{:S(2)}) copy-start(bf16[768,512]{1,0:T(8,128)(2,1)S(1)} %collective-permute-done.22) | copy-start | bytes 2359300
  119.6 18.5 %collective-permute-start.23 = (bf16[256,512]{1,0:T(8,128)(2,1)}, bf16[256,512]{1,0:T(8,128)(2,1)}, u32[]{:S(2)}, u32[]{:S(2)}) collective-permute-start(bf16[256,512]{1,0:T(8,128)(2,1)} %get-tuple-element.70), channel_id=1, source_target_pairs={{8,24},{12,28},{16,0},{20,4},{9,25},{13,29},{17,1},{21,5},{10,26},... | collective-permute-start | bytes 786440 | tf_op jit(solution)/shard_map/ppermute | solution.py:171
  120.9 17.3 %collective-permute-start.24 = (bf16[256,512]{1,0:T(8,128)(2,1)}, bf16[256,512]{1,0:T(8,128)(2,1)}, u32[]{:S(2)}, u32[]{:S(2)}) collective-permute-start(bf16[256,512]{1,0:T(8,128)(2,1)} %get-tuple-element.71), channel_id=1, source_target_pairs={{8,16},{12,20},{16,8},{20,12},{9,17},{13,21},{17,9},{21,13},{10,18... | collective-permute-start | bytes 786440 | tf_op jit(solution)/shard_map/ppermute | solution.py:173
  133.1 4.9 %copy-start.25 = (bf16[304,512]{1,0:T(8,128)(2,1)}, bf16[304,512]{1,0:T(8,128)(2,1)S(1)}, u32[]{:S(2)}) copy-start(bf16[304,512]{1,0:T(8,128)(2,1)S(1)} %collective-permute-done.14) | copy-start | bytes 933892
  133.2 5.0 %copy-start.12 = (bf16[256,512]{1,0:T(8,128)(2,1)S(1)}, bf16[256,512]{1,0:T(8,128)(2,1)}, u32[]{:S(2)}) copy-start(bf16[256,512]{1,0:T(8,128)(2,1)} %copy-done.11) | copy-start | bytes 786436
  134.1 14.0 %collective-permute-start.16 = (bf16[352,512]{1,0:T(8,128)(2,1)}, bf16[352,512]{1,0:T(8,128)(2,1)S(1)}, u32[]{:S(2)}, u32[]{:S(2)}) collective-permute-start(bf16[352,512]{1,0:T(8,128)(2,1)} %get-tuple-element.84), channel_id=1, source_target_pairs={{8,24},{12,28},{16,0},{20,4},{9,25},{13,29},{17,1},{21,5},{10,26},... | collective-permute-start | bytes 1081352 | tf_op jit(solution)/shard_map/ppermute | solution.py:171
  135.4 12.7 %collective-permute-start.17 = (bf16[352,512]{1,0:T(8,128)(2,1)}, bf16[352,512]{1,0:T(8,128)(2,1)}, u32[]{:S(2)}, u32[]{:S(2)}) collective-permute-start(bf16[352,512]{1,0:T(8,128)(2,1)} %get-tuple-element.85), channel_id=1, source_target_pairs={{8,16},{12,20},{16,8},{20,12},{9,17},{13,21},{17,9},{21,13},{10,18... | collective-permute-start | bytes 1081352 | tf_op jit(solution)/shard_map/ppermute | solution.py:173
  138.0 12.9 %copy-start.10 = (bf16[256,512]{1,0:T(8,128)(2,1)S(1)}, bf16[256,512]{1,0:T(8,128)(2,1)}, u32[]{:S(2)}) copy-start(bf16[256,512]{1,0:T(8,128)(2,1)} %copy-done.9) | copy-start | bytes 786436
  138.1 14.2 %copy-start.34 = (f32[128]{0:T(128)S(1)}, f32[128]{0:T(128)}, u32[]{:S(2)}) copy-start(f32[128]{0:T(128)} %get-tuple-element.58) | copy-start | bytes 1540
  138.1 14.2 %copy-start.35 = (f32[128]{0:T(128)S(1)}, f32[128]{0:T(128)}, u32[]{:S(2)}) copy-start(f32[128]{0:T(128)} %get-tuple-element.60) | copy-start | bytes 1540
  138.1 14.3 %copy-start.24 = (f32[128,1024]{1,0:T(8,128)S(1)}, f32[128,1024]{1,0:T(8,128)}, u32[]{:S(2)}) copy-start(f32[128,1024]{1,0:T(8,128)} %fusion.2) | copy-start | bytes 1572868
  149.0 5.2 %copy-start.22 = (bf16[8,48,256]{2,1,0:T(8,128)(2,1)}, bf16[8,48,256]{2,1,0:T(8,128)(2,1)S(1)}, u32[]{:S(2)}) copy-start(bf16[8,48,256]{2,1,0:T(8,128)(2,1)S(1)} %reshape_reshape.3) | copy-start | bytes 589828
  152.3 5.1 %collective-permute-start.27 = (f32[256]{0:T(256)S(1)}, f32[256]{0:T(256)S(1)}, u32[]{:S(2)}, u32[]{:S(2)}) collective-permute-start(f32[256]{0:T(256)S(1)} %fusion.48), channel_id=1, source_target_pairs={{0,1},{1,0},{2,3},{3,2},{4,5},{5,4},{6,7},{7,6},{8,9},{9,8},{10,11... | collective-permute-start | bytes 3080 | tf_op jit(solution)/shard_map/ppermute | solution.py:23
  155.9 17.5 %copy-start.37 = (s32[4]{0:T(128)S(1)}, s32[4]{0:T(128)}, u32[]{:S(2)}) copy-start(s32[4]{0:T(128)} %param.18) | copy-start | bytes 52
  155.9 17.5 %copy-start.27 = (pred[4,128,1]{2,1,0:T(8,128)(4,1)S(1)}, pred[4,128,1]{2,1,0:T(8,128)(4,1)}, u32[]{:S(2)}) copy-start(pred[4,128,1]{2,1,0:T(8,128)(4,1)} %broadcast_in_dim.28) | copy-start | bytes 1540
  156.0 17.5 %copy-start.31 = (s32[128]{0:T(128)S(1)}, s32[128]{0:T(128)}, u32[]{:S(2)}) copy-start(s32[128]{0:T(128)} %copy-done.30) | copy-start | bytes 1540
  156.7 3.1 %collective-permute-start.25 = (bf16[2,256,256]{2,1,0:T(8,128)(2,1)}, bf16[2,256,256]{2,1,0:T(8,128)(2,1)S(1)}, u32[]{:S(2)}, u32[]{:S(2)}) collective-permute-start(bf16[2,256,256]{2,1,0:T(8,128)(2,1)} %pad_maximum_fusion.7), channel_id=1, source_target_pairs={{0,1},{1,0},{2,3},{3,2},{4,5},{5,4},{6,7},{7,6},{8,9},{9,8},{10,11... | collective-permute-start | bytes 786440 | tf_op jit(solution)/shard_map/ppermute | solution.py:23
  157.3 24.4 %copy-start.15 = (bf16[4,128,1024]{2,1,0:T(8,128)(2,1)S(1)}, bf16[4,128,1024]{2,1,0:T(8,128)(2,1)}, u32[]{:S(2)}) copy-start(bf16[4,128,1024]{2,1,0:T(8,128)(2,1)} %query_ref.1) | copy-start | bytes 3145732
  157.3 24.4 %copy-start.16 = (bf16[4,128,256]{2,1,0:T(8,128)(2,1)S(1)}, bf16[4,128,256]{2,1,0:T(8,128)(2,1)}, u32[]{:S(2)}) copy-start(bf16[4,128,256]{2,1,0:T(8,128)(2,1)} %text_ref.1) | copy-start | bytes 786436
  157.3 17.2 %copy-start.23 = (bf16[8,48,256]{2,1,0:T(8,128)(2,1)S(1)}, bf16[8,48,256]{2,1,0:T(8,128)(2,1)}, u32[]{:S(2)}) copy-start(bf16[8,48,256]{2,1,0:T(8,128)(2,1)} %copy-done.22) | copy-start | bytes 589828
  157.4 3.9 %collective-permute-start.28 = (f32[256]{0:T(256)S(1)}, f32[256]{0:T(256)S(1)}, u32[]{:S(2)}, u32[]{:S(2)}) collective-permute-start(f32[256]{0:T(256)S(1)} %add.353), channel_id=1, source_target_pairs={{0,2},{1,3},{2,0},{3,1},{4,6},{5,7},{6,4},{7,5},{8,10},{9,11},{10,... | collective-permute-start | bytes 3080 | tf_op jit(solution)/shard_map/ppermute | solution.py:23
  159.9 5.2 %collective-permute-start.26 = (bf16[1,256,256]{2,1,0:T(8,128)(2,1)S(1)}, bf16[1,256,256]{2,1,0:T(8,128)(2,1)S(1)}, u32[]{:S(2)}, u32[]{:S(2)}) collective-permute-start(bf16[1,256,256]{2,1,0:T(8,128)(2,1)S(1)} %dynamic-slice_convert_fusion), channel_id=1, source_target_pairs={{0,2},{1,3},{2,0},{3,1},{4,6},{5,7},{6,4},{7,5},{8,10},{9,11},{10,... | collective-permute-start | bytes 393224 | tf_op jit(solution)/shard_map/ppermute | solution.py:23
  166.1 15.5 %all-to-all-start = ((bf16[8,64,256]{2,1,0:T(8,128)(2,1)}), bf16[8,64,256]{2,1,0:T(8,128)(2,1)S(1)}, u32[]{:S(2)}, u32[]{:S(2)}) async-start(bf16[8,64,256]{2,1,0:T(8,128)(2,1)} %bitcast.17), calls=%async_computation | async-start | bytes 524288 | tf_op jit(solution)/shard_map/all_to_all | solution.py:478
  (6 other events, 4.2 us)

commit v4 on v1

--- a/solution.py
+++ b/solution.py
@@ -124,10 +124,10 @@
     return jnp.concatenate([value] + extra, axis=0) if extra else value
 
 
-def send_direct(parts, small):
+def send_direct(parts, small, kinds=(1, 2, 3)):
     return [
-        lax.ppermute(ride(part, small), "seq", along([(a, a ^ k) for a in range(4)]))
-        for k, part in enumerate(parts[1:], 1)
+        lax.ppermute(ride(parts[k], small), "seq", along([(a, a ^ k) for a in range(4)]))
+        for k in kinds
     ]
 
 
@@ -139,7 +139,7 @@
     return total.astype(jnp.bfloat16)
 
 
-PLAN = (((0,), 0, 4), ((1,), 0, 4), ((0, 1), 4, 4))
+PLAN = (((0,), 0, 4), ((1,), 0, 4), ((0, 1), 4, 2), ((0, 1), 6, 2))
 RIDE = 2
 
 
@@ -160,10 +160,11 @@
     extra = small.shape[0]
     received = []
     for side in range(2):
-        own = w_merge[:, side * columns : (side + 1) * columns]
-        if side == 1:
-            own = jnp.concatenate([own, small], axis=0)
-            own, _ = lax.optimization_barrier((own, swapped))
+        if side == 0:
+            own = w_merge[:, :columns]
+        else:
+            source, _ = lax.optimization_barrier((w_merge, swapped))
+            own = jnp.concatenate([source[:, columns:], small], axis=0)
         others = []
         for offset in range(1, width):
             pairs = [
@@ -180,29 +181,23 @@
     scalars = jnp.concatenate([places, jnp.full((4,), member, jnp.int32)])
     early, _ = lax.optimization_barrier((moved[0], swapped))
     held = [order_rows(scalars, share_panels(early), share)]
-    kv = [0.0, 0.0]
-    squares = [0.0, 0.0]
-    everyone = None
     eighth = w_merge.shape[1] // 8
     sent = []
 
     def finish(step):
-        halves, first, count = PLAN[step]
+        _, first, count = PLAN[step]
         merged = sum_direct(*sent[step]).astype(jnp.float32)
         at = slice(first * eighth, (first + count) * eighth)
         gained = (merged * ln_gain[at].astype(jnp.float32)[None, :]).astype(jnp.bfloat16)
         squared = jnp.sum(merged * merged, axis=1)
-        product = jnp.dot(gained, w_kv[at], preferred_element_type=jnp.float32)
-        for i, h in enumerate(halves):
-            squares[h] = squares[h] + squared[i * half : (i + 1) * half]
-            kv[h] = kv[h] + product[i * half : (i + 1) * half]
-
+        return squared, jnp.dot(gained, w_kv[at], preferred_element_type=jnp.float32)
+
+    riding = []
     for step, (halves, first, count) in enumerate(PLAN):
         first, count = first * eighth, count * eighth
         if step == 1:
             late, _ = lax.optimization_barrier((moved[1], sent[0][0][0]))
             held.append(order_rows(scalars, share_panels(late), share))
-        riding = []
         if step == RIDE:
             received[1], _ = lax.optimization_barrier((received[1], sent[step - 1][0][0]))
             small = [small] + [other[-extra:] for other in received[1]]
@@ -218,34 +213,65 @@
             parts = jnp.concatenate(parts, axis=0)
             operands = [(jnp.roll(parts, member * w_merge.shape[0], axis=0), depth, inside)]
         parts = partial_products([held[h] for h in halves], operands, count)
-        if step:
-            before = [sent[step - 1][1][1]] + ([sent[step - 2][1][2]] if step >= 2 else [])
-            parts, _ = lax.optimization_barrier((parts, before))
-        sent.append((parts, send_direct(parts, riding)))
-    for step in range(len(PLAN)):
-        finish(step)
+        if step == 0:
+            sent.append((parts, send_direct(parts, [], (2, 3))))
+        elif step == 1:
+            parts, _ = lax.optimization_barrier((parts, sent[0][1]))
+            joined = jnp.concatenate([sent[0][0][1], parts[1]], axis=0)
+            far = send_direct(parts, [], (2, 3))
+            near = send_direct([None, joined], [], (1,))[0]
+            sent[0][1].append(near[:half])
+            sent.append((parts, far + [near[half:]]))
+        elif step == 2:
+            parts, _ = lax.optimization_barrier((parts, sent[1][1][0]))
+            sent.append((parts, send_direct(parts, riding)))
+        else:
+            parts, _ = lax.optimization_barrier((parts, (sent[1][1][1], sent[2][1][0])))
+            sent.append((parts, send_direct(parts, [])))
+    done = [finish(step) for step in range(len(PLAN) - 1)]
+
+    def complete(after):
+        parts, arrived = sent[-1]
+        arrived, after = lax.optimization_barrier((arrived, after))
+        sent[-1] = (parts, arrived)
+        done.append(finish(len(PLAN) - 1))
+        squares, kv = [
+            jnp.concatenate([done[0][i], done[1][i]], axis=0) + done[2][i] + done[3][i]
+            for i in range(2)
+        ]
+        return kv, squares, after
+
     rows = sent[RIDE][0][0].shape[0]
     everyone = riding + [other[rows:] for other in sent[RIDE][1]]
     everyone = jnp.stack(everyone).reshape((4,) + small_shape)
-    return jnp.concatenate(kv), jnp.concatenate(squares), everyone
+    return complete, everyone
 
 
 def scatter_heads(kv, squares):
     tp_count = lax.axis_size("tp")
     place = lax.axis_index("tp")
-    rows = kv.shape[0]
-    blocks = jnp.stack(jnp.split(kv, tp_count, axis=1))
+    width = kv.shape[1] // tp_count
+    blocks = None
     for bit in bits_of(tp_count):
-        paired = blocks.reshape(blocks.shape[0] // 2, 2, rows, blocks.shape[2])
         mine = (place // bit) % 2
-        keep = lax.dynamic_index_in_dim(paired, mine, 1, keepdims=False)
-        give = lax.dynamic_index_in_dim(paired, 1 - mine, 1, keepdims=False)
-        blocks = keep + flip(give.astype(jnp.bfloat16), "tp", bit).astype(jnp.float32)
+
+        def half(which):
+            if blocks is not None:
+                paired = blocks.reshape((-1, 2) + blocks.shape[1:])
+                return lax.dynamic_index_in_dim(paired, which, 1, keepdims=False)
+            columns = [
+                lax.dynamic_slice_in_dim(kv, (2 * i + which) * width, width, axis=1)
+                for i in range(tp_count // 2)
+            ]
+            return jnp.stack(columns)
+
+        arrived = flip(half(1 - mine).astype(jnp.bfloat16), "tp", bit)
+        blocks = half(mine) + arrived.astype(jnp.float32)
         squares = squares + flip(squares, "tp", bit)
     return blocks[0], squares
 
 
-SMALL_ROWS = 64
+SMALL_ROWS = 48
 
 
 def pack_small(prefix_cache, sources, tiles):
@@ -256,62 +282,53 @@
     return jnp.concatenate([prefix_cache[0], asks], axis=0)
 
 
-def attend_kernel(
-    place_ref, query_ref, prefix_ref, text_ref, pages_ref, pick_ref, seen_ref, all_ref, out_ref, vision_ref
-):
-    pages = pages_ref[...]
-    count = pages.shape[0]
-
-    def pick(index):
-        one_hot = lax.broadcasted_iota(jnp.int32, (index.shape[0], count), 1) == index
-        one_hot = jnp.where(one_hot, 1.0, 0.0).astype(jnp.bfloat16)
-        return jnp.dot(one_hot, pages, preferred_element_type=jnp.float32).astype(jnp.bfloat16)
-
-    @pl.when(pl.program_id(0) == 0)
-    def _():
-        vision_ref[...] = pick(all_ref[...])
-
-    window = pick(pick_ref[0])
-    keys_values = jnp.concatenate([prefix_ref[0], window, text_ref[0]], axis=0)
-    text_rows = text_ref.shape[1]
-    heads = keys_values.shape[1] // (2 * HD)
-    query = query_ref[0]
-    for head in range(heads):
-        keys = keys_values[:, 2 * head * HD : (2 * head + 1) * HD]
-        values = keys_values[:, (2 * head + 1) * HD : (2 * head + 2) * HD]
-        stacked = jnp.concatenate(
-            [
-                query[:, (head * GROUP + a) * HD : (head * GROUP + a + 1) * HD]
-                for a in range(GROUP)
-            ],
-            axis=0,
-        )
-        scores = lax.dot_general(
-            stacked, keys, (((1,), (1,)), ((), ())), preferred_element_type=jnp.float32
-        ) * (HD**-0.5)
+def stack_heads(query, head):
+    return jnp.concatenate(
+        [query[:, (head * GROUP + a) * HD : (head * GROUP + a + 1) * HD] for a in range(GROUP)], axis=0
+    )
+
+
+def score(stacked, keys):
+    return lax.dot_general(
+        stacked, keys, (((1,), (1,)), ((), ())), preferred_element_type=jnp.float32
+    ) * (HD**-0.5)
+
+
+def weigh(scores, values):
+    best = jnp.max(scores, axis=1, keepdims=True)
+    weights = jnp.exp(scores - best)
+    total = jnp.sum(weights, axis=1, keepdims=True)
+    return (
+        best,
+        total,
+        jnp.dot(weights.astype(jnp.bfloat16), values, preferred_element_type=jnp.float32),
+    )
+
+
+def text_kernel(place_ref, query_ref, prefix_ref, text_ref, result_ref, state_ref):
+    text = text_ref[0]
+    text_rows = text.shape[0]
+    keys_values = jnp.concatenate([prefix_ref[0], text], axis=0)
+    first = prefix_ref.shape[1]
+    for head in range(keys_values.shape[1] // (2 * HD)):
+        at = 2 * head * HD
+        scores = score(stack_heads(query_ref[0], head), keys_values[:, at : at + HD])
         row = lax.broadcasted_iota(jnp.int32, scores.shape, 0) % text_rows
-        column = lax.broadcasted_iota(jnp.int32, scores.shape, 1)
-        text_column = column - (scores.shape[1] - text_rows)
-        allowed = (text_column <= row) & (seen_ref[0] > 0)
-        scores = jnp.where(allowed, scores, -1e30)
-        best = jnp.max(scores, axis=1, keepdims=True)
-        weights = jnp.exp(scores - best)
-        total = jnp.sum(weights, axis=1, keepdims=True)
-        result = jnp.dot(weights.astype(jnp.bfloat16), values, preferred_element_type=jnp.float32)
-        result = (result / total).astype(jnp.bfloat16)
-        for a in range(GROUP):
-            out_ref[0, :, (head * GROUP + a) * HD : (head * GROUP + a + 1) * HD] = result[
-                a * text_rows : (a + 1) * text_rows
-            ]
-
-
-def attend(place, queries, prefixes, text_kv, pages, picks, seen, all_rows):
+        column = lax.broadcasted_iota(jnp.int32, scores.shape, 1) - first
+        scores = jnp.where(column <= row, scores, -1e30)
+        best, total, result = weigh(scores, keys_values[:, at + HD : at + 2 * HD])
+        result_ref[0, head] = result
+        lane = lax.broadcasted_iota(jnp.int32, result.shape, 1)
+        state_ref[0, head] = jnp.where(lane < HD // 2, best, total)
+
+
+def attend_text(place, queries, prefixes, text_kv):
     docs, rows, width = queries.shape
     kv_width = text_kv.shape[2]
-    vision_rows = all_rows.shape[0]
-    keys = seen.shape[2]
+    shape = (docs, kv_width // (2 * HD), GROUP * rows, HD)
+    out = pl.BlockSpec((1,) + shape[1:], lambda d, place: (d, 0, 0, 0))
     return pl.pallas_call(
-        attend_kernel,
+        text_kernel,
         grid_spec=pltpu.PrefetchScalarGridSpec(
             num_scalar_prefetch=1,
             grid=(docs,),
@@ -319,27 +336,77 @@
                 pl.BlockSpec((1, rows, width), lambda d, place: (d, 0, 0)),
                 pl.BlockSpec((1,) + prefixes.shape[1:], lambda d, place: (place[d], 0, 0)),
                 pl.BlockSpec((1, rows, kv_width), lambda d, place: (d, 0, 0)),
-                pl.BlockSpec(pages.shape, lambda d, place: (0, 0)),
-                pl.BlockSpec((1,) + picks.shape[1:], lambda d, place: (d, 0, 0)),
-                pl.BlockSpec((1, 1, keys), lambda d, place: (d, 0, 0)),
-                pl.BlockSpec(all_rows.shape, lambda d, place: (0, 0)),
             ],
-            out_specs=[
-                pl.BlockSpec((1, rows, width), lambda d, place: (d, 0, 0)),
-                pl.BlockSpec((vision_rows, kv_width), lambda d, place: (0, 0)),
-            ],
+            out_specs=[out, out],
         ),
+        out_shape=[jax.ShapeDtypeStruct(shape, jnp.float32)] * 2,
+        compiler_params=pltpu.CompilerParams(vmem_limit_bytes=VMEM),
+        cost_estimate=pl.CostEstimate(flops=0, bytes_accessed=width, transcendentals=0),
+    )(place, queries, prefixes, text_kv)
+
+
+def vision_kernel(
+    query_ref, pages_ref, pick_ref, seen_ref, all_ref, result_ref, state_ref, out_ref, vision_ref
+):
+    pages = pages_ref[...]
+    count = pages.shape[0]
+
+    def pick(index):
+        one_hot = lax.broadcasted_iota(jnp.int32, (index.shape[0], count), 1) == index
+        one_hot = jnp.where(one_hot, 1.0, 0.0).astype(jnp.bfloat16)
+        return jnp.dot(one_hot, pages, preferred_element_type=jnp.float32).astype(jnp.bfloat16)
+
+    @pl.when(pl.program_id(0) == 0)
+    def _():
+        vision_ref[...] = pick(all_ref[...])
+
+    window = pick(pick_ref[0])
+    rows = out_ref.shape[1]
+    for head in range(window.shape[1] // (2 * HD)):
+        at = 2 * head * HD
+        scores = score(stack_heads(query_ref[0], head), window[:, at : at + HD])
+        scores = jnp.where(seen_ref[0] > 0, scores, -1e30)
+        best, total, result = weigh(scores, window[:, at + HD : at + 2 * HD])
+        state = state_ref[0, head]
+        other_best, other_total = state[:, :1], state[:, HD // 2 : HD // 2 + 1]
+        top = jnp.maximum(best, other_best)
+        mine, other = jnp.exp(best - top), jnp.exp(other_best - top)
+        scale = 1.0 / (total * mine + other_total * other)
+        result = result * (mine * scale) + result_ref[0, head] * (other * scale)
+        result = result.astype(jnp.bfloat16)
+        for a in range(GROUP):
+            out_ref[0, :, (head * GROUP + a) * HD : (head * GROUP + a + 1) * HD] = result[
+                a * rows : (a + 1) * rows
+            ]
+
+
+def attend_vision(queries, pages, picks, seen, all_rows, result, state):
+    docs, rows, width = queries.shape
+    vision_rows = all_rows.shape[0]
+    partial = pl.BlockSpec((1,) + result.shape[1:], lambda d: (d, 0, 0, 0))
+    return pl.pallas_call(
+        vision_kernel,
+        grid=(docs,),
+        in_specs=[
+            pl.BlockSpec((1, rows, width), lambda d: (d, 0, 0)),
+            pl.BlockSpec(pages.shape, lambda d: (0, 0)),
+            pl.BlockSpec((1,) + picks.shape[1:], lambda d: (d, 0, 0)),
+            pl.BlockSpec((1,) + seen.shape[1:], lambda d: (d, 0, 0)),
+            pl.BlockSpec(all_rows.shape, lambda d: (0, 0)),
+            partial,
+            partial,
+        ],
+        out_specs=[
+            pl.BlockSpec((1, rows, width), lambda d: (d, 0, 0)),
+            pl.BlockSpec((vision_rows, pages.shape[1]), lambda d: (0, 0)),
+        ],
         out_shape=[
             jax.ShapeDtypeStruct(queries.shape, jnp.bfloat16),
-            jax.ShapeDtypeStruct((vision_rows, kv_width), jnp.bfloat16),
+            jax.ShapeDtypeStruct((vision_rows, pages.shape[1]), jnp.bfloat16),
         ],
         compiler_params=pltpu.CompilerParams(vmem_limit_bytes=VMEM),
-        cost_estimate=pl.CostEstimate(
-            flops=4 * docs * rows * width * keys,
-            bytes_accessed=8 * docs * rows * width,
-            transcendentals=docs * rows * keys * width // HD,
-        ),
-    )(place, queries, prefixes, text_kv, pages, picks, seen, all_rows)
+        cost_estimate=pl.CostEstimate(flops=0, bytes_accessed=width, transcendentals=0),
+    )(queries, pages, picks, seen, all_rows, result, state)
 
 
 def shards(
@@ -362,7 +429,7 @@
     capacity = max(2, 2 * page_count // seq_count)
     sources = page_src[:, 0]
 
-    kv, squares, small = merge_tiles(
+    complete, small = merge_tiles(
         panels, w_merge, ln_gain, w_kv, pack_small(prefix_cache, sources, page_tile)
     )
     width = seq_count // lax.axis_size("tp")
@@ -399,25 +466,17 @@
     page = jnp.minimum(starts[:, None] + step[None, :], page_count - 1)
     doc_rows = arrival[page][:, :, None] * panel_rows + within[None, None, :]
     doc_rows = jnp.where(inside[:, :, None], doc_rows, -1)
-    doc_count, query_rows, _ = queries.shape
+    doc_count = queries.shape[0]
     picks = doc_rows.reshape(doc_count, -1, 1)
-    seen = jnp.concatenate(
-        [
-            jnp.ones((doc_count, prefixes.shape[1]), jnp.int32),
-            (doc_rows >= 0).reshape(doc_count, -1).astype(jnp.int32),
-            jnp.ones((doc_count, query_rows), jnp.int32),
-        ],
-        axis=1,
-    )[:, None, :]
-
+    seen = (doc_rows >= 0).reshape(doc_count, 1, -1).astype(jnp.int32)
+    early = attend_text(place_of(prefix_id), queries, prefixes, text_kv)
+    kv, squares, (early, chooser) = complete((early, chooser))
     kv, squares = scatter_heads(kv, squares)
     row_scale = lax.rsqrt(squares / D + 1e-06)
     tile_kv = (kv * row_scale[:, None]).astype(jnp.bfloat16)
     outgoing = jnp.dot(chooser, tile_kv, preferred_element_type=jnp.float32).astype(jnp.bfloat16)
     pages = lax.all_to_all(outgoing, "seq", split_axis=0, concat_axis=0, tiled=True)
-    attended, vision_kv = attend(
-        place_of(prefix_id), queries, prefixes, text_kv, pages, picks, seen, all_rows
-    )
+    attended, vision_kv = attend_vision(queries, pages, picks, seen, all_rows, *early)
     return (attended, vision_kv)
 
 

time: 183 us -> 201 us (1.098)
  Pallas kernels: 20.4 us -> 30.8 us
  local copies, waits for them, and re-layouts: 13.9 us -> 18.6 us
  starting transfers between devices: 55.6 us -> 60 us
  waiting for transfers between devices: 75.1 us -> 71 us
  matrix products: 4.52 us -> 7.1 us
    pallas_call x1 -> x2, Pallas kernels: 5.51 us -> 15.1 us  [the longest x1 11.9 us: attend_vision(): pl.pallas_call(vision_kernel, grid=(docs,), in_specs=[pl.BlockSpec((1, ro...]
    ppermute x11, starting transfers between devices: 14.5 us -> 21.5 us  [flip(): return lax.ppermute(value, axis, [(i, i ^ bit) for i in range(count)])]
    all_to_all x1, starting transfers between devices: 13.9 us -> 7.92 us  [shards(): lax.all_to_all(outgoing, 'seq', split_axis=0, concat_axis=0, tiled=True)]
    ppermute x2, waiting for transfers between devices: 5.47 us -> 0.41 us  [merge_tiles(): others.append(lax.ppermute(own, 'seq', pairs))]
    unnamed x68, local copies, waits for them, and re-layouts: 2.49 us -> 6.94 us
    dot_general x3 -> x4, matrix products: 3.51 us -> 6.1 us  [finish(): jnp.dot(gained, w_kv[at], preferred_element_type=jnp.float32)]
    ppermute x9 -> x11, starting transfers between devices: 20 us -> 22.5 us  [send_direct(): lax.ppermute(ride(parts[k], small), 'seq', along([(a, a ^ k) for a in ran...]
    pallas_call x3 -> x4, Pallas kernels: 11.6 us -> 13.2 us  [partial_products(): pl.pallas_call(functools.partial(partial_kernel, halves), grid=(count //...]
  transfers between devices with their start and end apart: 25 -> 27, of which waited for: 11 -> 15; matrix products, arithmetic and copies ran while one was open for 13% -> 12% of each run, Pallas kernels for 8% -> 9%
where the time goes in v4:
time: 201 us; the launch traced here: 200 us
  waiting for transfers between devices  71 us (35%)
  starting transfers between devices  60 us (30%)
  Pallas kernels  30.8 us (15%)
  local copies, waits for them, and re-layouts  18.6 us (9%)
  other arithmetic  11.2 us (6%)
  matrix products  7.1 us (4%)
    ppermute x11, waiting for transfers between devices, send_direct(): lax.ppermute(ride(parts[k], small), 'seq', along([(a, a ^ k) for a in ran...  45.1 us
    ppermute x11, starting transfers between devices, send_direct(): lax.ppermute(ride(parts[k], small), 'seq', along([(a, a ^ k) for a in ran...  22.5 us
    ppermute x11, starting transfers between devices, flip(): return lax.ppermute(value, axis, [(i, i ^ bit) for i in range(count)])  21.5 us
    ppermute x11, waiting for transfers between devices, flip(): return lax.ppermute(value, axis, [(i, i ^ bit) for i in range(count)])  19 us
    pallas_call x4, Pallas kernels, partial_products(): pl.pallas_call(functools.partial(partial_kernel, halves), grid=(count //...  13.2 us
    pallas_call x1, Pallas kernels, attend_vision(): pl.pallas_call(vision_kernel, grid=(docs,), in_specs=[pl.BlockSpec((1, ro...  11.9 us
    all_to_all x1, starting transfers between devices, shards(): lax.all_to_all(outgoing, 'seq', split_axis=0, concat_axis=0, tiled=True)  7.92 us
    unnamed x68, local copies, waits for them, and re-layouts  6.94 us
  transfers between devices with their start and end apart: 27, of which 15 were waited for; matrix products, arithmetic and copies ran while one was open for 12% of the time, Pallas kernels for 9%

profile of v4, /device:TPU:0, one launch (start us, length us, event | category | flops | bytes accessed | tf_op | source)
XLA Modules:
  0.0 200.0 jit_solution(13264693991478838122)
XLA Ops:
  0.7 1.1 slice_bitcast_fusion
  1.8 3.0 %collective-permute-start.1 = (bf16[128,1280]{1,0:T(8,128)(2,1)S(1)}, bf16[128,1280]{1,0:T(8,128)(2,1)}, u32[]{:S(2)}, u32[]{:S(2)}) collective-permute-start(bf16[128,1280]{1,0:T(8,128)(2,1)S(1)} %get-tuple-element.94), channel_id=1, source_target_pairs={{0,2},{1,3},{2,0},{3,1},{4,6},{5,7},{6,4},{7,5},{8,10},{9,11},{10,... | collective-permute-start | bytes 983048 | tf_op jit(solution)/shard_map/ppermute | solution.py:23
  4.9 0.8 collective-permute-start
  5.7 2.5 %slice.78 = bf16[640,1024]{1,0:T(8,128)(2,1)} slice(bf16[640,2048]{1,0:T(8,128)(2,1)} %refs_2_.3), slice={[0:640], [0:1024]} | slice | bytes 2621440 | tf_op jit(solution)/shard_map/slice | solution.py:164
  8.2 1.5 collective-permute-start.6
  10.4 8.4 %collective-permute-done.1 = bf16[128,1280]{1,0:T(8,128)(2,1)} collective-permute-done((bf16[128,1280]{1,0:T(8,128)(2,1)S(1)}, bf16[128,1280]{1,0:T(8,128)(2,1)}, u32[]{:S(2)}, u32[]{:S(2)}) %collective-permute-start.1) | collective-permute-done | bytes 327712 | tf_op jit(solution)/shard_map/ppermute | solution.py:23
  18.9 2.6 %collective-permute-start.2 = (bf16[128,1280]{1,0:T(8,128)(2,1)S(1)}, bf16[128,1280]{1,0:T(8,128)(2,1)}, u32[]{:S(2)}, u32[]{:S(2)}) collective-permute-start(bf16[128,1280]{1,0:T(8,128)(2,1)S(1)} %collective-permute-done.refs_0_), channel_id=1, source_target_pairs={{0,2},{1,3},{2,0},{3,1},{4,6},{5,7},{6,4},{7,5},{8,10},{9,11},{10,... | collective-permute-start | bytes 983048 | tf_op jit(solution)/shard_map/ppermute | solution.py:23
  21.5 2.4 %collective-permute-start.3 = (bf16[128,1280]{1,0:T(8,128)(2,1)S(1)}, bf16[128,1280]{1,0:T(8,128)(2,1)}, u32[]{:S(2)}, u32[]{:S(2)}) collective-permute-start(bf16[128,1280]{1,0:T(8,128)(2,1)S(1)} %collective-permute-done.refs_0_), channel_id=1, source_target_pairs={{0,1},{1,0},{2,3},{3,2},{4,5},{5,4},{6,7},{7,6},{8,9},{9,8},{10,11... | collective-permute-start | bytes 983048 | tf_op jit(solution)/shard_map/ppermute | solution.py:23
  23.9 1.2 pad_maximum_fusion
  25.1 1.5 collective-permute-start.10
  26.6 4.2 %collective-permute-start.5 = (bf16[128,1280]{1,0:T(8,128)(2,1)}, bf16[128,1280]{1,0:T(8,128)(2,1)S(1)}, u32[]{:S(2)}, u32[]{:S(2)}) collective-permute-start(bf16[128,1280]{1,0:T(8,128)(2,1)} %collective-permute-done.1), channel_id=1, source_target_pairs={{2,0},{3,10},{0,16},{1,26},{6,4},{7,14},{4,20},{5,30},{10,2},{11,8... | collective-permute-start | bytes 983048 | tf_op jit(solution)/shard_map/ppermute | solution.py:37
  30.8 3.5 %collective-permute-start.4 = (bf16[128,1280]{1,0:T(8,128)(2,1)}, bf16[128,1280]{1,0:T(8,128)(2,1)}, u32[]{:S(2)}, u32[]{:S(2)}) collective-permute-start(bf16[128,1280]{1,0:T(8,128)(2,1)} %collective-permute-done.2.refs_1_), channel_id=1, source_target_pairs={{0,1},{1,0},{2,3},{3,2},{4,5},{5,4},{6,7},{7,6},{8,9},{9,8},{10,11... | collective-permute-start | bytes 983048 | tf_op jit(solution)/shard_map/ppermute | solution.py:23
  34.4 0.8 gather_fusion.2
  35.9 1.8 shard_map.122.refs_0_
  38.2 2.9 %shard_map.123 = (bf16[128,1024]{1,0:T(8,128)(2,1)S(1)}, bf16[128,1024]{1,0:T(8,128)(2,1)S(1)}, bf16[128,1024]{1,0:T(8,128)(2,1)S(1)}, bf16[128,1024]{1,0:T(8,128)(2,1)S(1)}) custom-call(bf16[512,1280]{1,0:T(8,128)(2,1)S(1)} %shard_map.122.refs_0_, bf16[640,2048]{1,0:T(8,128)(2,1)S(1)} %copy-done, bf16[640,1024]{1,0:T(8,128)(2,1)} %collective-permute-done.6.refs_2_), custom_call_target="tpu_custom_call" | custom-call | bytes 2048 | tf_op jit(solution)/shard_map/pallas_call | solution.py:106
  41.1 7.3 %collective-permute-start.7 = (bf16[128,1280]{1,0:T(8,128)(2,1)S(1)}, bf16[128,1280]{1,0:T(8,128)(2,1)S(1)}, u32[]{:S(2)}, u32[]{:S(2)}) collective-permute-start(bf16[128,1280]{1,0:T(8,128)(2,1)S(1)} %collective-permute-done.5.refs_0_), channel_id=1, source_target_pairs={{0,2},{1,3},{2,0},{3,1},{4,6},{5,7},{6,4},{7,5},{8,10},{9,11},{10,... | collective-permute-start | bytes 983048 | tf_op jit(solution)/shard_map/ppermute | solution.py:23
  48.5 2.9 %collective-permute-start.12 = (bf16[128,1024]{1,0:T(8,128)(2,1)S(1)}, bf16[128,1024]{1,0:T(8,128)(2,1)S(1)}, u32[]{:S(2)}, u32[]{:S(2)}) collective-permute-start(bf16[128,1024]{1,0:T(8,128)(2,1)S(1)} %get-tuple-element.51), channel_id=1, source_target_pairs={{0,24},{4,28},{8,16},{12,20},{16,8},{20,12},{24,0},{28,4},{1,25},{... | collective-permute-start | bytes 786440 | tf_op jit(solution)/shard_map/ppermute | solution.py:129
  51.4 4.0 %collective-permute-done.7.refs_1_ = bf16[128,1280]{1,0:T(8,128)(2,1)S(1)} collective-permute-done((bf16[128,1280]{1,0:T(8,128)(2,1)S(1)}, bf16[128,1280]{1,0:T(8,128)(2,1)S(1)}, u32[]{:S(2)}, u32[]{:S(2)}) %collective-permute-start.7) | collective-permute-done | bytes 327712 | tf_op jit(solution)/shard_map/ppermute | solution.py:23
  55.4 1.5 collective-permute-done.9.refs_3_
  57.6 4.0 %shard_map.125 = (bf16[128,1024]{1,0:T(8,128)(2,1)S(1)}, bf16[128,1024]{1,0:T(8,128)(2,1)S(1)}, bf16[128,1024]{1,0:T(8,128)(2,1)}, bf16[128,1024]{1,0:T(8,128)(2,1)}) custom-call(bf16[512,1280]{1,0:T(8,128)(2,1)S(1)} %shard_map.124.refs_0_.refs_1_, bf16[640,2048]{1,0:T(8,128)(2,1)S(1)} %copy-done, bf16[640,1024]{1,0:T(8,128)(2,1)} %collective-permute-done.6.refs_2_), custom_call_target="tpu_custom_call" | custom-call | bytes 2048 | tf_op jit(solution)/shard_map/pallas_call | solution.py:106
  61.6 7.3 %collective-permute-done.11 = bf16[128,1024]{1,0:T(8,128)(2,1)S(1)} collective-permute-done((bf16[128,1024]{1,0:T(8,128)(2,1)S(1)}, bf16[128,1024]{1,0:T(8,128)(2,1)S(1)}, u32[]{:S(2)}, u32[]{:S(2)}) %collective-permute-start.11) | collective-permute-done | bytes 262176 | tf_op jit(solution)/shard_map/ppermute | solution.py:129
  68.9 0.9 pad_maximum_fusion.1
  69.8 6.1 %collective-permute-start.21 = (bf16[256,1024]{1,0:T(8,128)(2,1)}, bf16[256,1024]{1,0:T(8,128)(2,1)}, u32[]{:S(2)}, u32[]{:S(2)}) collective-permute-start(bf16[256,1024]{1,0:T(8,128)(2,1)} %pad_maximum_fusion.1), channel_id=1, source_target_pairs={{0,8},{4,12},{8,0},{12,4},{16,24},{20,28},{24,16},{28,20},{1,9},{5... | collective-permute-start | bytes 1572872 | tf_op jit(solution)/shard_map/ppermute | solution.py:129
  76.7 0.8 broadcast_in_dim.19
  77.7 0.7 add.351
  78.4 0.8 add.360
  79.9 1.1 collective-permute-start.13
  81.4 0.8 slice_bitcast_fusion.5
  83.5 1.3 copy-done.2
  84.8 1.3 copy-done.4
  86.1 2.6 %shard_map.127 = (bf16[256,512]{1,0:T(8,128)(2,1)S(1)}, bf16[256,512]{1,0:T(8,128)(2,1)S(1)}, bf16[256,512]{1,0:T(8,128)(2,1)S(1)}, bf16[256,512]{1,0:T(8,128)(2,1)S(1)}) custom-call(bf16[512,1280]{1,0:T(8,128)(2,1)S(1)} %copy-done.2, bf16[512,1280]{1,0:T(8,128)(2,1)S(1)} %copy-done.4, bf16[640,2048]{1,0:T(8,128)(2,1)S(1)} %copy-done, ...), custom_call_target="tpu_custom_call" | custom-call | bytes 1024 | tf_op jit(solution)/shard_map/pallas_call | solution.py:106
  88.8 3.6 %shard_map.126 = (bf16[256,512]{1,0:T(8,128)(2,1)S(1)}, bf16[256,512]{1,0:T(8,128)(2,1)}, bf16[256,512]{1,0:T(8,128)(2,1)}, bf16[256,512]{1,0:T(8,128)(2,1)}) custom-call(bf16[512,1280]{1,0:T(8,128)(2,1)S(1)} %copy-done.2, bf16[512,1280]{1,0:T(8,128)(2,1)S(1)} %copy-done.4, bf16[640,2048]{1,0:T(8,128)(2,1)S(1)} %copy-done, ...), custom_call_target="tpu_custom_call" | custom-call | bytes 1024 | tf_op jit(solution)/shard_map/pallas_call | solution.py:106
  92.4 12.4 %collective-permute-done.14 = bf16[128,1024]{1,0:T(8,128)(2,1)} collective-permute-done((bf16[128,1024]{1,0:T(8,128)(2,1)}, bf16[128,1024]{1,0:T(8,128)(2,1)}, u32[]{:S(2)}, u32[]{:S(2)}) %collective-permute-start.14) | collective-permute-done | bytes 262176 | tf_op jit(solution)/shard_map/ppermute | solution.py:129
  105.0 1.3 collective-permute-start.20
  106.3 2.2 %collective-permute-start.15 = (bf16[304,512]{1,0:T(8,128)(2,1)S(1)}, bf16[304,512]{1,0:T(8,128)(2,1)S(1)}, u32[]{:S(2)}, u32[]{:S(2)}) collective-permute-start(bf16[304,512]{1,0:T(8,128)(2,1)S(1)} %get-tuple-element.102), channel_id=1, source_target_pairs={{0,8},{4,12},{8,0},{12,4},{16,24},{20,28},{24,16},{28,20},{1,9},{5... | collective-permute-start | bytes 933896 | tf_op jit(solution)/shard_map/ppermute | solution.py:129
  108.5 2.2 %fusion.7 = (f32[128]{0:T(128)}, bf16[128,1024]{1,0:T(8,128)(2,1)S(1)}, f32[128]{0:T(128)}, bf16[128,1024]{1,0:T(8,128)(2,1)S(1)}) fusion(bf16[256,1024]{1,0:T(8,128)(2,1)} %collective-permute-done.21, bf16[128,1024]{1,0:T(8,128)(2,1)S(1)} %copy-done.20, bf16[128,1024]{1,0:T(8,128)(2,1)S(1)} %copy-done.18, bf16[128,1024]{1,0:T(8,128)(2,1)S(1)} %get-tuple-element.43, ...), kind=kLoop, calls=%fused_computation.22 | loop fusion | flops 2883328 | bytes 2622464 | tf_op jit(solution)/shard_map/reduce_sum | solution.py:192
  110.7 1.2 fusion.2
  111.9 1.2 fusion
  113.2 13.4 %collective-permute-done.19 = bf16[304,512]{1,0:T(8,128)(2,1)S(1)} collective-permute-done((bf16[304,512]{1,0:T(8,128)(2,1)S(1)}, bf16[304,512]{1,0:T(8,128)(2,1)S(1)}, u32[]{:S(2)}, u32[]{:S(2)}) %collective-permute-start.19) | collective-permute-done | bytes 311328 | tf_op jit(solution)/shard_map/ppermute | solution.py:129
  126.6 1.4 collective-permute-done.15
  128.0 0.7 copy-done.16
  128.9 0.7 gather_fusion
  129.6 0.7 gather_fusion.1
  131.1 5.8 %collective-permute-start.16 = (bf16[256,512]{1,0:T(8,128)(2,1)}, bf16[256,512]{1,0:T(8,128)(2,1)S(1)}, u32[]{:S(2)}, u32[]{:S(2)}) collective-permute-start(bf16[256,512]{1,0:T(8,128)(2,1)} %get-tuple-element.65), channel_id=1, source_target_pairs={{0,8},{4,12},{8,0},{12,4},{16,24},{20,28},{24,16},{28,20},{1,9},{5... | collective-permute-start | bytes 786440 | tf_op jit(solution)/shard_map/ppermute | solution.py:129
  136.9 1.1 collective-permute-start.17
  138.0 1.5 collective-permute-start.18
  139.5 0.9 copy-done.9
  140.4 3.2 %shard_map.128 = (f32[4,1,1024,128]{3,2,1,0:T(8,128)S(1)}, f32[4,1,1024,128]{3,2,1,0:T(8,128)S(1)}) custom-call(s32[4]{0:T(128)S(1)} %fusion.37.place_ref, bf16[4,128,1024]{2,1,0:T(8,128)(2,1)S(1)} %copy-done.5, bf16[8,32,256]{2,1,0:T(8,128)(2,1)S(1)} %slice.107.prefix_ref, bf16[4,128,256]{2,1,0:T(8,128)(2,1)S(1)} %copy-done.9), custom_call_target="tpu_custom_call" | custom-call | bytes 1024 | tf_op jit(solution)/shard_map/pallas_call | solution.py:330
  143.6 2.2 %fusion.11 = (f32[256]{0:T(256)S(1)}, bf16[256,512]{1,0:T(8,128)(2,1)S(1)}) fusion(bf16[304,512]{1,0:T(8,128)(2,1)} %copy-done.15, bf16[304,512]{1,0:T(8,128)(2,1)} %copy-done.14, bf16[304,512]{1,0:T(8,128)(2,1)} %copy-done.16, bf16[256,512]{1,0:T(8,128)(2,1)} %copy-done.12), kind=kLoop, calls=%fused_computation.26 | loop fusion | flops 1441536 | bytes 1311744 | tf_op jit(solution)/shard_map/reduce_sum | solution.py:192
  145.8 2.0 convolution_add_fusion.1
  147.8 0.7 collective-permute-done.16
  148.6 9.9 %collective-permute-done.17 = bf16[256,512]{1,0:T(8,128)(2,1)S(1)} collective-permute-done((bf16[256,512]{1,0:T(8,128)(2,1)}, bf16[256,512]{1,0:T(8,128)(2,1)S(1)}, u32[]{:S(2)}, u32[]{:S(2)}) %collective-permute-start.17) | collective-permute-done | bytes 262176 | tf_op jit(solution)/shard_map/ppermute | solution.py:129
  158.7 1.7 convolution_add_fusion
  161.2 0.9 collective-permute-done.24
  162.9 1.4 collective-permute-start.23
  164.3 1.4 collective-permute-done.25
  165.7 2.6 %collective-permute-done.23 = bf16[1,256,256]{2,1,0:T(8,128)(2,1)S(1)} collective-permute-done((bf16[1,256,256]{2,1,0:T(8,128)(2,1)S(1)}, bf16[1,256,256]{2,1,0:T(8,128)(2,1)S(1)}, u32[]{:S(2)}, u32[]{:S(2)}) %collective-permute-start.23) | collective-permute-done | bytes 131104 | tf_op jit(solution)/shard_map/ppermute | solution.py:23
  168.3 1.0 convolution_convert_fusion
  169.3 7.9 %all-to-all-start = ((bf16[8,64,256]{2,1,0:T(8,128)(2,1)}), bf16[8,64,256]{2,1,0:T(8,128)(2,1)S(1)}, u32[]{:S(2)}, u32[]{:S(2)}) async-start(bf16[8,64,256]{2,1,0:T(8,128)(2,1)} %bitcast.56), calls=%async_computation | async-start | bytes 524288 | tf_op jit(solution)/shard_map/all_to_all | solution.py:478
  177.2 1.8 add_select_fusion.pick_ref
  179.0 6.5 %all-to-all-done = bf16[8,64,256]{2,1,0:T(8,128)(2,1)S(1)} async-done(((bf16[8,64,256]{2,1,0:T(8,128)(2,1)}), bf16[8,64,256]{2,1,0:T(8,128)(2,1)S(1)}, u32[]{:S(2)}, u32[]{:S(2)}) %all-to-all-start) | async-done | bytes 262176 | tf_op jit(solution)/shard_map/all_to_all | solution.py:478
  185.5 1.6 copy-done.7
  187.1 0.9 copy-done.8
  188.0 11.9 %shard_map.129 = (bf16[4,128,1024]{2,1,0:T(8,128)(2,1)}, bf16[256,256]{1,0:T(8,128)(2,1)}) custom-call(bf16[4,128,1024]{2,1,0:T(8,128)(2,1)S(1)} %copy-done.5, bf16[512,256]{1,0:T(8,128)(2,1)S(1)} %bitcast.55, s32[4,128,1]{2,1,0:T(8,128)S(1)} %copy-done.8, s32[4,1,128]{2,1,0:T(1,128)S(1)} %compare_convert_fusion.seen_ref, s32[256,1]{1,0:T(8,128)S(1)} %add.361.all_ref, ...), custom_call_target="tpu_custom_call" | custom-call | bytes 1024 | tf_op jit(solution)/shard_map/pallas_call | solution.py:387
  (147 shorter events, 9.0 us)
Async XLA Ops:
  0.6 9.0 %copy-start.31 = (s32[32,1]{0,1:T(1,128)S(1)}, s32[32,1]{0,1:T(1,128)}, u32[]{:S(2)}) copy-start(s32[32,1]{0,1:T(1,128)} %param.15) | copy-start | bytes 388
  0.6 9.2 %copy-start.32 = (s32[32]{0:T(128)S(1)}, s32[32]{0:T(128)}, u32[]{:S(2)}) copy-start(s32[32]{0:T(128)} %param.16) | copy-start | bytes 388
  0.7 9.2 %copy-start.33 = (s32[1,4]{1,0:T(1,128)S(1)}, s32[1,4]{1,0:T(1,128)}, u32[]{:S(2)}) copy-start(s32[1,4]{1,0:T(1,128)} %param.17) | copy-start | bytes 52
  0.7 9.5 %copy-start.23 = (bf16[1,32,256]{2,1,0:T(8,128)(2,1)S(1)}, bf16[1,32,256]{2,1,0:T(8,128)(2,1)}, u32[]{:S(2)}) copy-start(bf16[1,32,256]{2,1,0:T(8,128)(2,1)} %param.19) | copy-start | bytes 49156
  0.7 9.7 %copy-start.30 = (s32[4]{0:T(128)S(1)}, s32[4]{0:T(128)}, u32[]{:S(2)}) copy-start(s32[4]{0:T(128)} %param.18) | copy-start | bytes 52
  1.8 17.0 %collective-permute-start.1 = (bf16[128,1280]{1,0:T(8,128)(2,1)S(1)}, bf16[128,1280]{1,0:T(8,128)(2,1)}, u32[]{:S(2)}, u32[]{:S(2)}) collective-permute-start(bf16[128,1280]{1,0:T(8,128)(2,1)S(1)} %get-tuple-element.94), channel_id=1, source_target_pairs={{0,2},{1,3},{2,0},{3,1},{4,6},{5,7},{6,4},{7,5},{8,10},{9,11},{10,... | collective-permute-start | bytes 983048 | tf_op jit(solution)/shard_map/ppermute | solution.py:23
  4.9 19.1 %slice-start = ((bf16[640,2048]{1,0:T(8,128)(2,1)}), bf16[640,1024]{1,0:T(8,128)(2,1)S(1)}, s32[]{:S(2)}) async-start(bf16[640,2048]{1,0:T(8,128)(2,1)} %refs_2_.3), calls=%async_computation.1 | async-start | bytes 2621440 | tf_op jit(solution)/shard_map/slice | solution.py:167
  4.9 14.0 %collective-permute-start = (bf16[128,1280]{1,0:T(8,128)(2,1)S(1)}, bf16[128,1280]{1,0:T(8,128)(2,1)S(1)}, u32[]{:S(2)}, u32[]{:S(2)}) collective-permute-start(bf16[128,1280]{1,0:T(8,128)(2,1)S(1)} %get-tuple-element.95), channel_id=1, source_target_pairs={{0,0},{1,10},{2,16},{3,26},{4,4},{5,14},{6,20},{7,30},{8,2},{9,8},... | collective-permute-start | bytes 983048 | tf_op jit(solution)/shard_map/ppermute | solution.py:37
  8.2 30.0 %collective-permute-start.6 = (bf16[640,1024]{1,0:T(8,128)(2,1)}, bf16[640,1024]{1,0:T(8,128)(2,1)}, u32[]{:S(2)}, u32[]{:S(2)}) collective-permute-start(bf16[640,1024]{1,0:T(8,128)(2,1)} %slice.78), channel_id=1, source_target_pairs={{4,0},{0,4},{12,8},{8,12},{20,16},{16,20},{28,24},{24,28},{5,1},{1... | collective-permute-start | bytes 3932168 | tf_op jit(solution)/shard_map/ppermute | solution.py:175
  18.9 12.0 %collective-permute-start.2 = (bf16[128,1280]{1,0:T(8,128)(2,1)S(1)}, bf16[128,1280]{1,0:T(8,128)(2,1)}, u32[]{:S(2)}, u32[]{:S(2)}) collective-permute-start(bf16[128,1280]{1,0:T(8,128)(2,1)S(1)} %collective-permute-done.refs_0_), channel_id=1, source_target_pairs={{0,2},{1,3},{2,0},{3,1},{4,6},{5,7},{6,4},{7,5},{8,10},{9,11},{10,... | collective-permute-start | bytes 983048 | tf_op jit(solution)/shard_map/ppermute | solution.py:23
  21.5 14.2 %collective-permute-start.3 = (bf16[128,1280]{1,0:T(8,128)(2,1)S(1)}, bf16[128,1280]{1,0:T(8,128)(2,1)}, u32[]{:S(2)}, u32[]{:S(2)}) collective-permute-start(bf16[128,1280]{1,0:T(8,128)(2,1)S(1)} %collective-permute-done.refs_0_), channel_id=1, source_target_pairs={{0,1},{1,0},{2,3},{3,2},{4,5},{5,4},{6,7},{7,6},{8,9},{9,8},{10,11... | collective-permute-start | bytes 983048 | tf_op jit(solution)/shard_map/ppermute | solution.py:23
  23.9 11.2 %copy-start.26 = (bf16[2048]{0:T(1024)(128)(2,1)S(1)}, bf16[2048]{0:T(1024)(128)(2,1)}, u32[]{:S(2)}) copy-start(bf16[2048]{0:T(1024)(128)(2,1)} %param.13) | copy-start | bytes 12292
  25.1 56.3 %collective-permute-start.10 = (bf16[652,1024]{1,0:T(8,128)(2,1)}, bf16[652,1024]{1,0:T(8,128)(2,1)}, u32[]{:S(2)}, u32[]{:S(2)}) collective-permute-start(bf16[652,1024]{1,0:T(8,128)(2,1)} %pad_maximum_fusion), channel_id=1, source_target_pairs={{4,0},{0,4},{12,8},{8,12},{20,16},{16,20},{28,24},{24,28},{5,1},{1... | collective-permute-start | bytes 4005896 | tf_op jit(solution)/shard_map/ppermute | solution.py:175
  26.6 14.5 %collective-permute-start.5 = (bf16[128,1280]{1,0:T(8,128)(2,1)}, bf16[128,1280]{1,0:T(8,128)(2,1)S(1)}, u32[]{:S(2)}, u32[]{:S(2)}) collective-permute-start(bf16[128,1280]{1,0:T(8,128)(2,1)} %collective-permute-done.1), channel_id=1, source_target_pairs={{2,0},{3,10},{0,16},{1,26},{6,4},{7,14},{4,20},{5,30},{10,2},{11,8... | collective-permute-start | bytes 983048 | tf_op jit(solution)/shard_map/ppermute | solution.py:37
  30.8 5.1 %collective-permute-start.4 = (bf16[128,1280]{1,0:T(8,128)(2,1)}, bf16[128,1280]{1,0:T(8,128)(2,1)}, u32[]{:S(2)}, u32[]{:S(2)}) collective-permute-start(bf16[128,1280]{1,0:T(8,128)(2,1)} %collective-permute-done.2.refs_1_), channel_id=1, source_target_pairs={{0,1},{1,0},{2,3},{3,2},{4,5},{5,4},{6,7},{7,6},{8,9},{9,8},{10,11... | collective-permute-start | bytes 983048 | tf_op jit(solution)/shard_map/ppermute | solution.py:23
  34.4 3.8 %copy-start = (bf16[640,2048]{1,0:T(8,128)(2,1)S(1)}, bf16[640,2048]{1,0:T(8,128)(2,1)}, u32[]{:S(2)}) copy-start(bf16[640,2048]{1,0:T(8,128)(2,1)} %refs_2_.3) | copy-start | bytes 7864324
  37.8 3.3 %copy-start.1 = (bf16[512,1280]{1,0:T(8,128)(2,1)}, bf16[512,1280]{1,0:T(8,128)(2,1)S(1)}, u32[]{:S(2)}) copy-start(bf16[512,1280]{1,0:T(8,128)(2,1)S(1)} %shard_map.122.refs_0_) | copy-start | bytes 3932164
  41.1 14.2 %collective-permute-start.7 = (bf16[128,1280]{1,0:T(8,128)(2,1)S(1)}, bf16[128,1280]{1,0:T(8,128)(2,1)S(1)}, u32[]{:S(2)}, u32[]{:S(2)}) collective-permute-start(bf16[128,1280]{1,0:T(8,128)(2,1)S(1)} %collective-permute-done.5.refs_0_), channel_id=1, source_target_pairs={{0,2},{1,3},{2,0},{3,1},{4,6},{5,7},{6,4},{7,5},{8,10},{9,11},{10,... | collective-permute-start | bytes 983048 | tf_op jit(solution)/shard_map/ppermute | solution.py:23
  48.4 7.0 %collective-permute-start.8 = (bf16[128,1280]{1,0:T(8,128)(2,1)S(1)}, bf16[128,1280]{1,0:T(8,128)(2,1)S(1)}, u32[]{:S(2)}, u32[]{:S(2)}) collective-permute-start(bf16[128,1280]{1,0:T(8,128)(2,1)S(1)} %collective-permute-done.5.refs_0_), channel_id=1, source_target_pairs={{0,1},{1,0},{2,3},{3,2},{4,5},{5,4},{6,7},{7,6},{8,9},{9,8},{10,11... | collective-permute-start | bytes 983048 | tf_op jit(solution)/shard_map/ppermute | solution.py:23
  48.4 20.5 %collective-permute-start.11 = (bf16[128,1024]{1,0:T(8,128)(2,1)S(1)}, bf16[128,1024]{1,0:T(8,128)(2,1)S(1)}, u32[]{:S(2)}, u32[]{:S(2)}) collective-permute-start(bf16[128,1024]{1,0:T(8,128)(2,1)S(1)} %get-tuple-element.50), channel_id=1, source_target_pairs={{0,16},{4,20},{8,24},{12,28},{16,0},{20,4},{24,8},{28,12},{1,17},{... | collective-permute-start | bytes 786440 | tf_op jit(solution)/shard_map/ppermute | solution.py:129
  48.5 20.4 %collective-permute-start.12 = (bf16[128,1024]{1,0:T(8,128)(2,1)S(1)}, bf16[128,1024]{1,0:T(8,128)(2,1)S(1)}, u32[]{:S(2)}, u32[]{:S(2)}) collective-permute-start(bf16[128,1024]{1,0:T(8,128)(2,1)S(1)} %get-tuple-element.51), channel_id=1, source_target_pairs={{0,24},{4,28},{8,16},{12,20},{16,8},{20,12},{24,0},{28,4},{1,25},{... | collective-permute-start | bytes 786440 | tf_op jit(solution)/shard_map/ppermute | solution.py:129
  55.3 1.6 collective-permute-start.9
  57.6 4.0 %copy-start.3 = (bf16[512,1280]{1,0:T(8,128)(2,1)}, bf16[512,1280]{1,0:T(8,128)(2,1)S(1)}, u32[]{:S(2)}) copy-start(bf16[512,1280]{1,0:T(8,128)(2,1)S(1)} %shard_map.124.refs_0_.refs_1_) | copy-start | bytes 3932164
  68.9 0.9 copy-start.17
  68.9 7.0 %copy-start.19 = (bf16[128,1024]{1,0:T(8,128)(2,1)}, bf16[128,1024]{1,0:T(8,128)(2,1)S(1)}, u32[]{:S(2)}) copy-start(bf16[128,1024]{1,0:T(8,128)(2,1)S(1)} %collective-permute-done.12) | copy-start | bytes 786436
  69.8 38.7 %collective-permute-start.21 = (bf16[256,1024]{1,0:T(8,128)(2,1)}, bf16[256,1024]{1,0:T(8,128)(2,1)}, u32[]{:S(2)}, u32[]{:S(2)}) collective-permute-start(bf16[256,1024]{1,0:T(8,128)(2,1)} %pad_maximum_fusion.1), channel_id=1, source_target_pairs={{0,8},{4,12},{8,0},{12,4},{16,24},{20,28},{24,16},{28,20},{1,9},{5... | collective-permute-start | bytes 1572872 | tf_op jit(solution)/shard_map/ppermute | solution.py:129
  79.9 28.6 %collective-permute-start.13 = (bf16[128,1024]{1,0:T(8,128)(2,1)}, bf16[128,1024]{1,0:T(8,128)(2,1)}, u32[]{:S(2)}, u32[]{:S(2)}) collective-permute-start(bf16[128,1024]{1,0:T(8,128)(2,1)} %get-tuple-element.58), channel_id=1, source_target_pairs={{0,24},{4,28},{8,16},{12,20},{16,8},{20,12},{24,0},{28,4},{1,25},{... | collective-permute-start | bytes 786440 | tf_op jit(solution)/shard_map/ppermute | solution.py:129
  81.0 23.8 %collective-permute-start.14 = (bf16[128,1024]{1,0:T(8,128)(2,1)}, bf16[128,1024]{1,0:T(8,128)(2,1)}, u32[]{:S(2)}, u32[]{:S(2)}) collective-permute-start(bf16[128,1024]{1,0:T(8,128)(2,1)} %get-tuple-element.63), channel_id=1, source_target_pairs={{0,16},{4,20},{8,24},{12,28},{16,0},{20,4},{24,8},{28,12},{1,17},{... | collective-permute-start | bytes 786440 | tf_op jit(solution)/shard_map/ppermute | solution.py:129
  83.5 1.3 copy-start.2
  84.8 1.3 copy-start.4
  88.8 3.7 %copy-start.12 = (bf16[256,512]{1,0:T(8,128)(2,1)}, bf16[256,512]{1,0:T(8,128)(2,1)S(1)}, u32[]{:S(2)}) copy-start(bf16[256,512]{1,0:T(8,128)(2,1)S(1)} %get-tuple-element.75) | copy-start | bytes 786436
  88.8 16.1 %copy-start.21 = (bf16[48,512]{1,0:T(8,128)(2,1)S(1)}, bf16[48,512]{1,0:T(8,128)(2,1)}, u32[]{:S(2)}) copy-start(bf16[48,512]{1,0:T(8,128)(2,1)} %reshape.394) | copy-start | bytes 147460
  88.8 19.7 %copy-start.18 = (bf16[128,1024]{1,0:T(8,128)(2,1)S(1)}, bf16[128,1024]{1,0:T(8,128)(2,1)}, u32[]{:S(2)}) copy-start(bf16[128,1024]{1,0:T(8,128)(2,1)} %copy-done.17) | copy-start | bytes 786436
  88.8 19.7 %copy-start.20 = (bf16[128,1024]{1,0:T(8,128)(2,1)S(1)}, bf16[128,1024]{1,0:T(8,128)(2,1)}, u32[]{:S(2)}) copy-start(bf16[128,1024]{1,0:T(8,128)(2,1)} %copy-done.19) | copy-start | bytes 786436
  92.4 18.3 %copy-start.10 = (bf16[256,512]{1,0:T(8,128)(2,1)}, bf16[256,512]{1,0:T(8,128)(2,1)S(1)}, u32[]{:S(2)}) copy-start(bf16[256,512]{1,0:T(8,128)(2,1)S(1)} %get-tuple-element.76) | copy-start | bytes 786436
  104.9 5.8 %copy-start.13 = (bf16[2048,1024]{1,0:T(8,128)(2,1)S(1)}, bf16[2048,1024]{1,0:T(8,128)(2,1)}, u32[]{:S(2)}) copy-start(bf16[2048,1024]{1,0:T(8,128)(2,1)} %param.14) | copy-start | bytes 12582916
  104.9 5.8 %copy-start.27 = (f32[1024]{0:T(1024)S(1)}, f32[1024]{0:T(1024)}, u32[]{:S(2)}) copy-start(f32[1024]{0:T(1024)} %slice_convert_fusion.2) | copy-start | bytes 12292
  104.9 21.6 %collective-permute-start.19 = (bf16[304,512]{1,0:T(8,128)(2,1)S(1)}, bf16[304,512]{1,0:T(8,128)(2,1)S(1)}, u32[]{:S(2)}, u32[]{:S(2)}) collective-permute-start(bf16[304,512]{1,0:T(8,128)(2,1)S(1)} %get-tuple-element.100), channel_id=1, source_target_pairs={{0,16},{4,20},{8,24},{12,28},{16,0},{20,4},{24,8},{28,12},{1,17},{... | collective-permute-start | bytes 933896 | tf_op jit(solution)/shard_map/ppermute | solution.py:129
  105.0 21.6 %collective-permute-start.20 = (bf16[304,512]{1,0:T(8,128)(2,1)S(1)}, bf16[304,512]{1,0:T(8,128)(2,1)S(1)}, u32[]{:S(2)}, u32[]{:S(2)}) collective-permute-start(bf16[304,512]{1,0:T(8,128)(2,1)S(1)} %get-tuple-element.101), channel_id=1, source_target_pairs={{0,24},{4,28},{8,16},{12,20},{16,8},{20,12},{24,0},{28,4},{1,25},{... | collective-permute-start | bytes 933896 | tf_op jit(solution)/shard_map/ppermute | solution.py:129
  106.3 21.7 %collective-permute-start.15 = (bf16[304,512]{1,0:T(8,128)(2,1)S(1)}, bf16[304,512]{1,0:T(8,128)(2,1)S(1)}, u32[]{:S(2)}, u32[]{:S(2)}) collective-permute-start(bf16[304,512]{1,0:T(8,128)(2,1)S(1)} %get-tuple-element.102), channel_id=1, source_target_pairs={{0,8},{4,12},{8,0},{12,4},{16,24},{20,28},{24,16},{28,20},{1,9},{5... | collective-permute-start | bytes 933896 | tf_op jit(solution)/shard_map/ppermute | solution.py:129
  111.9 16.8 %copy-start.22 = (bf16[1,48,512]{2,1,0:T(8,128)(2,1)S(1)}, bf16[1,48,512]{2,1,0:T(8,128)(2,1)}, u32[]{:S(2)}) copy-start(bf16[1,48,512]{2,1,0:T(8,128)(2,1)} %stack_reshape.7) | copy-start | bytes 147460
  111.9 27.5 %copy-start.5 = (bf16[4,128,1024]{2,1,0:T(8,128)(2,1)S(1)}, bf16[4,128,1024]{2,1,0:T(8,128)(2,1)}, u32[]{:S(2)}) copy-start(bf16[4,128,1024]{2,1,0:T(8,128)(2,1)} %query_ref.3) | copy-start | bytes 3145732
  126.6 11.4 %copy-start.14 = (bf16[304,512]{1,0:T(8,128)(2,1)}, bf16[304,512]{1,0:T(8,128)(2,1)S(1)}, u32[]{:S(2)}) copy-start(bf16[304,512]{1,0:T(8,128)(2,1)S(1)} %collective-permute-done.19) | copy-start | bytes 933892
  126.6 11.4 %copy-start.15 = (bf16[304,512]{1,0:T(8,128)(2,1)}, bf16[304,512]{1,0:T(8,128)(2,1)S(1)}, u32[]{:S(2)}) copy-start(bf16[304,512]{1,0:T(8,128)(2,1)S(1)} %collective-permute-done.20) | copy-start | bytes 933892
  128.0 0.7 copy-start.16
  131.1 17.5 %collective-permute-start.16 = (bf16[256,512]{1,0:T(8,128)(2,1)}, bf16[256,512]{1,0:T(8,128)(2,1)S(1)}, u32[]{:S(2)}, u32[]{:S(2)}) collective-permute-start(bf16[256,512]{1,0:T(8,128)(2,1)} %get-tuple-element.65), channel_id=1, source_target_pairs={{0,8},{4,12},{8,0},{12,4},{16,24},{20,28},{24,16},{28,20},{1,9},{5... | collective-permute-start | bytes 786440 | tf_op jit(solution)/shard_map/ppermute | solution.py:129
  136.9 21.6 %collective-permute-start.17 = (bf16[256,512]{1,0:T(8,128)(2,1)}, bf16[256,512]{1,0:T(8,128)(2,1)S(1)}, u32[]{:S(2)}, u32[]{:S(2)}) collective-permute-start(bf16[256,512]{1,0:T(8,128)(2,1)} %get-tuple-element.66), channel_id=1, source_target_pairs={{0,16},{4,20},{8,24},{12,28},{16,0},{20,4},{24,8},{28,12},{1,17},{... | collective-permute-start | bytes 786440 | tf_op jit(solution)/shard_map/ppermute | solution.py:129
  138.0 20.4 %collective-permute-start.18 = (bf16[256,512]{1,0:T(8,128)(2,1)}, bf16[256,512]{1,0:T(8,128)(2,1)S(1)}, u32[]{:S(2)}, u32[]{:S(2)}) collective-permute-start(bf16[256,512]{1,0:T(8,128)(2,1)} %get-tuple-element.67), channel_id=1, source_target_pairs={{0,24},{4,28},{8,16},{12,20},{16,8},{20,12},{24,0},{28,4},{1,25},{... | collective-permute-start | bytes 786440 | tf_op jit(solution)/shard_map/ppermute | solution.py:129
  139.5 1.0 copy-start.9
  143.6 4.2 %copy-start.6 = (f32[4,1,1024,128]{3,2,1,0:T(8,128)}, f32[4,1,1024,128]{3,2,1,0:T(8,128)S(1)}, u32[]{:S(2)}) copy-start(f32[4,1,1024,128]{3,2,1,0:T(8,128)S(1)} %get-tuple-element.81.state_ref) | copy-start | bytes 6291460
  143.6 14.8 %copy-start.11 = (bf16[256,512]{1,0:T(8,128)(2,1)S(1)}, bf16[256,512]{1,0:T(8,128)(2,1)}, u32[]{:S(2)}) copy-start(bf16[256,512]{1,0:T(8,128)(2,1)} %copy-done.10) | copy-start | bytes 786436
  158.7 1.9 copy-start.28
  158.7 1.9 copy-start.29
  160.5 16.7 %copy-start.24 = (s32[4,1,128]{2,0,1:T(4,128)S(1)}, s32[4,1,128]{2,0,1:T(4,128)}, u32[]{:S(2)}) copy-start(s32[4,1,128]{2,0,1:T(4,128)} %add.351) | copy-start | bytes 6148
  160.5 16.7 %copy-start.25 = (s32[128]{0:T(128)S(1)}, s32[128]{0:T(128)}, u32[]{:S(2)}) copy-start(s32[128]{0:T(128)} %add.348) | copy-start | bytes 1540
  160.5 2.3 %collective-permute-start.22 = (bf16[2,256,256]{2,1,0:T(8,128)(2,1)S(1)}, bf16[2,256,256]{2,1,0:T(8,128)(2,1)S(1)}, u32[]{:S(2)}, u32[]{:S(2)}) collective-permute-start(bf16[2,256,256]{2,1,0:T(8,128)(2,1)S(1)} %pad_maximum_fusion.5), channel_id=1, source_target_pairs={{0,1},{1,0},{2,3},{3,2},{4,5},{5,4},{6,7},{7,6},{8,9},{9,8},{10,11... | collective-permute-start | bytes 786440 | tf_op jit(solution)/shard_map/ppermute | solution.py:23
  160.6 1.5 collective-permute-start.24
  162.1 3.6 %collective-permute-start.25 = (f32[256]{0:T(256)S(1)}, f32[256]{0:T(256)S(1)}, u32[]{:S(2)}, u32[]{:S(2)}) collective-permute-start(f32[256]{0:T(256)S(1)} %add.336), channel_id=1, source_target_pairs={{0,2},{1,3},{2,0},{3,1},{4,6},{5,7},{6,4},{7,5},{8,10},{9,11},{10,... | collective-permute-start | bytes 3080 | tf_op jit(solution)/shard_map/ppermute | solution.py:23
  162.9 5.4 %collective-permute-start.23 = (bf16[1,256,256]{2,1,0:T(8,128)(2,1)S(1)}, bf16[1,256,256]{2,1,0:T(8,128)(2,1)S(1)}, u32[]{:S(2)}, u32[]{:S(2)}) collective-permute-start(bf16[1,256,256]{2,1,0:T(8,128)(2,1)S(1)} %dynamic-slice_convert_fusion), channel_id=1, source_target_pairs={{0,2},{1,3},{2,0},{3,1},{4,6},{5,7},{6,4},{7,5},{8,10},{9,11},{10,... | collective-permute-start | bytes 393224 | tf_op jit(solution)/shard_map/ppermute | solution.py:23
  169.3 16.2 %all-to-all-start = ((bf16[8,64,256]{2,1,0:T(8,128)(2,1)}), bf16[8,64,256]{2,1,0:T(8,128)(2,1)S(1)}, u32[]{:S(2)}, u32[]{:S(2)}) async-start(bf16[8,64,256]{2,1,0:T(8,128)(2,1)} %bitcast.56), calls=%async_computation | async-start | bytes 524288 | tf_op jit(solution)/shard_map/all_to_all | solution.py:478
  185.5 1.6 copy-start.7
  187.1 0.9 copy-start.8

commit v5 on v3

--- a/solution.py
+++ b/solution.py
@@ -129,10 +129,9 @@
 BEYOND = ((1, 3), (2, 0))
 
 
-def send_direct(parts):
+def send_direct(parts, kinds):
     return [
-        lax.ppermute(part, "seq", along([(a, a ^ k) for a in range(4)]))
-        for k, part in enumerate(parts[1:], 1)
+        lax.ppermute(parts[k], "seq", along([(a, a ^ k) for a in range(4)])) for k in kinds
     ]
 
 
@@ -242,7 +241,7 @@
             late, _ = lax.optimization_barrier((moved[1], sent[0][0][0]))
             held.append(order_rows(scalars, share_panels(late), share))
         if step == RIDE:
-            received[1], _ = lax.optimization_barrier((received[1], sent[step - 1][1][0]))
+            received[1], _ = lax.optimization_barrier((received[1], sent[step - 1][0][0]))
             small = [small] + [other[-extra:] for other in received[1]]
             small_shape = (width,) + small[0].shape
             riding = [jnp.stack(small).reshape(-1, count)]
@@ -257,13 +256,17 @@
             operands = [(jnp.roll(parts, member * w_merge.shape[0], axis=0), depth, inside)]
         groups = ((0,), (1,), (2,), (3,)) if direct else ((0,), (1, 2, 3), (1,))
         parts = partial_products([held[h] for h in halves], operands, count, groups)
-        if step == 1:
+        if step == 0:
+            sent.append((parts, send_direct(parts, (2, 3))))
+        elif step == 1:
+            parts, _ = lax.optimization_barrier((parts, sent[0][1][0]))
+            joined = jnp.concatenate([sent[0][0][1], parts[1]], axis=0)
+            far = send_direct(parts, (2, 3))
+            near = send_direct([None, joined], (1,))[0]
+            sent[0][1].append(near[:half])
+            sent.append((parts, far + [near[half:]]))
+        else:
             parts, _ = lax.optimization_barrier((parts, sent[0][1][1]))
-        elif step:
-            parts, _ = lax.optimization_barrier((parts, sent[step - 2][1][-1 if step == 2 else 1]))
-        if direct:
-            sent.append((parts, send_direct(parts)))
-        else:
             sent.append((parts, send_sums(parts, riding if step == RIDE else [])))
     done = []
     everyone = None

time: 188 us -> 190 us (1.011)
  waiting for transfers between devices: 75.5 us -> 66.1 us
  starting transfers between devices: 46.8 us -> 53.7 us
  local copies, waits for them, and re-layouts: 17.3 us -> 21.1 us
    ppermute x6 -> x5, waiting for transfers between devices: 12 us -> 0.01 us  [send_direct(): lax.ppermute(parts[k], 'seq', along([(a, a ^ k) for a in range(4)]))]
    ppermute x2, starting transfers between devices: 2.93 us -> 10.1 us  [send_sums(): inward = lax.ppermute(ride(others, small), 'seq', along(INWARD))]
    reduce_sum x4 -> x3, other arithmetic: 7.45 us -> 4.37 us  [finish(): squared = jnp.sum(merged * merged, axis=1)]
    all_to_all x1, starting transfers between devices: 7.32 us -> 10.1 us  [shards(): lax.all_to_all(outgoing, 'seq', split_axis=0, concat_axis=0, tiled=True)]
    ppermute x11, waiting for transfers between devices: 21.6 us -> 18.8 us  [flip(): return lax.ppermute(value, axis, [(i, i ^ bit) for i in range(count)])]
    ppermute x6 -> x5, starting transfers between devices: 7.88 us -> 6.68 us  [send_direct(): lax.ppermute(parts[k], 'seq', along([(a, a ^ k) for a in range(4)]))]
    unnamed x80 -> x84, local copies, waits for them, and re-layouts: 5.68 us -> 5.98 us
  transfers between devices with their start and end apart: 30 -> 29, of which waited for: 13 -> 12; matrix products, arithmetic and copies ran while one was open for 17% -> 19% of each run, Pallas kernels for 7% -> 8%
where the time goes in v5:
time: 190 us; the launch traced here: 188 us
  waiting for transfers between devices  66.1 us (35%)
  starting transfers between devices  53.7 us (28%)
  local copies, waits for them, and re-layouts  21.1 us (11%)
  Pallas kernels  20.4 us (11%)
  other arithmetic  17.9 us (9%)
  matrix products  7.71 us (4%)
    ppermute x2, waiting for transfers between devices, send_sums(): inward = lax.ppermute(ride(others, small), 'seq', along(INWARD))  21.6 us
    ppermute x11, waiting for transfers between devices, flip(): return lax.ppermute(value, axis, [(i, i ^ bit) for i in range(count)])  18.8 us
    ppermute x11, starting transfers between devices, flip(): return lax.ppermute(value, axis, [(i, i ^ bit) for i in range(count)])  13.1 us
    pallas_call x4, Pallas kernels, partial_products(): pl.pallas_call(functools.partial(partial_kernel, halves, groups), grid=(c...  12.5 us
    ppermute x2, waiting for transfers between devices, finish_sums(): beyond = lax.ppermute(ride(beyond, extra), 'seq', along(BEYOND))  10.3 us
    all_to_all x1, starting transfers between devices, shards(): lax.all_to_all(outgoing, 'seq', split_axis=0, concat_axis=0, tiled=True)  10.1 us
    ppermute x2, starting transfers between devices, send_sums(): inward = lax.ppermute(ride(others, small), 'seq', along(INWARD))  10.1 us
    ppermute x2, waiting for transfers between devices, merge_tiles(): others.append(lax.ppermute(own, 'seq', pairs))  7.85 us
  transfers between devices with their start and end apart: 29, of which 12 were waited for; matrix products, arithmetic and copies ran while one was open for 19% of the time, Pallas kernels for 8%

profile of v5, /device:TPU:0, one launch (start us, length us, event | category | flops | bytes accessed | tf_op | source)
XLA Modules:
  0.0 188.3 jit_solution(12535427791514630560)
XLA Ops:
  0.6 1.1 slice_bitcast_fusion
  2.5 6.8 %collective-permute-start = (bf16[128,1280]{1,0:T(8,128)(2,1)S(1)}, bf16[128,1280]{1,0:T(8,128)(2,1)S(1)}, u32[]{:S(2)}, u32[]{:S(2)}) collective-permute-start(bf16[128,1280]{1,0:T(8,128)(2,1)S(1)} %get-tuple-element.81), channel_id=1, source_target_pairs={{0,2},{1,3},{2,0},{3,1},{4,6},{5,7},{6,4},{7,5},{8,10},{9,11},{10,... | collective-permute-start | bytes 983048 | tf_op jit(solution)/shard_map/ppermute | solution.py:23
  9.3 3.5 %fusion.60 = (bf16[640,1024]{1,0:T(8,128)(2,1)}, bf16[640,1024]{1,0:T(8,128)(2,1)}) fusion(bf16[640,2048]{1,0:T(8,128)(2,1)} %refs_2_.3), kind=kLoop, calls=%fused_computation.150 | loop fusion | bytes 5242880 | tf_op jit(solution)/shard_map/slice | solution.py:206
  12.7 1.6 collective-permute-start.7
  15.1 0.8 gather_fusion.2
  17.1 5.5 %collective-permute-done = bf16[128,1280]{1,0:T(8,128)(2,1)S(1)} collective-permute-done((bf16[128,1280]{1,0:T(8,128)(2,1)S(1)}, bf16[128,1280]{1,0:T(8,128)(2,1)S(1)}, u32[]{:S(2)}, u32[]{:S(2)}) %collective-permute-start) | collective-permute-done | bytes 327712 | tf_op jit(solution)/shard_map/ppermute | solution.py:23
  22.6 2.5 %collective-permute-start.4 = (bf16[128,1280]{1,0:T(8,128)(2,1)S(1)}, bf16[128,1280]{1,0:T(8,128)(2,1)S(1)}, u32[]{:S(2)}, u32[]{:S(2)}) collective-permute-start(bf16[128,1280]{1,0:T(8,128)(2,1)S(1)} %collective-permute-done.3.refs_0_), channel_id=1, source_target_pairs={{0,2},{1,3},{2,0},{3,1},{4,6},{5,7},{6,4},{7,5},{8,10},{9,11},{10,... | collective-permute-start | bytes 983048 | tf_op jit(solution)/shard_map/ppermute | solution.py:23
  25.1 2.6 %pad_maximum_fusion = bf16[652,1024]{1,0:T(8,128)(2,1)} fusion(bf16[12,1024]{1,0:T(8,128)(2,1)S(1)} %reshape.337, bf16[640,1024]{1,0:T(8,128)(2,1)} %get-tuple-element.67), kind=kLoop, calls=%fused_computation.9 | loop fusion | flops 2670592 | bytes 2670592 | tf_op jit(solution)/shard_map/concatenate | solution.py:208
  27.8 1.5 collective-permute-start.1
  29.3 3.3 %collective-permute-start.2 = (bf16[128,1280]{1,0:T(8,128)(2,1)}, bf16[128,1280]{1,0:T(8,128)(2,1)S(1)}, u32[]{:S(2)}, u32[]{:S(2)}) collective-permute-start(bf16[128,1280]{1,0:T(8,128)(2,1)} %copy-done.39), channel_id=1, source_target_pairs={{2,0},{3,10},{0,16},{1,26},{6,4},{7,14},{4,20},{5,30},{10,2},{11,8... | collective-permute-start | bytes 983048 | tf_op jit(solution)/shard_map/ppermute | solution.py:37
  33.2 1.8 collective-permute-start.6
  36.9 7.8 %collective-permute-done.7.refs_2_ = bf16[640,1024]{1,0:T(8,128)(2,1)} collective-permute-done((bf16[640,1024]{1,0:T(8,128)(2,1)}, bf16[640,1024]{1,0:T(8,128)(2,1)}, u32[]{:S(2)}, u32[]{:S(2)}) %collective-permute-start.7) | collective-permute-done | bytes 1310752 | tf_op jit(solution)/shard_map/ppermute | solution.py:217
  44.8 3.5 %shard_map.123 = (bf16[128,1024]{1,0:T(8,128)(2,1)S(1)}, bf16[128,1024]{1,0:T(8,128)(2,1)S(1)}, bf16[128,1024]{1,0:T(8,128)(2,1)}, bf16[128,1024]{1,0:T(8,128)(2,1)S(1)}) custom-call(bf16[512,1280]{1,0:T(8,128)(2,1)S(1)} %shard_map.122.refs_0_, bf16[640,2048]{1,0:T(8,128)(2,1)S(1)} %copy-done, bf16[640,1024]{1,0:T(8,128)(2,1)} %collective-permute-done.7.refs_2_), custom_call_target="tpu_custom_call" | custom-call | bytes 2048 | tf_op jit(solution)/shard_map/pallas_call | solution.py:109
  48.3 0.7 copy-done.5
  49.8 2.2 %collective-permute-start.11 = (bf16[128,1024]{1,0:T(8,128)(2,1)}, bf16[128,1024]{1,0:T(8,128)(2,1)}, u32[]{:S(2)}, u32[]{:S(2)}) collective-permute-start(bf16[128,1024]{1,0:T(8,128)(2,1)} %get-tuple-element.38), channel_id=1, source_target_pairs={{0,16},{4,20},{8,24},{12,28},{16,0},{20,4},{24,8},{28,12},{1,17},{... | collective-permute-start | bytes 786440 | tf_op jit(solution)/shard_map/ppermute | solution.py:134
  52.0 6.6 %collective-permute-done.8.refs_1_ = bf16[128,1280]{1,0:T(8,128)(2,1)S(1)} collective-permute-done((bf16[128,1280]{1,0:T(8,128)(2,1)S(1)}, bf16[128,1280]{1,0:T(8,128)(2,1)S(1)}, u32[]{:S(2)}, u32[]{:S(2)}) %collective-permute-start.8) | collective-permute-done | bytes 327712 | tf_op jit(solution)/shard_map/ppermute | solution.py:23
  59.2 1.4 stack_reshape.6
  60.6 0.8 broadcast_in_dim.28
  61.4 1.6 add.377
  62.9 0.7 broadcast_in_dim.27.seen_ref
  63.6 1.5 add.378.all_ref
  65.1 1.3 slice_convert_fusion.3
  66.4 1.7 shard_map.124.refs_0_.refs_1_
  68.2 3.7 %shard_map.125 = (bf16[128,1024]{1,0:T(8,128)(2,1)S(1)}, bf16[128,1024]{1,0:T(8,128)(2,1)S(1)}, bf16[128,1024]{1,0:T(8,128)(2,1)}, bf16[128,1024]{1,0:T(8,128)(2,1)}) custom-call(bf16[512,1280]{1,0:T(8,128)(2,1)S(1)} %shard_map.124.refs_0_.refs_1_, bf16[640,2048]{1,0:T(8,128)(2,1)S(1)} %copy-done, bf16[640,1024]{1,0:T(8,128)(2,1)} %collective-permute-done.7.refs_2_), custom_call_target="tpu_custom_call" | custom-call | bytes 2048 | tf_op jit(solution)/shard_map/pallas_call | solution.py:109
  71.9 1.9 %collective-permute-start.18 = (bf16[128,1024]{1,0:T(8,128)(2,1)}, bf16[128,1024]{1,0:T(8,128)(2,1)}, u32[]{:S(2)}, u32[]{:S(2)}) collective-permute-start(bf16[128,1024]{1,0:T(8,128)(2,1)} %get-tuple-element.49), channel_id=1, source_target_pairs={{0,16},{4,20},{8,24},{12,28},{16,0},{20,4},{24,8},{28,12},{1,17},{... | collective-permute-start | bytes 786440 | tf_op jit(solution)/shard_map/ppermute | solution.py:134
  73.8 2.0 %collective-permute-start.19 = (bf16[128,1024]{1,0:T(8,128)(2,1)}, bf16[128,1024]{1,0:T(8,128)(2,1)}, u32[]{:S(2)}, u32[]{:S(2)}) collective-permute-start(bf16[128,1024]{1,0:T(8,128)(2,1)} %get-tuple-element.50), channel_id=1, source_target_pairs={{0,24},{4,28},{8,16},{12,20},{16,8},{20,12},{24,0},{28,4},{1,25},{... | collective-permute-start | bytes 786440 | tf_op jit(solution)/shard_map/ppermute | solution.py:134
  75.9 0.9 pad_maximum_fusion.2
  77.2 0.8 slice_bitcast_fusion.2
  78.0 2.7 %shard_map.127 = (bf16[256,512]{1,0:T(8,128)(2,1)S(1)}, bf16[768,512]{1,0:T(8,128)(2,1)S(1)}, bf16[256,512]{1,0:T(8,128)(2,1)S(1)}) custom-call(bf16[512,1280]{1,0:T(8,128)(2,1)S(1)} %copy-done.2, bf16[512,1280]{1,0:T(8,128)(2,1)S(1)} %shard_map.124.refs_0_.refs_1_, bf16[640,2048]{1,0:T(8,128)(2,1)S(1)} %copy-done, ...), custom_call_target="tpu_custom_call" | custom-call | bytes 1024 | tf_op jit(solution)/shard_map/pallas_call | solution.py:109
  80.7 0.9 copy-done.3
  81.6 0.7 copy-done.9
  82.3 0.7 copy-done.18
  83.0 2.6 %shard_map.126 = (bf16[256,512]{1,0:T(8,128)(2,1)S(1)}, bf16[768,512]{1,0:T(8,128)(2,1)S(1)}, bf16[256,512]{1,0:T(8,128)(2,1)S(1)}) custom-call(bf16[512,1280]{1,0:T(8,128)(2,1)S(1)} %copy-done.2, bf16[512,1280]{1,0:T(8,128)(2,1)S(1)} %shard_map.124.refs_0_.refs_1_, bf16[640,2048]{1,0:T(8,128)(2,1)S(1)} %copy-done, ...), custom_call_target="tpu_custom_call" | custom-call | bytes 1024 | tf_op jit(solution)/shard_map/pallas_call | solution.py:109
  85.7 0.7 copy-done.7
  86.4 0.7 copy-done.13
  87.2 8.7 %collective-permute-start.21 = (bf16[768,512]{1,0:T(8,128)(2,1)}, bf16[768,512]{1,0:T(8,128)(2,1)}, u32[]{:S(2)}, u32[]{:S(2)}) collective-permute-start(bf16[768,512]{1,0:T(8,128)(2,1)} %copy-done.3), channel_id=1, source_target_pairs={{0,8},{4,12},{24,16},{28,20},{1,9},{5,13},{25,17},{29,21},{2,10},{... | collective-permute-start | bytes 2359304 | tf_op jit(solution)/shard_map/ppermute | solution.py:151
  96.0 1.3 collective-permute-start.14
  97.3 1.7 pad_maximum_fusion.7
  99.6 1.3 collective-permute-start.20
  100.9 1.3 collective-permute-start.13
  102.3 1.7 fusion.7
  104.0 2.9 %fusion.2 = f32[128,1024]{1,0:T(8,128)} fusion(bf16[2048,1024]{1,0:T(8,128)(2,1)} %param.14, bf16[128,1024]{1,0:T(8,128)(2,1)S(1)} %get-tuple-element.59, f32[1024]{0:T(1024)S(1)} %copy-done.36), kind=kOutput, calls=%fused_computation.5 | convolution fusion | flops 268828672 | bytes 2887680 | tf_op jit(solution)/shard_map/dot_general | solution.py:235
  107.0 7.6 %collective-permute-done.21 = bf16[768,512]{1,0:T(8,128)(2,1)} collective-permute-done((bf16[768,512]{1,0:T(8,128)(2,1)}, bf16[768,512]{1,0:T(8,128)(2,1)}, u32[]{:S(2)}, u32[]{:S(2)}) %collective-permute-start.21) | collective-permute-done | bytes 786464 | tf_op jit(solution)/shard_map/ppermute | solution.py:151
  114.6 1.2 add_convert_fusion.1
  115.8 1.3 collective-permute-start.22
  117.8 13.9 %collective-permute-done.14 = bf16[816,512]{1,0:T(8,128)(2,1)S(1)} collective-permute-done((bf16[816,512]{1,0:T(8,128)(2,1)S(1)}, bf16[816,512]{1,0:T(8,128)(2,1)S(1)}, u32[]{:S(2)}, u32[]{:S(2)}) %collective-permute-start.14) | collective-permute-done | bytes 835616 | tf_op jit(solution)/shard_map/ppermute | solution.py:151
  132.6 1.4 collective-permute-start.15
  134.0 0.7 collective-permute-start.16
  135.3 1.3 fusion.21
  136.6 10.3 %collective-permute-done.15 = bf16[352,512]{1,0:T(8,128)(2,1)S(1)} collective-permute-done((bf16[352,512]{1,0:T(8,128)(2,1)S(1)}, bf16[352,512]{1,0:T(8,128)(2,1)S(1)}, u32[]{:S(2)}, u32[]{:S(2)}) %collective-permute-start.15) | collective-permute-done | bytes 360480 | tf_op jit(solution)/shard_map/ppermute | solution.py:170
  146.9 0.7 copy-done.24
  149.6 1.3 fusion.15
  151.0 1.7 convolution_add_fusion.1
  152.7 1.7 convolution_add_fusion
  154.5 0.7 pad_maximum_fusion.8
  156.3 0.8 collective-permute-done.24
  157.2 1.1 collective-permute-start.25
  158.2 1.4 collective-permute-done.27
  159.6 3.4 %collective-permute-done.25 = bf16[1,256,256]{2,1,0:T(8,128)(2,1)S(1)} collective-permute-done((bf16[1,256,256]{2,1,0:T(8,128)(2,1)S(1)}, bf16[1,256,256]{2,1,0:T(8,128)(2,1)S(1)}, u32[]{:S(2)}, u32[]{:S(2)}) %collective-permute-start.25) | collective-permute-done | bytes 131104 | tf_op jit(solution)/shard_map/ppermute | solution.py:23
  163.0 1.0 convolution_convert_fusion
  164.0 10.1 %all-to-all-start = ((bf16[8,64,256]{2,1,0:T(8,128)(2,1)}), bf16[8,64,256]{2,1,0:T(8,128)(2,1)S(1)}, u32[]{:S(2)}, u32[]{:S(2)}) async-start(bf16[8,64,256]{2,1,0:T(8,128)(2,1)} %bitcast.17), calls=%async_computation | async-start | bytes 524288 | tf_op jit(solution)/shard_map/all_to_all | solution.py:481
  174.2 1.0 add_select_fusion.pick_ref
  175.3 7.5 %all-to-all-done = bf16[8,64,256]{2,1,0:T(8,128)(2,1)S(1)} async-done(((bf16[8,64,256]{2,1,0:T(8,128)(2,1)}), bf16[8,64,256]{2,1,0:T(8,128)(2,1)S(1)}, u32[]{:S(2)}, u32[]{:S(2)}) %all-to-all-start) | async-done | bytes 262176 | tf_op jit(solution)/shard_map/all_to_all | solution.py:481
  182.8 5.5 %shard_map.128 = (bf16[4,128,1024]{2,1,0:T(8,128)(2,1)}, bf16[256,256]{1,0:T(8,128)(2,1)}) custom-call(s32[4]{0:T(128)S(1)} %fusion.49.place_ref, bf16[4,128,1024]{2,1,0:T(8,128)(2,1)S(1)} %copy-done.15, bf16[8,32,256]{2,1,0:T(8,128)(2,1)S(1)} %slice.165.prefix_ref, bf16[4,128,256]{2,1,0:T(8,128)(2,1)S(1)} %copy-done.16, bf16[512,256]{1,0:T(8,128)(2,1)S(1)} %bitcast.53, ...), custom_call_target="tpu_custom_call" | custom-call | flops 603979776 | bytes 4194304 | tf_op jit(solution)/shard_map/pallas_call | solution.py:377
  (172 shorter events, 13.1 us)
Async XLA Ops:
  1.7 15.4 %collective-permute-start.3 = (bf16[128,1280]{1,0:T(8,128)(2,1)S(1)}, bf16[128,1280]{1,0:T(8,128)(2,1)S(1)}, u32[]{:S(2)}, u32[]{:S(2)}) collective-permute-start(bf16[128,1280]{1,0:T(8,128)(2,1)S(1)} %get-tuple-element.80), channel_id=1, source_target_pairs={{0,0},{1,10},{2,16},{3,26},{4,4},{5,14},{6,20},{7,30},{8,2},{9,8},... | collective-permute-start | bytes 983048 | tf_op jit(solution)/shard_map/ppermute | solution.py:37
  2.4 11.9 %copy-start.37 = (s32[32,1]{0,1:T(1,128)S(1)}, s32[32,1]{0,1:T(1,128)}, u32[]{:S(2)}) copy-start(s32[32,1]{0,1:T(1,128)} %param.15) | copy-start | bytes 388
  2.4 12.1 %copy-start.40 = (s32[1,4]{1,0:T(1,128)S(1)}, s32[1,4]{1,0:T(1,128)}, u32[]{:S(2)}) copy-start(s32[1,4]{1,0:T(1,128)} %param.17) | copy-start | bytes 52
  2.5 20.2 %collective-permute-start = (bf16[128,1280]{1,0:T(8,128)(2,1)S(1)}, bf16[128,1280]{1,0:T(8,128)(2,1)S(1)}, u32[]{:S(2)}, u32[]{:S(2)}) collective-permute-start(bf16[128,1280]{1,0:T(8,128)(2,1)S(1)} %get-tuple-element.81), channel_id=1, source_target_pairs={{0,2},{1,3},{2,0},{3,1},{4,6},{5,7},{6,4},{7,5},{8,10},{9,11},{10,... | collective-permute-start | bytes 983048 | tf_op jit(solution)/shard_map/ppermute | solution.py:23
  12.7 3.7 %copy-start.41 = (s32[32]{0:T(128)S(1)}, s32[32]{0:T(128)}, u32[]{:S(2)}) copy-start(s32[32]{0:T(128)} %param.16) | copy-start | bytes 388
  12.7 3.7 %copy-start.31 = (bf16[1,32,256]{2,1,0:T(8,128)(2,1)S(1)}, bf16[1,32,256]{2,1,0:T(8,128)(2,1)}, u32[]{:S(2)}) copy-start(bf16[1,32,256]{2,1,0:T(8,128)(2,1)} %param.19) | copy-start | bytes 49156
  12.7 3.8 %copy-start.35 = (bf16[2048]{0:T(1024)(128)(2,1)S(1)}, bf16[2048]{0:T(1024)(128)(2,1)}, u32[]{:S(2)}) copy-start(bf16[2048]{0:T(1024)(128)(2,1)} %param.13) | copy-start | bytes 12292
  12.7 32.0 %collective-permute-start.7 = (bf16[640,1024]{1,0:T(8,128)(2,1)}, bf16[640,1024]{1,0:T(8,128)(2,1)}, u32[]{:S(2)}, u32[]{:S(2)}) collective-permute-start(bf16[640,1024]{1,0:T(8,128)(2,1)} %get-tuple-element.66), channel_id=1, source_target_pairs={{4,0},{0,4},{12,8},{8,12},{20,16},{16,20},{28,24},{24,28},{5,1},{1... | collective-permute-start | bytes 3932168 | tf_op jit(solution)/shard_map/ppermute | solution.py:217
  16.2 20.7 %copy-start.33 = (s32[128]{0:T(128)}, s32[128]{0:T(128)S(1)}, u32[]{:S(2)}) copy-start(s32[128]{0:T(128)S(1)} %add.365) | copy-start | bytes 1540
  16.3 8.8 %copy-start.26 = (s32[4,16,8]{2,1,0:T(8,128)}, s32[4,16,8]{2,1,0:T(8,128)S(1)}, u32[]{:S(2)}) copy-start(s32[4,16,8]{2,1,0:T(8,128)S(1)} %add.362) | copy-start | bytes 6148
  16.5 8.6 %copy-start.28 = (bf16[48,256]{1,0:T(8,128)(2,1)}, bf16[48,256]{1,0:T(8,128)(2,1)S(1)}, u32[]{:S(2)}) copy-start(bf16[48,256]{1,0:T(8,128)(2,1)S(1)} %pad_maximum_fusion.11) | copy-start | bytes 73732
  22.6 2.5 %copy-start.39 = (bf16[128,1280]{1,0:T(8,128)(2,1)}, bf16[128,1280]{1,0:T(8,128)(2,1)S(1)}, u32[]{:S(2)}) copy-start(bf16[128,1280]{1,0:T(8,128)(2,1)S(1)} %collective-permute-done) | copy-start | bytes 983044
  22.6 10.6 %collective-permute-start.4 = (bf16[128,1280]{1,0:T(8,128)(2,1)S(1)}, bf16[128,1280]{1,0:T(8,128)(2,1)S(1)}, u32[]{:S(2)}, u32[]{:S(2)}) collective-permute-start(bf16[128,1280]{1,0:T(8,128)(2,1)S(1)} %collective-permute-done.3.refs_0_), channel_id=1, source_target_pairs={{0,2},{1,3},{2,0},{3,1},{4,6},{5,7},{6,4},{7,5},{8,10},{9,11},{10,... | collective-permute-start | bytes 983048 | tf_op jit(solution)/shard_map/ppermute | solution.py:23
  25.1 19.7 %copy-start = (bf16[640,2048]{1,0:T(8,128)(2,1)S(1)}, bf16[640,2048]{1,0:T(8,128)(2,1)}, u32[]{:S(2)}) copy-start(bf16[640,2048]{1,0:T(8,128)(2,1)} %refs_2_.3) | copy-start | bytes 7864324
  27.8 49.5 %collective-permute-start.1 = (bf16[652,1024]{1,0:T(8,128)(2,1)}, bf16[652,1024]{1,0:T(8,128)(2,1)}, u32[]{:S(2)}, u32[]{:S(2)}) collective-permute-start(bf16[652,1024]{1,0:T(8,128)(2,1)} %pad_maximum_fusion), channel_id=1, source_target_pairs={{4,0},{0,4},{12,8},{8,12},{20,16},{16,20},{28,24},{24,28},{5,1},{1... | collective-permute-start | bytes 4005896 | tf_op jit(solution)/shard_map/ppermute | solution.py:217
  29.3 6.4 %collective-permute-start.5 = (bf16[128,1280]{1,0:T(8,128)(2,1)S(1)}, bf16[128,1280]{1,0:T(8,128)(2,1)S(1)}, u32[]{:S(2)}, u32[]{:S(2)}) collective-permute-start(bf16[128,1280]{1,0:T(8,128)(2,1)S(1)} %collective-permute-done.3.refs_0_), channel_id=1, source_target_pairs={{0,1},{1,0},{2,3},{3,2},{4,5},{5,4},{6,7},{7,6},{8,9},{9,8},{10,11... | collective-permute-start | bytes 983048 | tf_op jit(solution)/shard_map/ppermute | solution.py:23
  29.3 19.7 %collective-permute-start.2 = (bf16[128,1280]{1,0:T(8,128)(2,1)}, bf16[128,1280]{1,0:T(8,128)(2,1)S(1)}, u32[]{:S(2)}, u32[]{:S(2)}) collective-permute-start(bf16[128,1280]{1,0:T(8,128)(2,1)} %copy-done.39), channel_id=1, source_target_pairs={{2,0},{3,10},{0,16},{1,26},{6,4},{7,14},{4,20},{5,30},{10,2},{11,8... | collective-permute-start | bytes 983048 | tf_op jit(solution)/shard_map/ppermute | solution.py:37
  33.2 3.0 %collective-permute-start.6 = (bf16[128,1280]{1,0:T(8,128)(2,1)S(1)}, bf16[128,1280]{1,0:T(8,128)(2,1)S(1)}, u32[]{:S(2)}, u32[]{:S(2)}) collective-permute-start(bf16[128,1280]{1,0:T(8,128)(2,1)S(1)} %collective-permute-done.4.refs_1_), channel_id=1, source_target_pairs={{0,1},{1,0},{2,3},{3,2},{4,5},{5,4},{6,7},{7,6},{8,9},{9,8},{10,11... | collective-permute-start | bytes 983048 | tf_op jit(solution)/shard_map/ppermute | solution.py:23
  36.9 11.4 %copy-start.1 = (bf16[512,1280]{1,0:T(8,128)(2,1)}, bf16[512,1280]{1,0:T(8,128)(2,1)S(1)}, u32[]{:S(2)}) copy-start(bf16[512,1280]{1,0:T(8,128)(2,1)S(1)} %shard_map.122.refs_0_) | copy-start | bytes 3932164
  49.0 9.6 %copy-start.17 = (bf16[128,1024]{1,0:T(8,128)(2,1)}, bf16[128,1024]{1,0:T(8,128)(2,1)S(1)}, u32[]{:S(2)}) copy-start(bf16[128,1024]{1,0:T(8,128)(2,1)S(1)} %get-tuple-element.44) | copy-start | bytes 786436
  49.0 9.6 %collective-permute-start.8 = (bf16[128,1280]{1,0:T(8,128)(2,1)S(1)}, bf16[128,1280]{1,0:T(8,128)(2,1)S(1)}, u32[]{:S(2)}, u32[]{:S(2)}) collective-permute-start(bf16[128,1280]{1,0:T(8,128)(2,1)S(1)} %collective-permute-done.2.refs_0_), channel_id=1, source_target_pairs={{0,2},{1,3},{2,0},{3,1},{4,6},{5,7},{6,4},{7,5},{8,10},{9,11},{10,... | collective-permute-start | bytes 983048 | tf_op jit(solution)/shard_map/ppermute | solution.py:23
  49.7 16.7 %collective-permute-start.9 = (bf16[128,1280]{1,0:T(8,128)(2,1)S(1)}, bf16[128,1280]{1,0:T(8,128)(2,1)}, u32[]{:S(2)}, u32[]{:S(2)}) collective-permute-start(bf16[128,1280]{1,0:T(8,128)(2,1)S(1)} %collective-permute-done.2.refs_0_), channel_id=1, source_target_pairs={{0,1},{1,0},{2,3},{3,2},{4,5},{5,4},{6,7},{7,6},{8,9},{9,8},{10,11... | collective-permute-start | bytes 983048 | tf_op jit(solution)/shard_map/ppermute | solution.py:23
  49.8 22.2 %collective-permute-start.11 = (bf16[128,1024]{1,0:T(8,128)(2,1)}, bf16[128,1024]{1,0:T(8,128)(2,1)}, u32[]{:S(2)}, u32[]{:S(2)}) collective-permute-start(bf16[128,1024]{1,0:T(8,128)(2,1)} %get-tuple-element.38), channel_id=1, source_target_pairs={{0,16},{4,20},{8,24},{12,28},{16,0},{20,4},{24,8},{28,12},{1,17},{... | collective-permute-start | bytes 786440 | tf_op jit(solution)/shard_map/ppermute | solution.py:134
  58.6 7.8 %collective-permute-start.10 = (bf16[128,1280]{1,0:T(8,128)(2,1)S(1)}, bf16[128,1280]{1,0:T(8,128)(2,1)}, u32[]{:S(2)}, u32[]{:S(2)}) collective-permute-start(bf16[128,1280]{1,0:T(8,128)(2,1)S(1)} %collective-permute-done.8.refs_1_), channel_id=1, source_target_pairs={{0,1},{1,0},{2,3},{3,2},{4,5},{5,4},{6,7},{7,6},{8,9},{9,8},{10,11... | collective-permute-start | bytes 983048 | tf_op jit(solution)/shard_map/ppermute | solution.py:23
  66.4 20.7 %collective-permute-start.12 = (bf16[128,1024]{1,0:T(8,128)(2,1)}, bf16[128,1024]{1,0:T(8,128)(2,1)}, u32[]{:S(2)}, u32[]{:S(2)}) collective-permute-start(bf16[128,1024]{1,0:T(8,128)(2,1)} %copy-done.17), channel_id=1, source_target_pairs={{0,24},{4,28},{8,16},{12,20},{16,8},{20,12},{24,0},{28,4},{1,25},{... | collective-permute-start | bytes 786440 | tf_op jit(solution)/shard_map/ppermute | solution.py:134
  68.2 9.8 %copy-start.30 = (bf16[1,12,1024]{2,1,0:T(8,128)(2,1)S(1)}, bf16[1,12,1024]{2,1,0:T(8,128)(2,1)}, u32[]{:S(2)}) copy-start(bf16[1,12,1024]{2,1,0:T(8,128)(2,1)} %stack_reshape.6) | copy-start | bytes 73732
  68.2 9.8 %copy-start.2 = (bf16[512,1280]{1,0:T(8,128)(2,1)S(1)}, bf16[512,1280]{1,0:T(8,128)(2,1)}, u32[]{:S(2)}) copy-start(bf16[512,1280]{1,0:T(8,128)(2,1)} %copy-done.1) | copy-start | bytes 3932164
  71.9 6.1 %copy-start.11 = (bf16[128,1024]{1,0:T(8,128)(2,1)}, bf16[128,1024]{1,0:T(8,128)(2,1)S(1)}, u32[]{:S(2)}) copy-start(bf16[128,1024]{1,0:T(8,128)(2,1)S(1)} %get-tuple-element.39) | copy-start | bytes 786436
  71.9 27.7 %collective-permute-start.18 = (bf16[128,1024]{1,0:T(8,128)(2,1)}, bf16[128,1024]{1,0:T(8,128)(2,1)}, u32[]{:S(2)}, u32[]{:S(2)}) collective-permute-start(bf16[128,1024]{1,0:T(8,128)(2,1)} %get-tuple-element.49), channel_id=1, source_target_pairs={{0,16},{4,20},{8,24},{12,28},{16,0},{20,4},{24,8},{28,12},{1,17},{... | collective-permute-start | bytes 786440 | tf_op jit(solution)/shard_map/ppermute | solution.py:134
  73.8 27.1 %collective-permute-start.19 = (bf16[128,1024]{1,0:T(8,128)(2,1)}, bf16[128,1024]{1,0:T(8,128)(2,1)}, u32[]{:S(2)}, u32[]{:S(2)}) collective-permute-start(bf16[128,1024]{1,0:T(8,128)(2,1)} %get-tuple-element.50), channel_id=1, source_target_pairs={{0,24},{4,28},{8,16},{12,20},{16,8},{20,12},{24,0},{28,4},{1,25},{... | collective-permute-start | bytes 786440 | tf_op jit(solution)/shard_map/ppermute | solution.py:134
  76.8 25.5 %collective-permute-start.17 = (bf16[256,1024]{1,0:T(8,128)(2,1)}, bf16[256,1024]{1,0:T(8,128)(2,1)}, u32[]{:S(2)}, u32[]{:S(2)}) collective-permute-start(bf16[256,1024]{1,0:T(8,128)(2,1)} %pad_maximum_fusion.2), channel_id=1, source_target_pairs={{0,8},{4,12},{8,0},{12,4},{16,24},{20,28},{24,16},{28,20},{1,9},{5... | collective-permute-start | bytes 1572872 | tf_op jit(solution)/shard_map/ppermute | solution.py:134
  80.7 0.9 copy-start.3
  87.1 12.5 %copy-start.19 = (bf16[256,512]{1,0:T(8,128)(2,1)S(1)}, bf16[256,512]{1,0:T(8,128)(2,1)}, u32[]{:S(2)}) copy-start(bf16[256,512]{1,0:T(8,128)(2,1)} %copy-done.18) | copy-start | bytes 786436
  87.1 15.1 %copy-start.6 = (bf16[128,1024]{1,0:T(8,128)(2,1)S(1)}, bf16[128,1024]{1,0:T(8,128)(2,1)}, u32[]{:S(2)}) copy-start(bf16[128,1024]{1,0:T(8,128)(2,1)} %copy-done.5) | copy-start | bytes 786436
  87.1 15.2 %copy-start.12 = (bf16[128,1024]{1,0:T(8,128)(2,1)S(1)}, bf16[128,1024]{1,0:T(8,128)(2,1)}, u32[]{:S(2)}) copy-start(bf16[128,1024]{1,0:T(8,128)(2,1)} %copy-done.11) | copy-start | bytes 786436
  87.2 27.5 %collective-permute-start.21 = (bf16[768,512]{1,0:T(8,128)(2,1)}, bf16[768,512]{1,0:T(8,128)(2,1)}, u32[]{:S(2)}, u32[]{:S(2)}) collective-permute-start(bf16[768,512]{1,0:T(8,128)(2,1)} %copy-done.3), channel_id=1, source_target_pairs={{0,8},{4,12},{24,16},{28,20},{1,9},{5,13},{25,17},{29,21},{2,10},{... | collective-permute-start | bytes 2359304 | tf_op jit(solution)/shard_map/ppermute | solution.py:151
  95.9 8.1 %copy-start.36 = (f32[1024]{0:T(1024)S(1)}, f32[1024]{0:T(1024)}, u32[]{:S(2)}) copy-start(f32[1024]{0:T(1024)} %slice_convert_fusion.2) | copy-start | bytes 12292
  96.0 35.7 %collective-permute-start.14 = (bf16[816,512]{1,0:T(8,128)(2,1)S(1)}, bf16[816,512]{1,0:T(8,128)(2,1)S(1)}, u32[]{:S(2)}, u32[]{:S(2)}) collective-permute-start(bf16[816,512]{1,0:T(8,128)(2,1)S(1)} %pad_maximum_fusion.1), channel_id=1, source_target_pairs={{0,8},{4,12},{24,16},{28,20},{1,9},{5,13},{25,17},{29,21},{2,10},{... | collective-permute-start | bytes 2506760 | tf_op jit(solution)/shard_map/ppermute | solution.py:151
  99.6 35.6 %collective-permute-start.20 = (bf16[256,512]{1,0:T(8,128)(2,1)S(1)}, bf16[256,512]{1,0:T(8,128)(2,1)S(1)}, u32[]{:S(2)}, u32[]{:S(2)}) collective-permute-start(bf16[256,512]{1,0:T(8,128)(2,1)S(1)} %copy-done.19), channel_id=1, source_target_pairs={{8,0},{12,4},{16,24},{20,28},{9,1},{13,5},{17,25},{21,29},{10,2},{... | collective-permute-start | bytes 786440 | tf_op jit(solution)/shard_map/ppermute | solution.py:152
  100.9 30.9 %collective-permute-start.13 = (bf16[304,512]{1,0:T(8,128)(2,1)}, bf16[304,512]{1,0:T(8,128)(2,1)S(1)}, u32[]{:S(2)}, u32[]{:S(2)}) collective-permute-start(bf16[304,512]{1,0:T(8,128)(2,1)} %pad_maximum_fusion.7), channel_id=1, source_target_pairs={{8,0},{12,4},{16,24},{20,28},{9,1},{13,5},{17,25},{21,29},{10,2},{... | collective-permute-start | bytes 933896 | tf_op jit(solution)/shard_map/ppermute | solution.py:152
  104.0 10.6 %copy-start.4 = (bf16[768,512]{1,0:T(8,128)(2,1)S(1)}, bf16[768,512]{1,0:T(8,128)(2,1)}, u32[]{:S(2)}) copy-start(bf16[768,512]{1,0:T(8,128)(2,1)} %copy-done.3) | copy-start | bytes 2359300
  107.0 27.8 %copy-start.20 = (bf16[2048,1024]{1,0:T(8,128)(2,1)S(1)}, bf16[2048,1024]{1,0:T(8,128)(2,1)}, u32[]{:S(2)}) copy-start(bf16[2048,1024]{1,0:T(8,128)(2,1)} %param.14) | copy-start | bytes 12582916
  115.8 19.5 %collective-permute-start.22 = (bf16[256,512]{1,0:T(8,128)(2,1)S(1)}, bf16[256,512]{1,0:T(8,128)(2,1)S(1)}, u32[]{:S(2)}, u32[]{:S(2)}) collective-permute-start(bf16[256,512]{1,0:T(8,128)(2,1)S(1)} %get-tuple-element.70), channel_id=1, source_target_pairs={{8,24},{12,28},{16,0},{20,4},{9,25},{13,29},{17,1},{21,5},{10,26},... | collective-permute-start | bytes 786440 | tf_op jit(solution)/shard_map/ppermute | solution.py:170
  117.1 18.2 %collective-permute-start.23 = (bf16[256,512]{1,0:T(8,128)(2,1)S(1)}, bf16[256,512]{1,0:T(8,128)(2,1)S(1)}, u32[]{:S(2)}, u32[]{:S(2)}) collective-permute-start(bf16[256,512]{1,0:T(8,128)(2,1)S(1)} %get-tuple-element.71), channel_id=1, source_target_pairs={{8,16},{12,20},{16,8},{20,12},{9,17},{13,21},{17,9},{21,13},{10,18... | collective-permute-start | bytes 786440 | tf_op jit(solution)/shard_map/ppermute | solution.py:172
  132.6 2.7 %copy-start.10 = (bf16[256,512]{1,0:T(8,128)(2,1)S(1)}, bf16[256,512]{1,0:T(8,128)(2,1)}, u32[]{:S(2)}) copy-start(bf16[256,512]{1,0:T(8,128)(2,1)} %copy-done.9) | copy-start | bytes 786436
  132.6 14.2 %collective-permute-start.15 = (bf16[352,512]{1,0:T(8,128)(2,1)S(1)}, bf16[352,512]{1,0:T(8,128)(2,1)S(1)}, u32[]{:S(2)}, u32[]{:S(2)}) collective-permute-start(bf16[352,512]{1,0:T(8,128)(2,1)S(1)} %get-tuple-element.86), channel_id=1, source_target_pairs={{8,24},{12,28},{16,0},{20,4},{9,25},{13,29},{17,1},{21,5},{10,26},... | collective-permute-start | bytes 1081352 | tf_op jit(solution)/shard_map/ppermute | solution.py:170
  134.0 12.8 %collective-permute-start.16 = (bf16[352,512]{1,0:T(8,128)(2,1)S(1)}, bf16[352,512]{1,0:T(8,128)(2,1)S(1)}, u32[]{:S(2)}, u32[]{:S(2)}) collective-permute-start(bf16[352,512]{1,0:T(8,128)(2,1)S(1)} %get-tuple-element.87), channel_id=1, source_target_pairs={{8,16},{12,20},{16,8},{20,12},{9,17},{13,21},{17,9},{21,13},{10,18... | collective-permute-start | bytes 1081352 | tf_op jit(solution)/shard_map/ppermute | solution.py:172
  134.7 12.8 %copy-start.29 = (bf16[1,48,512]{2,1,0:T(8,128)(2,1)S(1)}, bf16[1,48,512]{2,1,0:T(8,128)(2,1)}, u32[]{:S(2)}) copy-start(bf16[1,48,512]{2,1,0:T(8,128)(2,1)} %stack_reshape.7) | copy-start | bytes 147460
  135.2 14.4 %copy-start.8 = (bf16[256,512]{1,0:T(8,128)(2,1)S(1)}, bf16[256,512]{1,0:T(8,128)(2,1)}, u32[]{:S(2)}) copy-start(bf16[256,512]{1,0:T(8,128)(2,1)} %copy-done.7) | copy-start | bytes 786436
  135.2 15.8 %copy-start.23 = (f32[128,1024]{1,0:T(8,128)S(1)}, f32[128,1024]{1,0:T(8,128)}, u32[]{:S(2)}) copy-start(f32[128,1024]{1,0:T(8,128)} %fusion.2) | copy-start | bytes 1572868
  135.2 15.8 %copy-start.32 = (f32[512]{0:T(512)S(1)}, f32[512]{0:T(512)}, u32[]{:S(2)}) copy-start(f32[512]{0:T(512)} %get-tuple-element.89) | copy-start | bytes 6148
  147.7 1.8 copy-start.21
  150.9 5.0 %collective-permute-start.26 = (f32[256]{0:T(256)S(1)}, f32[256]{0:T(256)S(1)}, u32[]{:S(2)}, u32[]{:S(2)}) collective-permute-start(f32[256]{0:T(256)S(1)} %fusion.48), channel_id=1, source_target_pairs={{0,1},{1,0},{2,3},{3,2},{4,5},{5,4},{6,7},{7,6},{8,9},{9,8},{10,11... | collective-permute-start | bytes 3080 | tf_op jit(solution)/shard_map/ppermute | solution.py:23
  154.4 19.7 %copy-start.38 = (s32[4]{0:T(128)S(1)}, s32[4]{0:T(128)}, u32[]{:S(2)}) copy-start(s32[4]{0:T(128)} %param.18) | copy-start | bytes 52
  154.5 19.7 %copy-start.27 = (pred[4,128,1]{2,1,0:T(8,128)(4,1)S(1)}, pred[4,128,1]{2,1,0:T(8,128)(4,1)}, u32[]{:S(2)}) copy-start(pred[4,128,1]{2,1,0:T(8,128)(4,1)} %broadcast_in_dim.28) | copy-start | bytes 1540
  154.5 19.7 %copy-start.34 = (s32[128]{0:T(128)S(1)}, s32[128]{0:T(128)}, u32[]{:S(2)}) copy-start(s32[128]{0:T(128)} %copy-done.33) | copy-start | bytes 1540
  155.2 1.9 collective-permute-start.24
  155.8 27.0 %copy-start.14 = (s32[256,1]{1,0:T(8,128)S(1)}, s32[256,1]{1,0:T(8,128)}, u32[]{:S(2)}) copy-start(s32[256,1]{1,0:T(8,128)} %add.378.all_ref) | copy-start | bytes 3076
  155.8 27.0 %copy-start.15 = (bf16[4,128,1024]{2,1,0:T(8,128)(2,1)S(1)}, bf16[4,128,1024]{2,1,0:T(8,128)(2,1)}, u32[]{:S(2)}) copy-start(bf16[4,128,1024]{2,1,0:T(8,128)(2,1)} %query_ref.1) | copy-start | bytes 3145732
  155.8 27.0 %copy-start.16 = (bf16[4,128,256]{2,1,0:T(8,128)(2,1)S(1)}, bf16[4,128,256]{2,1,0:T(8,128)(2,1)}, u32[]{:S(2)}) copy-start(bf16[4,128,256]{2,1,0:T(8,128)(2,1)} %text_ref.1) | copy-start | bytes 786436
  155.8 19.4 %copy-start.22 = (bf16[8,48,256]{2,1,0:T(8,128)(2,1)S(1)}, bf16[8,48,256]{2,1,0:T(8,128)(2,1)}, u32[]{:S(2)}) copy-start(bf16[8,48,256]{2,1,0:T(8,128)(2,1)} %copy-done.21) | copy-start | bytes 589828
  156.0 3.6 %collective-permute-start.27 = (f32[256]{0:T(256)S(1)}, f32[256]{0:T(256)S(1)}, u32[]{:S(2)}, u32[]{:S(2)}) collective-permute-start(f32[256]{0:T(256)S(1)} %add.353), channel_id=1, source_target_pairs={{0,2},{1,3},{2,0},{3,1},{4,6},{5,7},{6,4},{7,5},{8,10},{9,11},{10,... | collective-permute-start | bytes 3080 | tf_op jit(solution)/shard_map/ppermute | solution.py:23
  157.2 5.8 %collective-permute-start.25 = (bf16[1,256,256]{2,1,0:T(8,128)(2,1)S(1)}, bf16[1,256,256]{2,1,0:T(8,128)(2,1)S(1)}, u32[]{:S(2)}, u32[]{:S(2)}) collective-permute-start(bf16[1,256,256]{2,1,0:T(8,128)(2,1)S(1)} %dynamic-slice_convert_fusion), channel_id=1, source_target_pairs={{0,2},{1,3},{2,0},{3,1},{4,6},{5,7},{6,4},{7,5},{8,10},{9,11},{10,... | collective-permute-start | bytes 393224 | tf_op jit(solution)/shard_map/ppermute | solution.py:23
  164.0 18.8 %all-to-all-start = ((bf16[8,64,256]{2,1,0:T(8,128)(2,1)}), bf16[8,64,256]{2,1,0:T(8,128)(2,1)S(1)}, u32[]{:S(2)}, u32[]{:S(2)}) async-start(bf16[8,64,256]{2,1,0:T(8,128)(2,1)} %bitcast.17), calls=%async_computation | async-start | bytes 524288 | tf_op jit(solution)/shard_map/all_to_all | solution.py:481
  (7 other events, 5.0 us)

commit v6 on v1

--- a/solution.py
+++ b/solution.py
@@ -83,8 +83,8 @@
     )(scalars, *held)
 
 
-def partial_kernel(halves, *refs):
-    rows_refs, weights_refs, out_refs = refs[:halves], refs[halves:-4], refs[-4:]
+def partial_kernel(halves, riding, *refs):
+    rows_refs, weights_refs, out_refs = refs[:halves], refs[halves : -4 - riding], refs[-4:]
     weights = jnp.concatenate([ref[...] for ref in weights_refs], axis=0)
     for half, rows_ref in enumerate(rows_refs):
         total = jnp.dot(rows_ref[...], weights, preferred_element_type=jnp.float32)
@@ -92,9 +92,12 @@
         rows = total.shape[0] // 4
         for k, out_ref in enumerate(out_refs):
             out_ref[half * rows : (half + 1) * rows] = total[k * rows : (k + 1) * rows]
-
-
-def partial_products(held, weights, count):
+    if riding:
+        for out_ref in out_refs[1:]:
+            out_ref[halves * rows :] = refs[-5][...]
+
+
+def partial_products(held, weights, count, riding):
     halves = len(held)
     rows, depth = held[0].shape
     tile = min(count, 512)
@@ -102,17 +105,18 @@
     def block(used, first):
         return pl.BlockSpec((used, tile), lambda i: (0, i + first // tile))
 
-    out = halves * rows // 4
+    outs = [halves * rows // 4 + (sum(r.shape[0] for r in riding) if k else 0) for k in range(4)]
     return pl.pallas_call(
-        functools.partial(partial_kernel, halves),
+        functools.partial(partial_kernel, halves, len(riding)),
         grid=(count // tile,),
         in_specs=[pl.BlockSpec((rows, depth), lambda i: (0, 0))] * halves
-        + [block(used, first) for _, used, first in weights],
-        out_specs=[pl.BlockSpec((out, tile), lambda i: (0, i))] * 4,
-        out_shape=[jax.ShapeDtypeStruct((out, count), jnp.bfloat16)] * 4,
+        + [block(used, first) for _, used, first in weights]
+        + [block(r.shape[0], 0) for r in riding],
+        out_specs=[pl.BlockSpec((out, tile), lambda i: (0, i)) for out in outs],
+        out_shape=[jax.ShapeDtypeStruct((out, count), jnp.bfloat16) for out in outs],
         compiler_params=pltpu.CompilerParams(vmem_limit_bytes=VMEM),
         cost_estimate=pl.CostEstimate(flops=0, bytes_accessed=2 * count, transcendentals=0),
-    )(*held, *[array for array, _, _ in weights])
+    )(*held, *[array for array, _, _ in weights], *riding)
 
 
 def along(pairs):
@@ -120,13 +124,9 @@
     return [(a * width + i, b * width + i) for a, b in pairs for i in range(width)]
 
 
-def ride(value, extra):
-    return jnp.concatenate([value] + extra, axis=0) if extra else value
-
-
-def send_direct(parts, small):
+def send_direct(parts):
     return [
-        lax.ppermute(ride(part, small), "seq", along([(a, a ^ k) for a in range(4)]))
+        lax.ppermute(part, "seq", along([(a, a ^ k) for a in range(4)]))
         for k, part in enumerate(parts[1:], 1)
     ]
 
@@ -217,11 +217,11 @@
             parts += [other[: w_merge.shape[0]] for other in received[side]]
             parts = jnp.concatenate(parts, axis=0)
             operands = [(jnp.roll(parts, member * w_merge.shape[0], axis=0), depth, inside)]
-        parts = partial_products([held[h] for h in halves], operands, count)
+        parts = partial_products([held[h] for h in halves], operands, count, riding)
         if step:
             before = [sent[step - 1][1][1]] + ([sent[step - 2][1][2]] if step >= 2 else [])
             parts, _ = lax.optimization_barrier((parts, before))
-        sent.append((parts, send_direct(parts, riding)))
+        sent.append((parts, send_direct(parts)))
     for step in range(len(PLAN)):
         finish(step)
     rows = sent[RIDE][0][0].shape[0]
@@ -233,14 +233,23 @@
 def scatter_heads(kv, squares):
     tp_count = lax.axis_size("tp")
     place = lax.axis_index("tp")
-    rows = kv.shape[0]
-    blocks = jnp.stack(jnp.split(kv, tp_count, axis=1))
+    width = kv.shape[1] // tp_count
+    blocks = None
     for bit in bits_of(tp_count):
-        paired = blocks.reshape(blocks.shape[0] // 2, 2, rows, blocks.shape[2])
         mine = (place // bit) % 2
-        keep = lax.dynamic_index_in_dim(paired, mine, 1, keepdims=False)
-        give = lax.dynamic_index_in_dim(paired, 1 - mine, 1, keepdims=False)
-        blocks = keep + flip(give.astype(jnp.bfloat16), "tp", bit).astype(jnp.float32)
+
+        def half(which):
+            if blocks is not None:
+                paired = blocks.reshape((-1, 2) + blocks.shape[1:])
+                return lax.dynamic_index_in_dim(paired, which, 1, keepdims=False)
+            columns = [
+                lax.dynamic_slice_in_dim(kv, (2 * i + which) * width, width, axis=1)
+                for i in range(tp_count // 2)
+            ]
+            return jnp.stack(columns)
+
+        arrived = flip(half(1 - mine).astype(jnp.bfloat16), "tp", bit)
+        blocks = half(mine) + arrived.astype(jnp.float32)
         squares = squares + flip(squares, "tp", bit)
     return blocks[0], squares
 

time: 183 us -> 184 us (level)
  waiting for transfers between devices: 75.1 us -> 68.8 us
  local copies, waits for them, and re-layouts: 13.9 us -> 17.4 us
  starting transfers between devices: 55.6 us -> 58.4 us
    ppermute x2, waiting for transfers between devices: 5.47 us -> 0.01 us  [merge_tiles(): others.append(lax.ppermute(own, 'seq', pairs))]
    ppermute x11, starting transfers between devices: 14.5 us -> 19.3 us  [flip(): return lax.ppermute(value, axis, [(i, i ^ bit) for i in range(count)])]
    ppermute x9, starting transfers between devices: 20 us -> 16.2 us  [send_direct(): lax.ppermute(part, 'seq', along([(a, a ^ k) for a in range(4)]))]
    unnamed x68 -> x74, local copies, waits for them, and re-layouts: 2.49 us -> 4.84 us
  transfers between devices with their start and end apart: 25 -> 25, of which waited for: 11 -> 9; matrix products, arithmetic and copies ran while one was open for 13% -> 13% of each run, Pallas kernels for 8% -> 9%
where the time goes in v6:
time: 184 us; the launch traced here: 183 us
  waiting for transfers between devices  68.8 us (37%)
  starting transfers between devices  58.4 us (32%)
  Pallas kernels  21.5 us (12%)
  local copies, waits for them, and re-layouts  17.4 us (9%)
  other arithmetic  11.4 us (6%)
  matrix products  4.55 us (2%)
    ppermute x9, waiting for transfers between devices, send_direct(): lax.ppermute(part, 'seq', along([(a, a ^ k) for a in range(4)]))  42.5 us
    ppermute x11, starting transfers between devices, flip(): return lax.ppermute(value, axis, [(i, i ^ bit) for i in range(count)])  19.3 us
    ppermute x11, waiting for transfers between devices, flip(): return lax.ppermute(value, axis, [(i, i ^ bit) for i in range(count)])  17.9 us
    ppermute x9, starting transfers between devices, send_direct(): lax.ppermute(part, 'seq', along([(a, a ^ k) for a in range(4)]))  16.2 us
    all_to_all x1, starting transfers between devices, shards(): lax.all_to_all(outgoing, 'seq', split_axis=0, concat_axis=0, tiled=True)  14.7 us
    pallas_call x3, Pallas kernels, partial_products(): pl.pallas_call(functools.partial(partial_kernel, halves, len(riding)), gr...  12.6 us
    all_to_all x1, waiting for transfers between devices, shards(): lax.all_to_all(outgoing, 'seq', split_axis=0, concat_axis=0, tiled=True)  8.35 us
    pallas_call x1, Pallas kernels, attend(): pl.pallas_call(attend_kernel, grid_spec=pltpu.PrefetchScalarGridSpec(num_...  5.5 us
  transfers between devices with their start and end apart: 25, of which 9 were waited for; matrix products, arithmetic and copies ran while one was open for 13% of the time, Pallas kernels for 9%

profile of v6, /device:TPU:0, one launch (start us, length us, event | category | flops | bytes accessed | tf_op | source)
XLA Modules:
  0.0 183.4 jit_solution(10153499355861015419)
XLA Ops:
  0.6 1.1 slice_bitcast_fusion.1
  1.7 3.0 %collective-permute-start = (bf16[128,1280]{1,0:T(8,128)(2,1)S(1)}, bf16[128,1280]{1,0:T(8,128)(2,1)S(1)}, u32[]{:S(2)}, u32[]{:S(2)}) collective-permute-start(bf16[128,1280]{1,0:T(8,128)(2,1)S(1)} %get-tuple-element.62), channel_id=1, source_target_pairs={{0,2},{1,3},{2,0},{3,1},{4,6},{5,7},{6,4},{7,5},{8,10},{9,11},{10,... | collective-permute-start | bytes 983048 | tf_op jit(solution)/shard_map/ppermute | solution.py:23
  4.8 0.8 collective-permute-start.3
  5.6 3.5 %fusion.57 = (bf16[640,1024]{1,0:T(8,128)(2,1)}, bf16[640,1024]{1,0:T(8,128)(2,1)}) fusion(bf16[640,2048]{1,0:T(8,128)(2,1)} %refs_2_.1), kind=kLoop, calls=%fused_computation.133 | loop fusion | bytes 5242880 | tf_op jit(solution)/shard_map/slice | solution.py:163
  9.1 1.5 collective-permute-start.7
  10.8 0.5 fusion.55
  11.6 0.8 gather_fusion.2
  12.7 6.1 %collective-permute-done = bf16[128,1280]{1,0:T(8,128)(2,1)S(1)} collective-permute-done((bf16[128,1280]{1,0:T(8,128)(2,1)S(1)}, bf16[128,1280]{1,0:T(8,128)(2,1)S(1)}, u32[]{:S(2)}, u32[]{:S(2)}) %collective-permute-start) | collective-permute-done | bytes 327712 | tf_op jit(solution)/shard_map/ppermute | solution.py:23
  18.8 2.5 %collective-permute-start.4 = (bf16[128,1280]{1,0:T(8,128)(2,1)S(1)}, bf16[128,1280]{1,0:T(8,128)(2,1)}, u32[]{:S(2)}, u32[]{:S(2)}) collective-permute-start(bf16[128,1280]{1,0:T(8,128)(2,1)S(1)} %collective-permute-done.3.refs_0_), channel_id=1, source_target_pairs={{0,2},{1,3},{2,0},{3,1},{4,6},{5,7},{6,4},{7,5},{8,10},{9,11},{10,... | collective-permute-start | bytes 983048 | tf_op jit(solution)/shard_map/ppermute | solution.py:23
  21.3 2.6 %pad_maximum_fusion = bf16[656,1024]{1,0:T(8,128)(2,1)} fusion(bf16[16,1024]{1,0:T(8,128)(2,1)S(1)} %reshape.336, bf16[640,1024]{1,0:T(8,128)(2,1)} %get-tuple-element.56), kind=kLoop, calls=%fused_computation.17 | loop fusion | flops 2686976 | bytes 2686976 | tf_op jit(solution)/shard_map/concatenate | solution.py:165
  23.9 1.5 collective-permute-start.1
  25.6 0.6 broadcast_in_dim.24
  26.1 0.6 add.329
  27.0 0.5 copy-done.12
  27.5 2.2 %collective-permute-start.5 = (bf16[128,1280]{1,0:T(8,128)(2,1)S(1)}, bf16[128,1280]{1,0:T(8,128)(2,1)S(1)}, u32[]{:S(2)}, u32[]{:S(2)}) collective-permute-start(bf16[128,1280]{1,0:T(8,128)(2,1)S(1)} %collective-permute-done.3.refs_0_), channel_id=1, source_target_pairs={{0,1},{1,0},{2,3},{3,2},{4,5},{5,4},{6,7},{7,6},{8,9},{9,8},{10,11... | collective-permute-start | bytes 983048 | tf_op jit(solution)/shard_map/ppermute | solution.py:23
  29.7 4.5 %collective-permute-start.2 = (bf16[128,1280]{1,0:T(8,128)(2,1)}, bf16[128,1280]{1,0:T(8,128)(2,1)S(1)}, u32[]{:S(2)}, u32[]{:S(2)}) collective-permute-start(bf16[128,1280]{1,0:T(8,128)(2,1)} %copy-done.34), channel_id=1, source_target_pairs={{2,0},{3,10},{0,16},{1,26},{6,4},{7,14},{4,20},{5,30},{10,2},{11,8... | collective-permute-start | bytes 983048 | tf_op jit(solution)/shard_map/ppermute | solution.py:37
  34.2 3.5 %collective-permute-start.6 = (bf16[128,1280]{1,0:T(8,128)(2,1)}, bf16[128,1280]{1,0:T(8,128)(2,1)S(1)}, u32[]{:S(2)}, u32[]{:S(2)}) collective-permute-start(bf16[128,1280]{1,0:T(8,128)(2,1)} %collective-permute-done.4.refs_1_), channel_id=1, source_target_pairs={{0,1},{1,0},{2,3},{3,2},{4,5},{5,4},{6,7},{7,6},{8,9},{9,8},{10,11... | collective-permute-start | bytes 983048 | tf_op jit(solution)/shard_map/ppermute | solution.py:23
  37.7 0.6 slice_convert_fusion.3
  38.3 0.9 collective-permute-done.6.refs_3_
  39.2 1.6 shard_map.122.refs_0_
  40.8 3.9 %shard_map.123 = (bf16[128,1024]{1,0:T(8,128)(2,1)S(1)}, bf16[128,1024]{1,0:T(8,128)(2,1)S(1)}, bf16[128,1024]{1,0:T(8,128)(2,1)}, bf16[128,1024]{1,0:T(8,128)(2,1)S(1)}) custom-call(bf16[512,1280]{1,0:T(8,128)(2,1)S(1)} %shard_map.122.refs_0_, bf16[640,2048]{1,0:T(8,128)(2,1)S(1)} %copy-done, bf16[640,1024]{1,0:T(8,128)(2,1)} %collective-permute-done.7.refs_2_), custom_call_target="tpu_custom_call" | custom-call | bytes 2048 | tf_op jit(solution)/shard_map/pallas_call | solution.py:109
  44.8 0.7 copy-done.9
  45.5 5.1 %collective-permute-start.8 = (bf16[128,1280]{1,0:T(8,128)(2,1)S(1)}, bf16[128,1280]{1,0:T(8,128)(2,1)S(1)}, u32[]{:S(2)}, u32[]{:S(2)}) collective-permute-start(bf16[128,1280]{1,0:T(8,128)(2,1)S(1)} %collective-permute-done.2.refs_0_), channel_id=1, source_target_pairs={{0,2},{1,3},{2,0},{3,1},{4,6},{5,7},{6,4},{7,5},{8,10},{9,11},{10,... | collective-permute-start | bytes 983048 | tf_op jit(solution)/shard_map/ppermute | solution.py:23
  50.7 0.7 add_add_fusion
  51.4 0.7 collective-permute-start.11
  52.1 6.6 %collective-permute-done.8.refs_1_ = bf16[128,1280]{1,0:T(8,128)(2,1)S(1)} collective-permute-done((bf16[128,1280]{1,0:T(8,128)(2,1)S(1)}, bf16[128,1280]{1,0:T(8,128)(2,1)S(1)}, u32[]{:S(2)}, u32[]{:S(2)}) %collective-permute-start.8) | collective-permute-done | bytes 327712 | tf_op jit(solution)/shard_map/ppermute | solution.py:23
  58.7 1.4 stack_reshape.6
  60.1 1.3 iota_add_fusion.1
  61.4 0.7 collective-permute-start.13
  62.1 1.7 shard_map.124.refs_0_.refs_1_
  63.8 3.7 %shard_map.125 = (bf16[128,1024]{1,0:T(8,128)(2,1)S(1)}, bf16[128,1024]{1,0:T(8,128)(2,1)}, bf16[128,1024]{1,0:T(8,128)(2,1)S(1)}, bf16[128,1024]{1,0:T(8,128)(2,1)}) custom-call(bf16[512,1280]{1,0:T(8,128)(2,1)S(1)} %shard_map.124.refs_0_.refs_1_, bf16[640,2048]{1,0:T(8,128)(2,1)S(1)} %copy-done, bf16[640,1024]{1,0:T(8,128)(2,1)} %collective-permute-done.7.refs_2_), custom_call_target="tpu_custom_call" | custom-call | bytes 2048 | tf_op jit(solution)/shard_map/pallas_call | solution.py:109
  67.6 0.7 copy-done.3
  68.2 3.7 %collective-permute-start.12 = (bf16[128,1024]{1,0:T(8,128)(2,1)S(1)}, bf16[128,1024]{1,0:T(8,128)(2,1)S(1)}, u32[]{:S(2)}, u32[]{:S(2)}) collective-permute-start(bf16[128,1024]{1,0:T(8,128)(2,1)S(1)} %get-tuple-element.41), channel_id=1, source_target_pairs={{0,16},{4,20},{8,24},{12,28},{16,0},{20,4},{24,8},{28,12},{1,17},{... | collective-permute-start | bytes 786440 | tf_op jit(solution)/shard_map/ppermute | solution.py:129
  71.9 2.9 %collective-permute-start.18 = (bf16[128,1024]{1,0:T(8,128)(2,1)}, bf16[128,1024]{1,0:T(8,128)(2,1)}, u32[]{:S(2)}, u32[]{:S(2)}) collective-permute-start(bf16[128,1024]{1,0:T(8,128)(2,1)} %get-tuple-element.48), channel_id=1, source_target_pairs={{0,8},{4,12},{8,0},{12,4},{16,24},{20,28},{24,16},{28,20},{1,9},{5... | collective-permute-start | bytes 786440 | tf_op jit(solution)/shard_map/ppermute | solution.py:129
  74.8 0.8 slice_bitcast_fusion.5
  75.6 5.0 %shard_map.126 = (bf16[256,1024]{1,0:T(8,128)(2,1)S(1)}, bf16[288,1024]{1,0:T(8,128)(2,1)}, bf16[288,1024]{1,0:T(8,128)(2,1)S(1)}, bf16[288,1024]{1,0:T(8,128)(2,1)S(1)}) custom-call(bf16[512,1280]{1,0:T(8,128)(2,1)S(1)} %copy-done.2, bf16[512,1280]{1,0:T(8,128)(2,1)S(1)} %shard_map.124.refs_0_.refs_1_, bf16[640,2048]{1,0:T(8,128)(2,1)S(1)} %copy-done, ...), custom_call_target="tpu_custom_call" | custom-call | bytes 2048 | tf_op jit(solution)/shard_map/pallas_call | solution.py:109
  80.6 0.8 copy-done.6
  81.5 0.8 copy-done.7
  82.3 6.7 %collective-permute-done.12 = bf16[128,1024]{1,0:T(8,128)(2,1)S(1)} collective-permute-done((bf16[128,1024]{1,0:T(8,128)(2,1)S(1)}, bf16[128,1024]{1,0:T(8,128)(2,1)S(1)}, u32[]{:S(2)}, u32[]{:S(2)}) %collective-permute-start.12) | collective-permute-done | bytes 262176 | tf_op jit(solution)/shard_map/ppermute | solution.py:129
  89.0 0.7 copy-done.16
  89.7 4.7 %collective-permute-start.14 = (bf16[288,1024]{1,0:T(8,128)(2,1)}, bf16[288,1024]{1,0:T(8,128)(2,1)S(1)}, u32[]{:S(2)}, u32[]{:S(2)}) collective-permute-start(bf16[288,1024]{1,0:T(8,128)(2,1)} %get-tuple-element.43), channel_id=1, source_target_pairs={{0,8},{4,12},{8,0},{12,4},{16,24},{20,28},{24,16},{28,20},{1,9},{5... | collective-permute-start | bytes 1769480 | tf_op jit(solution)/shard_map/ppermute | solution.py:129
  94.5 0.8 broadcast_in_dim.28
  95.3 0.9 add.341
  96.3 3.4 %collective-permute-start.15 = (bf16[288,1024]{1,0:T(8,128)(2,1)}, bf16[288,1024]{1,0:T(8,128)(2,1)S(1)}, u32[]{:S(2)}, u32[]{:S(2)}) collective-permute-start(bf16[288,1024]{1,0:T(8,128)(2,1)} %copy-done.7), channel_id=1, source_target_pairs={{0,16},{4,20},{8,24},{12,28},{16,0},{20,4},{24,8},{28,12},{1,17},{... | collective-permute-start | bytes 1769480 | tf_op jit(solution)/shard_map/ppermute | solution.py:129
  99.7 2.0 %fusion.15 = (f32[128]{0:T(128)S(1)}, bf16[128,1024]{1,0:T(8,128)(2,1)}) fusion(bf16[128,1024]{1,0:T(8,128)(2,1)} %copy-done.15, bf16[128,1024]{1,0:T(8,128)(2,1)} %collective-permute-done.11, bf16[128,1024]{1,0:T(8,128)(2,1)} %collective-permute-done.17, bf16[128,1024]{1,0:T(8,128)(2,1)S(1)} %get-tuple-element.28), kind=kLoop, calls=%fused_computation.31 | loop fusion | flops 1441664 | bytes 1311232 | tf_op jit(solution)/shard_map/reduce_sum | solution.py:194
  101.7 1.9 %fusion.17 = (f32[128]{0:T(128)S(1)}, bf16[128,1024]{1,0:T(8,128)(2,1)}) fusion(bf16[128,1024]{1,0:T(8,128)(2,1)} %collective-permute-done.19, bf16[128,1024]{1,0:T(8,128)(2,1)S(1)} %copy-done.17, bf16[128,1024]{1,0:T(8,128)(2,1)} %collective-permute-done.18, bf16[128,1024]{1,0:T(8,128)(2,1)S(1)} %copy-done.4), kind=kLoop, calls=%fused_computation.33 | loop fusion | flops 1441664 | bytes 1311232 | tf_op jit(solution)/shard_map/reduce_sum | solution.py:194
  103.7 15.1 %collective-permute-done.14 = bf16[288,1024]{1,0:T(8,128)(2,1)S(1)} collective-permute-done((bf16[288,1024]{1,0:T(8,128)(2,1)}, bf16[288,1024]{1,0:T(8,128)(2,1)S(1)}, u32[]{:S(2)}, u32[]{:S(2)}) %collective-permute-start.14) | collective-permute-done | bytes 589856 | tf_op jit(solution)/shard_map/ppermute | solution.py:129
  118.8 20.7 %collective-permute-done.15 = bf16[288,1024]{1,0:T(8,128)(2,1)S(1)} collective-permute-done((bf16[288,1024]{1,0:T(8,128)(2,1)}, bf16[288,1024]{1,0:T(8,128)(2,1)S(1)}, u32[]{:S(2)}, u32[]{:S(2)}) %collective-permute-start.15) | collective-permute-done | bytes 589856 | tf_op jit(solution)/shard_map/ppermute | solution.py:129
  139.7 0.6 gather_fusion
  140.3 0.6 gather_fusion.1
  141.3 0.4 fusion.13
  141.9 2.6 %fusion = f32[256,1024]{1,0:T(8,128)S(1)} fusion(bf16[2048,1024]{1,0:T(8,128)(2,1)} %param.14, bf16[256,1024]{1,0:T(8,128)(2,1)S(1)} %get-tuple-element.53, f32[1024]{0:T(1024)S(1)} %copy-done.29), kind=kOutput, calls=%fused_computation.3 | convolution fusion | flops 537657344 | bytes 3674112 | tf_op jit(solution)/shard_map/dot_general | solution.py:195
  144.6 0.5 fusion.9
  145.1 0.4 copy-done.18
  145.5 0.5 fusion.6
  146.1 0.3 collective-permute-start.20
  146.6 1.5 collective-permute-start.23
  148.2 1.1 collective-permute-start.21
  149.3 1.0 collective-permute-done.23
  150.2 3.4 %collective-permute-done.21 = bf16[1,256,256]{2,1,0:T(8,128)(2,1)S(1)} collective-permute-done((bf16[1,256,256]{2,1,0:T(8,128)(2,1)S(1)}, bf16[1,256,256]{2,1,0:T(8,128)(2,1)S(1)}, u32[]{:S(2)}, u32[]{:S(2)}) %collective-permute-start.21) | collective-permute-done | bytes 131104 | tf_op jit(solution)/shard_map/ppermute | solution.py:23
  153.6 1.0 convolution_convert_fusion
  154.6 14.7 %all-to-all-start = ((bf16[8,64,256]{2,1,0:T(8,128)(2,1)}), bf16[8,64,256]{2,1,0:T(8,128)(2,1)S(1)}, u32[]{:S(2)}, u32[]{:S(2)}) async-start(bf16[8,64,256]{2,1,0:T(8,128)(2,1)} %bitcast.19), calls=%async_computation | async-start | bytes 524288 | tf_op jit(solution)/shard_map/all_to_all | solution.py:426
  169.5 8.3 %all-to-all-done = bf16[8,64,256]{2,1,0:T(8,128)(2,1)S(1)} async-done(((bf16[8,64,256]{2,1,0:T(8,128)(2,1)}), bf16[8,64,256]{2,1,0:T(8,128)(2,1)S(1)}, u32[]{:S(2)}, u32[]{:S(2)}) %all-to-all-start) | async-done | bytes 262176 | tf_op jit(solution)/shard_map/all_to_all | solution.py:426
  177.9 5.5 %shard_map.127 = (bf16[4,128,1024]{2,1,0:T(8,128)(2,1)}, bf16[256,256]{1,0:T(8,128)(2,1)}) custom-call(s32[4]{0:T(128)S(1)} %fusion.47.place_ref, bf16[4,128,1024]{2,1,0:T(8,128)(2,1)S(1)} %copy-done.5, bf16[8,32,256]{2,1,0:T(8,128)(2,1)S(1)} %slice.107.prefix_ref, bf16[4,128,256]{2,1,0:T(8,128)(2,1)S(1)} %copy-done.8, bf16[512,256]{1,0:T(8,128)(2,1)S(1)} %bitcast.57, ...), custom_call_target="tpu_custom_call" | custom-call | flops 603979776 | bytes 4194304 | tf_op jit(solution)/shard_map/pallas_call | solution.py:322
  (145 shorter events, 2.7 us)
Async XLA Ops:
  1.7 17.0 %collective-permute-start = (bf16[128,1280]{1,0:T(8,128)(2,1)S(1)}, bf16[128,1280]{1,0:T(8,128)(2,1)S(1)}, u32[]{:S(2)}, u32[]{:S(2)}) collective-permute-start(bf16[128,1280]{1,0:T(8,128)(2,1)S(1)} %get-tuple-element.62), channel_id=1, source_target_pairs={{0,2},{1,3},{2,0},{3,1},{4,6},{5,7},{6,4},{7,5},{8,10},{9,11},{10,... | collective-permute-start | bytes 983048 | tf_op jit(solution)/shard_map/ppermute | solution.py:23
  4.8 5.8 %copy-start.31 = (s32[32,1]{0,1:T(1,128)S(1)}, s32[32,1]{0,1:T(1,128)}, u32[]{:S(2)}) copy-start(s32[32,1]{0,1:T(1,128)} %param.15) | copy-start | bytes 388
  4.8 6.5 %copy-start.36 = (s32[1,4]{1,0:T(1,128)S(1)}, s32[1,4]{1,0:T(1,128)}, u32[]{:S(2)}) copy-start(s32[1,4]{1,0:T(1,128)} %param.17) | copy-start | bytes 52
  4.8 14.0 %collective-permute-start.3 = (bf16[128,1280]{1,0:T(8,128)(2,1)S(1)}, bf16[128,1280]{1,0:T(8,128)(2,1)S(1)}, u32[]{:S(2)}, u32[]{:S(2)}) collective-permute-start(bf16[128,1280]{1,0:T(8,128)(2,1)S(1)} %get-tuple-element.63), channel_id=1, source_target_pairs={{0,0},{1,10},{2,16},{3,26},{4,4},{5,14},{6,20},{7,30},{8,2},{9,8},... | collective-permute-start | bytes 983048 | tf_op jit(solution)/shard_map/ppermute | solution.py:37
  9.1 3.3 %copy-start.35 = (s32[32]{0:T(128)S(1)}, s32[32]{0:T(128)}, u32[]{:S(2)}) copy-start(s32[32]{0:T(128)} %param.16) | copy-start | bytes 388
  9.1 3.5 %copy-start.24 = (bf16[1,32,256]{2,1,0:T(8,128)(2,1)S(1)}, bf16[1,32,256]{2,1,0:T(8,128)(2,1)}, u32[]{:S(2)}) copy-start(bf16[1,32,256]{2,1,0:T(8,128)(2,1)} %param.19) | copy-start | bytes 49156
  9.1 31.7 %collective-permute-start.7 = (bf16[640,1024]{1,0:T(8,128)(2,1)}, bf16[640,1024]{1,0:T(8,128)(2,1)}, u32[]{:S(2)}, u32[]{:S(2)}) collective-permute-start(bf16[640,1024]{1,0:T(8,128)(2,1)} %get-tuple-element.57), channel_id=1, source_target_pairs={{4,0},{0,4},{12,8},{8,12},{20,16},{16,20},{28,24},{24,28},{5,1},{1... | collective-permute-start | bytes 3932168 | tf_op jit(solution)/shard_map/ppermute | solution.py:174
  11.6 26.1 %copy-start.27 = (bf16[2048]{0:T(1024)(128)(2,1)S(1)}, bf16[2048]{0:T(1024)(128)(2,1)}, u32[]{:S(2)}) copy-start(bf16[2048]{0:T(1024)(128)(2,1)} %param.13) | copy-start | bytes 12292
  12.6 8.7 %copy-start.14 = (bf16[64,256]{1,0:T(8,128)(2,1)}, bf16[64,256]{1,0:T(8,128)(2,1)S(1)}, u32[]{:S(2)}) copy-start(bf16[64,256]{1,0:T(8,128)(2,1)S(1)} %pad_maximum_fusion.4) | copy-start | bytes 98308
  18.8 2.5 %copy-start.34 = (bf16[128,1280]{1,0:T(8,128)(2,1)}, bf16[128,1280]{1,0:T(8,128)(2,1)S(1)}, u32[]{:S(2)}) copy-start(bf16[128,1280]{1,0:T(8,128)(2,1)S(1)} %collective-permute-done) | copy-start | bytes 983044
  18.8 15.4 %collective-permute-start.4 = (bf16[128,1280]{1,0:T(8,128)(2,1)S(1)}, bf16[128,1280]{1,0:T(8,128)(2,1)}, u32[]{:S(2)}, u32[]{:S(2)}) collective-permute-start(bf16[128,1280]{1,0:T(8,128)(2,1)S(1)} %collective-permute-done.3.refs_0_), channel_id=1, source_target_pairs={{0,2},{1,3},{2,0},{3,1},{4,6},{5,7},{6,4},{7,5},{8,10},{9,11},{10,... | collective-permute-start | bytes 983048 | tf_op jit(solution)/shard_map/ppermute | solution.py:23
  21.3 19.6 %copy-start = (bf16[640,2048]{1,0:T(8,128)(2,1)S(1)}, bf16[640,2048]{1,0:T(8,128)(2,1)}, u32[]{:S(2)}) copy-start(bf16[640,2048]{1,0:T(8,128)(2,1)} %refs_2_.1) | copy-start | bytes 7864324
  23.9 50.9 %collective-permute-start.1 = (bf16[656,1024]{1,0:T(8,128)(2,1)}, bf16[656,1024]{1,0:T(8,128)(2,1)}, u32[]{:S(2)}, u32[]{:S(2)}) collective-permute-start(bf16[656,1024]{1,0:T(8,128)(2,1)} %pad_maximum_fusion), channel_id=1, source_target_pairs={{4,0},{0,4},{12,8},{8,12},{20,16},{16,20},{28,24},{24,28},{5,1},{1... | collective-permute-start | bytes 4030472 | tf_op jit(solution)/shard_map/ppermute | solution.py:174
  26.8 0.6 copy-start.12
  27.5 10.9 %collective-permute-start.5 = (bf16[128,1280]{1,0:T(8,128)(2,1)S(1)}, bf16[128,1280]{1,0:T(8,128)(2,1)S(1)}, u32[]{:S(2)}, u32[]{:S(2)}) collective-permute-start(bf16[128,1280]{1,0:T(8,128)(2,1)S(1)} %collective-permute-done.3.refs_0_), channel_id=1, source_target_pairs={{0,1},{1,0},{2,3},{3,2},{4,5},{5,4},{6,7},{7,6},{8,9},{9,8},{10,11... | collective-permute-start | bytes 983048 | tf_op jit(solution)/shard_map/ppermute | solution.py:23
  29.7 15.1 %collective-permute-start.2 = (bf16[128,1280]{1,0:T(8,128)(2,1)}, bf16[128,1280]{1,0:T(8,128)(2,1)S(1)}, u32[]{:S(2)}, u32[]{:S(2)}) collective-permute-start(bf16[128,1280]{1,0:T(8,128)(2,1)} %copy-done.34), channel_id=1, source_target_pairs={{2,0},{3,10},{0,16},{1,26},{6,4},{7,14},{4,20},{5,30},{10,2},{11,8... | collective-permute-start | bytes 983048 | tf_op jit(solution)/shard_map/ppermute | solution.py:37
  34.2 5.0 %collective-permute-start.6 = (bf16[128,1280]{1,0:T(8,128)(2,1)}, bf16[128,1280]{1,0:T(8,128)(2,1)S(1)}, u32[]{:S(2)}, u32[]{:S(2)}) collective-permute-start(bf16[128,1280]{1,0:T(8,128)(2,1)} %collective-permute-done.4.refs_1_), channel_id=1, source_target_pairs={{0,1},{1,0},{2,3},{3,2},{4,5},{5,4},{6,7},{7,6},{8,9},{9,8},{10,11... | collective-permute-start | bytes 983048 | tf_op jit(solution)/shard_map/ppermute | solution.py:23
  40.8 4.0 %copy-start.1 = (bf16[512,1280]{1,0:T(8,128)(2,1)}, bf16[512,1280]{1,0:T(8,128)(2,1)S(1)}, u32[]{:S(2)}) copy-start(bf16[512,1280]{1,0:T(8,128)(2,1)S(1)} %shard_map.122.refs_0_) | copy-start | bytes 3932164
  40.8 9.8 %copy-start.25 = (s32[128]{0:T(128)S(1)}, s32[128]{0:T(128)}, u32[]{:S(2)}) copy-start(s32[128]{0:T(128)} %add.329) | copy-start | bytes 1540
  40.8 9.8 %copy-start.30 = (pred[4,128]{1,0:T(4,128)(4,1)S(1)}, pred[4,128]{1,0:T(4,128)(4,1)}, u32[]{:S(2)}) copy-start(pred[4,128]{1,0:T(4,128)(4,1)} %broadcast_in_dim.24) | copy-start | bytes 1540
  44.8 0.7 copy-start.9
  44.8 13.9 %copy-start.10 = (bf16[128,1024]{1,0:T(8,128)(2,1)}, bf16[128,1024]{1,0:T(8,128)(2,1)S(1)}, u32[]{:S(2)}) copy-start(bf16[128,1024]{1,0:T(8,128)(2,1)S(1)} %get-tuple-element.42) | copy-start | bytes 786436
  45.5 13.2 %collective-permute-start.8 = (bf16[128,1280]{1,0:T(8,128)(2,1)S(1)}, bf16[128,1280]{1,0:T(8,128)(2,1)S(1)}, u32[]{:S(2)}, u32[]{:S(2)}) collective-permute-start(bf16[128,1280]{1,0:T(8,128)(2,1)S(1)} %collective-permute-done.2.refs_0_), channel_id=1, source_target_pairs={{0,2},{1,3},{2,0},{3,1},{4,6},{5,7},{6,4},{7,5},{8,10},{9,11},{10,... | collective-permute-start | bytes 983048 | tf_op jit(solution)/shard_map/ppermute | solution.py:23
  51.4 10.7 %collective-permute-start.9 = (bf16[128,1280]{1,0:T(8,128)(2,1)S(1)}, bf16[128,1280]{1,0:T(8,128)(2,1)}, u32[]{:S(2)}, u32[]{:S(2)}) collective-permute-start(bf16[128,1280]{1,0:T(8,128)(2,1)S(1)} %collective-permute-done.2.refs_0_), channel_id=1, source_target_pairs={{0,1},{1,0},{2,3},{3,2},{4,5},{5,4},{6,7},{7,6},{8,9},{9,8},{10,11... | collective-permute-start | bytes 983048 | tf_op jit(solution)/shard_map/ppermute | solution.py:23
  51.4 16.9 %collective-permute-start.11 = (bf16[128,1024]{1,0:T(8,128)(2,1)}, bf16[128,1024]{1,0:T(8,128)(2,1)}, u32[]{:S(2)}, u32[]{:S(2)}) collective-permute-start(bf16[128,1024]{1,0:T(8,128)(2,1)} %get-tuple-element.34), channel_id=1, source_target_pairs={{0,16},{4,20},{8,24},{12,28},{16,0},{20,4},{24,8},{28,12},{1,17},{... | collective-permute-start | bytes 786440 | tf_op jit(solution)/shard_map/ppermute | solution.py:129
  58.7 3.4 %collective-permute-start.10 = (bf16[128,1280]{1,0:T(8,128)(2,1)S(1)}, bf16[128,1280]{1,0:T(8,128)(2,1)}, u32[]{:S(2)}, u32[]{:S(2)}) collective-permute-start(bf16[128,1280]{1,0:T(8,128)(2,1)S(1)} %collective-permute-done.8.refs_1_), channel_id=1, source_target_pairs={{0,1},{1,0},{2,3},{3,2},{4,5},{5,4},{6,7},{7,6},{8,9},{9,8},{10,11... | collective-permute-start | bytes 983048 | tf_op jit(solution)/shard_map/ppermute | solution.py:23
  61.4 20.9 %collective-permute-start.13 = (bf16[128,1024]{1,0:T(8,128)(2,1)}, bf16[128,1024]{1,0:T(8,128)(2,1)S(1)}, u32[]{:S(2)}, u32[]{:S(2)}) collective-permute-start(bf16[128,1024]{1,0:T(8,128)(2,1)} %copy-done.10), channel_id=1, source_target_pairs={{0,24},{4,28},{8,16},{12,20},{16,8},{20,12},{24,0},{28,4},{1,25},{... | collective-permute-start | bytes 786440 | tf_op jit(solution)/shard_map/ppermute | solution.py:129
  62.1 37.6 %collective-permute-start.17 = (bf16[128,1024]{1,0:T(8,128)(2,1)}, bf16[128,1024]{1,0:T(8,128)(2,1)}, u32[]{:S(2)}, u32[]{:S(2)}) collective-permute-start(bf16[128,1024]{1,0:T(8,128)(2,1)} %copy-done.9), channel_id=1, source_target_pairs={{0,8},{4,12},{8,0},{12,4},{16,24},{20,28},{24,16},{28,20},{1,9},{5... | collective-permute-start | bytes 786440 | tf_op jit(solution)/shard_map/ppermute | solution.py:129
  63.8 11.8 %copy-start.21 = (bf16[1,16,1024]{2,1,0:T(8,128)(2,1)S(1)}, bf16[1,16,1024]{2,1,0:T(8,128)(2,1)}, u32[]{:S(2)}) copy-start(bf16[1,16,1024]{2,1,0:T(8,128)(2,1)} %stack_reshape.6) | copy-start | bytes 98308
  63.8 11.8 %copy-start.2 = (bf16[512,1280]{1,0:T(8,128)(2,1)S(1)}, bf16[512,1280]{1,0:T(8,128)(2,1)}, u32[]{:S(2)}) copy-start(bf16[512,1280]{1,0:T(8,128)(2,1)} %copy-done.1) | copy-start | bytes 3932164
  67.6 0.7 copy-start.3
  68.2 20.8 %collective-permute-start.12 = (bf16[128,1024]{1,0:T(8,128)(2,1)S(1)}, bf16[128,1024]{1,0:T(8,128)(2,1)S(1)}, u32[]{:S(2)}, u32[]{:S(2)}) collective-permute-start(bf16[128,1024]{1,0:T(8,128)(2,1)S(1)} %get-tuple-element.41), channel_id=1, source_target_pairs={{0,16},{4,20},{8,24},{12,28},{16,0},{20,4},{24,8},{28,12},{1,17},{... | collective-permute-start | bytes 786440 | tf_op jit(solution)/shard_map/ppermute | solution.py:129
  71.9 29.8 %collective-permute-start.18 = (bf16[128,1024]{1,0:T(8,128)(2,1)}, bf16[128,1024]{1,0:T(8,128)(2,1)}, u32[]{:S(2)}, u32[]{:S(2)}) collective-permute-start(bf16[128,1024]{1,0:T(8,128)(2,1)} %get-tuple-element.48), channel_id=1, source_target_pairs={{0,8},{4,12},{8,0},{12,4},{16,24},{20,28},{24,16},{28,20},{1,9},{5... | collective-permute-start | bytes 786440 | tf_op jit(solution)/shard_map/ppermute | solution.py:129
  74.8 26.9 %collective-permute-start.19 = (bf16[128,1024]{1,0:T(8,128)(2,1)}, bf16[128,1024]{1,0:T(8,128)(2,1)}, u32[]{:S(2)}, u32[]{:S(2)}) collective-permute-start(bf16[128,1024]{1,0:T(8,128)(2,1)} %get-tuple-element.49), channel_id=1, source_target_pairs={{0,24},{4,28},{8,16},{12,20},{16,8},{20,12},{24,0},{28,4},{1,25},{... | collective-permute-start | bytes 786440 | tf_op jit(solution)/shard_map/ppermute | solution.py:129
  75.6 19.7 %copy-start.13 = (s32[4,16,8]{2,1,0:T(8,128)S(1)}, s32[4,16,8]{2,1,0:T(8,128)}, u32[]{:S(2)}) copy-start(s32[4,16,8]{2,1,0:T(8,128)} %copy-done.12) | copy-start | bytes 6148
  75.6 20.5 %copy-start.23 = (s32[4,288]{1,0:T(4,128)S(1)}, s32[4,288]{1,0:T(4,128)}, u32[]{:S(2)}) copy-start(s32[4,288]{1,0:T(4,128)} %add_add_fusion) | copy-start | bytes 13828
  75.6 20.5 %copy-start.22 = (s32[32,8]{1,0:T(8,128)S(1)}, s32[32,8]{1,0:T(8,128)}, u32[]{:S(2)}) copy-start(s32[32,8]{1,0:T(8,128)} %iota_add_fusion.1) | copy-start | bytes 3076
  80.6 0.8 copy-start.6
  81.5 0.8 copy-start.7
  82.3 19.4 %copy-start.4 = (bf16[128,1024]{1,0:T(8,128)(2,1)S(1)}, bf16[128,1024]{1,0:T(8,128)(2,1)}, u32[]{:S(2)}) copy-start(bf16[128,1024]{1,0:T(8,128)(2,1)} %copy-done.3) | copy-start | bytes 786436
  82.3 6.7 %copy-start.15 = (bf16[128,1024]{1,0:T(8,128)(2,1)}, bf16[128,1024]{1,0:T(8,128)(2,1)S(1)}, u32[]{:S(2)}) copy-start(bf16[128,1024]{1,0:T(8,128)(2,1)S(1)} %collective-permute-done.13) | copy-start | bytes 786436
  89.0 0.7 copy-start.16
  89.7 29.0 %collective-permute-start.14 = (bf16[288,1024]{1,0:T(8,128)(2,1)}, bf16[288,1024]{1,0:T(8,128)(2,1)S(1)}, u32[]{:S(2)}, u32[]{:S(2)}) collective-permute-start(bf16[288,1024]{1,0:T(8,128)(2,1)} %get-tuple-element.43), channel_id=1, source_target_pairs={{0,8},{4,12},{8,0},{12,4},{16,24},{20,28},{24,16},{28,20},{1,9},{5... | collective-permute-start | bytes 1769480 | tf_op jit(solution)/shard_map/ppermute | solution.py:129
  94.5 7.3 %copy-start.17 = (bf16[128,1024]{1,0:T(8,128)(2,1)S(1)}, bf16[128,1024]{1,0:T(8,128)(2,1)}, u32[]{:S(2)}) copy-start(bf16[128,1024]{1,0:T(8,128)(2,1)} %copy-done.16) | copy-start | bytes 786436
  96.3 43.1 %collective-permute-start.15 = (bf16[288,1024]{1,0:T(8,128)(2,1)}, bf16[288,1024]{1,0:T(8,128)(2,1)S(1)}, u32[]{:S(2)}, u32[]{:S(2)}) collective-permute-start(bf16[288,1024]{1,0:T(8,128)(2,1)} %copy-done.7), channel_id=1, source_target_pairs={{0,16},{4,20},{8,24},{12,28},{16,0},{20,4},{24,8},{28,12},{1,17},{... | collective-permute-start | bytes 1769480 | tf_op jit(solution)/shard_map/ppermute | solution.py:129
  101.7 37.7 %collective-permute-start.16 = (bf16[288,1024]{1,0:T(8,128)(2,1)}, bf16[288,1024]{1,0:T(8,128)(2,1)S(1)}, u32[]{:S(2)}, u32[]{:S(2)}) collective-permute-start(bf16[288,1024]{1,0:T(8,128)(2,1)} %copy-done.6), channel_id=1, source_target_pairs={{0,24},{4,28},{8,16},{12,20},{16,8},{20,12},{24,0},{28,4},{1,25},{... | collective-permute-start | bytes 1769480 | tf_op jit(solution)/shard_map/ppermute | solution.py:129
  118.8 23.2 %copy-start.29 = (f32[1024]{0:T(1024)S(1)}, f32[1024]{0:T(1024)}, u32[]{:S(2)}) copy-start(f32[1024]{0:T(1024)} %get-tuple-element.67) | copy-start | bytes 12292
  141.3 3.2 %copy-start.33 = (bf16[2048,1024]{1,0:T(8,128)(2,1)S(1)}, bf16[2048,1024]{1,0:T(8,128)(2,1)}, u32[]{:S(2)}) copy-start(bf16[2048,1024]{1,0:T(8,128)(2,1)} %param.14) | copy-start | bytes 12582916
  141.8 4.8 %collective-permute-start.22 = (f32[256]{0:T(256)S(1)}, f32[256]{0:T(256)S(1)}, u32[]{:S(2)}, u32[]{:S(2)}) collective-permute-start(f32[256]{0:T(256)S(1)} %pad_maximum_fusion.5), channel_id=1, source_target_pairs={{0,1},{1,0},{2,3},{3,2},{4,5},{5,4},{6,7},{7,6},{8,9},{9,8},{10,11... | collective-permute-start | bytes 3080 | tf_op jit(solution)/shard_map/ppermute | solution.py:23
  141.9 2.7 %copy-start.19 = (bf16[128,1024]{1,0:T(8,128)(2,1)S(1)}, bf16[128,1024]{1,0:T(8,128)(2,1)}, u32[]{:S(2)}) copy-start(bf16[128,1024]{1,0:T(8,128)(2,1)} %get-tuple-element.55) | copy-start | bytes 786436
  141.9 2.7 %copy-start.28 = (f32[1024]{0:T(1024)S(1)}, f32[1024]{0:T(1024)}, u32[]{:S(2)}) copy-start(f32[1024]{0:T(1024)} %get-tuple-element.66) | copy-start | bytes 12292
  144.6 1.0 copy-start.18
  146.1 23.3 %copy-start.32 = (s32[4]{0:T(128)S(1)}, s32[4]{0:T(128)}, u32[]{:S(2)}) copy-start(s32[4]{0:T(128)} %param.18) | copy-start | bytes 52
  146.1 23.3 %copy-start.11 = (s32[4,128,1]{2,1,0:T(8,128)S(1)}, s32[4,128,1]{2,1,0:T(8,128)}, u32[]{:S(2)}) copy-start(s32[4,128,1]{2,1,0:T(8,128)} %add.341) | copy-start | bytes 6148
  146.1 23.3 %copy-start.20 = (pred[4,128,1]{2,1,0:T(8,128)(4,1)S(1)}, pred[4,128,1]{2,1,0:T(8,128)(4,1)}, u32[]{:S(2)}) copy-start(pred[4,128,1]{2,1,0:T(8,128)(4,1)} %broadcast_in_dim.28) | copy-start | bytes 1540
  146.1 23.3 %copy-start.26 = (s32[128]{0:T(128)S(1)}, s32[128]{0:T(128)}, u32[]{:S(2)}) copy-start(s32[128]{0:T(128)} %add.329) | copy-start | bytes 1540
  146.1 2.0 %collective-permute-start.20 = (bf16[2,256,256]{2,1,0:T(8,128)(2,1)S(1)}, bf16[2,256,256]{2,1,0:T(8,128)(2,1)S(1)}, u32[]{:S(2)}, u32[]{:S(2)}) collective-permute-start(bf16[2,256,256]{2,1,0:T(8,128)(2,1)S(1)} %pad_maximum_fusion.2), channel_id=1, source_target_pairs={{0,1},{1,0},{2,3},{3,2},{4,5},{5,4},{6,7},{7,6},{8,9},{9,8},{10,11... | collective-permute-start | bytes 786440 | tf_op jit(solution)/shard_map/ppermute | solution.py:23
  146.5 31.4 %copy-start.5 = (bf16[4,128,1024]{2,1,0:T(8,128)(2,1)S(1)}, bf16[4,128,1024]{2,1,0:T(8,128)(2,1)}, u32[]{:S(2)}) copy-start(bf16[4,128,1024]{2,1,0:T(8,128)(2,1)} %query_ref.1) | copy-start | bytes 3145732
  146.5 31.4 %copy-start.8 = (bf16[4,128,256]{2,1,0:T(8,128)(2,1)S(1)}, bf16[4,128,256]{2,1,0:T(8,128)(2,1)}, u32[]{:S(2)}) copy-start(bf16[4,128,256]{2,1,0:T(8,128)(2,1)} %text_ref.1) | copy-start | bytes 786436
  146.6 3.6 %collective-permute-start.23 = (f32[256]{0:T(256)S(1)}, f32[256]{0:T(256)S(1)}, u32[]{:S(2)}, u32[]{:S(2)}) collective-permute-start(f32[256]{0:T(256)S(1)} %fusion.56), channel_id=1, source_target_pairs={{0,2},{1,3},{2,0},{3,1},{4,6},{5,7},{6,4},{7,5},{8,10},{9,11},{10,... | collective-permute-start | bytes 3080 | tf_op jit(solution)/shard_map/ppermute | solution.py:23
  148.2 5.4 %collective-permute-start.21 = (bf16[1,256,256]{2,1,0:T(8,128)(2,1)S(1)}, bf16[1,256,256]{2,1,0:T(8,128)(2,1)S(1)}, u32[]{:S(2)}, u32[]{:S(2)}) collective-permute-start(bf16[1,256,256]{2,1,0:T(8,128)(2,1)S(1)} %dynamic-slice_convert_fusion), channel_id=1, source_target_pairs={{0,2},{1,3},{2,0},{3,1},{4,6},{5,7},{6,4},{7,5},{8,10},{9,11},{10,... | collective-permute-start | bytes 393224 | tf_op jit(solution)/shard_map/ppermute | solution.py:23
  154.6 23.2 %all-to-all-start = ((bf16[8,64,256]{2,1,0:T(8,128)(2,1)}), bf16[8,64,256]{2,1,0:T(8,128)(2,1)S(1)}, u32[]{:S(2)}, u32[]{:S(2)}) async-start(bf16[8,64,256]{2,1,0:T(8,128)(2,1)} %bitcast.19), calls=%async_computation | async-start | bytes 524288 | tf_op jit(solution)/shard_map/all_to_all | solution.py:426

commit v7 on v6

--- a/solution.py
+++ b/solution.py
@@ -219,7 +219,8 @@
             operands = [(jnp.roll(parts, member * w_merge.shape[0], axis=0), depth, inside)]
         parts = partial_products([held[h] for h in halves], operands, count, riding)
         if step:
-            before = [sent[step - 1][1][1]] + ([sent[step - 2][1][2]] if step >= 2 else [])
+            before = [sent[step - 1][1][1 if step == 1 else 0]]
+            before += [sent[step - 2][1][2]] if step >= 2 else []
             parts, _ = lax.optimization_barrier((parts, before))
         sent.append((parts, send_direct(parts)))
     for step in range(len(PLAN)):
@@ -254,7 +255,7 @@
     return blocks[0], squares
 
 
-SMALL_ROWS = 64
+SMALL_ROWS = 48
 
 
 def pack_small(prefix_cache, sources, tiles):

time: 184 us -> 182 us (0.989)
  starting transfers between devices: 58.4 us -> 54.6 us
  local copies, waits for them, and re-layouts: 17.4 us -> 20.4 us
    ppermute x9, starting transfers between devices: 16.2 us -> 12.2 us  [send_direct(): lax.ppermute(part, 'seq', along([(a, a ^ k) for a in range(4)]))]
    unnamed x74 -> x66, local copies, waits for them, and re-layouts: 4.84 us -> 6.27 us
  transfers between devices with their start and end apart: 25 -> 25, of which waited for: 9 -> 9; matrix products, arithmetic and copies ran while one was open for 13% -> 14% of each run, Pallas kernels for 9% -> 9%
where the time goes in v7:
time: 182 us; the launch traced here: 181 us
  waiting for transfers between devices  67.4 us (37%)
  starting transfers between devices  54.6 us (30%)
  Pallas kernels  21.8 us (12%)
  local copies, waits for them, and re-layouts  20.4 us (11%)
  other arithmetic  10.8 us (6%)
  matrix products  4.59 us (3%)
    ppermute x9, waiting for transfers between devices, send_direct(): lax.ppermute(part, 'seq', along([(a, a ^ k) for a in range(4)]))  40.7 us
    ppermute x11, starting transfers between devices, flip(): return lax.ppermute(value, axis, [(i, i ^ bit) for i in range(count)])  19.1 us
    ppermute x11, waiting for transfers between devices, flip(): return lax.ppermute(value, axis, [(i, i ^ bit) for i in range(count)])  18.2 us
    all_to_all x1, starting transfers between devices, shards(): lax.all_to_all(outgoing, 'seq', split_axis=0, concat_axis=0, tiled=True)  15.1 us
    pallas_call x3, Pallas kernels, partial_products(): pl.pallas_call(functools.partial(partial_kernel, halves, len(riding)), gr...  13 us
    ppermute x9, starting transfers between devices, send_direct(): lax.ppermute(part, 'seq', along([(a, a ^ k) for a in range(4)]))  12.2 us
    all_to_all x1, waiting for transfers between devices, shards(): lax.all_to_all(outgoing, 'seq', split_axis=0, concat_axis=0, tiled=True)  8.47 us
    unnamed x66, local copies, waits for them, and re-layouts  6.27 us
  transfers between devices with their start and end apart: 25, of which 9 were waited for; matrix products, arithmetic and copies ran while one was open for 14% of the time, Pallas kernels for 9%

profile of v7, /device:TPU:0, one launch (start us, length us, event | category | flops | bytes accessed | tf_op | source)
XLA Modules:
  0.0 181.0 jit_solution(17052199531672753717)
XLA Ops:
  0.6 1.1 slice_bitcast_fusion.1
  1.7 3.0 %collective-permute-start = (bf16[128,1280]{1,0:T(8,128)(2,1)S(1)}, bf16[128,1280]{1,0:T(8,128)(2,1)S(1)}, u32[]{:S(2)}, u32[]{:S(2)}) collective-permute-start(bf16[128,1280]{1,0:T(8,128)(2,1)S(1)} %get-tuple-element.62), channel_id=1, source_target_pairs={{0,2},{1,3},{2,0},{3,1},{4,6},{5,7},{6,4},{7,5},{8,10},{9,11},{10,... | collective-permute-start | bytes 983048 | tf_op jit(solution)/shard_map/ppermute | solution.py:23
  4.8 0.8 collective-permute-start.3
  5.6 3.5 %fusion.57 = (bf16[640,1024]{1,0:T(8,128)(2,1)}, bf16[640,1024]{1,0:T(8,128)(2,1)}) fusion(bf16[640,2048]{1,0:T(8,128)(2,1)} %refs_2_.1), kind=kLoop, calls=%fused_computation.133 | loop fusion | bytes 5242880 | tf_op jit(solution)/shard_map/slice | solution.py:163
  9.1 1.5 collective-permute-start.7
  10.7 0.5 fusion.55
  11.6 0.8 gather_fusion.2
  12.6 6.2 %collective-permute-done = bf16[128,1280]{1,0:T(8,128)(2,1)S(1)} collective-permute-done((bf16[128,1280]{1,0:T(8,128)(2,1)S(1)}, bf16[128,1280]{1,0:T(8,128)(2,1)S(1)}, u32[]{:S(2)}, u32[]{:S(2)}) %collective-permute-start) | collective-permute-done | bytes 327712 | tf_op jit(solution)/shard_map/ppermute | solution.py:23
  18.8 2.5 %collective-permute-start.4 = (bf16[128,1280]{1,0:T(8,128)(2,1)S(1)}, bf16[128,1280]{1,0:T(8,128)(2,1)}, u32[]{:S(2)}, u32[]{:S(2)}) collective-permute-start(bf16[128,1280]{1,0:T(8,128)(2,1)S(1)} %collective-permute-done.3.refs_0_), channel_id=1, source_target_pairs={{0,2},{1,3},{2,0},{3,1},{4,6},{5,7},{6,4},{7,5},{8,10},{9,11},{10,... | collective-permute-start | bytes 983048 | tf_op jit(solution)/shard_map/ppermute | solution.py:23
  21.3 2.7 %pad_maximum_fusion = bf16[652,1024]{1,0:T(8,128)(2,1)} fusion(bf16[12,1024]{1,0:T(8,128)(2,1)S(1)} %reshape.336, bf16[640,1024]{1,0:T(8,128)(2,1)} %get-tuple-element.56), kind=kLoop, calls=%fused_computation.17 | loop fusion | flops 2670592 | bytes 2670592 | tf_op jit(solution)/shard_map/concatenate | solution.py:165
  23.9 1.5 collective-permute-start.1
  25.6 0.6 broadcast_in_dim.24
  26.2 0.6 add.329
  27.0 0.5 copy-done.15
  27.5 2.2 %collective-permute-start.5 = (bf16[128,1280]{1,0:T(8,128)(2,1)S(1)}, bf16[128,1280]{1,0:T(8,128)(2,1)S(1)}, u32[]{:S(2)}, u32[]{:S(2)}) collective-permute-start(bf16[128,1280]{1,0:T(8,128)(2,1)S(1)} %collective-permute-done.3.refs_0_), channel_id=1, source_target_pairs={{0,1},{1,0},{2,3},{3,2},{4,5},{5,4},{6,7},{7,6},{8,9},{9,8},{10,11... | collective-permute-start | bytes 983048 | tf_op jit(solution)/shard_map/ppermute | solution.py:23
  29.8 4.5 %collective-permute-start.2 = (bf16[128,1280]{1,0:T(8,128)(2,1)}, bf16[128,1280]{1,0:T(8,128)(2,1)S(1)}, u32[]{:S(2)}, u32[]{:S(2)}) collective-permute-start(bf16[128,1280]{1,0:T(8,128)(2,1)} %copy-done.30), channel_id=1, source_target_pairs={{2,0},{3,10},{0,16},{1,26},{6,4},{7,14},{4,20},{5,30},{10,2},{11,8... | collective-permute-start | bytes 983048 | tf_op jit(solution)/shard_map/ppermute | solution.py:37
  34.2 3.5 %collective-permute-start.6 = (bf16[128,1280]{1,0:T(8,128)(2,1)}, bf16[128,1280]{1,0:T(8,128)(2,1)S(1)}, u32[]{:S(2)}, u32[]{:S(2)}) collective-permute-start(bf16[128,1280]{1,0:T(8,128)(2,1)} %collective-permute-done.4.refs_1_), channel_id=1, source_target_pairs={{0,1},{1,0},{2,3},{3,2},{4,5},{5,4},{6,7},{7,6},{8,9},{9,8},{10,11... | collective-permute-start | bytes 983048 | tf_op jit(solution)/shard_map/ppermute | solution.py:23
  37.8 0.6 slice_convert_fusion.3
  38.4 0.9 collective-permute-done.6.refs_3_
  39.2 1.6 shard_map.122.refs_0_
  40.9 3.9 %shard_map.123 = (bf16[128,1024]{1,0:T(8,128)(2,1)S(1)}, bf16[128,1024]{1,0:T(8,128)(2,1)S(1)}, bf16[128,1024]{1,0:T(8,128)(2,1)}, bf16[128,1024]{1,0:T(8,128)(2,1)S(1)}) custom-call(bf16[512,1280]{1,0:T(8,128)(2,1)S(1)} %shard_map.122.refs_0_, bf16[640,2048]{1,0:T(8,128)(2,1)S(1)} %copy-done, bf16[640,1024]{1,0:T(8,128)(2,1)} %collective-permute-done.7.refs_2_), custom_call_target="tpu_custom_call" | custom-call | bytes 2048 | tf_op jit(solution)/shard_map/pallas_call | solution.py:109
  44.9 0.7 copy-done.11
  45.5 5.0 %collective-permute-start.8 = (bf16[128,1280]{1,0:T(8,128)(2,1)S(1)}, bf16[128,1280]{1,0:T(8,128)(2,1)S(1)}, u32[]{:S(2)}, u32[]{:S(2)}) collective-permute-start(bf16[128,1280]{1,0:T(8,128)(2,1)S(1)} %collective-permute-done.2.refs_0_), channel_id=1, source_target_pairs={{0,2},{1,3},{2,0},{3,1},{4,6},{5,7},{6,4},{7,5},{8,10},{9,11},{10,... | collective-permute-start | bytes 983048 | tf_op jit(solution)/shard_map/ppermute | solution.py:23
  50.6 0.7 add_add_fusion
  51.3 0.8 collective-permute-start.11
  52.1 6.6 %collective-permute-done.8.refs_1_ = bf16[128,1280]{1,0:T(8,128)(2,1)S(1)} collective-permute-done((bf16[128,1280]{1,0:T(8,128)(2,1)S(1)}, bf16[128,1280]{1,0:T(8,128)(2,1)S(1)}, u32[]{:S(2)}, u32[]{:S(2)}) %collective-permute-start.8) | collective-permute-done | bytes 327712 | tf_op jit(solution)/shard_map/ppermute | solution.py:23
  58.7 1.4 stack_reshape.6
  60.1 1.3 iota_add_fusion.1
  61.4 0.7 collective-permute-start.13
  62.1 1.7 shard_map.124.refs_0_.refs_1_
  63.9 4.1 %shard_map.125 = (bf16[128,1024]{1,0:T(8,128)(2,1)S(1)}, bf16[128,1024]{1,0:T(8,128)(2,1)}, bf16[128,1024]{1,0:T(8,128)(2,1)}, bf16[128,1024]{1,0:T(8,128)(2,1)}) custom-call(bf16[512,1280]{1,0:T(8,128)(2,1)S(1)} %shard_map.124.refs_0_.refs_1_, bf16[640,2048]{1,0:T(8,128)(2,1)S(1)} %copy-done, bf16[640,1024]{1,0:T(8,128)(2,1)} %collective-permute-done.7.refs_2_), custom_call_target="tpu_custom_call" | custom-call | bytes 2048 | tf_op jit(solution)/shard_map/pallas_call | solution.py:109
  67.9 0.7 copy-done.5
  68.6 2.8 %collective-permute-start.12 = (bf16[128,1024]{1,0:T(8,128)(2,1)}, bf16[128,1024]{1,0:T(8,128)(2,1)}, u32[]{:S(2)}, u32[]{:S(2)}) collective-permute-start(bf16[128,1024]{1,0:T(8,128)(2,1)} %get-tuple-element.41), channel_id=1, source_target_pairs={{0,8},{4,12},{8,0},{12,4},{16,24},{20,28},{24,16},{28,20},{1,9},{5... | collective-permute-start | bytes 786440 | tf_op jit(solution)/shard_map/ppermute | solution.py:129
  71.4 3.4 %collective-permute-start.18 = (bf16[128,1024]{1,0:T(8,128)(2,1)}, bf16[128,1024]{1,0:T(8,128)(2,1)}, u32[]{:S(2)}, u32[]{:S(2)}) collective-permute-start(bf16[128,1024]{1,0:T(8,128)(2,1)} %get-tuple-element.48), channel_id=1, source_target_pairs={{0,16},{4,20},{8,24},{12,28},{16,0},{20,4},{24,8},{28,12},{1,17},{... | collective-permute-start | bytes 786440 | tf_op jit(solution)/shard_map/ppermute | solution.py:129
  74.8 0.8 slice_bitcast_fusion.5
  75.7 1.3 copy-done.2
  77.0 1.3 copy-done.4
  78.3 5.0 %shard_map.126 = (bf16[256,1024]{1,0:T(8,128)(2,1)S(1)}, bf16[280,1024]{1,0:T(8,128)(2,1)}, bf16[280,1024]{1,0:T(8,128)(2,1)S(1)}, bf16[280,1024]{1,0:T(8,128)(2,1)S(1)}) custom-call(bf16[512,1280]{1,0:T(8,128)(2,1)S(1)} %copy-done.2, bf16[512,1280]{1,0:T(8,128)(2,1)S(1)} %copy-done.4, bf16[640,2048]{1,0:T(8,128)(2,1)S(1)} %copy-done, ...), custom_call_target="tpu_custom_call" | custom-call | bytes 2048 | tf_op jit(solution)/shard_map/pallas_call | solution.py:109
  83.3 0.8 copy-done.8
  84.1 0.8 copy-done.9
  84.9 4.0 %collective-permute-done.12 = bf16[128,1024]{1,0:T(8,128)(2,1)} collective-permute-done((bf16[128,1024]{1,0:T(8,128)(2,1)}, bf16[128,1024]{1,0:T(8,128)(2,1)}, u32[]{:S(2)}, u32[]{:S(2)}) %collective-permute-start.12) | collective-permute-done | bytes 262176 | tf_op jit(solution)/shard_map/ppermute | solution.py:129
  89.1 1.6 add.341
  90.7 0.8 add.342.all_ref
  91.5 1.9 %collective-permute-start.15 = (bf16[280,1024]{1,0:T(8,128)(2,1)}, bf16[280,1024]{1,0:T(8,128)(2,1)S(1)}, u32[]{:S(2)}, u32[]{:S(2)}) collective-permute-start(bf16[280,1024]{1,0:T(8,128)(2,1)} %copy-done.9), channel_id=1, source_target_pairs={{0,16},{4,20},{8,24},{12,28},{16,0},{20,4},{24,8},{28,12},{1,17},{... | collective-permute-start | bytes 1720328 | tf_op jit(solution)/shard_map/ppermute | solution.py:129
  93.4 1.3 fusion.15
  94.8 0.9 stack_reshape.7
  95.6 2.6 %collective-permute-start.16 = (bf16[280,1024]{1,0:T(8,128)(2,1)}, bf16[280,1024]{1,0:T(8,128)(2,1)S(1)}, u32[]{:S(2)}, u32[]{:S(2)}) collective-permute-start(bf16[280,1024]{1,0:T(8,128)(2,1)} %copy-done.8), channel_id=1, source_target_pairs={{0,24},{4,28},{8,16},{12,20},{16,8},{20,12},{24,0},{28,4},{1,25},{... | collective-permute-start | bytes 1720328 | tf_op jit(solution)/shard_map/ppermute | solution.py:129
  98.2 2.0 %fusion.17 = (f32[128]{0:T(128)S(1)}, bf16[128,1024]{1,0:T(8,128)(2,1)}) fusion(bf16[128,1024]{1,0:T(8,128)(2,1)} %collective-permute-done.19, bf16[128,1024]{1,0:T(8,128)(2,1)} %collective-permute-done.18, bf16[128,1024]{1,0:T(8,128)(2,1)} %collective-permute-done.12, bf16[128,1024]{1,0:T(8,128)(2,1)S(1)} %copy-done.6), kind=kLoop, calls=%fused_computation.33 | loop fusion | flops 1441664 | bytes 1311232 | tf_op jit(solution)/shard_map/reduce_sum | solution.py:194
  100.2 13.8 %collective-permute-done.14 = bf16[280,1024]{1,0:T(8,128)(2,1)S(1)} collective-permute-done((bf16[280,1024]{1,0:T(8,128)(2,1)}, bf16[280,1024]{1,0:T(8,128)(2,1)S(1)}, u32[]{:S(2)}, u32[]{:S(2)}) %collective-permute-start.14) | collective-permute-done | bytes 573472 | tf_op jit(solution)/shard_map/ppermute | solution.py:129
  114.0 22.9 %collective-permute-done.15 = bf16[280,1024]{1,0:T(8,128)(2,1)S(1)} collective-permute-done((bf16[280,1024]{1,0:T(8,128)(2,1)}, bf16[280,1024]{1,0:T(8,128)(2,1)S(1)}, u32[]{:S(2)}, u32[]{:S(2)}) %collective-permute-start.15) | collective-permute-done | bytes 573472 | tf_op jit(solution)/shard_map/ppermute | solution.py:129
  137.2 0.6 gather_fusion
  137.8 0.6 gather_fusion.1
  139.5 2.6 %fusion = f32[256,1024]{1,0:T(8,128)S(1)} fusion(bf16[2048,1024]{1,0:T(8,128)(2,1)} %param.14, bf16[256,1024]{1,0:T(8,128)(2,1)S(1)} %get-tuple-element.53, f32[1024]{0:T(1024)S(1)} %copy-done.25), kind=kOutput, calls=%fused_computation.3 | convolution fusion | flops 537657344 | bytes 3674112 | tf_op jit(solution)/shard_map/dot_general | solution.py:195
  142.1 0.5 fusion.9
  142.6 0.5 fusion.6
  143.2 0.4 collective-permute-start.20
  143.8 1.1 collective-permute-start.23
  145.0 1.1 collective-permute-start.21
  146.1 1.3 collective-permute-done.23
  147.5 3.3 %collective-permute-done.21 = bf16[1,256,256]{2,1,0:T(8,128)(2,1)S(1)} collective-permute-done((bf16[1,256,256]{2,1,0:T(8,128)(2,1)S(1)}, bf16[1,256,256]{2,1,0:T(8,128)(2,1)S(1)}, u32[]{:S(2)}, u32[]{:S(2)}) %collective-permute-start.21) | collective-permute-done | bytes 131104 | tf_op jit(solution)/shard_map/ppermute | solution.py:23
  150.7 1.0 convolution_convert_fusion
  151.7 15.1 %all-to-all-start = ((bf16[8,64,256]{2,1,0:T(8,128)(2,1)}), bf16[8,64,256]{2,1,0:T(8,128)(2,1)S(1)}, u32[]{:S(2)}, u32[]{:S(2)}) async-start(bf16[8,64,256]{2,1,0:T(8,128)(2,1)} %bitcast.17), calls=%async_computation | async-start | bytes 524288 | tf_op jit(solution)/shard_map/all_to_all | solution.py:427
  167.1 8.5 %all-to-all-done = bf16[8,64,256]{2,1,0:T(8,128)(2,1)S(1)} async-done(((bf16[8,64,256]{2,1,0:T(8,128)(2,1)}), bf16[8,64,256]{2,1,0:T(8,128)(2,1)S(1)}, u32[]{:S(2)}, u32[]{:S(2)}) %all-to-all-start) | async-done | bytes 262176 | tf_op jit(solution)/shard_map/all_to_all | solution.py:427
  175.5 5.5 %shard_map.127 = (bf16[4,128,1024]{2,1,0:T(8,128)(2,1)}, bf16[256,256]{1,0:T(8,128)(2,1)}) custom-call(s32[4]{0:T(128)S(1)} %fusion.47.place_ref, bf16[4,128,1024]{2,1,0:T(8,128)(2,1)S(1)} %copy-done.7, bf16[8,32,256]{2,1,0:T(8,128)(2,1)S(1)} %slice.107.prefix_ref, bf16[4,128,256]{2,1,0:T(8,128)(2,1)S(1)} %copy-done.10, bf16[512,256]{1,0:T(8,128)(2,1)S(1)} %bitcast.53, ...), custom_call_target="tpu_custom_call" | custom-call | flops 603979776 | bytes 4194304 | tf_op jit(solution)/shard_map/pallas_call | solution.py:323
  (139 shorter events, 3.1 us)
Async XLA Ops:
  1.7 17.0 %collective-permute-start = (bf16[128,1280]{1,0:T(8,128)(2,1)S(1)}, bf16[128,1280]{1,0:T(8,128)(2,1)S(1)}, u32[]{:S(2)}, u32[]{:S(2)}) collective-permute-start(bf16[128,1280]{1,0:T(8,128)(2,1)S(1)} %get-tuple-element.62), channel_id=1, source_target_pairs={{0,2},{1,3},{2,0},{3,1},{4,6},{5,7},{6,4},{7,5},{8,10},{9,11},{10,... | collective-permute-start | bytes 983048 | tf_op jit(solution)/shard_map/ppermute | solution.py:23
  4.8 5.8 %copy-start.27 = (s32[32,1]{0,1:T(1,128)S(1)}, s32[32,1]{0,1:T(1,128)}, u32[]{:S(2)}) copy-start(s32[32,1]{0,1:T(1,128)} %param.15) | copy-start | bytes 388
  4.8 6.5 %copy-start.32 = (s32[1,4]{1,0:T(1,128)S(1)}, s32[1,4]{1,0:T(1,128)}, u32[]{:S(2)}) copy-start(s32[1,4]{1,0:T(1,128)} %param.17) | copy-start | bytes 52
  4.8 14.0 %collective-permute-start.3 = (bf16[128,1280]{1,0:T(8,128)(2,1)S(1)}, bf16[128,1280]{1,0:T(8,128)(2,1)S(1)}, u32[]{:S(2)}, u32[]{:S(2)}) collective-permute-start(bf16[128,1280]{1,0:T(8,128)(2,1)S(1)} %get-tuple-element.63), channel_id=1, source_target_pairs={{0,0},{1,10},{2,16},{3,26},{4,4},{5,14},{6,20},{7,30},{8,2},{9,8},... | collective-permute-start | bytes 983048 | tf_op jit(solution)/shard_map/ppermute | solution.py:37
  9.1 3.3 %copy-start.31 = (s32[32]{0:T(128)S(1)}, s32[32]{0:T(128)}, u32[]{:S(2)}) copy-start(s32[32]{0:T(128)} %param.16) | copy-start | bytes 388
  9.1 3.5 %copy-start.20 = (bf16[1,32,256]{2,1,0:T(8,128)(2,1)S(1)}, bf16[1,32,256]{2,1,0:T(8,128)(2,1)}, u32[]{:S(2)}) copy-start(bf16[1,32,256]{2,1,0:T(8,128)(2,1)} %param.19) | copy-start | bytes 49156
  9.1 31.8 %collective-permute-start.7 = (bf16[640,1024]{1,0:T(8,128)(2,1)}, bf16[640,1024]{1,0:T(8,128)(2,1)}, u32[]{:S(2)}, u32[]{:S(2)}) collective-permute-start(bf16[640,1024]{1,0:T(8,128)(2,1)} %get-tuple-element.57), channel_id=1, source_target_pairs={{4,0},{0,4},{12,8},{8,12},{20,16},{16,20},{28,24},{24,28},{5,1},{1... | collective-permute-start | bytes 3932168 | tf_op jit(solution)/shard_map/ppermute | solution.py:174
  11.6 26.2 %copy-start.23 = (bf16[2048]{0:T(1024)(128)(2,1)S(1)}, bf16[2048]{0:T(1024)(128)(2,1)}, u32[]{:S(2)}) copy-start(bf16[2048]{0:T(1024)(128)(2,1)} %param.13) | copy-start | bytes 12292
  12.6 8.7 %copy-start.17 = (bf16[48,256]{1,0:T(8,128)(2,1)}, bf16[48,256]{1,0:T(8,128)(2,1)S(1)}, u32[]{:S(2)}) copy-start(bf16[48,256]{1,0:T(8,128)(2,1)S(1)} %pad_maximum_fusion.4) | copy-start | bytes 73732
  18.8 2.5 %copy-start.30 = (bf16[128,1280]{1,0:T(8,128)(2,1)}, bf16[128,1280]{1,0:T(8,128)(2,1)S(1)}, u32[]{:S(2)}) copy-start(bf16[128,1280]{1,0:T(8,128)(2,1)S(1)} %collective-permute-done) | copy-start | bytes 983044
  18.8 15.4 %collective-permute-start.4 = (bf16[128,1280]{1,0:T(8,128)(2,1)S(1)}, bf16[128,1280]{1,0:T(8,128)(2,1)}, u32[]{:S(2)}, u32[]{:S(2)}) collective-permute-start(bf16[128,1280]{1,0:T(8,128)(2,1)S(1)} %collective-permute-done.3.refs_0_), channel_id=1, source_target_pairs={{0,2},{1,3},{2,0},{3,1},{4,6},{5,7},{6,4},{7,5},{8,10},{9,11},{10,... | collective-permute-start | bytes 983048 | tf_op jit(solution)/shard_map/ppermute | solution.py:23
  21.3 19.6 %copy-start = (bf16[640,2048]{1,0:T(8,128)(2,1)S(1)}, bf16[640,2048]{1,0:T(8,128)(2,1)}, u32[]{:S(2)}) copy-start(bf16[640,2048]{1,0:T(8,128)(2,1)} %refs_2_.1) | copy-start | bytes 7864324
  23.9 50.9 %collective-permute-start.1 = (bf16[652,1024]{1,0:T(8,128)(2,1)}, bf16[652,1024]{1,0:T(8,128)(2,1)}, u32[]{:S(2)}, u32[]{:S(2)}) collective-permute-start(bf16[652,1024]{1,0:T(8,128)(2,1)} %pad_maximum_fusion), channel_id=1, source_target_pairs={{4,0},{0,4},{12,8},{8,12},{20,16},{16,20},{28,24},{24,28},{5,1},{1... | collective-permute-start | bytes 4005896 | tf_op jit(solution)/shard_map/ppermute | solution.py:174
  26.9 0.6 copy-start.15
  27.5 10.9 %collective-permute-start.5 = (bf16[128,1280]{1,0:T(8,128)(2,1)S(1)}, bf16[128,1280]{1,0:T(8,128)(2,1)S(1)}, u32[]{:S(2)}, u32[]{:S(2)}) collective-permute-start(bf16[128,1280]{1,0:T(8,128)(2,1)S(1)} %collective-permute-done.3.refs_0_), channel_id=1, source_target_pairs={{0,1},{1,0},{2,3},{3,2},{4,5},{5,4},{6,7},{7,6},{8,9},{9,8},{10,11... | collective-permute-start | bytes 983048 | tf_op jit(solution)/shard_map/ppermute | solution.py:23
  29.8 15.1 %collective-permute-start.2 = (bf16[128,1280]{1,0:T(8,128)(2,1)}, bf16[128,1280]{1,0:T(8,128)(2,1)S(1)}, u32[]{:S(2)}, u32[]{:S(2)}) collective-permute-start(bf16[128,1280]{1,0:T(8,128)(2,1)} %copy-done.30), channel_id=1, source_target_pairs={{2,0},{3,10},{0,16},{1,26},{6,4},{7,14},{4,20},{5,30},{10,2},{11,8... | collective-permute-start | bytes 983048 | tf_op jit(solution)/shard_map/ppermute | solution.py:37
  34.2 5.0 %collective-permute-start.6 = (bf16[128,1280]{1,0:T(8,128)(2,1)}, bf16[128,1280]{1,0:T(8,128)(2,1)S(1)}, u32[]{:S(2)}, u32[]{:S(2)}) collective-permute-start(bf16[128,1280]{1,0:T(8,128)(2,1)} %collective-permute-done.4.refs_1_), channel_id=1, source_target_pairs={{0,1},{1,0},{2,3},{3,2},{4,5},{5,4},{6,7},{7,6},{8,9},{9,8},{10,11... | collective-permute-start | bytes 983048 | tf_op jit(solution)/shard_map/ppermute | solution.py:23
  40.8 4.0 %copy-start.1 = (bf16[512,1280]{1,0:T(8,128)(2,1)}, bf16[512,1280]{1,0:T(8,128)(2,1)S(1)}, u32[]{:S(2)}) copy-start(bf16[512,1280]{1,0:T(8,128)(2,1)S(1)} %shard_map.122.refs_0_) | copy-start | bytes 3932164
  40.8 9.7 %copy-start.21 = (s32[128]{0:T(128)S(1)}, s32[128]{0:T(128)}, u32[]{:S(2)}) copy-start(s32[128]{0:T(128)} %add.329) | copy-start | bytes 1540
  40.9 9.7 %copy-start.26 = (pred[4,128]{1,0:T(4,128)(4,1)S(1)}, pred[4,128]{1,0:T(4,128)(4,1)}, u32[]{:S(2)}) copy-start(pred[4,128]{1,0:T(4,128)(4,1)} %broadcast_in_dim.24) | copy-start | bytes 1540
  44.8 0.7 copy-start.11
  44.8 13.9 %copy-start.12 = (bf16[128,1024]{1,0:T(8,128)(2,1)}, bf16[128,1024]{1,0:T(8,128)(2,1)S(1)}, u32[]{:S(2)}) copy-start(bf16[128,1024]{1,0:T(8,128)(2,1)S(1)} %get-tuple-element.42) | copy-start | bytes 786436
  45.5 13.2 %collective-permute-start.8 = (bf16[128,1280]{1,0:T(8,128)(2,1)S(1)}, bf16[128,1280]{1,0:T(8,128)(2,1)S(1)}, u32[]{:S(2)}, u32[]{:S(2)}) collective-permute-start(bf16[128,1280]{1,0:T(8,128)(2,1)S(1)} %collective-permute-done.2.refs_0_), channel_id=1, source_target_pairs={{0,2},{1,3},{2,0},{3,1},{4,6},{5,7},{6,4},{7,5},{8,10},{9,11},{10,... | collective-permute-start | bytes 983048 | tf_op jit(solution)/shard_map/ppermute | solution.py:23
  51.3 10.8 %collective-permute-start.9 = (bf16[128,1280]{1,0:T(8,128)(2,1)S(1)}, bf16[128,1280]{1,0:T(8,128)(2,1)}, u32[]{:S(2)}, u32[]{:S(2)}) collective-permute-start(bf16[128,1280]{1,0:T(8,128)(2,1)S(1)} %collective-permute-done.2.refs_0_), channel_id=1, source_target_pairs={{0,1},{1,0},{2,3},{3,2},{4,5},{5,4},{6,7},{7,6},{8,9},{9,8},{10,11... | collective-permute-start | bytes 983048 | tf_op jit(solution)/shard_map/ppermute | solution.py:23
  51.3 17.3 %collective-permute-start.11 = (bf16[128,1024]{1,0:T(8,128)(2,1)}, bf16[128,1024]{1,0:T(8,128)(2,1)}, u32[]{:S(2)}, u32[]{:S(2)}) collective-permute-start(bf16[128,1024]{1,0:T(8,128)(2,1)} %get-tuple-element.34), channel_id=1, source_target_pairs={{0,16},{4,20},{8,24},{12,28},{16,0},{20,4},{24,8},{28,12},{1,17},{... | collective-permute-start | bytes 786440 | tf_op jit(solution)/shard_map/ppermute | solution.py:129
  58.7 3.4 %collective-permute-start.10 = (bf16[128,1280]{1,0:T(8,128)(2,1)S(1)}, bf16[128,1280]{1,0:T(8,128)(2,1)}, u32[]{:S(2)}, u32[]{:S(2)}) collective-permute-start(bf16[128,1280]{1,0:T(8,128)(2,1)S(1)} %collective-permute-done.8.refs_1_), channel_id=1, source_target_pairs={{0,1},{1,0},{2,3},{3,2},{4,5},{5,4},{6,7},{7,6},{8,9},{9,8},{10,11... | collective-permute-start | bytes 983048 | tf_op jit(solution)/shard_map/ppermute | solution.py:23
  61.4 23.5 %collective-permute-start.13 = (bf16[128,1024]{1,0:T(8,128)(2,1)}, bf16[128,1024]{1,0:T(8,128)(2,1)}, u32[]{:S(2)}, u32[]{:S(2)}) collective-permute-start(bf16[128,1024]{1,0:T(8,128)(2,1)} %copy-done.12), channel_id=1, source_target_pairs={{0,24},{4,28},{8,16},{12,20},{16,8},{20,12},{24,0},{28,4},{1,25},{... | collective-permute-start | bytes 786440 | tf_op jit(solution)/shard_map/ppermute | solution.py:129
  62.1 31.3 %collective-permute-start.17 = (bf16[128,1024]{1,0:T(8,128)(2,1)}, bf16[128,1024]{1,0:T(8,128)(2,1)}, u32[]{:S(2)}, u32[]{:S(2)}) collective-permute-start(bf16[128,1024]{1,0:T(8,128)(2,1)} %copy-done.11), channel_id=1, source_target_pairs={{0,8},{4,12},{8,0},{12,4},{16,24},{20,28},{24,16},{28,20},{1,9},{5... | collective-permute-start | bytes 786440 | tf_op jit(solution)/shard_map/ppermute | solution.py:129
  63.8 4.1 %copy-start.3 = (bf16[512,1280]{1,0:T(8,128)(2,1)}, bf16[512,1280]{1,0:T(8,128)(2,1)S(1)}, u32[]{:S(2)}) copy-start(bf16[512,1280]{1,0:T(8,128)(2,1)S(1)} %shard_map.124.refs_0_.refs_1_) | copy-start | bytes 3932164
  63.9 11.8 %copy-start.18 = (bf16[1,12,1024]{2,1,0:T(8,128)(2,1)S(1)}, bf16[1,12,1024]{2,1,0:T(8,128)(2,1)}, u32[]{:S(2)}) copy-start(bf16[1,12,1024]{2,1,0:T(8,128)(2,1)} %stack_reshape.6) | copy-start | bytes 73732
  67.9 0.7 copy-start.5
  68.6 20.2 %collective-permute-start.12 = (bf16[128,1024]{1,0:T(8,128)(2,1)}, bf16[128,1024]{1,0:T(8,128)(2,1)}, u32[]{:S(2)}, u32[]{:S(2)}) collective-permute-start(bf16[128,1024]{1,0:T(8,128)(2,1)} %get-tuple-element.41), channel_id=1, source_target_pairs={{0,8},{4,12},{8,0},{12,4},{16,24},{20,28},{24,16},{28,20},{1,9},{5... | collective-permute-start | bytes 786440 | tf_op jit(solution)/shard_map/ppermute | solution.py:129
  71.4 26.8 %collective-permute-start.18 = (bf16[128,1024]{1,0:T(8,128)(2,1)}, bf16[128,1024]{1,0:T(8,128)(2,1)}, u32[]{:S(2)}, u32[]{:S(2)}) collective-permute-start(bf16[128,1024]{1,0:T(8,128)(2,1)} %get-tuple-element.48), channel_id=1, source_target_pairs={{0,16},{4,20},{8,24},{12,28},{16,0},{20,4},{24,8},{28,12},{1,17},{... | collective-permute-start | bytes 786440 | tf_op jit(solution)/shard_map/ppermute | solution.py:129
  74.8 23.4 %collective-permute-start.19 = (bf16[128,1024]{1,0:T(8,128)(2,1)}, bf16[128,1024]{1,0:T(8,128)(2,1)}, u32[]{:S(2)}, u32[]{:S(2)}) collective-permute-start(bf16[128,1024]{1,0:T(8,128)(2,1)} %get-tuple-element.49), channel_id=1, source_target_pairs={{0,24},{4,28},{8,16},{12,20},{16,8},{20,12},{24,0},{28,4},{1,25},{... | collective-permute-start | bytes 786440 | tf_op jit(solution)/shard_map/ppermute | solution.py:129
  75.6 15.0 %copy-start.14 = (bf16[2,12,1024]{2,1,0:T(8,128)(2,1)}, bf16[2,12,1024]{2,1,0:T(8,128)(2,1)S(1)}, u32[]{:S(2)}) copy-start(bf16[2,12,1024]{2,1,0:T(8,128)(2,1)S(1)} %pad_maximum_fusion.3) | copy-start | bytes 147460
  75.7 1.3 copy-start.2
  77.0 1.3 copy-start.4
  78.3 12.4 %copy-start.19 = (s32[4,288]{1,0:T(4,128)S(1)}, s32[4,288]{1,0:T(4,128)}, u32[]{:S(2)}) copy-start(s32[4,288]{1,0:T(4,128)} %add_add_fusion) | copy-start | bytes 13828
  83.3 0.8 copy-start.8
  84.1 0.8 copy-start.9
  84.9 13.3 %copy-start.6 = (bf16[128,1024]{1,0:T(8,128)(2,1)S(1)}, bf16[128,1024]{1,0:T(8,128)(2,1)}, u32[]{:S(2)}) copy-start(bf16[128,1024]{1,0:T(8,128)(2,1)} %copy-done.5) | copy-start | bytes 786436
  88.9 25.2 %collective-permute-start.14 = (bf16[280,1024]{1,0:T(8,128)(2,1)}, bf16[280,1024]{1,0:T(8,128)(2,1)S(1)}, u32[]{:S(2)}, u32[]{:S(2)}) collective-permute-start(bf16[280,1024]{1,0:T(8,128)(2,1)} %get-tuple-element.43), channel_id=1, source_target_pairs={{0,8},{4,12},{8,0},{12,4},{16,24},{20,28},{24,16},{28,20},{1,9},{5... | collective-permute-start | bytes 1720328 | tf_op jit(solution)/shard_map/ppermute | solution.py:129
  91.5 45.5 %collective-permute-start.15 = (bf16[280,1024]{1,0:T(8,128)(2,1)}, bf16[280,1024]{1,0:T(8,128)(2,1)S(1)}, u32[]{:S(2)}, u32[]{:S(2)}) collective-permute-start(bf16[280,1024]{1,0:T(8,128)(2,1)} %copy-done.9), channel_id=1, source_target_pairs={{0,16},{4,20},{8,24},{12,28},{16,0},{20,4},{24,8},{28,12},{1,17},{... | collective-permute-start | bytes 1720328 | tf_op jit(solution)/shard_map/ppermute | solution.py:129
  95.6 41.3 %collective-permute-start.16 = (bf16[280,1024]{1,0:T(8,128)(2,1)}, bf16[280,1024]{1,0:T(8,128)(2,1)S(1)}, u32[]{:S(2)}, u32[]{:S(2)}) collective-permute-start(bf16[280,1024]{1,0:T(8,128)(2,1)} %copy-done.8), channel_id=1, source_target_pairs={{0,24},{4,28},{8,16},{12,20},{16,8},{20,12},{24,0},{28,4},{1,25},{... | collective-permute-start | bytes 1720328 | tf_op jit(solution)/shard_map/ppermute | solution.py:129
  100.2 39.2 %copy-start.25 = (f32[1024]{0:T(1024)S(1)}, f32[1024]{0:T(1024)}, u32[]{:S(2)}) copy-start(f32[1024]{0:T(1024)} %get-tuple-element.67) | copy-start | bytes 12292
  138.8 3.3 %copy-start.29 = (bf16[2048,1024]{1,0:T(8,128)(2,1)S(1)}, bf16[2048,1024]{1,0:T(8,128)(2,1)}, u32[]{:S(2)}) copy-start(bf16[2048,1024]{1,0:T(8,128)(2,1)} %param.14) | copy-start | bytes 12582916
  139.3 4.5 %collective-permute-start.22 = (f32[256]{0:T(256)S(1)}, f32[256]{0:T(256)S(1)}, u32[]{:S(2)}, u32[]{:S(2)}) collective-permute-start(f32[256]{0:T(256)S(1)} %pad_maximum_fusion.5), channel_id=1, source_target_pairs={{0,1},{1,0},{2,3},{3,2},{4,5},{5,4},{6,7},{7,6},{8,9},{9,8},{10,11... | collective-permute-start | bytes 3080 | tf_op jit(solution)/shard_map/ppermute | solution.py:23
  139.4 2.7 %copy-start.16 = (bf16[128,1024]{1,0:T(8,128)(2,1)S(1)}, bf16[128,1024]{1,0:T(8,128)(2,1)}, u32[]{:S(2)}) copy-start(bf16[128,1024]{1,0:T(8,128)(2,1)} %get-tuple-element.55) | copy-start | bytes 786436
  139.4 2.7 %copy-start.24 = (f32[1024]{0:T(1024)S(1)}, f32[1024]{0:T(1024)}, u32[]{:S(2)}) copy-start(f32[1024]{0:T(1024)} %get-tuple-element.66) | copy-start | bytes 12292
  143.2 23.7 %copy-start.28 = (s32[4]{0:T(128)S(1)}, s32[4]{0:T(128)}, u32[]{:S(2)}) copy-start(s32[4]{0:T(128)} %param.18) | copy-start | bytes 52
  143.2 23.7 %copy-start.13 = (s32[4,128,1]{2,1,0:T(8,128)S(1)}, s32[4,128,1]{2,1,0:T(8,128)}, u32[]{:S(2)}) copy-start(s32[4,128,1]{2,1,0:T(8,128)} %add.341) | copy-start | bytes 6148
  143.2 23.7 %copy-start.22 = (s32[128]{0:T(128)S(1)}, s32[128]{0:T(128)}, u32[]{:S(2)}) copy-start(s32[128]{0:T(128)} %add.329) | copy-start | bytes 1540
  143.2 1.7 collective-permute-start.20
  143.7 31.8 %copy-start.7 = (bf16[4,128,1024]{2,1,0:T(8,128)(2,1)S(1)}, bf16[4,128,1024]{2,1,0:T(8,128)(2,1)}, u32[]{:S(2)}) copy-start(bf16[4,128,1024]{2,1,0:T(8,128)(2,1)} %query_ref.1) | copy-start | bytes 3145732
  143.7 31.8 %copy-start.10 = (bf16[4,128,256]{2,1,0:T(8,128)(2,1)S(1)}, bf16[4,128,256]{2,1,0:T(8,128)(2,1)}, u32[]{:S(2)}) copy-start(bf16[4,128,256]{2,1,0:T(8,128)(2,1)} %text_ref.1) | copy-start | bytes 786436
  143.8 3.6 %collective-permute-start.23 = (f32[256]{0:T(256)S(1)}, f32[256]{0:T(256)S(1)}, u32[]{:S(2)}, u32[]{:S(2)}) collective-permute-start(f32[256]{0:T(256)S(1)} %fusion.56), channel_id=1, source_target_pairs={{0,2},{1,3},{2,0},{3,1},{4,6},{5,7},{6,4},{7,5},{8,10},{9,11},{10,... | collective-permute-start | bytes 3080 | tf_op jit(solution)/shard_map/ppermute | solution.py:23
  145.0 5.7 %collective-permute-start.21 = (bf16[1,256,256]{2,1,0:T(8,128)(2,1)S(1)}, bf16[1,256,256]{2,1,0:T(8,128)(2,1)S(1)}, u32[]{:S(2)}, u32[]{:S(2)}) collective-permute-start(bf16[1,256,256]{2,1,0:T(8,128)(2,1)S(1)} %dynamic-slice_convert_fusion), channel_id=1, source_target_pairs={{0,2},{1,3},{2,0},{3,1},{4,6},{5,7},{6,4},{7,5},{8,10},{9,11},{10,... | collective-permute-start | bytes 393224 | tf_op jit(solution)/shard_map/ppermute | solution.py:23
  151.7 23.8 %all-to-all-start = ((bf16[8,64,256]{2,1,0:T(8,128)(2,1)}), bf16[8,64,256]{2,1,0:T(8,128)(2,1)S(1)}, u32[]{:S(2)}, u32[]{:S(2)}) async-start(bf16[8,64,256]{2,1,0:T(8,128)(2,1)} %bitcast.17), calls=%async_computation | async-start | bytes 524288 | tf_op jit(solution)/shard_map/all_to_all | solution.py:427

commit v8 on v7

--- a/solution.py
+++ b/solution.py
@@ -180,22 +180,16 @@
     scalars = jnp.concatenate([places, jnp.full((4,), member, jnp.int32)])
     early, _ = lax.optimization_barrier((moved[0], swapped))
     held = [order_rows(scalars, share_panels(early), share)]
-    kv = [0.0, 0.0]
-    squares = [0.0, 0.0]
-    everyone = None
     eighth = w_merge.shape[1] // 8
     sent = []
 
     def finish(step):
-        halves, first, count = PLAN[step]
+        _, first, count = PLAN[step]
         merged = sum_direct(*sent[step]).astype(jnp.float32)
         at = slice(first * eighth, (first + count) * eighth)
         gained = (merged * ln_gain[at].astype(jnp.float32)[None, :]).astype(jnp.bfloat16)
         squared = jnp.sum(merged * merged, axis=1)
-        product = jnp.dot(gained, w_kv[at], preferred_element_type=jnp.float32)
-        for i, h in enumerate(halves):
-            squares[h] = squares[h] + squared[i * half : (i + 1) * half]
-            kv[h] = kv[h] + product[i * half : (i + 1) * half]
+        return squared, jnp.dot(gained, w_kv[at], preferred_element_type=jnp.float32)
 
     for step, (halves, first, count) in enumerate(PLAN):
         first, count = first * eighth, count * eighth
@@ -223,12 +217,12 @@
             before += [sent[step - 2][1][2]] if step >= 2 else []
             parts, _ = lax.optimization_barrier((parts, before))
         sent.append((parts, send_direct(parts)))
-    for step in range(len(PLAN)):
-        finish(step)
+    done = [finish(step) for step in range(len(PLAN))]
+    squares, kv = [jnp.concatenate([done[0][i], done[1][i]], axis=0) + done[2][i] for i in range(2)]
     rows = sent[RIDE][0][0].shape[0]
     everyone = riding + [other[rows:] for other in sent[RIDE][1]]
     everyone = jnp.stack(everyone).reshape((4,) + small_shape)
-    return jnp.concatenate(kv), jnp.concatenate(squares), everyone
+    return kv, squares, everyone
 
 
 def scatter_heads(kv, squares):

time: 182 us -> 190 us (1.044)
  starting transfers between devices: 54.6 us -> 59.7 us
  matrix products: 4.59 us -> 7.51 us
    ppermute x11, waiting for transfers between devices: 18.2 us -> 8.35 us  [flip(): return lax.ppermute(value, axis, [(i, i ^ bit) for i in range(count)])]
    ppermute x9, waiting for transfers between devices: 40.7 us -> 49.3 us  [send_direct(): lax.ppermute(part, 'seq', along([(a, a ^ k) for a in range(4)]))]
    ppermute x9, starting transfers between devices: 12.2 us -> 19.2 us  [send_direct(): lax.ppermute(part, 'seq', along([(a, a ^ k) for a in range(4)]))]
    dot_general x3, matrix products: 3.57 us -> 6.49 us  [finish(): jnp.dot(gained, w_kv[at], preferred_element_type=jnp.float32)]
  transfers between devices with their start and end apart: 25 -> 25, of which waited for: 9 -> 11; matrix products, arithmetic and copies ran while one was open for 14% -> 15% of each run, Pallas kernels for 9% -> 8%
where the time goes in v8:
time: 190 us; the launch traced here: 189 us
  waiting for transfers between devices  66.8 us (35%)
  starting transfers between devices  59.7 us (31%)
  local copies, waits for them, and re-layouts  21.9 us (12%)
  Pallas kernels  20.6 us (11%)
  other arithmetic  11.2 us (6%)
  matrix products  7.51 us (4%)
    ppermute x9, waiting for transfers between devices, send_direct(): lax.ppermute(part, 'seq', along([(a, a ^ k) for a in range(4)]))  49.3 us
    ppermute x9, starting transfers between devices, send_direct(): lax.ppermute(part, 'seq', along([(a, a ^ k) for a in range(4)]))  19.2 us
    ppermute x11, starting transfers between devices, flip(): return lax.ppermute(value, axis, [(i, i ^ bit) for i in range(count)])  18.6 us
    all_to_all x1, starting transfers between devices, shards(): lax.all_to_all(outgoing, 'seq', split_axis=0, concat_axis=0, tiled=True)  13.7 us
    pallas_call x3, Pallas kernels, partial_products(): pl.pallas_call(functools.partial(partial_kernel, halves, len(riding)), gr...  12.8 us
    ppermute x11, waiting for transfers between devices, flip(): return lax.ppermute(value, axis, [(i, i ^ bit) for i in range(count)])  8.35 us
    all_to_all x1, waiting for transfers between devices, shards(): lax.all_to_all(outgoing, 'seq', split_axis=0, concat_axis=0, tiled=True)  8.04 us
    dot_general x3, matrix products, finish(): jnp.dot(gained, w_kv[at], preferred_element_type=jnp.float32)  6.49 us
  transfers between devices with their start and end apart: 25, of which 11 were waited for; matrix products, arithmetic and copies ran while one was open for 15% of the time, Pallas kernels for 8%

profile of v8, /device:TPU:0, one launch (start us, length us, event | category | flops | bytes accessed | tf_op | source)
XLA Modules:
  0.0 189.0 jit_solution(8586871416115065931)
XLA Ops:
  0.6 1.8 slice_bitcast_fusion.1
  2.5 3.0 %collective-permute-start = (bf16[128,1280]{1,0:T(8,128)(2,1)}, bf16[128,1280]{1,0:T(8,128)(2,1)}, u32[]{:S(2)}, u32[]{:S(2)}) collective-permute-start(bf16[128,1280]{1,0:T(8,128)(2,1)} %get-tuple-element.62), channel_id=1, source_target_pairs={{0,2},{1,3},{2,0},{3,1},{4,6},{5,7},{6,4},{7,5},{8,10},{9,11},{10,... | collective-permute-start | bytes 983048 | tf_op jit(solution)/shard_map/ppermute | solution.py:23
  5.4 0.8 collective-permute-start.3
  6.2 3.5 %fusion.45 = (bf16[640,1024]{1,0:T(8,128)(2,1)}, bf16[640,1024]{1,0:T(8,128)(2,1)}) fusion(bf16[640,2048]{1,0:T(8,128)(2,1)} %refs_2_.1), kind=kLoop, calls=%fused_computation.117 | loop fusion | bytes 5242880 | tf_op jit(solution)/shard_map/slice | solution.py:163
  9.7 1.5 collective-permute-start.7
  11.9 0.8 gather_fusion.2
  13.9 2.6 %pad_maximum_fusion = bf16[652,1024]{1,0:T(8,128)(2,1)} fusion(bf16[12,1024]{1,0:T(8,128)(2,1)S(1)} %reshape.336, bf16[640,1024]{1,0:T(8,128)(2,1)} %get-tuple-element.56), kind=kLoop, calls=%fused_computation.10 | loop fusion | flops 2670592 | bytes 2670592 | tf_op jit(solution)/shard_map/concatenate | solution.py:165
  16.5 3.3 %collective-permute-done = bf16[128,1280]{1,0:T(8,128)(2,1)} collective-permute-done((bf16[128,1280]{1,0:T(8,128)(2,1)}, bf16[128,1280]{1,0:T(8,128)(2,1)}, u32[]{:S(2)}, u32[]{:S(2)}) %collective-permute-start) | collective-permute-done | bytes 327712 | tf_op jit(solution)/shard_map/ppermute | solution.py:23
  19.7 2.5 %collective-permute-start.4 = (bf16[128,1280]{1,0:T(8,128)(2,1)S(1)}, bf16[128,1280]{1,0:T(8,128)(2,1)}, u32[]{:S(2)}, u32[]{:S(2)}) collective-permute-start(bf16[128,1280]{1,0:T(8,128)(2,1)S(1)} %collective-permute-done.3.refs_0_), channel_id=1, source_target_pairs={{0,2},{1,3},{2,0},{3,1},{4,6},{5,7},{6,4},{7,5},{8,10},{9,11},{10,... | collective-permute-start | bytes 983048 | tf_op jit(solution)/shard_map/ppermute | solution.py:23
  22.2 1.5 collective-permute-start.1
  23.7 0.6 pad.6.clone
  24.3 0.7 pad.8.clone
  25.0 0.6 slice_convert_fusion.2
  25.6 1.9 %collective-permute-start.5 = (bf16[128,1280]{1,0:T(8,128)(2,1)S(1)}, bf16[128,1280]{1,0:T(8,128)(2,1)S(1)}, u32[]{:S(2)}, u32[]{:S(2)}) collective-permute-start(bf16[128,1280]{1,0:T(8,128)(2,1)S(1)} %collective-permute-done.3.refs_0_), channel_id=1, source_target_pairs={{0,1},{1,0},{2,3},{3,2},{4,5},{5,4},{6,7},{7,6},{8,9},{9,8},{10,11... | collective-permute-start | bytes 983048 | tf_op jit(solution)/shard_map/ppermute | solution.py:23
  27.5 4.5 %collective-permute-start.2 = (bf16[128,1280]{1,0:T(8,128)(2,1)}, bf16[128,1280]{1,0:T(8,128)(2,1)S(1)}, u32[]{:S(2)}, u32[]{:S(2)}) collective-permute-start(bf16[128,1280]{1,0:T(8,128)(2,1)} %collective-permute-done), channel_id=1, source_target_pairs={{2,0},{3,10},{0,16},{1,26},{6,4},{7,14},{4,20},{5,30},{10,2},{11,8... | collective-permute-start | bytes 983048 | tf_op jit(solution)/shard_map/ppermute | solution.py:37
  32.0 3.5 %collective-permute-start.6 = (bf16[128,1280]{1,0:T(8,128)(2,1)}, bf16[128,1280]{1,0:T(8,128)(2,1)S(1)}, u32[]{:S(2)}, u32[]{:S(2)}) collective-permute-start(bf16[128,1280]{1,0:T(8,128)(2,1)} %collective-permute-done.4.refs_1_), channel_id=1, source_target_pairs={{0,1},{1,0},{2,3},{3,2},{4,5},{5,4},{6,7},{7,6},{8,9},{9,8},{10,11... | collective-permute-start | bytes 983048 | tf_op jit(solution)/shard_map/ppermute | solution.py:23
  35.5 0.7 iota_add_fusion.1
  36.2 0.8 collective-permute-done.6.refs_3_
  37.0 1.6 shard_map.122.refs_0_
  38.6 1.1 collective-permute-done.7.refs_2_
  39.7 3.6 %shard_map.123 = (bf16[128,1024]{1,0:T(8,128)(2,1)S(1)}, bf16[128,1024]{1,0:T(8,128)(2,1)}, bf16[128,1024]{1,0:T(8,128)(2,1)}, bf16[128,1024]{1,0:T(8,128)(2,1)}) custom-call(bf16[512,1280]{1,0:T(8,128)(2,1)S(1)} %shard_map.122.refs_0_, bf16[640,2048]{1,0:T(8,128)(2,1)S(1)} %copy-done, bf16[640,1024]{1,0:T(8,128)(2,1)} %collective-permute-done.7.refs_2_), custom_call_target="tpu_custom_call" | custom-call | bytes 2048 | tf_op jit(solution)/shard_map/pallas_call | solution.py:109
  43.3 5.9 %collective-permute-start.11 = (bf16[128,1024]{1,0:T(8,128)(2,1)}, bf16[128,1024]{1,0:T(8,128)(2,1)}, u32[]{:S(2)}, u32[]{:S(2)}) collective-permute-start(bf16[128,1024]{1,0:T(8,128)(2,1)} %get-tuple-element.34), channel_id=1, source_target_pairs={{0,16},{4,20},{8,24},{12,28},{16,0},{20,4},{24,8},{28,12},{1,17},{... | collective-permute-start | bytes 786440 | tf_op jit(solution)/shard_map/ppermute | solution.py:129
  49.2 1.2 collective-permute-start.13
  50.8 3.3 %collective-permute-start.8 = (bf16[128,1280]{1,0:T(8,128)(2,1)S(1)}, bf16[128,1280]{1,0:T(8,128)(2,1)S(1)}, u32[]{:S(2)}, u32[]{:S(2)}) collective-permute-start(bf16[128,1280]{1,0:T(8,128)(2,1)S(1)} %collective-permute-done.2.refs_0_), channel_id=1, source_target_pairs={{0,2},{1,3},{2,0},{3,1},{4,6},{5,7},{6,4},{7,5},{8,10},{9,11},{10,... | collective-permute-start | bytes 983048 | tf_op jit(solution)/shard_map/ppermute | solution.py:23
  54.1 0.7 add_add_fusion
  54.8 1.4 stack_reshape.6
  56.1 0.8 broadcast_in_dim.28
  56.9 1.6 add.333
  58.5 0.7 broadcast_in_dim.27.seen_ref
  59.2 1.5 add.334.all_ref
  60.7 7.0 %collective-permute-done.11 = bf16[128,1024]{1,0:T(8,128)(2,1)} collective-permute-done((bf16[128,1024]{1,0:T(8,128)(2,1)}, bf16[128,1024]{1,0:T(8,128)(2,1)}, u32[]{:S(2)}, u32[]{:S(2)}) %collective-permute-start.11) | collective-permute-done | bytes 262176 | tf_op jit(solution)/shard_map/ppermute | solution.py:129
  68.2 0.8 collective-permute-done.17
  69.0 2.5 %fusion.12 = (f32[128]{0:T(128)}, bf16[128,1024]{1,0:T(8,128)(2,1)}) fusion(bf16[128,1024]{1,0:T(8,128)(2,1)} %collective-permute-done.13, bf16[128,1024]{1,0:T(8,128)(2,1)} %collective-permute-done.11, bf16[128,1024]{1,0:T(8,128)(2,1)} %collective-permute-done.17, bf16[128,1024]{1,0:T(8,128)(2,1)S(1)} %get-tuple-element.28), kind=kLoop, calls=%fused_computation.22 | loop fusion | flops 1441664 | bytes 1311232 | tf_op jit(solution)/shard_map/reduce_sum | solution.py:191
  71.5 0.7 shard_map.124.refs_0_.refs_1_
  72.2 4.1 %shard_map.125 = (bf16[128,1024]{1,0:T(8,128)(2,1)S(1)}, bf16[128,1024]{1,0:T(8,128)(2,1)}, bf16[128,1024]{1,0:T(8,128)(2,1)}, bf16[128,1024]{1,0:T(8,128)(2,1)}) custom-call(bf16[512,1280]{1,0:T(8,128)(2,1)S(1)} %shard_map.124.refs_0_.refs_1_, bf16[640,2048]{1,0:T(8,128)(2,1)S(1)} %copy-done, bf16[640,1024]{1,0:T(8,128)(2,1)} %collective-permute-done.7.refs_2_), custom_call_target="tpu_custom_call" | custom-call | bytes 2048 | tf_op jit(solution)/shard_map/pallas_call | solution.py:109
  76.3 4.9 %collective-permute-start.12 = (bf16[128,1024]{1,0:T(8,128)(2,1)}, bf16[128,1024]{1,0:T(8,128)(2,1)}, u32[]{:S(2)}, u32[]{:S(2)}) collective-permute-start(bf16[128,1024]{1,0:T(8,128)(2,1)} %get-tuple-element.41), channel_id=1, source_target_pairs={{0,8},{4,12},{8,0},{12,4},{16,24},{20,28},{24,16},{28,20},{1,9},{5... | collective-permute-start | bytes 786440 | tf_op jit(solution)/shard_map/ppermute | solution.py:129
  81.1 2.4 %collective-permute-start.19 = (bf16[128,1024]{1,0:T(8,128)(2,1)}, bf16[128,1024]{1,0:T(8,128)(2,1)}, u32[]{:S(2)}, u32[]{:S(2)}) collective-permute-start(bf16[128,1024]{1,0:T(8,128)(2,1)} %get-tuple-element.48), channel_id=1, source_target_pairs={{0,24},{4,28},{8,16},{12,20},{16,8},{20,12},{24,0},{28,4},{1,25},{... | collective-permute-start | bytes 786440 | tf_op jit(solution)/shard_map/ppermute | solution.py:129
  83.5 0.8 slice_bitcast_fusion.5
  84.4 1.3 copy-done.2
  85.7 1.3 copy-done.4
  87.0 5.1 %shard_map.126 = (bf16[256,1024]{1,0:T(8,128)(2,1)S(1)}, bf16[280,1024]{1,0:T(8,128)(2,1)}, bf16[280,1024]{1,0:T(8,128)(2,1)S(1)}, bf16[280,1024]{1,0:T(8,128)(2,1)S(1)}) custom-call(bf16[512,1280]{1,0:T(8,128)(2,1)S(1)} %copy-done.2, bf16[512,1280]{1,0:T(8,128)(2,1)S(1)} %copy-done.4, bf16[640,2048]{1,0:T(8,128)(2,1)S(1)} %copy-done, ...), custom_call_target="tpu_custom_call" | custom-call | bytes 2048 | tf_op jit(solution)/shard_map/pallas_call | solution.py:109
  92.1 0.8 copy-done.7
  93.0 0.8 copy-done.9
  93.8 1.1 collective-permute-start.14
  94.8 1.2 fusion.4
  96.1 1.0 collective-permute-start.15
  97.1 2.4 %collective-permute-start.16 = (bf16[280,1024]{1,0:T(8,128)(2,1)S(1)}, bf16[280,1024]{1,0:T(8,128)(2,1)}, u32[]{:S(2)}, u32[]{:S(2)}) collective-permute-start(bf16[280,1024]{1,0:T(8,128)(2,1)S(1)} %copy-done.8), channel_id=1, source_target_pairs={{0,24},{4,28},{8,16},{12,20},{16,8},{20,12},{24,0},{28,4},{1,25},{... | collective-permute-start | bytes 1720328 | tf_op jit(solution)/shard_map/ppermute | solution.py:129
  99.5 3.3 %collective-permute-done.18 = bf16[128,1024]{1,0:T(8,128)(2,1)} collective-permute-done((bf16[128,1024]{1,0:T(8,128)(2,1)}, bf16[128,1024]{1,0:T(8,128)(2,1)}, u32[]{:S(2)}, u32[]{:S(2)}) %collective-permute-start.18) | collective-permute-done | bytes 262176 | tf_op jit(solution)/shard_map/ppermute | solution.py:129
  102.8 1.4 fusion.14
  104.2 2.8 %fusion.2 = f32[128,1024]{1,0:T(8,128)} fusion(bf16[2048,1024]{1,0:T(8,128)(2,1)} %param.14, bf16[128,1024]{1,0:T(8,128)(2,1)S(1)} %get-tuple-element.53, f32[1024]{0:T(1024)S(1)} %copy-done.25), kind=kOutput, calls=%fused_computation.5 | convolution fusion | flops 268828672 | bytes 2887680 | tf_op jit(solution)/shard_map/dot_general | solution.py:192
  107.0 11.3 %collective-permute-done.14 = bf16[280,1024]{1,0:T(8,128)(2,1)S(1)} collective-permute-done((bf16[280,1024]{1,0:T(8,128)(2,1)}, bf16[280,1024]{1,0:T(8,128)(2,1)S(1)}, u32[]{:S(2)}, u32[]{:S(2)}) %collective-permute-start.14) | collective-permute-done | bytes 573472 | tf_op jit(solution)/shard_map/ppermute | solution.py:129
  118.3 26.9 %collective-permute-done.15 = bf16[280,1024]{1,0:T(8,128)(2,1)S(1)} collective-permute-done((bf16[280,1024]{1,0:T(8,128)(2,1)S(1)}, bf16[280,1024]{1,0:T(8,128)(2,1)S(1)}, u32[]{:S(2)}, u32[]{:S(2)}) %collective-permute-start.15) | collective-permute-done | bytes 573472 | tf_op jit(solution)/shard_map/ppermute | solution.py:129
  145.2 0.9 slice_bitcast_fusion.2
  146.3 0.6 gather_fusion
  146.9 0.6 gather_fusion.1
  147.9 1.4 fusion.10
  149.5 2.4 %fusion.6 = f32[256,1024]{1,0:T(8,128)S(1)} fusion(bf16[2048,1024]{1,0:T(8,128)(2,1)} %param.14, f32[128,1024]{1,0:T(8,128)S(1)} %copy-done.32, f32[128,1024]{1,0:T(8,128)} %fusion.4, bf16[256,1024]{1,0:T(8,128)(2,1)S(1)} %get-tuple-element.55, f32[1024]{0:T(1024)S(1)} %copy-done.24), kind=kOutput, calls=%fused_computation.9 | convolution fusion | flops 538181632 | bytes 4722688 | tf_op jit(solution)/shard_map/dot_general | solution.py:192
  152.8 2.4 %collective-permute-start.23 = (f32[256]{0:T(256)S(1)}, f32[256]{0:T(256)S(1)}, u32[]{:S(2)}, u32[]{:S(2)}) collective-permute-start(f32[256]{0:T(256)S(1)} %add.309), channel_id=1, source_target_pairs={{0,2},{1,3},{2,0},{3,1},{4,6},{5,7},{6,4},{7,5},{8,10},{9,11},{10,... | collective-permute-start | bytes 3080 | tf_op jit(solution)/shard_map/ppermute | solution.py:23
  155.3 0.9 collective-permute-start.21
  156.8 3.8 %collective-permute-done.21 = bf16[1,256,256]{2,1,0:T(8,128)(2,1)S(1)} collective-permute-done((bf16[1,256,256]{2,1,0:T(8,128)(2,1)S(1)}, bf16[1,256,256]{2,1,0:T(8,128)(2,1)S(1)}, u32[]{:S(2)}, u32[]{:S(2)}) %collective-permute-start.21) | collective-permute-done | bytes 131104 | tf_op jit(solution)/shard_map/ppermute | solution.py:23
  160.5 1.0 convolution_convert_fusion
  161.5 13.7 %all-to-all-start = ((bf16[8,64,256]{2,1,0:T(8,128)(2,1)}), bf16[8,64,256]{2,1,0:T(8,128)(2,1)S(1)}, u32[]{:S(2)}, u32[]{:S(2)}) async-start(bf16[8,64,256]{2,1,0:T(8,128)(2,1)} %bitcast.17), calls=%async_computation | async-start | bytes 524288 | tf_op jit(solution)/shard_map/all_to_all | solution.py:421
  175.4 8.0 %all-to-all-done = bf16[8,64,256]{2,1,0:T(8,128)(2,1)S(1)} async-done(((bf16[8,64,256]{2,1,0:T(8,128)(2,1)}), bf16[8,64,256]{2,1,0:T(8,128)(2,1)S(1)}, u32[]{:S(2)}, u32[]{:S(2)}) %all-to-all-start) | async-done | bytes 262176 | tf_op jit(solution)/shard_map/all_to_all | solution.py:421
  183.4 5.5 %shard_map.127 = (bf16[4,128,1024]{2,1,0:T(8,128)(2,1)}, bf16[256,256]{1,0:T(8,128)(2,1)}) custom-call(s32[4]{0:T(128)S(1)} %fusion.36.place_ref, bf16[4,128,1024]{2,1,0:T(8,128)(2,1)S(1)} %copy-done.6, bf16[8,32,256]{2,1,0:T(8,128)(2,1)S(1)} %slice.91.prefix_ref, bf16[4,128,256]{2,1,0:T(8,128)(2,1)S(1)} %copy-done.11, bf16[512,256]{1,0:T(8,128)(2,1)S(1)} %bitcast.53, ...), custom_call_target="tpu_custom_call" | custom-call | flops 603979776 | bytes 4194304 | tf_op jit(solution)/shard_map/pallas_call | solution.py:317
  (138 shorter events, 5.2 us)
Async XLA Ops:
  2.5 17.3 %collective-permute-start = (bf16[128,1280]{1,0:T(8,128)(2,1)}, bf16[128,1280]{1,0:T(8,128)(2,1)}, u32[]{:S(2)}, u32[]{:S(2)}) collective-permute-start(bf16[128,1280]{1,0:T(8,128)(2,1)} %get-tuple-element.62), channel_id=1, source_target_pairs={{0,2},{1,3},{2,0},{3,1},{4,6},{5,7},{6,4},{7,5},{8,10},{9,11},{10,... | collective-permute-start | bytes 983048 | tf_op jit(solution)/shard_map/ppermute | solution.py:23
  5.4 5.8 %copy-start.27 = (s32[32,1]{0,1:T(1,128)S(1)}, s32[32,1]{0,1:T(1,128)}, u32[]{:S(2)}) copy-start(s32[32,1]{0,1:T(1,128)} %param.15) | copy-start | bytes 388
  5.4 6.0 %copy-start.30 = (s32[1,4]{1,0:T(1,128)S(1)}, s32[1,4]{1,0:T(1,128)}, u32[]{:S(2)}) copy-start(s32[1,4]{1,0:T(1,128)} %param.17) | copy-start | bytes 52
  5.4 14.3 %collective-permute-start.3 = (bf16[128,1280]{1,0:T(8,128)(2,1)S(1)}, bf16[128,1280]{1,0:T(8,128)(2,1)S(1)}, u32[]{:S(2)}, u32[]{:S(2)}) collective-permute-start(bf16[128,1280]{1,0:T(8,128)(2,1)S(1)} %get-tuple-element.63), channel_id=1, source_target_pairs={{0,0},{1,10},{2,16},{3,26},{4,4},{5,14},{6,20},{7,30},{8,2},{9,8},... | collective-permute-start | bytes 983048 | tf_op jit(solution)/shard_map/ppermute | solution.py:37
  9.7 3.5 %copy-start.31 = (s32[32]{0:T(128)S(1)}, s32[32]{0:T(128)}, u32[]{:S(2)}) copy-start(s32[32]{0:T(128)} %param.16) | copy-start | bytes 388
  9.7 3.5 %copy-start.18 = (bf16[1,32,256]{2,1,0:T(8,128)(2,1)S(1)}, bf16[1,32,256]{2,1,0:T(8,128)(2,1)}, u32[]{:S(2)}) copy-start(bf16[1,32,256]{2,1,0:T(8,128)(2,1)} %param.19) | copy-start | bytes 49156
  9.7 30.0 %collective-permute-start.7 = (bf16[640,1024]{1,0:T(8,128)(2,1)}, bf16[640,1024]{1,0:T(8,128)(2,1)}, u32[]{:S(2)}, u32[]{:S(2)}) collective-permute-start(bf16[640,1024]{1,0:T(8,128)(2,1)} %get-tuple-element.57), channel_id=1, source_target_pairs={{4,0},{0,4},{12,8},{8,12},{20,16},{16,20},{28,24},{24,28},{5,1},{1... | collective-permute-start | bytes 3932168 | tf_op jit(solution)/shard_map/ppermute | solution.py:174
  11.9 13.1 %copy-start.23 = (bf16[2048]{0:T(1024)(128)(2,1)S(1)}, bf16[2048]{0:T(1024)(128)(2,1)}, u32[]{:S(2)}) copy-start(bf16[2048]{0:T(1024)(128)(2,1)} %param.13) | copy-start | bytes 12292
  13.0 22.5 %copy-start.21 = (s32[128]{0:T(128)}, s32[128]{0:T(128)S(1)}, u32[]{:S(2)}) copy-start(s32[128]{0:T(128)S(1)} %add.321) | copy-start | bytes 1540
  13.1 0.6 copy-start.13
  13.2 0.6 copy-start.16
  13.8 25.9 %copy-start = (bf16[640,2048]{1,0:T(8,128)(2,1)S(1)}, bf16[640,2048]{1,0:T(8,128)(2,1)}, u32[]{:S(2)}) copy-start(bf16[640,2048]{1,0:T(8,128)(2,1)} %refs_2_.1) | copy-start | bytes 7864324
  19.7 12.2 %collective-permute-start.4 = (bf16[128,1280]{1,0:T(8,128)(2,1)S(1)}, bf16[128,1280]{1,0:T(8,128)(2,1)}, u32[]{:S(2)}, u32[]{:S(2)}) collective-permute-start(bf16[128,1280]{1,0:T(8,128)(2,1)S(1)} %collective-permute-done.3.refs_0_), channel_id=1, source_target_pairs={{0,2},{1,3},{2,0},{3,1},{4,6},{5,7},{6,4},{7,5},{8,10},{9,11},{10,... | collective-permute-start | bytes 983048 | tf_op jit(solution)/shard_map/ppermute | solution.py:23
  22.2 61.3 %collective-permute-start.1 = (bf16[652,1024]{1,0:T(8,128)(2,1)}, bf16[652,1024]{1,0:T(8,128)(2,1)}, u32[]{:S(2)}, u32[]{:S(2)}) collective-permute-start(bf16[652,1024]{1,0:T(8,128)(2,1)} %pad_maximum_fusion), channel_id=1, source_target_pairs={{4,0},{0,4},{12,8},{8,12},{20,16},{16,20},{28,24},{24,28},{5,1},{1... | collective-permute-start | bytes 4005896 | tf_op jit(solution)/shard_map/ppermute | solution.py:174
  25.6 10.6 %collective-permute-start.5 = (bf16[128,1280]{1,0:T(8,128)(2,1)S(1)}, bf16[128,1280]{1,0:T(8,128)(2,1)S(1)}, u32[]{:S(2)}, u32[]{:S(2)}) collective-permute-start(bf16[128,1280]{1,0:T(8,128)(2,1)S(1)} %collective-permute-done.3.refs_0_), channel_id=1, source_target_pairs={{0,1},{1,0},{2,3},{3,2},{4,5},{5,4},{6,7},{7,6},{8,9},{9,8},{10,11... | collective-permute-start | bytes 983048 | tf_op jit(solution)/shard_map/ppermute | solution.py:23
  27.5 15.8 %collective-permute-start.2 = (bf16[128,1280]{1,0:T(8,128)(2,1)}, bf16[128,1280]{1,0:T(8,128)(2,1)S(1)}, u32[]{:S(2)}, u32[]{:S(2)}) collective-permute-start(bf16[128,1280]{1,0:T(8,128)(2,1)} %collective-permute-done), channel_id=1, source_target_pairs={{2,0},{3,10},{0,16},{1,26},{6,4},{7,14},{4,20},{5,30},{10,2},{11,8... | collective-permute-start | bytes 983048 | tf_op jit(solution)/shard_map/ppermute | solution.py:37
  32.0 5.0 %collective-permute-start.6 = (bf16[128,1280]{1,0:T(8,128)(2,1)}, bf16[128,1280]{1,0:T(8,128)(2,1)S(1)}, u32[]{:S(2)}, u32[]{:S(2)}) collective-permute-start(bf16[128,1280]{1,0:T(8,128)(2,1)} %collective-permute-done.4.refs_1_), channel_id=1, source_target_pairs={{0,1},{1,0},{2,3},{3,2},{4,5},{5,4},{6,7},{7,6},{8,9},{9,8},{10,11... | collective-permute-start | bytes 983048 | tf_op jit(solution)/shard_map/ppermute | solution.py:23
  38.6 4.7 %copy-start.1 = (bf16[512,1280]{1,0:T(8,128)(2,1)}, bf16[512,1280]{1,0:T(8,128)(2,1)S(1)}, u32[]{:S(2)}) copy-start(bf16[512,1280]{1,0:T(8,128)(2,1)S(1)} %shard_map.122.refs_0_) | copy-start | bytes 3932164
  38.6 15.5 %copy-start.19 = (s32[288]{0:T(512)S(1)}, s32[288]{0:T(512)}, u32[]{:S(2)}) copy-start(s32[288]{0:T(512)} %pad.6.clone) | copy-start | bytes 3460
  38.6 15.5 %copy-start.20 = (s32[288]{0:T(512)S(1)}, s32[288]{0:T(512)}, u32[]{:S(2)}) copy-start(s32[288]{0:T(512)} %pad.8.clone) | copy-start | bytes 3460
  43.3 24.4 %collective-permute-start.11 = (bf16[128,1024]{1,0:T(8,128)(2,1)}, bf16[128,1024]{1,0:T(8,128)(2,1)}, u32[]{:S(2)}, u32[]{:S(2)}) collective-permute-start(bf16[128,1024]{1,0:T(8,128)(2,1)} %get-tuple-element.34), channel_id=1, source_target_pairs={{0,16},{4,20},{8,24},{12,28},{16,0},{20,4},{24,8},{28,12},{1,17},{... | collective-permute-start | bytes 786440 | tf_op jit(solution)/shard_map/ppermute | solution.py:129
  49.2 19.0 %collective-permute-start.13 = (bf16[128,1024]{1,0:T(8,128)(2,1)}, bf16[128,1024]{1,0:T(8,128)(2,1)}, u32[]{:S(2)}, u32[]{:S(2)}) collective-permute-start(bf16[128,1024]{1,0:T(8,128)(2,1)} %get-tuple-element.42), channel_id=1, source_target_pairs={{0,24},{4,28},{8,16},{12,20},{16,8},{20,12},{24,0},{28,4},{1,25},{... | collective-permute-start | bytes 786440 | tf_op jit(solution)/shard_map/ppermute | solution.py:129
  50.5 18.5 %collective-permute-start.17 = (bf16[128,1024]{1,0:T(8,128)(2,1)}, bf16[128,1024]{1,0:T(8,128)(2,1)}, u32[]{:S(2)}, u32[]{:S(2)}) collective-permute-start(bf16[128,1024]{1,0:T(8,128)(2,1)} %get-tuple-element.46), channel_id=1, source_target_pairs={{0,8},{4,12},{8,0},{12,4},{16,24},{20,28},{24,16},{28,20},{1,9},{5... | collective-permute-start | bytes 786440 | tf_op jit(solution)/shard_map/ppermute | solution.py:129
  50.8 16.9 %collective-permute-start.8 = (bf16[128,1280]{1,0:T(8,128)(2,1)S(1)}, bf16[128,1280]{1,0:T(8,128)(2,1)S(1)}, u32[]{:S(2)}, u32[]{:S(2)}) collective-permute-start(bf16[128,1280]{1,0:T(8,128)(2,1)S(1)} %collective-permute-done.2.refs_0_), channel_id=1, source_target_pairs={{0,2},{1,3},{2,0},{3,1},{4,6},{5,7},{6,4},{7,5},{8,10},{9,11},{10,... | collective-permute-start | bytes 983048 | tf_op jit(solution)/shard_map/ppermute | solution.py:23
  67.7 3.8 %collective-permute-start.9 = (bf16[128,1280]{1,0:T(8,128)(2,1)S(1)}, bf16[128,1280]{1,0:T(8,128)(2,1)S(1)}, u32[]{:S(2)}, u32[]{:S(2)}) collective-permute-start(bf16[128,1280]{1,0:T(8,128)(2,1)S(1)} %collective-permute-done.2.refs_0_), channel_id=1, source_target_pairs={{0,1},{1,0},{2,3},{3,2},{4,5},{5,4},{6,7},{7,6},{8,9},{9,8},{10,11... | collective-permute-start | bytes 983048 | tf_op jit(solution)/shard_map/ppermute | solution.py:23
  67.8 3.7 %collective-permute-start.10 = (bf16[128,1280]{1,0:T(8,128)(2,1)S(1)}, bf16[128,1280]{1,0:T(8,128)(2,1)S(1)}, u32[]{:S(2)}, u32[]{:S(2)}) collective-permute-start(bf16[128,1280]{1,0:T(8,128)(2,1)S(1)} %collective-permute-done.8.refs_1_), channel_id=1, source_target_pairs={{0,1},{1,0},{2,3},{3,2},{4,5},{5,4},{6,7},{7,6},{8,9},{9,8},{10,11... | collective-permute-start | bytes 983048 | tf_op jit(solution)/shard_map/ppermute | solution.py:23
  72.2 4.1 %copy-start.3 = (bf16[512,1280]{1,0:T(8,128)(2,1)}, bf16[512,1280]{1,0:T(8,128)(2,1)S(1)}, u32[]{:S(2)}) copy-start(bf16[512,1280]{1,0:T(8,128)(2,1)S(1)} %shard_map.124.refs_0_.refs_1_) | copy-start | bytes 3932164
  72.2 12.1 %copy-start.17 = (bf16[1,12,1024]{2,1,0:T(8,128)(2,1)S(1)}, bf16[1,12,1024]{2,1,0:T(8,128)(2,1)}, u32[]{:S(2)}) copy-start(bf16[1,12,1024]{2,1,0:T(8,128)(2,1)} %stack_reshape.6) | copy-start | bytes 73732
  76.3 17.5 %collective-permute-start.12 = (bf16[128,1024]{1,0:T(8,128)(2,1)}, bf16[128,1024]{1,0:T(8,128)(2,1)}, u32[]{:S(2)}, u32[]{:S(2)}) collective-permute-start(bf16[128,1024]{1,0:T(8,128)(2,1)} %get-tuple-element.41), channel_id=1, source_target_pairs={{0,8},{4,12},{8,0},{12,4},{16,24},{20,28},{24,16},{28,20},{1,9},{5... | collective-permute-start | bytes 786440 | tf_op jit(solution)/shard_map/ppermute | solution.py:129
  81.1 21.7 %collective-permute-start.18 = (bf16[128,1024]{1,0:T(8,128)(2,1)}, bf16[128,1024]{1,0:T(8,128)(2,1)}, u32[]{:S(2)}, u32[]{:S(2)}) collective-permute-start(bf16[128,1024]{1,0:T(8,128)(2,1)} %get-tuple-element.47), channel_id=1, source_target_pairs={{0,16},{4,20},{8,24},{12,28},{16,0},{20,4},{24,8},{28,12},{1,17},{... | collective-permute-start | bytes 786440 | tf_op jit(solution)/shard_map/ppermute | solution.py:129
  81.1 21.7 %collective-permute-start.19 = (bf16[128,1024]{1,0:T(8,128)(2,1)}, bf16[128,1024]{1,0:T(8,128)(2,1)}, u32[]{:S(2)}, u32[]{:S(2)}) collective-permute-start(bf16[128,1024]{1,0:T(8,128)(2,1)} %get-tuple-element.48), channel_id=1, source_target_pairs={{0,24},{4,28},{8,16},{12,20},{16,8},{20,12},{24,0},{28,4},{1,25},{... | collective-permute-start | bytes 786440 | tf_op jit(solution)/shard_map/ppermute | solution.py:129
  84.3 1.3 copy-start.2
  85.7 1.3 copy-start.4
  87.0 7.9 %copy-start.14 = (bf16[128,1024]{1,0:T(8,128)(2,1)S(1)}, bf16[128,1024]{1,0:T(8,128)(2,1)}, u32[]{:S(2)}) copy-start(bf16[128,1024]{1,0:T(8,128)(2,1)} %get-tuple-element.51) | copy-start | bytes 786436
  87.0 7.9 %copy-start.25 = (f32[1024]{0:T(1024)S(1)}, f32[1024]{0:T(1024)}, u32[]{:S(2)}) copy-start(f32[1024]{0:T(1024)} %get-tuple-element.67) | copy-start | bytes 12292
  87.0 7.9 %copy-start.29 = (bf16[2048,1024]{1,0:T(8,128)(2,1)S(1)}, bf16[2048,1024]{1,0:T(8,128)(2,1)}, u32[]{:S(2)}) copy-start(bf16[2048,1024]{1,0:T(8,128)(2,1)} %param.14) | copy-start | bytes 12582916
  92.1 0.8 copy-start.7
  92.9 0.8 copy-start.9
  93.8 2.3 %copy-start.10 = (bf16[280,1024]{1,0:T(8,128)(2,1)S(1)}, bf16[280,1024]{1,0:T(8,128)(2,1)}, u32[]{:S(2)}) copy-start(bf16[280,1024]{1,0:T(8,128)(2,1)} %copy-done.9) | copy-start | bytes 1720324
  93.8 3.3 %copy-start.8 = (bf16[280,1024]{1,0:T(8,128)(2,1)S(1)}, bf16[280,1024]{1,0:T(8,128)(2,1)}, u32[]{:S(2)}) copy-start(bf16[280,1024]{1,0:T(8,128)(2,1)} %copy-done.7) | copy-start | bytes 1720324
  93.8 24.6 %collective-permute-start.14 = (bf16[280,1024]{1,0:T(8,128)(2,1)}, bf16[280,1024]{1,0:T(8,128)(2,1)S(1)}, u32[]{:S(2)}, u32[]{:S(2)}) collective-permute-start(bf16[280,1024]{1,0:T(8,128)(2,1)} %get-tuple-element.43), channel_id=1, source_target_pairs={{0,8},{4,12},{8,0},{12,4},{16,24},{20,28},{24,16},{28,20},{1,9},{5... | collective-permute-start | bytes 1720328 | tf_op jit(solution)/shard_map/ppermute | solution.py:129
  96.1 49.1 %collective-permute-start.15 = (bf16[280,1024]{1,0:T(8,128)(2,1)S(1)}, bf16[280,1024]{1,0:T(8,128)(2,1)S(1)}, u32[]{:S(2)}, u32[]{:S(2)}) collective-permute-start(bf16[280,1024]{1,0:T(8,128)(2,1)S(1)} %copy-done.10), channel_id=1, source_target_pairs={{0,16},{4,20},{8,24},{12,28},{16,0},{20,4},{24,8},{28,12},{1,17},{... | collective-permute-start | bytes 1720328 | tf_op jit(solution)/shard_map/ppermute | solution.py:129
  97.1 48.1 %collective-permute-start.16 = (bf16[280,1024]{1,0:T(8,128)(2,1)S(1)}, bf16[280,1024]{1,0:T(8,128)(2,1)}, u32[]{:S(2)}, u32[]{:S(2)}) collective-permute-start(bf16[280,1024]{1,0:T(8,128)(2,1)S(1)} %copy-done.8), channel_id=1, source_target_pairs={{0,24},{4,28},{8,16},{12,20},{16,8},{20,12},{24,0},{28,4},{1,25},{... | collective-permute-start | bytes 1720328 | tf_op jit(solution)/shard_map/ppermute | solution.py:129
  107.0 42.4 %copy-start.26 = (f32[128]{0:T(128)S(1)}, f32[128]{0:T(128)}, u32[]{:S(2)}) copy-start(f32[128]{0:T(128)} %get-tuple-element.50) | copy-start | bytes 1540
  107.0 42.5 %copy-start.24 = (f32[1024]{0:T(1024)S(1)}, f32[1024]{0:T(1024)}, u32[]{:S(2)}) copy-start(f32[1024]{0:T(1024)} %get-tuple-element.66) | copy-start | bytes 12292
  145.2 4.2 %copy-start.32 = (f32[128,1024]{1,0:T(8,128)S(1)}, f32[128,1024]{1,0:T(8,128)}, u32[]{:S(2)}) copy-start(f32[128,1024]{1,0:T(8,128)} %fusion.2) | copy-start | bytes 1572868
  149.4 3.4 %collective-permute-start.22 = (f32[256]{0:T(256)S(1)}, f32[256]{0:T(256)S(1)}, u32[]{:S(2)}, u32[]{:S(2)}) collective-permute-start(f32[256]{0:T(256)S(1)} %maximum_add_fusion.1), channel_id=1, source_target_pairs={{0,1},{1,0},{2,3},{3,2},{4,5},{5,4},{6,7},{7,6},{8,9},{9,8},{10,11... | collective-permute-start | bytes 3080 | tf_op jit(solution)/shard_map/ppermute | solution.py:23
  152.0 23.3 %copy-start.28 = (s32[4]{0:T(128)S(1)}, s32[4]{0:T(128)}, u32[]{:S(2)}) copy-start(s32[4]{0:T(128)} %param.18) | copy-start | bytes 52
  152.0 23.3 %copy-start.12 = (s32[4,128,1]{2,1,0:T(8,128)S(1)}, s32[4,128,1]{2,1,0:T(8,128)}, u32[]{:S(2)}) copy-start(s32[4,128,1]{2,1,0:T(8,128)} %add.333) | copy-start | bytes 6148
  152.0 23.3 %copy-start.15 = (pred[4,128,1]{2,1,0:T(8,128)(4,1)S(1)}, pred[4,128,1]{2,1,0:T(8,128)(4,1)}, u32[]{:S(2)}) copy-start(pred[4,128,1]{2,1,0:T(8,128)(4,1)} %broadcast_in_dim.28) | copy-start | bytes 1540
  152.0 23.3 %copy-start.22 = (s32[128]{0:T(128)S(1)}, s32[128]{0:T(128)}, u32[]{:S(2)}) copy-start(s32[128]{0:T(128)} %copy-done.21) | copy-start | bytes 1540
  152.0 3.2 %collective-permute-start.20 = (bf16[2,256,256]{2,1,0:T(8,128)(2,1)S(1)}, bf16[2,256,256]{2,1,0:T(8,128)(2,1)S(1)}, u32[]{:S(2)}, u32[]{:S(2)}) collective-permute-start(bf16[2,256,256]{2,1,0:T(8,128)(2,1)S(1)} %pad_maximum_fusion.1), channel_id=1, source_target_pairs={{0,1},{1,0},{2,3},{3,2},{4,5},{5,4},{6,7},{7,6},{8,9},{9,8},{10,11... | collective-permute-start | bytes 786440 | tf_op jit(solution)/shard_map/ppermute | solution.py:23
  152.6 30.8 %copy-start.5 = (s32[256,1]{1,0:T(8,128)S(1)}, s32[256,1]{1,0:T(8,128)}, u32[]{:S(2)}) copy-start(s32[256,1]{1,0:T(8,128)} %add.334.all_ref) | copy-start | bytes 3076
  152.7 30.8 %copy-start.6 = (bf16[4,128,1024]{2,1,0:T(8,128)(2,1)S(1)}, bf16[4,128,1024]{2,1,0:T(8,128)(2,1)}, u32[]{:S(2)}) copy-start(bf16[4,128,1024]{2,1,0:T(8,128)(2,1)} %query_ref.1) | copy-start | bytes 3145732
  152.7 30.8 %copy-start.11 = (bf16[4,128,256]{2,1,0:T(8,128)(2,1)S(1)}, bf16[4,128,256]{2,1,0:T(8,128)(2,1)}, u32[]{:S(2)}) copy-start(bf16[4,128,256]{2,1,0:T(8,128)(2,1)} %text_ref.1) | copy-start | bytes 786436
  152.8 3.9 %collective-permute-start.23 = (f32[256]{0:T(256)S(1)}, f32[256]{0:T(256)S(1)}, u32[]{:S(2)}, u32[]{:S(2)}) collective-permute-start(f32[256]{0:T(256)S(1)} %add.309), channel_id=1, source_target_pairs={{0,2},{1,3},{2,0},{3,1},{4,6},{5,7},{6,4},{7,5},{8,10},{9,11},{10,... | collective-permute-start | bytes 3080 | tf_op jit(solution)/shard_map/ppermute | solution.py:23
  155.3 5.2 %collective-permute-start.21 = (bf16[1,256,256]{2,1,0:T(8,128)(2,1)S(1)}, bf16[1,256,256]{2,1,0:T(8,128)(2,1)S(1)}, u32[]{:S(2)}, u32[]{:S(2)}) collective-permute-start(bf16[1,256,256]{2,1,0:T(8,128)(2,1)S(1)} %dynamic-slice_convert_fusion), channel_id=1, source_target_pairs={{0,2},{1,3},{2,0},{3,1},{4,6},{5,7},{6,4},{7,5},{8,10},{9,11},{10,... | collective-permute-start | bytes 393224 | tf_op jit(solution)/shard_map/ppermute | solution.py:23
  161.5 21.9 %all-to-all-start = ((bf16[8,64,256]{2,1,0:T(8,128)(2,1)}), bf16[8,64,256]{2,1,0:T(8,128)(2,1)S(1)}, u32[]{:S(2)}, u32[]{:S(2)}) async-start(bf16[8,64,256]{2,1,0:T(8,128)(2,1)} %bitcast.17), calls=%async_computation | async-start | bytes 524288 | tf_op jit(solution)/shard_map/all_to_all | solution.py:421
